TPU v7x, 32 devices: a whole 2x2x4 slice. The times are simulated.
32 devices in a mesh: mol: 2 (over y), pair: 4 (over z), tile: 2 (over x), sub: 2 (over core).
Axes of the slice: x: 2, y: 2, z: 4, core: 2. Of those that a mesh axis runs over, the one named last changes fastest.
Arguments:
- lambda_amps: bfloat16 [8, 2, 32, 128, 512], P(('mol', 'pair'), 'sub', None, None, 'tile'), parts along dimension 0, may hold values from -6 to 6
- integral_tiles: bfloat16 [8, 128, 128], P(('mol', 'pair')), parts along dimension 0, may hold values from -0.5 to 0.5
- tile_of: int32 [8, 2, 32], P(('mol', 'pair'), 'sub'), parts along dimension 0, may hold values from 0 to 3
- tile_mask: int32 [8, 2, 32, 4], P(('mol', 'pair'), 'sub', None, 'tile'), parts along dimension 0, may hold values 0 or 1
- pair_list: int32 [512, 2], P('mol'), parts along dimension 0, may hold values from 0 to 399
- coupling: float32 [800, 400], P('mol'), parts along dimension 0, may hold values from -1 to 1
- pair_gap: float32 [8, 2, 32], P('mol', 'sub'), parts along dimension 0, may hold values from 0.5 to 4
- row_energy: float32 [256], P(('mol', 'pair')), parts along dimension 0, may hold values from 0.5 to 4
- col_energy: float32 [1024], P(('mol', 'tile')), parts along dimension 0, may hold values from 0.5 to 4
Outputs:
- new_lambda: bfloat16 [8, 2, 32, 128, 512], P('mol', 'sub', None, 'pair', 'tile'), parts along dimension 0
There are 2 independent parts, one for each index of `mol`. A program takes and returns all parts, laid end to end along the dimension named above; each array names one. Nothing has to cross between parts.
Inputs may be any that keep to these rules, and one draw needn't show every extreme that they name: `tile_of`: an index into the 4 integral tiles.
All inputs are finite; a program needn't handle non-finite values. No bound on the sum of `tile_mask` on one device may be relied on, other than what follows from the above.
Results may differ from a plain program's by a relative error of at most 0.0055.
Values may be sent and summed in bfloat16 or wider, within the bound.
No kernel may reach another device: no remote copies, remote signals or barrier semaphores. Data moves between devices by JAX's collectives and lax.ppermute only.
A program may use at most 64 MiB of HBM per device.

v0:
```python
import math

import jax
import jax.numpy as jnp
from jax import lax
from jax.sharding import PartitionSpec as P


def column_tables(coupling, col_pairs):
    left_table = jnp.take(coupling.T, col_pairs[:, 0], axis=0).T
    right_table = jnp.take(coupling.T, col_pairs[:, 1], axis=0).T
    return (left_table, right_table)


def cycle_rows(left_table, right_table, row_pairs, flat_rhs):
    left_part = jnp.take(left_table, row_pairs[:, 0], axis=0)
    right_part = jnp.take(right_table, row_pairs[:, 1], axis=0)
    weights = (left_part * right_part).astype(jnp.bfloat16)
    return jnp.dot(weights, flat_rhs, preferred_element_type=jnp.float32)


def cycle_all(coupling, pair_list, col_pairs, flat_rhs):
    total_pairs = pair_list.shape[0]
    step_rows = math.gcd(total_pairs, 512)
    row_blocks = pair_list.reshape(total_pairs // step_rows, step_rows, 2)
    left_table, right_table = column_tables(coupling, col_pairs)

    def one_block(row_pairs):
        return cycle_rows(left_table, right_table, row_pairs, flat_rhs)

    return lax.map(one_block, row_blocks).reshape(total_pairs, -1)


def local(
    lambda_amps,
    integral_tiles,
    tile_of,
    tile_mask,
    pair_list,
    coupling,
    pair_gap,
    row_energy,
    col_energy,
):
    pair_count = lambda_amps.shape[2]
    tile_rows = lambda_amps.shape[3]
    col_count = lambda_amps.shape[4]
    owners = lax.axis_size("pair")
    sub_count = lax.axis_size("sub")
    wanted = tile_of.reshape(pair_count)
    empty_tiles = jnp.zeros((pair_count, tile_rows, tile_rows), integral_tiles.dtype)
    shard_piece = lax.all_gather(integral_tiles, "pair", axis=0, tiled=True)
    inside = (wanted >= 0) & (wanted < shard_piece.shape[0])
    taken_rows = shard_piece[jnp.clip(wanted, 0, shard_piece.shape[0] - 1)]
    chosen = jnp.where(inside[:, None, None], taken_rows, empty_tiles)
    amplitudes = lambda_amps.reshape(pair_count, tile_rows, col_count)
    ladder = jnp.einsum("pac,pcb->pab", chosen, amplitudes, preferred_element_type=jnp.float32)
    blocks = tile_mask.shape[3]
    keep_mask = tile_mask.reshape(pair_count, 1, blocks, 1).astype(jnp.float32)
    ladder = (
        ladder.reshape(pair_count, tile_rows, blocks, col_count // blocks) * keep_mask
    ).reshape(pair_count, tile_rows, col_count)
    dressed = (amplitudes.astype(jnp.float32) + ladder).astype(jnp.bfloat16)
    dressed = dressed.reshape(1, 1, pair_count, tile_rows, col_count)
    relayed = lax.all_to_all(dressed, "pair", split_axis=3, concat_axis=0, tiled=True)
    sub_index = lax.axis_index("sub")
    block_ids = jnp.arange(owners, dtype=jnp.int32) * sub_count + sub_index
    mine_ids = (
        block_ids[:, None] * pair_count + jnp.arange(pair_count, dtype=jnp.int32)[None, :]
    ).reshape(-1)
    col_pairs = pair_list[mine_ids]
    flat_rhs = relayed.reshape(owners * pair_count, -1)
    partial_value = cycle_all(coupling, pair_list, col_pairs, flat_rhs)
    partial_value = partial_value.reshape(
        owners, sub_count, pair_count, relayed.shape[3], col_count
    )
    cycle_term = lax.psum_scatter(
        partial_value.astype(jnp.bfloat16), "sub", scatter_dimension=1, tiled=True
    ).astype(jnp.float32)
    total_sum = relayed.astype(jnp.float32) + cycle_term
    energy_gap = (
        pair_gap[:, :, :, None, None]
        + row_energy[None, None, None, :, None]
        + col_energy[None, None, None, None, :]
    )
    return (-total_sum / energy_gap).astype(jnp.bfloat16)


def solution(mesh):
    placed = (
        P(("mol", "pair"), "sub", None, None, "tile"),
        P(("mol", "pair"), None, None),
        P(("mol", "pair"), "sub", None),
        P(("mol", "pair"), "sub", None, "tile"),
        P("mol", None),
        P("mol", None),
        P("mol", "sub", None),
        P(("mol", "pair")),
        P(("mol", "tile")),
    )
    return jax.shard_map(
        local,
        mesh=mesh,
        in_specs=placed,
        out_specs=P("mol", "sub", None, "pair", "tile"),
        check_vma=False,
    )
```

profile of v0, /device:TPU:0, one launch (start us, length us, event | category | flops | bytes accessed | tf_op | source)
XLA Modules:
  0.0 131.2 jit_solution(14051899233420167629)
XLA Ops:
  6.5 0.8 fusion.11
  7.3 0.7 and_bitcast_fusion
  8.0 15.3 %all_gather.3 = bf16[4,128,128]{2,1,0:T(8,128)(2,1)S(1)} all-gather(bf16[1,128,128]{2,1,0:T(8,128)(2,1)} %param.14), channel_id=1, replica_groups=mesh['mol'=2,'pair'=4,'tile'=2,'sub'=2] {'pair'}, dimensions={0}, use_global_device_ids=true | all-gather | bytes 163840 | tf_op jit(solution)/shard_map/all_gather | solution.py:52
  23.3 0.7 convert_bitcast_fusion
  24.0 0.1 copy.26
  24.1 0.1 mul.32
  24.2 0.7 gather_fusion
  24.9 0.0 copy-done
  24.9 0.8 fusion.4
  25.7 2.5 %copy.27 = bf16[1,1,32,128,256]{4,2,1,0,3:T(8,128)(2,1)} copy(bf16[1,1,32,128,256]{4,3,2,1,0:T(8,128)(2,1)S(1)} %fusion.4) | data formatting | bytes 4194304 | tf_op jit(solution)/shard_map/reshape | solution.py:64
  28.2 0.0 copy-start.1
  28.2 5.1 %all-to-all-start = ((bf16[1,1,32,128,256]{4,2,1,0,3:T(8,128)(2,1)}), bf16[1,1,32,128,256]{4,2,1,0,3:T(8,128)(2,1)S(1)}, u32[]{:S(2)}, u32[]{:S(2)}) async-start(bf16[1,1,32,128,256]{4,2,1,0,3:T(8,128)(2,1)} %copy.27), calls=%async_computation | async-start | bytes 4194304 | tf_op jit(solution)/shard_map/all_to_all | solution.py:65
  33.3 0.0 all-reduce.3.cloned.1.call-start
  33.3 0.0 copy-done.1
  33.3 0.1 copy.28
  33.5 0.1 iota_add_fusion
  33.5 0.1 add.127
  33.6 1.4 %copy.29 = f32[400,400]{0,1:T(8,128)S(1)} copy(f32[400,400]{1,0:T(8,128)} %param.18) | data formatting | bytes 1280000 | tf_op args[5]
  35.1 0.6 gather_fusion.1
  35.7 0.2 slice_reduce_fusion.1
  35.9 0.8 gather_fusion.2
  36.7 0.1 select_bitcast_fusion.1
  36.8 0.1 copy.30
  36.9 0.8 gather_fusion.4
  37.7 0.1 select_bitcast_fusion
  37.8 0.1 copy.31
  38.0 0.7 gather_fusion.3
  38.7 0.7 gather_fusion.5
  39.5 0.1 fusion.10
  39.6 38.7 %all-to-all-done = bf16[1,1,32,128,256]{4,2,1,0,3:T(8,128)(2,1)S(1)} async-done(((bf16[1,1,32,128,256]{4,2,1,0,3:T(8,128)(2,1)}), bf16[1,1,32,128,256]{4,2,1,0,3:T(8,128)(2,1)S(1)}, u32[]{:S(2)}, u32[]{:S(2)}) %all-to-all-start) | async-done | bytes 2097184 | tf_op jit(solution)/shard_map/all_to_all | solution.py:65
  78.3 1.2 copy.32
  79.5 2.7 %copy.40 = bf16[16,8,32,256]{3,1,2,0:T(8,128)(2,1)} copy(bf16[16,8,32,256]{3,2,1,0:T(8,128)(2,1)S(1)} %bitcast.68) | data formatting | bytes 4194304
  82.2 4.1 %copy.33 = bf16[8192,128]{1,0:T(8,128)(2,1)} copy(bf16[8192,128]{0,1:T(8,128)(2,1)} %bitcast.67) | data formatting | bytes 4194304 | tf_op jit(solution)/shard_map/while/body/eval_jaxpr/dot_general | solution.py:19
  86.3 4.8 %convolution_convert_fusion = bf16[4,2,32,32,256]{4,2,3,1,0:T(8,128)(2,1)} fusion(bf16[4,2,32,128,1]{3,2,4,1,0:T(8,128)(2,1)S(1)} %bitcast.69, bf16[32,256,128,1,1]{2,1,0,4,3:T(8,128)(2,1)} %bitcast.66), kind=kOutput, calls=%fused_computation.11 | convolution fusion | flops 538968064 | bytes 6356992 | tf_op jit(solution)/shard_map/while/body/eval_jaxpr/dot_general | solution.py:19
  91.1 0.0 copy-start.5
  91.1 0.0 copy-start.2
  91.1 0.0 copy-start.4
  91.1 0.0 copy-start.3
  91.1 0.0 all-reduce.3.cloned.1.call-update
  91.1 0.6 copy-done.5
  91.7 0.6 dynamic-slice.1
  92.3 0.0 copy-done.2
  92.3 0.0 copy-done.4
  92.3 0.1 broadcast_add_fusion
  92.4 26.4 %all-reduce.3.cloned.1.call-done = bf16[4,2,32,32,256]{4,2,3,1,0:T(8,128)(2,1)} async-done(((bf16[4,2,32,32,256]{4,2,3,1,0:T(8,128)(2,1)}), bf16[4,2,32,32,256]{4,2,3,1,0:T(8,128)(2,1)}) %all-reduce.3.cloned.1.call-update) | async-done | bytes 4194320
  118.8 0.0 copy-done.3
  118.8 3.0 %fusion.2 = bf16[4,1,32,32,256]{4,2,3,1,0:T(8,128)(2,1)S(1)} fusion(bf16[4,1,32,32,256]{4,2,3,1,0:T(8,128)(2,1)S(1)} %bitcast.65, bf16[4,2,32,32,256]{4,2,3,1,0:T(8,128)(2,1)} %all-reduce.3.cloned.1.call-done, u32[]{:T(128)} %bitcast.37, f32[256]{0:T(256)S(1)} %copy-done.3, f32[4,32,32]{1,2,0:T(8,128)S(1)} %broadcast_add_fusion), kind=kLoop, calls=%fused_computation.9 | loop fusion | flops 7340032 | bytes 6308868 | tf_op jit(solution)/shard_map/convert_element_type | solution.py:86
  121.8 2.5 %copy.34 = bf16[4,1,32,32,256]{4,3,2,1,0:T(8,128)(2,1)} copy(bf16[4,1,32,32,256]{4,2,3,1,0:T(8,128)(2,1)S(1)} %fusion.2) | data formatting | bytes 4194304 | tf_op jit(solution)/shard_map/convert_element_type | solution.py:86
  (16 shorter events, 0.1 us)
Async XLA Ops:
  6.5 18.4 %copy-start = (bf16[1,1,32,128,256]{4,3,2,1,0:T(8,128)(2,1)S(1)}, bf16[1,1,32,128,256]{4,3,2,1,0:T(8,128)(2,1)}, u32[]{:S(2)}) copy-start(bf16[1,1,32,128,256]{4,3,2,1,0:T(8,128)(2,1)} %param.13) | copy-start | bytes 6291460
  28.2 5.1 %copy-start.1 = (s32[256,2]{0,1:T(2,128)S(1)}, s32[256,2]{0,1:T(2,128)}, u32[]{:S(2)}) copy-start(s32[256,2]{0,1:T(2,128)} %param.17) | copy-start | bytes 6148
  28.2 50.1 %all-to-all-start = ((bf16[1,1,32,128,256]{4,2,1,0,3:T(8,128)(2,1)}), bf16[1,1,32,128,256]{4,2,1,0,3:T(8,128)(2,1)S(1)}, u32[]{:S(2)}, u32[]{:S(2)}) async-start(bf16[1,1,32,128,256]{4,2,1,0,3:T(8,128)(2,1)} %copy.27), calls=%async_computation | async-start | bytes 4194304 | tf_op jit(solution)/shard_map/all_to_all | solution.py:65
  33.3 85.5 %all-reduce.3.cloned.1.call-start = ((), (), s32[]{:S(2)}) async-start(), calls=%async_computation.1 | async-start | bytes 8388608
  91.1 0.7 copy-start.5
  91.1 1.2 copy-start.2
  91.1 1.2 copy-start.4
  91.1 27.7 %copy-start.3 = (f32[256]{0:T(256)S(1)}, f32[256]{0:T(256)}, u32[]{:S(2)}) copy-start(f32[256]{0:T(256)} %param.21) | copy-start | bytes 3076
Sparse Core Ops, SparseCore 0:
  91.2 27.5 all-reduce.2
where the time goes:
time: 132 us; the launch traced here: 131 us
  waiting for transfers between devices  65.1 us (49%)
  local copies, waits for them, and re-layouts  20.9 us (16%)
  blocking collectives  15.3 us (12%)
  between operations  13.6 us (10%)
  other arithmetic  5.67 us (4%)
  matrix products  5.55 us (4%)
  starting transfers between devices  5.1 us (4%)
    all_to_all x1, waiting for transfers between devices, local(): lax.all_to_all(dressed, 'pair', split_axis=3, concat_axis=0, tiled=True)  38.7 us
    unnamed x2, waiting for transfers between devices  26.4 us
    all_gather x1, blocking collectives, local(): shard_piece = lax.all_gather(integral_tiles, 'pair', axis=0, tiled=True)  15.3 us
    unnamed x17, local copies, waits for them, and re-layouts  5.55 us
    all_to_all x1, starting transfers between devices, local(): lax.all_to_all(dressed, 'pair', split_axis=3, concat_axis=0, tiled=True)  5.09 us
    dot_general x1, matrix products, cycle_rows(): return jnp.dot(weights, flat_rhs, preferred_element_type=jnp.float32)  4.79 us
    dot_general x1, local copies, waits for them, and re-layouts, cycle_rows(): return jnp.dot(weights, flat_rhs, preferred_element_type=jnp.float32)  4.06 us
    convert_element_type x1, other arithmetic, local(): return (-total_sum / energy_gap).astype(jnp.bfloat16)  2.99 us
  transfers between devices with their start and end apart: 2, of which 2 were waited for; matrix products, arithmetic and copies ran while one was open for 5% of the time, Pallas kernels for 0%

commit v1 on v0

--- a/solution.py
+++ b/solution.py
@@ -1,9 +1,15 @@
+import functools
 import math
 
 import jax
 import jax.numpy as jnp
 from jax import lax
+from jax.experimental import pallas as pl
+from jax.experimental.pallas import tpu as pltpu
 from jax.sharding import PartitionSpec as P
+
+ROWS = 16
+LANES = 128
 
 
 def column_tables(coupling, col_pairs):
@@ -12,11 +18,10 @@
     return (left_table, right_table)
 
 
-def cycle_rows(left_table, right_table, row_pairs, flat_rhs):
+def cycle_rows(left_table, right_table, row_pairs):
     left_part = jnp.take(left_table, row_pairs[:, 0], axis=0)
     right_part = jnp.take(right_table, row_pairs[:, 1], axis=0)
-    weights = (left_part * right_part).astype(jnp.bfloat16)
-    return jnp.dot(weights, flat_rhs, preferred_element_type=jnp.float32)
+    return (left_part * right_part).astype(jnp.bfloat16)
 
 
 def cycle_all(coupling, pair_list, col_pairs, flat_rhs):
@@ -26,12 +31,13 @@
     left_table, right_table = column_tables(coupling, col_pairs)
 
     def one_block(row_pairs):
-        return cycle_rows(left_table, right_table, row_pairs, flat_rhs)
+        weights = cycle_rows(left_table, right_table, row_pairs)
+        return jnp.dot(weights, flat_rhs, preferred_element_type=jnp.float32)
 
     return lax.map(one_block, row_blocks).reshape(total_pairs, -1)
 
 
-def local(
+def local_general(
     lambda_amps,
     integral_tiles,
     tile_of,
@@ -86,6 +92,194 @@
     return (-total_sum / energy_gap).astype(jnp.bfloat16)
 
 
+def dress_kernel(owners, rows, me_ref, tile_of_ref, mask_ref, *refs):
+    tile_refs, lam_ref = refs[:owners], refs[owners]
+    chunks = rows // ROWS
+    out_refs = refs[owners + 1 : owners + 1 + owners * chunks]
+    tiles, dressed = refs[owners + 1 + owners * chunks :]
+    me = me_ref[0]
+    step = pl.program_id(0)
+
+    @pl.when(step == 0)
+    def _():
+        for k in range(owners):
+            tiles[k] = tile_refs[k][0]
+
+    block = lam_ref.shape[2]
+    for i in range(block):
+        pair = step * block + i
+        amps = lam_ref[0, 0, i]
+        ladder = jnp.dot(
+            tiles[tile_of_ref[0, 0, pair] ^ me], amps, preferred_element_type=jnp.float32
+        )
+        for part in range(mask_ref.shape[3]):
+            width = amps.shape[1] // mask_ref.shape[3]
+            cols = slice(part * width, (part + 1) * width)
+            keep = mask_ref[0, 0, pair, part].astype(jnp.float32)
+            dressed[i, :, cols] = (
+                amps[:, cols].astype(jnp.float32) + keep * ladder[:, cols]
+            ).astype(jnp.bfloat16)
+        for k in range(owners):
+            for c in range(chunks):
+                start = pl.multiple_of((me ^ k) * rows + c * ROWS, ROWS)
+                out_refs[k * chunks + c][i] = dressed[i, pl.ds(start, ROWS), :]
+
+
+def dress(me, tile_of, tile_mask, tiles, lambda_amps):
+    owners = len(tiles)
+    pairs, tile_rows, cols = lambda_amps.shape[2:]
+    rows = tile_rows // owners
+    block = 8
+    pieces = owners * (rows // ROWS)
+    smem = pl.BlockSpec(memory_space=pltpu.SMEM)
+    whole_tile = pl.BlockSpec((1, tile_rows, tile_rows), lambda i: (0, 0, 0))
+    return pl.pallas_call(
+        functools.partial(dress_kernel, owners, rows),
+        grid=(pairs // block,),
+        in_specs=[smem] * 3
+        + [whole_tile] * owners
+        + [pl.BlockSpec((1, 1, block, tile_rows, cols), lambda i: (0, 0, i, 0, 0))],
+        out_specs=[pl.BlockSpec((block, ROWS, cols), lambda i: (i, 0, 0))] * pieces,
+        out_shape=[jax.ShapeDtypeStruct((pairs, ROWS, cols), jnp.bfloat16)] * pieces,
+        scratch_shapes=[
+            pltpu.VMEM((owners, tile_rows, tile_rows), jnp.bfloat16),
+            pltpu.VMEM((block, tile_rows, cols), jnp.bfloat16),
+        ],
+        compiler_params=pltpu.CompilerParams(vmem_limit_bytes=24 * 2**20),
+        cost_estimate=pl.CostEstimate(
+            flops=2 * pairs * tile_rows * tile_rows * cols,
+            bytes_accessed=4 * pairs * tile_rows * cols,
+            transcendentals=0,
+        ),
+    )(me, tile_of, tile_mask, *tiles, lambda_amps)
+
+
+def finish_kernel(pieces, chunk, me_ref, row_ref, w_ref, gap_ref, col_ref, *refs):
+    piece_refs = refs[:pieces]
+    out_ref, xs, ys = refs[-3:]
+    owners = pieces // 2
+    me = me_ref[0]
+    pairs, rows, cols = piece_refs[0].shape
+    for j in range(pieces):
+        values = piece_refs[j][...].reshape(pairs * rows, cols).astype(jnp.float32)
+        xs[pl.ds(j * pairs * rows, pairs * rows), :] = values
+    weights = w_ref[...]
+    base = gap_ref[...]
+    col = col_ref[...]
+    mine = owners * pairs
+    for a in range(rows):
+        part = xs[pl.ds(a, pieces * pairs, stride=rows), :]
+        cycle = jnp.dot(weights, part.astype(jnp.bfloat16), preferred_element_type=jnp.float32)
+        energy = base + row_ref[chunk * rows + a] + col
+        ys[pl.ds(a, mine, stride=rows), :] = -(part[:mine] + cycle) / energy
+    for k in range(owners):
+        values = ys[pl.ds(k * pairs * rows, pairs * rows), :].astype(jnp.bfloat16)
+        out_ref[me ^ k, 0] = values.reshape(pairs, rows, cols)
+
+
+def finish(chunk, me, row_energy, weights, gaps, col_energy, pieces, before, shape):
+    pairs, rows, cols = pieces[0].shape
+    owners = len(pieces) // 2
+    parts = cols // LANES
+    smem = pl.BlockSpec(memory_space=pltpu.SMEM)
+    args = [me, row_energy, weights, gaps, col_energy, *pieces]
+    in_specs = [
+        smem,
+        smem,
+        pl.BlockSpec(weights.shape, lambda i: (0, 0)),
+        pl.BlockSpec(gaps.shape, lambda i: (0, 0)),
+        pl.BlockSpec((1, LANES), lambda i: (0, i)),
+    ] + [pl.BlockSpec((pairs, rows, LANES), lambda i: (0, 0, i))] * len(pieces)
+    aliases = {}
+    if before is not None:
+        aliases = {len(args): 0}
+        args.append(before)
+        in_specs.append(pl.BlockSpec(memory_space=pl.ANY))
+    return pl.pallas_call(
+        functools.partial(finish_kernel, len(pieces), chunk),
+        grid=(parts,),
+        in_specs=in_specs,
+        out_specs=pl.BlockSpec(
+            (owners, 1, pairs, rows, LANES), lambda i: (0, 0, 0, chunk, i)
+        ),
+        out_shape=jax.ShapeDtypeStruct(shape, jnp.bfloat16),
+        scratch_shapes=[
+            pltpu.VMEM((len(pieces) * pairs * rows, LANES), jnp.float32),
+            pltpu.VMEM((owners * pairs * rows, LANES), jnp.float32),
+        ],
+        input_output_aliases=aliases,
+        compiler_params=pltpu.CompilerParams(vmem_limit_bytes=24 * 2**20),
+        cost_estimate=pl.CostEstimate(
+            flops=2 * weights.size * rows * cols,
+            bytes_accessed=3 * len(pieces) * pairs * rows * cols,
+            transcendentals=0,
+        ),
+    )(*args)
+
+
+def local_chunked(
+    lambda_amps,
+    integral_tiles,
+    tile_of,
+    tile_mask,
+    pair_list,
+    coupling,
+    pair_gap,
+    row_energy,
+    col_energy,
+):
+    pairs, tile_rows, cols = lambda_amps.shape[2:]
+    owners = lax.axis_size("pair")
+    subs = lax.axis_size("sub")
+    rows = tile_rows // owners
+    chunks = rows // ROWS
+    me = lax.axis_index("pair")
+    sub = lax.axis_index("sub")
+    me_ref = me.reshape(1).astype(jnp.int32)
+
+    def to_owner(value, k):
+        return lax.ppermute(value, "pair", [(o, o ^ k) for o in range(owners)])
+
+    def to_sibling(value):
+        return lax.ppermute(value, "sub", [(0, 1), (1, 0)])
+
+    tiles = [integral_tiles] + [to_owner(integral_tiles, k) for k in range(1, owners)]
+    sent = dress(me_ref, tile_of, tile_mask, tiles, lambda_amps)
+    order = list(range(owners - 1, 0, -1))
+
+    direct = [[None] * owners for _ in range(chunks)]
+    other = [[None] * owners for _ in range(chunks)]
+    for c in range(chunks):
+        direct[c][0] = sent[c]
+        other[c][0] = to_sibling(sent[c])
+        for k in order:
+            piece = sent[k * chunks + c]
+            direct[c][k] = to_owner(piece, k)
+            other[c][k] = to_sibling(direct[c][k])
+
+    slot_owner = me ^ jnp.arange(owners, dtype=jnp.int32)
+    sub_of = jnp.stack([sub, 1 - sub]).astype(jnp.int32)
+    block_ids = slot_owner[None, :] * subs + sub_of[:, None]
+    ids = (
+        block_ids[:, :, None] * pairs + jnp.arange(pairs, dtype=jnp.int32)
+    ).reshape(-1)
+    slot_pairs = pair_list[ids]
+    left_table, right_table = column_tables(coupling, slot_pairs)
+    weights = cycle_rows(left_table, right_table, slot_pairs[: owners * pairs])
+    gaps = jnp.broadcast_to(
+        pair_gap[slot_owner].reshape(owners * pairs, 1), (owners * pairs, LANES)
+    )
+    col = col_energy.reshape(1, cols)
+
+    shape = (owners, 1, pairs, rows, cols)
+    result = None
+    for c in range(chunks):
+        result = finish(
+            c, me_ref, row_energy, weights, gaps, col, direct[c] + other[c], result, shape
+        )
+    return result
+
+
 def solution(mesh):
     placed = (
         P(("mol", "pair"), "sub", None, None, "tile"),
@@ -98,6 +292,17 @@
         P(("mol", "pair")),
         P(("mol", "tile")),
     )
+    owners, subs = mesh.shape["pair"], mesh.shape["sub"]
+
+    def local(*args):
+        tile_rows, cols = args[0].shape[3:]
+        rows = tile_rows // owners
+        power = owners & (owners - 1) == 0
+        fits = rows % ROWS == 0 and cols % LANES == 0 and args[1].shape[0] == 1
+        if power and fits and subs == 2 and args[0].shape[2] % 8 == 0:
+            return local_chunked(*args)
+        return local_general(*args)
+
     return jax.shard_map(
         local,
         mesh=mesh,

time: 132 us -> 85.5 us (0.65)
  waiting for transfers between devices: 65.1 us -> 25.3 us
  blocking collectives: 15.3 us -> 0 us
  between operations: 13.6 us -> 0.16 us
  Pallas kernels: 0 us -> 11.2 us
  starting transfers between devices: 5.1 us -> 15.1 us
  matrix products: 5.55 us -> 0 us
  local copies, waits for them, and re-layouts: 20.9 us -> 26.2 us
    all_to_all x1 -> x0, waiting for transfers between devices: 38.7 us -> none  [local(): lax.all_to_all(dressed, 'pair', split_axis=3, concat_axis=0, tiled=True)]
    unnamed x2 -> x0, waiting for transfers between devices: 26.4 us -> none
    ppermute x0 -> x17, waiting for transfers between devices: none -> 25.3 us  [the longest x9 25.2 us: to_owner(): return lax.ppermute(value, 'pair', [(o, o ^ k) for o in range(owners)])]
    all_gather x1 -> x0, blocking collectives: 15.3 us -> none  [local(): shard_piece = lax.all_gather(integral_tiles, 'pair', axis=0, tiled=True)]
    ppermute x0 -> x17, starting transfers between devices: none -> 15.1 us  [the longest x9 13.6 us: to_owner(): return lax.ppermute(value, 'pair', [(o, o ^ k) for o in range(owners)])]
    pallas_call x0 -> x3, Pallas kernels: none -> 11.2 us  [the longest x2 8.87 us: finish(): pl.pallas_call(functools.partial(finish_kernel, len(pieces), chunk), grid...]
    dot_general x2 -> x0, matrix products: 5.55 us -> none  [the longest x1 4.79 us: cycle_rows(): return jnp.dot(weights, flat_rhs, preferred_element_type=jnp.float32)]
    all_to_all x1 -> x0, starting transfers between devices: 5.09 us -> none  [local(): lax.all_to_all(dressed, 'pair', split_axis=3, concat_axis=0, tiled=True)]
  transfers between devices with their start and end apart: 2 -> 17, of which waited for: 2 -> 4; matrix products, arithmetic and copies ran while one was open for 5% -> 33% of each run, Pallas kernels for 0% -> 5%
where the time goes in v1:
time: 85.5 us; the launch traced here: 84.2 us
  local copies, waits for them, and re-layouts  26.2 us (31%)
  waiting for transfers between devices  25.3 us (30%)
  starting transfers between devices  15.1 us (18%)
  Pallas kernels  11.2 us (13%)
  other arithmetic  6.34 us (7%)
    ppermute x9, waiting for transfers between devices, to_owner(): return lax.ppermute(value, 'pair', [(o, o ^ k) for o in range(owners)])  25.2 us
    ppermute x9, starting transfers between devices, to_owner(): return lax.ppermute(value, 'pair', [(o, o ^ k) for o in range(owners)])  13.6 us
    pallas_call x2, Pallas kernels, finish(): pl.pallas_call(functools.partial(finish_kernel, len(pieces), chunk), grid...  8.87 us
    unnamed x19, local copies, waits for them, and re-layouts  8.56 us
    gather x1, local copies, waits for them, and re-layouts, column_tables(): left_table = jnp.take(coupling.T, col_pairs[:, 0], axis=0).T  3.16 us
    gather x1, local copies, waits for them, and re-layouts, column_tables(): right_table = jnp.take(coupling.T, col_pairs[:, 1], axis=0).T  3.14 us
    gather x1, local copies, waits for them, and re-layouts, cycle_rows(): right_part = jnp.take(right_table, row_pairs[:, 1], axis=0)  2.4 us
    pallas_call x1, Pallas kernels, dress(): pl.pallas_call(functools.partial(dress_kernel, owners, rows), grid=(pairs...  2.29 us
  transfers between devices with their start and end apart: 17, of which 4 were waited for; matrix products, arithmetic and copies ran while one was open for 33% of the time, Pallas kernels for 5%

profile of v1, /device:TPU:0, one launch (start us, length us, event | category | flops | bytes accessed | tf_op | source)
XLA Modules:
  0.0 84.2 jit_solution(11329547016505068942)
XLA Ops:
  0.0 4.0 %collective-permute-start.1 = (bf16[1,128,128]{2,1,0:T(8,128)(2,1)}, bf16[1,128,128]{2,1,0:T(8,128)(2,1)S(1)}, u32[]{:S(2)}, u32[]{:S(2)}) collective-permute-start(bf16[1,128,128]{2,1,0:T(8,128)(2,1)} %refs_0_.1), channel_id=1, source_target_pairs={{0,8},{4,12},{8,0},{12,4},{1,9},{5,13},{9,1},{13,5},{2,10},{6,14},... | collective-permute-start | bytes 98312 | tf_op jit(solution)/shard_map/ppermute | solution.py:241
  4.0 1.6 %collective-permute-start = (bf16[1,128,128]{2,1,0:T(8,128)(2,1)}, bf16[1,128,128]{2,1,0:T(8,128)(2,1)S(1)}, u32[]{:S(2)}, u32[]{:S(2)}) collective-permute-start(bf16[1,128,128]{2,1,0:T(8,128)(2,1)} %refs_0_.1), channel_id=1, source_target_pairs={{0,4},{4,0},{8,12},{12,8},{1,5},{5,1},{9,13},{13,9},{2,6},{6,2},{1... | collective-permute-start | bytes 98312 | tf_op jit(solution)/shard_map/ppermute | solution.py:241
  5.6 0.1 pad_add_fusion
  5.7 0.1 add_multiply_fusion
  5.8 0.1 iota_add_fusion
  5.9 0.1 add.82
  6.0 0.8 copy.16
  6.8 0.7 gather_fusion
  7.5 0.2 slice_reduce_fusion.3
  7.7 0.2 slice_reduce_fusion.1
  7.9 0.6 compare_and_fusion
  8.5 0.8 copy.20.mask_ref
  9.3 2.3 %collective-permute-done.2.refs_3_ = bf16[1,128,128]{2,1,0:T(8,128)(2,1)S(1)} collective-permute-done((bf16[1,128,128]{2,1,0:T(8,128)(2,1)}, bf16[1,128,128]{2,1,0:T(8,128)(2,1)S(1)}, u32[]{:S(2)}, u32[]{:S(2)}) %collective-permute-start.2) | collective-permute-done | bytes 32800 | tf_op jit(solution)/shard_map/ppermute | solution.py:241
  11.5 1.6 %copy-done.1 = bf16[1,1,32,128,256]{4,3,2,1,0:T(8,128)(2,1)S(1)} copy-done((bf16[1,1,32,128,256]{4,3,2,1,0:T(8,128)(2,1)S(1)}, bf16[1,1,32,128,256]{4,3,2,1,0:T(8,128)(2,1)}, u32[]{:S(2)}) %copy-start.1) | copy-done | bytes 2097176
  13.1 0.8 copy-done.4
  13.9 0.7 copy-done.7
  14.5 2.3 %shard_map.91 = (bf16[32,16,256]{2,1,0:T(8,128)(2,1)S(1)}, bf16[32,16,256]{2,1,0:T(8,128)(2,1)S(1)}, bf16[32,16,256]{2,1,0:T(8,128)(2,1)S(1)}, bf16[32,16,256]{2...) custom-call(s32[1]{0:T(128)} %bitcast.me_ref, ...), custom_call_target="tpu_custom_call" | custom-call | flops 268435456 | bytes 4194304 | tf_op jit(solution)/shard_map/pallas_call | solution.py:136
  16.8 0.1 collective-permute-start.3
  16.9 2.2 %collective-permute-start.4 = (bf16[32,16,256]{2,1,0:T(8,128)(2,1)S(1)}, bf16[32,16,256]{2,1,0:T(8,128)(2,1)S(1)}, u32[]{:S(2)}, u32[]{:S(2)}) collective-permute-start(bf16[32,16,256]{2,1,0:T(8,128)(2,1)S(1)} %get-tuple-element.17), channel_id=1, source_target_pairs={{0,8},{4,12},{8,0},{12,4},{1,9},{5,13},{9,1},{13,5},{2,10},{6,14},... | collective-permute-start | bytes 786440 | tf_op jit(solution)/shard_map/ppermute | solution.py:241
  19.1 0.1 collective-permute-start.10
  19.2 2.7 %collective-permute-start.11 = (bf16[32,16,256]{2,1,0:T(8,128)(2,1)S(1)}, bf16[32,16,256]{2,1,0:T(8,128)(2,1)S(1)}, u32[]{:S(2)}, u32[]{:S(2)}) collective-permute-start(bf16[32,16,256]{2,1,0:T(8,128)(2,1)S(1)} %get-tuple-element.21), channel_id=1, source_target_pairs={{0,8},{4,12},{8,0},{12,4},{1,9},{5,13},{9,1},{13,5},{2,10},{6,14},... | collective-permute-start | bytes 786440 | tf_op jit(solution)/shard_map/ppermute | solution.py:241
  21.9 2.3 %copy.17 = f32[400,400]{0,1:T(8,128)} copy(f32[400,400]{1,0:T(8,128)} %param.18) | data formatting | bytes 1280000 | tf_op args[5]
  24.2 3.2 %gather_fusion.2 = f32[256,400]{1,0:T(8,128)} fusion(f32[400,400]{1,0:T(8,128)} %bitcast.16, s32[1024]{0:T(1024)S(1)} %pad_clamp_fusion.4), kind=kCustom, calls=%fused_computation.clone | custom fusion | bytes 820224 | tf_op jit(solution)/shard_map/jit(_take)/gather | solution.py:16
  27.4 2.0 %select_bitcast_fusion.1 = f32[400,256]{0,1:T(8,128)} fusion(f32[256,400]{1,0:T(8,128)} %gather_fusion.2, pred[256]{0:T(512)(128)(4,1)S(1)} %get-tuple-element.30), kind=kLoop, calls=%fused_computation.7 | loop fusion | flops 102400 | bytes 819456 | tf_op jit(solution)/shard_map/transpose | solution.py:16
  29.3 1.6 %collective-permute-start.5 = (bf16[32,16,256]{2,1,0:T(8,128)(2,1)S(1)}, bf16[32,16,256]{2,1,0:T(8,128)(2,1)S(1)}, u32[]{:S(2)}, u32[]{:S(2)}) collective-permute-start(bf16[32,16,256]{2,1,0:T(8,128)(2,1)S(1)} %get-tuple-element.18), channel_id=1, source_target_pairs={{0,12},{4,8},{8,4},{12,0},{1,13},{5,9},{9,5},{13,1},{2,14},{6,10},... | collective-permute-start | bytes 786440 | tf_op jit(solution)/shard_map/ppermute | solution.py:241
  30.9 2.1 %collective-permute-done.3.refs_1_ = bf16[32,16,256]{2,1,0:T(8,128)(2,1)S(1)} collective-permute-done((bf16[32,16,256]{2,1,0:T(8,128)(2,1)S(1)}, bf16[32,16,256]{2,1,0:T(8,128)(2,1)S(1)}, u32[]{:S(2)}, u32[]{:S(2)}) %collective-permute-start.3) | collective-permute-done | bytes 262176 | tf_op jit(solution)/shard_map/ppermute | solution.py:241
  33.0 1.3 %collective-permute-start.12 = (bf16[32,16,256]{2,1,0:T(8,128)(2,1)S(1)}, bf16[32,16,256]{2,1,0:T(8,128)(2,1)S(1)}, u32[]{:S(2)}, u32[]{:S(2)}) collective-permute-start(bf16[32,16,256]{2,1,0:T(8,128)(2,1)S(1)} %get-tuple-element.22), channel_id=1, source_target_pairs={{0,12},{4,8},{8,4},{12,0},{1,13},{5,9},{9,5},{13,1},{2,14},{6,10},... | collective-permute-start | bytes 786440 | tf_op jit(solution)/shard_map/ppermute | solution.py:241
  34.4 4.3 %collective-permute-done.10.refs_1_ = bf16[32,16,256]{2,1,0:T(8,128)(2,1)S(1)} collective-permute-done((bf16[32,16,256]{2,1,0:T(8,128)(2,1)S(1)}, bf16[32,16,256]{2,1,0:T(8,128)(2,1)S(1)}, u32[]{:S(2)}, u32[]{:S(2)}) %collective-permute-start.10) | collective-permute-done | bytes 262176 | tf_op jit(solution)/shard_map/ppermute | solution.py:241
  38.7 16.6 %collective-permute-done.11.refs_2_ = bf16[32,16,256]{2,1,0:T(8,128)(2,1)S(1)} collective-permute-done((bf16[32,16,256]{2,1,0:T(8,128)(2,1)S(1)}, bf16[32,16,256]{2,1,0:T(8,128)(2,1)S(1)}, u32[]{:S(2)}, u32[]{:S(2)}) %collective-permute-start.11) | collective-permute-done | bytes 262176 | tf_op jit(solution)/shard_map/ppermute | solution.py:241
  55.3 3.1 %gather_fusion.4 = f32[256,400]{1,0:T(8,128)} fusion(f32[400,400]{1,0:T(8,128)} %bitcast.17, s32[1024]{0:T(1024)S(1)} %pad_clamp_fusion.2), kind=kCustom, calls=%fused_computation.2.clone | custom fusion | bytes 820224 | tf_op jit(solution)/shard_map/jit(_take)/gather | solution.py:17
  58.4 1.9 %select_bitcast_fusion = f32[400,256]{0,1:T(8,128)} fusion(f32[256,400]{1,0:T(8,128)} %gather_fusion.4, pred[256]{0:T(512)(128)(4,1)S(1)} %get-tuple-element.29), kind=kLoop, calls=%fused_computation.6 | loop fusion | flops 102400 | bytes 819456 | tf_op jit(solution)/shard_map/transpose | solution.py:17
  60.4 0.5 collective-permute-start.6
  60.9 0.1 collective-permute-start.7
  60.9 0.4 collective-permute-start.8
  61.4 0.7 copy-done.2
  62.1 0.4 collective-permute-start.16
  62.6 0.6 pad_clamp_fusion.3
  63.2 0.6 gather_fusion.1
  63.7 0.6 broadcast_in_dim.31
  64.4 2.0 %copy.18 = f32[400,256]{1,0:T(8,128)} copy(f32[400,256]{0,1:T(8,128)} %select_bitcast_fusion.1) | data formatting | bytes 819200 | tf_op jit(solution)/shard_map/transpose | solution.py:16
  66.4 2.0 %copy.19 = f32[400,256]{1,0:T(8,128)} copy(f32[400,256]{0,1:T(8,128)} %select_bitcast_fusion) | data formatting | bytes 819200 | tf_op jit(solution)/shard_map/transpose | solution.py:17
  68.3 1.9 %gather_fusion.3 = f32[128,256]{1,0:T(8,128)S(1)} fusion(f32[400,256]{1,0:T(8,128)} %copy.18, s32[1024]{0:T(1024)} %pad_clamp_fusion.3), kind=kCustom, calls=%fused_computation.1.clone | custom fusion | bytes 262656 | tf_op jit(solution)/shard_map/jit(_take)/gather | solution.py:22
  70.2 2.4 %gather_fusion.5 = f32[128,256]{1,0:T(8,128)} fusion(f32[400,256]{1,0:T(8,128)} %copy.19, s32[1024]{0:T(1024)S(1)} %pad_clamp_fusion.1), kind=kCustom, calls=%fused_computation.3.clone | custom fusion | bytes 262656 | tf_op jit(solution)/shard_map/jit(_take)/gather | solution.py:23
  72.6 1.0 %fusion.w_ref = bf16[128,256]{1,0:T(8,128)(2,1)S(1)} fusion(f32[128,256]{1,0:T(8,128)} %gather_fusion.5, f32[128,256]{1,0:T(8,128)S(1)} %gather_fusion.3, pred[128]{0:T(512)(128)(4,1)} %get-tuple-element.33, pred[128]{0:T(512)(128)(4,1)} %get-tuple-element.34), kind=kLoop, calls=%fused_computation.11 | loop fusion | flops 131072 | bytes 327936 | tf_op jit(solution)/shard_map/convert_element_type | solution.py:24
  73.7 0.7 broadcast_in_dim.32.gap_ref
  74.4 0.9 %copy-done.3 = bf16[32,16,256]{2,1,0:T(8,128)(2,1)S(1)} copy-done((bf16[32,16,256]{2,1,0:T(8,128)(2,1)S(1)}, bf16[32,16,256]{2,1,0:T(8,128)(2,1)}, u32[]{:S(2)}) %copy-start.3) | copy-done | bytes 262168
  75.3 4.6 %shard_map.92.refs_8_ = bf16[4,1,32,32,256]{4,3,2,1,0:T(8,128)(2,1)} custom-call(s32[1]{0:T(128)} %bitcast.me_ref, f32[32]{0:T(128)S(1)} %copy-done.6, bf16[128,256]{1,0:T(8,128)(2,1)S(1)} %fusion.w_ref, f32[128,128]{1,0:T(8,128)S(1)} %broadcast_in_dim.32.gap_ref, f32[1,256]{1,0:T(1,128)S(1)} %bitcast.14, ...), custom_call_target="tpu_custom_call" | custom-call | flops 268435456 | bytes 3145728 | tf_op jit(solution)/shard_map/pallas_call | solution.py:198
  80.0 4.2 %shard_map.93 = bf16[4,1,32,32,256]{4,3,2,1,0:T(8,128)(2,1)} custom-call(s32[1]{0:T(128)} %bitcast.me_ref, f32[32]{0:T(128)S(1)} %copy-done.6, bf16[128,256]{1,0:T(8,128)(2,1)S(1)} %fusion.w_ref, f32[128,128]{1,0:T(8,128)S(1)} %broadcast_in_dim.32.gap_ref, f32[1,256]{1,0:T(1,128)S(1)} %bitcast.15, ...), custom_call_target="tpu_custom_call", output_to_operand_aliasing={{}: (13, {})} | custom-call | flops 268435456 | bytes 3145728 | tf_op jit(solution)/shard_map/pallas_call | solution.py:198
  (40 shorter events, 0.2 us)
Async XLA Ops:
  0.0 63.2 %copy-start = (f32[4,1,32]{2,1,0:T(1,128)S(1)}, f32[4,1,32]{2,1,0:T(1,128)}, u32[]{:S(2)}) copy-start(f32[4,1,32]{2,1,0:T(1,128)} %param.19) | copy-start | bytes 1540
  0.0 9.3 %collective-permute-start.1 = (bf16[1,128,128]{2,1,0:T(8,128)(2,1)}, bf16[1,128,128]{2,1,0:T(8,128)(2,1)S(1)}, u32[]{:S(2)}, u32[]{:S(2)}) collective-permute-start(bf16[1,128,128]{2,1,0:T(8,128)(2,1)} %refs_0_.1), channel_id=1, source_target_pairs={{0,8},{4,12},{8,0},{12,4},{1,9},{5,13},{9,1},{13,5},{2,10},{6,14},... | collective-permute-start | bytes 98312 | tf_op jit(solution)/shard_map/ppermute | solution.py:241
  4.0 5.2 %collective-permute-start = (bf16[1,128,128]{2,1,0:T(8,128)(2,1)}, bf16[1,128,128]{2,1,0:T(8,128)(2,1)S(1)}, u32[]{:S(2)}, u32[]{:S(2)}) collective-permute-start(bf16[1,128,128]{2,1,0:T(8,128)(2,1)} %refs_0_.1), channel_id=1, source_target_pairs={{0,4},{4,0},{8,12},{12,8},{1,5},{5,1},{9,13},{13,9},{2,6},{6,2},{1... | collective-permute-start | bytes 98312 | tf_op jit(solution)/shard_map/ppermute | solution.py:241
  5.6 5.9 %collective-permute-start.2 = (bf16[1,128,128]{2,1,0:T(8,128)(2,1)}, bf16[1,128,128]{2,1,0:T(8,128)(2,1)S(1)}, u32[]{:S(2)}, u32[]{:S(2)}) collective-permute-start(bf16[1,128,128]{2,1,0:T(8,128)(2,1)} %refs_0_.1), channel_id=1, source_target_pairs={{0,12},{4,8},{8,4},{12,0},{1,13},{5,9},{9,5},{13,1},{2,14},{6,10},... | collective-permute-start | bytes 98312 | tf_op jit(solution)/shard_map/ppermute | solution.py:241
  11.5 1.6 %copy-start.1 = (bf16[1,1,32,128,256]{4,3,2,1,0:T(8,128)(2,1)S(1)}, bf16[1,1,32,128,256]{4,3,2,1,0:T(8,128)(2,1)}, u32[]{:S(2)}) copy-start(bf16[1,1,32,128,256]{4,3,2,1,0:T(8,128)(2,1)} %refs_4_.1) | copy-start | bytes 6291460
  13.1 0.8 copy-start.4
  13.9 0.7 copy-start.7
  16.8 16.2 %collective-permute-start.3 = (bf16[32,16,256]{2,1,0:T(8,128)(2,1)S(1)}, bf16[32,16,256]{2,1,0:T(8,128)(2,1)S(1)}, u32[]{:S(2)}, u32[]{:S(2)}) collective-permute-start(bf16[32,16,256]{2,1,0:T(8,128)(2,1)S(1)} %get-tuple-element.16), channel_id=1, source_target_pairs={{0,4},{4,0},{8,12},{12,8},{1,5},{5,1},{9,13},{13,9},{2,6},{6,2},{1... | collective-permute-start | bytes 786440 | tf_op jit(solution)/shard_map/ppermute | solution.py:241
  16.9 17.5 %collective-permute-start.4 = (bf16[32,16,256]{2,1,0:T(8,128)(2,1)S(1)}, bf16[32,16,256]{2,1,0:T(8,128)(2,1)S(1)}, u32[]{:S(2)}, u32[]{:S(2)}) collective-permute-start(bf16[32,16,256]{2,1,0:T(8,128)(2,1)S(1)} %get-tuple-element.17), channel_id=1, source_target_pairs={{0,8},{4,12},{8,0},{12,4},{1,9},{5,13},{9,1},{13,5},{2,10},{6,14},... | collective-permute-start | bytes 786440 | tf_op jit(solution)/shard_map/ppermute | solution.py:241
  19.1 19.6 %collective-permute-start.10 = (bf16[32,16,256]{2,1,0:T(8,128)(2,1)S(1)}, bf16[32,16,256]{2,1,0:T(8,128)(2,1)S(1)}, u32[]{:S(2)}, u32[]{:S(2)}) collective-permute-start(bf16[32,16,256]{2,1,0:T(8,128)(2,1)S(1)} %get-tuple-element.20), channel_id=1, source_target_pairs={{0,4},{4,0},{8,12},{12,8},{1,5},{5,1},{9,13},{13,9},{2,6},{6,2},{1... | collective-permute-start | bytes 786440 | tf_op jit(solution)/shard_map/ppermute | solution.py:241
  19.2 36.1 %collective-permute-start.11 = (bf16[32,16,256]{2,1,0:T(8,128)(2,1)S(1)}, bf16[32,16,256]{2,1,0:T(8,128)(2,1)S(1)}, u32[]{:S(2)}, u32[]{:S(2)}) collective-permute-start(bf16[32,16,256]{2,1,0:T(8,128)(2,1)S(1)} %get-tuple-element.21), channel_id=1, source_target_pairs={{0,8},{4,12},{8,0},{12,4},{1,9},{5,13},{9,1},{13,5},{2,10},{6,14},... | collective-permute-start | bytes 786440 | tf_op jit(solution)/shard_map/ppermute | solution.py:241
  29.3 31.0 %collective-permute-start.5 = (bf16[32,16,256]{2,1,0:T(8,128)(2,1)S(1)}, bf16[32,16,256]{2,1,0:T(8,128)(2,1)S(1)}, u32[]{:S(2)}, u32[]{:S(2)}) collective-permute-start(bf16[32,16,256]{2,1,0:T(8,128)(2,1)S(1)} %get-tuple-element.18), channel_id=1, source_target_pairs={{0,12},{4,8},{8,4},{12,0},{1,13},{5,9},{9,5},{13,1},{2,14},{6,10},... | collective-permute-start | bytes 786440 | tf_op jit(solution)/shard_map/ppermute | solution.py:241
  33.0 27.8 %collective-permute-start.12 = (bf16[32,16,256]{2,1,0:T(8,128)(2,1)S(1)}, bf16[32,16,256]{2,1,0:T(8,128)(2,1)S(1)}, u32[]{:S(2)}, u32[]{:S(2)}) collective-permute-start(bf16[32,16,256]{2,1,0:T(8,128)(2,1)S(1)} %get-tuple-element.22), channel_id=1, source_target_pairs={{0,12},{4,8},{8,4},{12,0},{1,13},{5,9},{9,5},{13,1},{2,14},{6,10},... | collective-permute-start | bytes 786440 | tf_op jit(solution)/shard_map/ppermute | solution.py:241
  34.4 26.6 %collective-permute-start.13 = (bf16[32,16,256]{2,1,0:T(8,128)(2,1)S(1)}, bf16[32,16,256]{2,1,0:T(8,128)(2,1)S(1)}, u32[]{:S(2)}, u32[]{:S(2)}) collective-permute-start(bf16[32,16,256]{2,1,0:T(8,128)(2,1)S(1)} %get-tuple-element.19.refs_0_), channel_id=1, source_target_pairs={{0,1},{1,0},{2,3},{3,2},{4,5},{5,4},{6,7},{7,6},{8,9},{9,8},{10,11... | collective-permute-start | bytes 786440 | tf_op jit(solution)/shard_map/ppermute | solution.py:244
  38.7 22.7 %collective-permute-start.14 = (bf16[32,16,256]{2,1,0:T(8,128)(2,1)S(1)}, bf16[32,16,256]{2,1,0:T(8,128)(2,1)S(1)}, u32[]{:S(2)}, u32[]{:S(2)}) collective-permute-start(bf16[32,16,256]{2,1,0:T(8,128)(2,1)S(1)} %collective-permute-done.10.refs_1_), channel_id=1, source_target_pairs={{0,1},{1,0},{2,3},{3,2},{4,5},{5,4},{6,7},{7,6},{8,9},{9,8},{10,11... | collective-permute-start | bytes 786440 | tf_op jit(solution)/shard_map/ppermute | solution.py:244
  55.3 6.9 %collective-permute-start.15 = (bf16[32,16,256]{2,1,0:T(8,128)(2,1)S(1)}, bf16[32,16,256]{2,1,0:T(8,128)(2,1)}, u32[]{:S(2)}, u32[]{:S(2)}) collective-permute-start(bf16[32,16,256]{2,1,0:T(8,128)(2,1)S(1)} %collective-permute-done.11.refs_2_), channel_id=1, source_target_pairs={{0,1},{1,0},{2,3},{3,2},{4,5},{5,4},{6,7},{7,6},{8,9},{9,8},{10,11... | collective-permute-start | bytes 786440 | tf_op jit(solution)/shard_map/ppermute | solution.py:244
  60.4 19.6 %collective-permute-start.6 = (bf16[32,16,256]{2,1,0:T(8,128)(2,1)S(1)}, bf16[32,16,256]{2,1,0:T(8,128)(2,1)S(1)}, u32[]{:S(2)}, u32[]{:S(2)}) collective-permute-start(bf16[32,16,256]{2,1,0:T(8,128)(2,1)S(1)} %get-tuple-element.15.refs_0_), channel_id=1, source_target_pairs={{0,1},{1,0},{2,3},{3,2},{4,5},{5,4},{6,7},{7,6},{8,9},{9,8},{10,11... | collective-permute-start | bytes 786440 | tf_op jit(solution)/shard_map/ppermute | solution.py:244
  60.9 19.1 %collective-permute-start.7 = (bf16[32,16,256]{2,1,0:T(8,128)(2,1)S(1)}, bf16[32,16,256]{2,1,0:T(8,128)(2,1)S(1)}, u32[]{:S(2)}, u32[]{:S(2)}) collective-permute-start(bf16[32,16,256]{2,1,0:T(8,128)(2,1)S(1)} %collective-permute-done.3.refs_1_), channel_id=1, source_target_pairs={{0,1},{1,0},{2,3},{3,2},{4,5},{5,4},{6,7},{7,6},{8,9},{9,8},{10,11... | collective-permute-start | bytes 786440 | tf_op jit(solution)/shard_map/ppermute | solution.py:244
  60.9 19.0 %collective-permute-start.8 = (bf16[32,16,256]{2,1,0:T(8,128)(2,1)S(1)}, bf16[32,16,256]{2,1,0:T(8,128)(2,1)S(1)}, u32[]{:S(2)}, u32[]{:S(2)}) collective-permute-start(bf16[32,16,256]{2,1,0:T(8,128)(2,1)S(1)} %collective-permute-done.4.refs_2_), channel_id=1, source_target_pairs={{0,1},{1,0},{2,3},{3,2},{4,5},{5,4},{6,7},{7,6},{8,9},{9,8},{10,11... | collective-permute-start | bytes 786440 | tf_op jit(solution)/shard_map/ppermute | solution.py:244
  61.4 0.7 copy-start.2
  62.1 17.9 %collective-permute-start.9 = (bf16[32,16,256]{2,1,0:T(8,128)(2,1)S(1)}, bf16[32,16,256]{2,1,0:T(8,128)(2,1)S(1)}, u32[]{:S(2)}, u32[]{:S(2)}) collective-permute-start(bf16[32,16,256]{2,1,0:T(8,128)(2,1)S(1)} %collective-permute-done.5.refs_3_), channel_id=1, source_target_pairs={{0,1},{1,0},{2,3},{3,2},{4,5},{5,4},{6,7},{7,6},{8,9},{9,8},{10,11... | collective-permute-start | bytes 786440 | tf_op jit(solution)/shard_map/ppermute | solution.py:244
  62.1 11.5 %collective-permute-start.16 = (bf16[32,16,256]{2,1,0:T(8,128)(2,1)S(1)}, bf16[32,16,256]{2,1,0:T(8,128)(2,1)}, u32[]{:S(2)}, u32[]{:S(2)}) collective-permute-start(bf16[32,16,256]{2,1,0:T(8,128)(2,1)S(1)} %collective-permute-done.12.refs_3_), channel_id=1, source_target_pairs={{0,1},{1,0},{2,3},{3,2},{4,5},{5,4},{6,7},{7,6},{8,9},{9,8},{10,11... | collective-permute-start | bytes 786440 | tf_op jit(solution)/shard_map/ppermute | solution.py:244
  64.4 10.0 %copy-start.5 = (f32[256]{0:T(256)S(1)}, f32[256]{0:T(256)}, u32[]{:S(2)}) copy-start(f32[256]{0:T(256)} %param.21) | copy-start | bytes 3076
  64.4 10.0 %copy-start.6 = (f32[32]{0:T(128)S(1)}, f32[32]{0:T(128)}, u32[]{:S(2)}) copy-start(f32[32]{0:T(128)} %row_ref.3) | copy-start | bytes 388
  74.4 1.0 %copy-start.3 = (bf16[32,16,256]{2,1,0:T(8,128)(2,1)S(1)}, bf16[32,16,256]{2,1,0:T(8,128)(2,1)}, u32[]{:S(2)}) copy-start(bf16[32,16,256]{2,1,0:T(8,128)(2,1)} %copy-done.2) | copy-start | bytes 786436

commit v2 on v1

v2 whole, which is shorter than its diff:
```python
import functools
import math

import jax
import jax.numpy as jnp
from jax import lax
from jax.experimental import pallas as pl
from jax.experimental.pallas import tpu as pltpu
from jax.sharding import PartitionSpec as P

ROWS = 16
LANES = 128
VMEM_BYTES = 24 * 2**20


def column_tables(coupling, col_pairs):
    left_table = jnp.take(coupling.T, col_pairs[:, 0], axis=0).T
    right_table = jnp.take(coupling.T, col_pairs[:, 1], axis=0).T
    return (left_table, right_table)


def cycle_rows(left_table, right_table, row_pairs):
    left_part = jnp.take(left_table, row_pairs[:, 0], axis=0)
    right_part = jnp.take(right_table, row_pairs[:, 1], axis=0)
    return (left_part * right_part).astype(jnp.bfloat16)


def cycle_all(coupling, pair_list, col_pairs, flat_rhs):
    total_pairs = pair_list.shape[0]
    step_rows = math.gcd(total_pairs, 512)
    row_blocks = pair_list.reshape(total_pairs // step_rows, step_rows, 2)
    left_table, right_table = column_tables(coupling, col_pairs)

    def one_block(row_pairs):
        weights = cycle_rows(left_table, right_table, row_pairs)
        return jnp.dot(weights, flat_rhs, preferred_element_type=jnp.float32)

    return lax.map(one_block, row_blocks).reshape(total_pairs, -1)


def local_general(
    lambda_amps,
    integral_tiles,
    tile_of,
    tile_mask,
    pair_list,
    coupling,
    pair_gap,
    row_energy,
    col_energy,
):
    pair_count = lambda_amps.shape[2]
    tile_rows = lambda_amps.shape[3]
    col_count = lambda_amps.shape[4]
    owners = lax.axis_size("pair")
    sub_count = lax.axis_size("sub")
    wanted = tile_of.reshape(pair_count)
    empty_tiles = jnp.zeros((pair_count, tile_rows, tile_rows), integral_tiles.dtype)
    shard_piece = lax.all_gather(integral_tiles, "pair", axis=0, tiled=True)
    inside = (wanted >= 0) & (wanted < shard_piece.shape[0])
    taken_rows = shard_piece[jnp.clip(wanted, 0, shard_piece.shape[0] - 1)]
    chosen = jnp.where(inside[:, None, None], taken_rows, empty_tiles)
    amplitudes = lambda_amps.reshape(pair_count, tile_rows, col_count)
    ladder = jnp.einsum("pac,pcb->pab", chosen, amplitudes, preferred_element_type=jnp.float32)
    blocks = tile_mask.shape[3]
    keep_mask = tile_mask.reshape(pair_count, 1, blocks, 1).astype(jnp.float32)
    ladder = (
        ladder.reshape(pair_count, tile_rows, blocks, col_count // blocks) * keep_mask
    ).reshape(pair_count, tile_rows, col_count)
    dressed = (amplitudes.astype(jnp.float32) + ladder).astype(jnp.bfloat16)
    dressed = dressed.reshape(1, 1, pair_count, tile_rows, col_count)
    relayed = lax.all_to_all(dressed, "pair", split_axis=3, concat_axis=0, tiled=True)
    sub_index = lax.axis_index("sub")
    block_ids = jnp.arange(owners, dtype=jnp.int32) * sub_count + sub_index
    mine_ids = (
        block_ids[:, None] * pair_count + jnp.arange(pair_count, dtype=jnp.int32)[None, :]
    ).reshape(-1)
    col_pairs = pair_list[mine_ids]
    flat_rhs = relayed.reshape(owners * pair_count, -1)
    partial_value = cycle_all(coupling, pair_list, col_pairs, flat_rhs)
    partial_value = partial_value.reshape(
        owners, sub_count, pair_count, relayed.shape[3], col_count
    )
    cycle_term = lax.psum_scatter(
        partial_value.astype(jnp.bfloat16), "sub", scatter_dimension=1, tiled=True
    ).astype(jnp.float32)
    total_sum = relayed.astype(jnp.float32) + cycle_term
    energy_gap = (
        pair_gap[:, :, :, None, None]
        + row_energy[None, None, None, :, None]
        + col_energy[None, None, None, None, :]
    )
    return (-total_sum / energy_gap).astype(jnp.bfloat16)


def one_hot(shape, hits):
    return jnp.where(hits, 1.0, 0.0).astype(jnp.bfloat16).reshape(shape)


def swap_matrix():
    size = ROWS * ROWS
    to = lax.broadcasted_iota(jnp.int32, (size, size), 0)
    frm = lax.broadcasted_iota(jnp.int32, (size, size), 1)
    hits = to == (frm % ROWS) * ROWS + frm // ROWS
    return one_hot((size, size), hits)


def split3(value):
    high = value.astype(jnp.bfloat16)
    rest = value - high.astype(jnp.float32)
    mid = rest.astype(jnp.bfloat16)
    low = (rest - mid.astype(jnp.float32)).astype(jnp.bfloat16)
    return high, mid, low


def pick_columns(value, columns):
    high, mid, low = (
        jnp.dot(part, columns, preferred_element_type=jnp.float32) for part in split3(value)
    )
    return high + (mid + low)


def pick_rows(columns, value):
    dims = (((0,), (0,)), ((), ()))
    high, mid, low = (
        lax.dot_general(columns, part, dims, preferred_element_type=jnp.float32)
        for part in split3(value)
    )
    return high + (mid + low)


def weights_kernel(pair_ref, coupling_ref, gap_ref, sub_ref, w_ref, gaps_ref, full):
    total = pair_ref.shape[1]
    depth = coupling_ref.shape[0]
    orbital = lax.broadcasted_iota(jnp.int32, (depth, total), 0)
    coupling = coupling_ref[...]
    product = None
    for side in range(2):
        columns = one_hot((depth, total), orbital == pair_ref[side : side + 1, :])
        picked = pick_rows(columns, pick_columns(coupling, columns))
        product = picked if product is None else product * picked
    full[...] = product
    owners, _, pairs = gap_ref.shape
    subs = total // (owners * pairs)
    diagonal = lax.broadcasted_iota(jnp.int32, (pairs, pairs), 0) == lax.broadcasted_iota(
        jnp.int32, (pairs, pairs), 1
    )
    for o in range(owners):
        start = pl.multiple_of((o * subs + sub_ref[0]) * pairs, pairs)
        rows = pl.ds(o * pairs, pairs)
        w_ref[rows, :] = full[pl.ds(start, pairs), :].astype(jnp.bfloat16)
        column = jnp.sum(jnp.where(diagonal, gap_ref[o], 0.0), axis=1, keepdims=True)
        gaps_ref[rows, :] = jnp.broadcast_to(column, (pairs, LANES))


def make_weights(pair_list, coupling, pair_gap, sub_ref):
    owners, _, pairs = pair_gap.shape
    total = pair_list.shape[0]
    mine = owners * pairs
    vmem = pl.BlockSpec(memory_space=pltpu.VMEM)
    return pl.pallas_call(
        weights_kernel,
        in_specs=[vmem, vmem, vmem, pl.BlockSpec(memory_space=pltpu.SMEM)],
        out_specs=[vmem, vmem],
        out_shape=[
            jax.ShapeDtypeStruct((mine, total), jnp.bfloat16),
            jax.ShapeDtypeStruct((mine, LANES), jnp.float32),
        ],
        scratch_shapes=[pltpu.VMEM((total, total), jnp.float32)],
        compiler_params=pltpu.CompilerParams(vmem_limit_bytes=VMEM_BYTES),
        cost_estimate=pl.CostEstimate(
            flops=12 * total * coupling.size, bytes_accessed=4 * coupling.size, transcendentals=0
        ),
    )(pair_list.T, coupling, pair_gap, sub_ref)


def dress_kernel(owners, rows, chunk, me_ref, tile_of_ref, mask_ref, *refs):
    tile_refs, lam_ref = refs[:owners], refs[owners]
    out_refs = refs[owners + 1 : 2 * owners + 1]
    tiles = refs[-1]
    me = me_ref[0]
    step = pl.program_id(0)
    starts = [pl.multiple_of((me ^ k) * rows + chunk * ROWS, ROWS) for k in range(owners)]

    @pl.when(step == 0)
    def _():
        for k in range(owners):
            for j in range(owners):
                tiles[k, pl.ds(j * ROWS, ROWS), :] = tile_refs[k][0, pl.ds(starts[j], ROWS), :]

    block = lam_ref.shape[2]
    parts = mask_ref.shape[2]
    for i in range(block):
        pair = step * block + i
        ladder = jnp.dot(
            tiles[tile_of_ref[0, 0, pair] ^ me],
            lam_ref[0, 0, i],
            preferred_element_type=jnp.float32,
        )
        width = ladder.shape[1] // parts
        for part in range(parts):
            keep = mask_ref[0, 0, part, pair].astype(jnp.float32)
            cols = slice(part * width, (part + 1) * width)
            for k in range(owners):
                amps = lam_ref[0, 0, i, pl.ds(starts[k], ROWS), cols].astype(jnp.float32)
                kept = keep * ladder[k * ROWS : (k + 1) * ROWS, cols]
                out_refs[k][i, :, cols] = (amps + kept).astype(jnp.bfloat16)


def dress(chunk, me, tile_of, tile_mask, tiles, lambda_amps):
    owners = len(tiles)
    pairs, tile_rows, cols = lambda_amps.shape[2:]
    rows = tile_rows // owners
    block = 8
    smem = pl.BlockSpec(memory_space=pltpu.SMEM)
    whole_tile = pl.BlockSpec((1, tile_rows, tile_rows), lambda i: (0, 0, 0))
    return pl.pallas_call(
        functools.partial(dress_kernel, owners, rows, chunk),
        grid=(pairs // block,),
        in_specs=[smem] * 3
        + [whole_tile] * owners
        + [pl.BlockSpec((1, 1, block, tile_rows, cols), lambda i: (0, 0, i, 0, 0))],
        out_specs=[pl.BlockSpec((block, ROWS, cols), lambda i: (i, 0, 0))] * owners,
        out_shape=[jax.ShapeDtypeStruct((pairs, ROWS, cols), jnp.bfloat16)] * owners,
        scratch_shapes=[pltpu.VMEM((owners, owners * ROWS, tile_rows), jnp.bfloat16)],
        compiler_params=pltpu.CompilerParams(vmem_limit_bytes=VMEM_BYTES),
        cost_estimate=pl.CostEstimate(
            flops=2 * pairs * owners * ROWS * tile_rows * cols,
            bytes_accessed=3 * pairs * tile_rows * cols,
            transcendentals=0,
        ),
    )(me, tile_of, jnp.swapaxes(tile_mask, 2, 3), *tiles, lambda_amps)


def finish_kernel(pieces, chunk, place_ref, row_ref, w_ref, gap_ref, col_ref, *refs):
    piece_refs = refs[:pieces]
    out_ref, landed, xs, ys, done, in_sems, out_sems = refs[-7:]
    pairs, rows, cols = piece_refs[0].shape
    owners = pieces // 2
    halves = pairs // ROWS
    me, sub = place_ref[0], place_ref[1]
    arrivals = [
        pltpu.make_async_copy(piece_refs[j], landed.at[j], in_sems.at[j]) for j in range(pieces)
    ]
    for copy in arrivals:
        copy.start()
    swap = swap_matrix()
    for j in range(pieces):
        arrivals[j].wait()
        block = ((me ^ (j % owners)) * 2 + (sub ^ (j // owners))) * pairs
        for h in range(halves):
            rows_in = landed[j, pl.ds(h * ROWS, ROWS)].reshape(ROWS * rows, cols)
            turned = jnp.dot(swap, rows_in, preferred_element_type=jnp.float32)
            place = pl.multiple_of(block + h * ROWS, ROWS)
            xs[:, pl.ds(place, ROWS), :] = turned.astype(jnp.bfloat16).reshape(rows, ROWS, cols)
    weights = w_ref[...]
    col = col_ref[...]
    for a in range(rows):
        cycle = jnp.dot(weights, xs[a], preferred_element_type=jnp.float32)
        row = row_ref[chunk * rows + a]
        for o in range(owners):
            mine = slice(o * pairs, (o + 1) * pairs)
            start = pl.multiple_of((o * 2 + sub) * pairs, pairs)
            own = xs[a, pl.ds(start, pairs), :].astype(jnp.float32)
            level = gap_ref[mine, :] + row
            energy = jnp.concatenate([level] * (cols // LANES), axis=1) + col
            value = (-(own + cycle[mine]) / energy).astype(jnp.bfloat16)
            for h in range(halves):
                ys[o * halves + h, pl.ds(a * ROWS, ROWS), :] = value[h * ROWS : (h + 1) * ROWS]
    leaving = []
    for g in range(owners * halves):
        turned = jnp.dot(swap, ys[g], preferred_element_type=jnp.float32)
        done[g] = turned.astype(jnp.bfloat16).reshape(ROWS, rows, cols)
        o, h = g // halves, g % halves
        copy = pltpu.make_async_copy(
            done.at[g],
            out_ref.at[o, 0, pl.ds(h * ROWS, ROWS), pl.ds(chunk * rows, rows), :],
            out_sems.at[g],
        )
        copy.start()
        leaving.append(copy)
    for copy in leaving:
        copy.wait()


def finish(chunk, place, row_energy, weights, gaps, col_energy, pieces, before, shape):
    pairs, rows, cols = pieces[0].shape
    owners = len(pieces) // 2
    groups = owners * (pairs // ROWS)
    smem = pl.BlockSpec(memory_space=pltpu.SMEM)
    vmem = pl.BlockSpec(memory_space=pltpu.VMEM)
    anywhere = pl.BlockSpec(memory_space=pl.ANY)
    args = [place, row_energy, weights, gaps, col_energy, *pieces]
    in_specs = [smem, smem, vmem, vmem, vmem] + [anywhere] * len(pieces)
    aliases = {}
    if before is not None:
        aliases = {len(args): 0}
        args.append(before)
        in_specs.append(anywhere)
    return pl.pallas_call(
        functools.partial(finish_kernel, len(pieces), chunk),
        in_specs=in_specs,
        out_specs=anywhere,
        out_shape=jax.ShapeDtypeStruct(shape, jnp.bfloat16),
        scratch_shapes=[
            pltpu.VMEM((len(pieces), pairs, rows, cols), jnp.bfloat16),
            pltpu.VMEM((rows, len(pieces) * pairs, cols), jnp.bfloat16),
            pltpu.VMEM((groups, ROWS * rows, cols), jnp.bfloat16),
            pltpu.VMEM((groups, ROWS, rows, cols), jnp.bfloat16),
            pltpu.SemaphoreType.DMA((len(pieces),)),
            pltpu.SemaphoreType.DMA((groups,)),
        ],
        input_output_aliases=aliases,
        compiler_params=pltpu.CompilerParams(vmem_limit_bytes=VMEM_BYTES),
        cost_estimate=pl.CostEstimate(
            flops=8 * weights.size * rows * cols,
            bytes_accessed=3 * len(pieces) * pairs * rows * cols,
            transcendentals=0,
        ),
    )(*args)


def local_chunked(
    lambda_amps,
    integral_tiles,
    tile_of,
    tile_mask,
    pair_list,
    coupling,
    pair_gap,
    row_energy,
    col_energy,
):
    pairs, tile_rows, cols = lambda_amps.shape[2:]
    owners = lax.axis_size("pair")
    rows = tile_rows // owners
    chunks = rows // ROWS
    me = lax.axis_index("pair").astype(jnp.int32)
    sub = lax.axis_index("sub").astype(jnp.int32)
    place = jnp.stack([me, sub])

    def to_owner(value, k):
        return lax.ppermute(value, "pair", [(o, o ^ k) for o in range(owners)])

    def to_sibling(value):
        return lax.ppermute(value, "sub", [(0, 1), (1, 0)])

    def after(value, earlier):
        return value if earlier is None else lax.optimization_barrier((value, earlier))[0]

    tiles = [integral_tiles] + [to_owner(integral_tiles, k) for k in range(1, owners)]
    weights, gaps = make_weights(pair_list, coupling, pair_gap, sub.reshape(1))
    sent = [
        dress(c, me.reshape(1), tile_of, tile_mask, tiles, lambda_amps) for c in range(chunks)
    ]
    direct = [[sent[c][0]] + [None] * (owners - 1) for c in range(chunks)]
    other = [[None] * owners for _ in range(chunks)]
    queue = [(c, k) for c in range(chunks) for k in range(owners - 1, 0, -1)]
    ahead = 4
    for n, (c, k) in enumerate(queue):
        earlier = None
        if n >= ahead:
            was, slot = queue[n - ahead]
            earlier = direct[was][slot]
            earlier = (earlier, weights)
        direct[c][k] = to_owner(after(sent[c][k], earlier), k)

    shape = (owners, 1, pairs, rows, cols)
    col = col_energy.reshape(1, cols)
    result = None
    for c in range(chunks):
        other[c][0] = to_sibling(after(sent[c][0], direct[c][owners - 1]))
        for k in range(owners - 1, 0, -1):
            other[c][k] = to_sibling(after(direct[c][k], result if k == 1 else None))
        result = finish(
            c, place, row_energy, weights, gaps, col, direct[c] + other[c], result, shape
        )
    return result


def solution(mesh):
    placed = (
        P(("mol", "pair"), "sub", None, None, "tile"),
        P(("mol", "pair"), None, None),
        P(("mol", "pair"), "sub", None),
        P(("mol", "pair"), "sub", None, "tile"),
        P("mol", None),
        P("mol", None),
        P("mol", "sub", None),
        P(("mol", "pair")),
        P(("mol", "tile")),
    )
    owners, subs = mesh.shape["pair"], mesh.shape["sub"]

    def local(*args):
        tile_rows, cols = args[0].shape[3:]
        rows = tile_rows // owners
        power = owners & (owners - 1) == 0
        fits = rows % ROWS == 0 and cols % LANES == 0 and args[1].shape[0] == 1
        if power and fits and subs == 2 and args[0].shape[2] % ROWS == 0:
            return local_chunked(*args)
        return local_general(*args)

    return jax.shard_map(
        local,
        mesh=mesh,
        in_specs=placed,
        out_specs=P("mol", "sub", None, "pair", "tile"),
        check_vma=False,
    )
```

time: 85.5 us -> 72.6 us (0.85); the launches traced: 84.2 us -> 72.3 us
  local copies, waits for them, and re-layouts: 26.2 us -> 5.13 us
  starting transfers between devices: 15.1 us -> 22 us
  other arithmetic: 6.34 us -> 0.07 us
  Pallas kernels: 11.2 us -> 15.6 us
  waiting for transfers between devices: 25.3 us -> 29.5 us
    gather x6 -> x0, local copies, waits for them, and re-layouts: 11.9 us -> none  [the longest x1 3.16 us: column_tables(): left_table = jnp.take(coupling.T, col_pairs[:, 0], axis=0).T]
    ppermute x9, starting transfers between devices: 13.6 us -> 20.4 us  [to_owner(): return lax.ppermute(value, 'pair', [(o, o ^ k) for o in range(owners)])]
    pallas_call x3 -> x5, Pallas kernels: 11.2 us -> 15.6 us  [the longest x2 9.09 us: finish(): pl.pallas_call(functools.partial(finish_kernel, len(pieces), chunk), in_s...]
    transpose x2 -> x0, local copies, waits for them, and re-layouts: 3.97 us -> none  [the longest x1 1.99 us: column_tables(): left_table = jnp.take(coupling.T, col_pairs[:, 0], axis=0).T]
    transpose x2 -> x0, other arithmetic: 3.9 us -> none  [the longest x1 1.96 us: column_tables(): left_table = jnp.take(coupling.T, col_pairs[:, 0], axis=0).T]
    unnamed x19 -> x22, local copies, waits for them, and re-layouts: 8.56 us -> 5.13 us
    ppermute x9, waiting for transfers between devices: 25.2 us -> 28 us  [to_owner(): return lax.ppermute(value, 'pair', [(o, o ^ k) for o in range(owners)])]
    ppermute x8, waiting for transfers between devices: 0.02 us -> 1.41 us  [to_sibling(): return lax.ppermute(value, 'sub', [(0, 1), (1, 0)])]
  transfers between devices with their start and end apart: 17 -> 17, of which waited for: 4 -> 8; matrix products, arithmetic and copies ran while one was open for 33% -> 0% of each run, Pallas kernels for 5% -> 13%
where the time goes in v2:
time: 72.6 us; the launch traced here: 72.3 us
  waiting for transfers between devices  29.5 us (41%)
  starting transfers between devices  22 us (30%)
  Pallas kernels  15.6 us (21%)
  local copies, waits for them, and re-layouts  5.13 us (7%)
    ppermute x9, waiting for transfers between devices, to_owner(): return lax.ppermute(value, 'pair', [(o, o ^ k) for o in range(owners)])  28 us
    ppermute x9, starting transfers between devices, to_owner(): return lax.ppermute(value, 'pair', [(o, o ^ k) for o in range(owners)])  20.4 us
    pallas_call x2, Pallas kernels, finish(): pl.pallas_call(functools.partial(finish_kernel, len(pieces), chunk), in_s...  9.09 us
    unnamed x22, local copies, waits for them, and re-layouts  5.13 us
    pallas_call x2, Pallas kernels, dress(): pl.pallas_call(functools.partial(dress_kernel, owners, rows, chunk), grid...  4.12 us
    pallas_call x1, Pallas kernels, make_weights(): pl.pallas_call(weights_kernel, in_specs=[vmem, vmem, vmem, pl.BlockSpec(m...  2.42 us
    ppermute x8, starting transfers between devices, to_sibling(): return lax.ppermute(value, 'sub', [(0, 1), (1, 0)])  1.52 us
  transfers between devices with their start and end apart: 17, of which 8 were waited for; matrix products, arithmetic and copies ran while one was open for 0% of the time, Pallas kernels for 13%

profile of v2, /device:TPU:0, one launch (start us, length us, event | category | flops | bytes accessed | tf_op | source)
XLA Modules:
  0.0 72.3 jit_solution(11680287332450114955)
XLA Ops:
  0.0 5.0 %collective-permute-start.2 = (bf16[1,128,128]{2,1,0:T(8,128)(2,1)}, bf16[1,128,128]{2,1,0:T(8,128)(2,1)S(1)}, u32[]{:S(2)}, u32[]{:S(2)}) collective-permute-start(bf16[1,128,128]{2,1,0:T(8,128)(2,1)} %refs_0_.3), channel_id=1, source_target_pairs={{0,12},{4,8},{8,4},{12,0},{1,13},{5,9},{9,5},{13,1},{2,14},{6,10},... | collective-permute-start | bytes 98312 | tf_op jit(solution)/shard_map/ppermute | solution.py:343
  5.0 0.0 collective-permute-start.1
  5.1 0.6 collective-permute-start
  5.6 1.5 %collective-permute-done.2.refs_3_ = bf16[1,128,128]{2,1,0:T(8,128)(2,1)S(1)} collective-permute-done((bf16[1,128,128]{2,1,0:T(8,128)(2,1)}, bf16[1,128,128]{2,1,0:T(8,128)(2,1)S(1)}, u32[]{:S(2)}, u32[]{:S(2)}) %collective-permute-start.2) | collective-permute-done | bytes 32800 | tf_op jit(solution)/shard_map/ppermute | solution.py:343
  7.2 2.9 %collective-permute-done.1.refs_2_ = bf16[1,128,128]{2,1,0:T(8,128)(2,1)S(1)} collective-permute-done((bf16[1,128,128]{2,1,0:T(8,128)(2,1)}, bf16[1,128,128]{2,1,0:T(8,128)(2,1)S(1)}, u32[]{:S(2)}, u32[]{:S(2)}) %collective-permute-start.1) | collective-permute-done | bytes 32800 | tf_op jit(solution)/shard_map/ppermute | solution.py:343
  10.1 0.0 collective-permute-done.refs_1_
  10.1 1.6 %copy-done = bf16[1,1,32,128,256]{4,3,2,1,0:T(8,128)(2,1)S(1)} copy-done((bf16[1,1,32,128,256]{4,3,2,1,0:T(8,128)(2,1)S(1)}, bf16[1,1,32,128,256]{4,3,2,1,0:T(8,128)(2,1)}, u32[]{:S(2)}) %copy-start) | copy-done | bytes 2097176
  11.7 0.8 %copy-done.1 = bf16[1,128,128]{2,1,0:T(8,128)(2,1)S(1)} copy-done((bf16[1,128,128]{2,1,0:T(8,128)(2,1)S(1)}, bf16[1,128,128]{2,1,0:T(8,128)(2,1)}, u32[]{:S(2)}) %copy-start.1) | copy-done | bytes 32792
  12.4 0.7 copy-done.2
  13.1 0.7 copy-done.4
  13.8 1.6 %shard_map.93 = (bf16[32,16,256]{2,1,0:T(8,128)(2,1)S(1)}, bf16[32,16,256]{2,1,0:T(8,128)(2,1)S(1)}, bf16[32,16,256]{2,1,0:T(8,128)(2,1)S(1)}, bf16[32,16,256]{2,1,0:T(8,128)(2,1)S(1)}) custom-call(s32[1]{0:T(128)} %bitcast.me_ref, s32[1,1,32]{2,1,0:T(1,128)S(1)} %copy-done.4, s32[1,1,2,32]{3,2,1,0:T(2,128)S(1)} %bitcast.5, ...), custom_call_target="tpu_custom_call" | custom-call | flops 134217728 | bytes 3145728 | tf_op jit(solution)/shard_map/pallas_call | solution.py:217
  15.3 0.0 copy-start.3
  15.4 0.0 copy-start.5
  15.4 2.1 %collective-permute-start.3 = (bf16[32,16,256]{2,1,0:T(8,128)(2,1)S(1)}, bf16[32,16,256]{2,1,0:T(8,128)(2,1)S(1)}, u32[]{:S(2)}, u32[]{:S(2)}) collective-permute-start(bf16[32,16,256]{2,1,0:T(8,128)(2,1)S(1)} %get-tuple-element.24), channel_id=1, source_target_pairs={{0,8},{4,12},{8,0},{12,4},{1,9},{5,13},{9,1},{13,5},{2,10},{6,14},... | collective-permute-start | bytes 786440 | tf_op jit(solution)/shard_map/ppermute | solution.py:343
  17.4 0.1 collective-permute-start.5
  17.6 1.3 %collective-permute-start.9 = (bf16[32,16,256]{2,1,0:T(8,128)(2,1)S(1)}, bf16[32,16,256]{2,1,0:T(8,128)(2,1)S(1)}, u32[]{:S(2)}, u32[]{:S(2)}) collective-permute-start(bf16[32,16,256]{2,1,0:T(8,128)(2,1)S(1)} %get-tuple-element.32), channel_id=1, source_target_pairs={{0,4},{4,0},{8,12},{12,8},{1,5},{5,1},{9,13},{13,9},{2,6},{6,2},{1... | collective-permute-start | bytes 786440 | tf_op jit(solution)/shard_map/ppermute | solution.py:343
  18.9 2.6 %shard_map.92 = (bf16[32,16,256]{2,1,0:T(8,128)(2,1)S(1)}, bf16[32,16,256]{2,1,0:T(8,128)(2,1)S(1)}, bf16[32,16,256]{2,1,0:T(8,128)(2,1)S(1)}, bf16[32,16,256]{2,1,0:T(8,128)(2,1)}) custom-call(s32[1]{0:T(128)} %bitcast.me_ref, s32[1,1,32]{2,1,0:T(1,128)S(1)} %copy-done.4, s32[1,1,2,32]{3,2,1,0:T(2,128)S(1)} %bitcast.6, bf16[1,128,128]{2,1,0:T(8,128)(2,1)S(1)} %copy-done.1, ...), custom_call_target="tpu_custom_call" | custom-call | flops 134217728 | bytes 3145728 | tf_op jit(solution)/shard_map/pallas_call | solution.py:217
  21.5 0.7 copy-done.7
  22.2 0.7 copy-done.8
  22.9 2.4 %collective-permute-start.7 = (bf16[32,16,256]{2,1,0:T(8,128)(2,1)}, bf16[32,16,256]{2,1,0:T(8,128)(2,1)S(1)}, u32[]{:S(2)}, u32[]{:S(2)}) collective-permute-start(bf16[32,16,256]{2,1,0:T(8,128)(2,1)} %get-tuple-element.29), channel_id=1, source_target_pairs={{0,12},{4,8},{8,4},{12,0},{1,13},{5,9},{9,5},{13,1},{2,14},{6,10},... | collective-permute-start | bytes 786440 | tf_op jit(solution)/shard_map/ppermute | solution.py:343
  25.3 10.9 %collective-permute-done.3.refs_2_ = bf16[32,16,256]{2,1,0:T(8,128)(2,1)S(1)} collective-permute-done((bf16[32,16,256]{2,1,0:T(8,128)(2,1)S(1)}, bf16[32,16,256]{2,1,0:T(8,128)(2,1)S(1)}, u32[]{:S(2)}, u32[]{:S(2)}) %collective-permute-start.3) | collective-permute-done | bytes 262176 | tf_op jit(solution)/shard_map/ppermute | solution.py:343
  36.2 0.0 collective-permute-start.12
  36.2 0.0 collective-permute-done.5.refs_3_
  36.2 0.5 collective-permute-start.10
  36.7 0.0 collective-permute-start.13
  36.7 4.0 %collective-permute-done.9.refs_1_ = bf16[32,16,256]{2,1,0:T(8,128)(2,1)S(1)} collective-permute-done((bf16[32,16,256]{2,1,0:T(8,128)(2,1)S(1)}, bf16[32,16,256]{2,1,0:T(8,128)(2,1)S(1)}, u32[]{:S(2)}, u32[]{:S(2)}) %collective-permute-start.9) | collective-permute-done | bytes 262176 | tf_op jit(solution)/shard_map/ppermute | solution.py:343
  40.7 0.0 collective-permute-start.11
  40.7 2.4 %shard_map.91 = (bf16[128,256]{1,0:T(8,128)(2,1)S(1)}, f32[128,128]{1,0:T(8,128)S(1)}) custom-call(s32[2,256]{1,0:T(2,128)S(1)} %bitcast.9, f32[400,400]{1,0:T(8,128)S(1)} %copy-done.6, f32[4,1,32]{2,1,0:T(1,128)S(1)} %copy-done.10, s32[1]{0:T(128)} %bitcast.1.sub_ref), custom_call_target="tpu_custom_call" | custom-call | flops 491520000 | bytes 640000 | tf_op jit(solution)/shard_map/pallas_call | solution.py:161
  43.1 0.0 collective-permute-done.7.refs_3_
  43.1 8.0 %collective-permute-start.4 = (bf16[32,16,256]{2,1,0:T(8,128)(2,1)}, bf16[32,16,256]{2,1,0:T(8,128)(2,1)S(1)}, u32[]{:S(2)}, u32[]{:S(2)}) collective-permute-start(bf16[32,16,256]{2,1,0:T(8,128)(2,1)} %copy-done.8), channel_id=1, source_target_pairs={{0,4},{4,0},{8,12},{12,8},{1,5},{5,1},{9,13},{13,9},{2,6},{6,2},{1... | collective-permute-start | bytes 786440 | tf_op jit(solution)/shard_map/ppermute | solution.py:343
  51.2 0.0 collective-permute-done.12.refs_6_
  51.2 0.9 %collective-permute-start.6 = (bf16[32,16,256]{2,1,0:T(8,128)(2,1)}, bf16[32,16,256]{2,1,0:T(8,128)(2,1)S(1)}, u32[]{:S(2)}, u32[]{:S(2)}) collective-permute-start(bf16[32,16,256]{2,1,0:T(8,128)(2,1)} %copy-done.7), channel_id=1, source_target_pairs={{0,8},{4,12},{8,0},{12,4},{1,9},{5,13},{9,1},{13,5},{2,10},{6,14},... | collective-permute-start | bytes 786440 | tf_op jit(solution)/shard_map/ppermute | solution.py:343
  52.1 0.1 pad_add_fusion.place_ref
  52.1 0.0 collective-permute-done.10.refs_4_
  52.1 0.0 collective-permute-start.8
  52.2 0.0 collective-permute-done.13.refs_7_
  52.2 0.5 collective-permute-start.16
  52.7 0.0 collective-permute-done.11.refs_5_
  52.7 4.5 %shard_map.94.refs_8_ = bf16[4,1,32,32,256]{4,3,2,1,0:T(8,128)(2,1)} custom-call(s32[2]{0:T(128)S(1)} %pad_add_fusion.place_ref, f32[32]{0:T(128)S(1)} %copy-done.5, bf16[128,256]{1,0:T(8,128)(2,1)S(1)} %get-tuple-element.20.w_ref, f32[128,128]{1,0:T(8,128)S(1)} %get-tuple-element.21.gap_ref, f32[1,256]{1,0:T(1,128)S(1)} %bitcast.7, ...), custom_call_target="tpu_custom_call" | custom-call | flops 1073741824 | bytes 3145728 | tf_op jit(solution)/shard_map/pallas_call | solution.py:300
  57.2 5.1 %collective-permute-done.4.refs_1_ = bf16[32,16,256]{2,1,0:T(8,128)(2,1)S(1)} collective-permute-done((bf16[32,16,256]{2,1,0:T(8,128)(2,1)}, bf16[32,16,256]{2,1,0:T(8,128)(2,1)S(1)}, u32[]{:S(2)}, u32[]{:S(2)}) %collective-permute-start.4) | collective-permute-done | bytes 262176 | tf_op jit(solution)/shard_map/ppermute | solution.py:343
  62.4 3.5 %collective-permute-done.6.refs_2_ = bf16[32,16,256]{2,1,0:T(8,128)(2,1)S(1)} collective-permute-done((bf16[32,16,256]{2,1,0:T(8,128)(2,1)}, bf16[32,16,256]{2,1,0:T(8,128)(2,1)S(1)}, u32[]{:S(2)}, u32[]{:S(2)}) %collective-permute-start.6) | collective-permute-done | bytes 262176 | tf_op jit(solution)/shard_map/ppermute | solution.py:343
  65.9 0.0 collective-permute-start.15
  65.9 0.5 collective-permute-start.14
  66.4 0.0 collective-permute-done.8.refs_4_
  66.4 0.0 collective-permute-done.16.refs_7_
  66.4 1.0 %collective-permute-done.15.refs_6_ = bf16[32,16,256]{2,1,0:T(8,128)(2,1)S(1)} collective-permute-done((bf16[32,16,256]{2,1,0:T(8,128)(2,1)S(1)}, bf16[32,16,256]{2,1,0:T(8,128)(2,1)S(1)}, u32[]{:S(2)}, u32[]{:S(2)}) %collective-permute-start.15) | collective-permute-done | bytes 262176 | tf_op jit(solution)/shard_map/ppermute | solution.py:346
  67.4 0.4 collective-permute-done.14.refs_5_
  67.8 4.6 %shard_map.95 = bf16[4,1,32,32,256]{4,3,2,1,0:T(8,128)(2,1)} custom-call(s32[2]{0:T(128)S(1)} %pad_add_fusion.place_ref, f32[32]{0:T(128)S(1)} %copy-done.5, bf16[128,256]{1,0:T(8,128)(2,1)S(1)} %get-tuple-element.20.w_ref, f32[128,128]{1,0:T(8,128)S(1)} %get-tuple-element.21.gap_ref, f32[1,256]{1,0:T(1,128)S(1)} %bitcast.8, ...), custom_call_target="tpu_custom_call", output_to_operand_aliasing={{}: (13, {})} | custom-call | flops 1073741824 | bytes 3145728 | tf_op jit(solution)/shard_map/pallas_call | solution.py:300
  (14 shorter events, 0.0 us)
Async XLA Ops:
  0.0 7.2 %collective-permute-start.2 = (bf16[1,128,128]{2,1,0:T(8,128)(2,1)}, bf16[1,128,128]{2,1,0:T(8,128)(2,1)S(1)}, u32[]{:S(2)}, u32[]{:S(2)}) collective-permute-start(bf16[1,128,128]{2,1,0:T(8,128)(2,1)} %refs_0_.3), channel_id=1, source_target_pairs={{0,12},{4,8},{8,4},{12,0},{1,13},{5,9},{9,5},{13,1},{2,14},{6,10},... | collective-permute-start | bytes 98312 | tf_op jit(solution)/shard_map/ppermute | solution.py:343
  5.0 5.0 %collective-permute-start.1 = (bf16[1,128,128]{2,1,0:T(8,128)(2,1)}, bf16[1,128,128]{2,1,0:T(8,128)(2,1)S(1)}, u32[]{:S(2)}, u32[]{:S(2)}) collective-permute-start(bf16[1,128,128]{2,1,0:T(8,128)(2,1)} %refs_0_.3), channel_id=1, source_target_pairs={{0,8},{4,12},{8,0},{12,4},{1,9},{5,13},{9,1},{13,5},{2,10},{6,14},... | collective-permute-start | bytes 98312 | tf_op jit(solution)/shard_map/ppermute | solution.py:343
  5.1 5.0 %collective-permute-start = (bf16[1,128,128]{2,1,0:T(8,128)(2,1)}, bf16[1,128,128]{2,1,0:T(8,128)(2,1)S(1)}, u32[]{:S(2)}, u32[]{:S(2)}) collective-permute-start(bf16[1,128,128]{2,1,0:T(8,128)(2,1)} %refs_0_.3), channel_id=1, source_target_pairs={{0,4},{4,0},{8,12},{12,8},{1,5},{5,1},{9,13},{13,9},{2,6},{6,2},{1... | collective-permute-start | bytes 98312 | tf_op jit(solution)/shard_map/ppermute | solution.py:343
  10.1 1.6 %copy-start = (bf16[1,1,32,128,256]{4,3,2,1,0:T(8,128)(2,1)S(1)}, bf16[1,1,32,128,256]{4,3,2,1,0:T(8,128)(2,1)}, u32[]{:S(2)}) copy-start(bf16[1,1,32,128,256]{4,3,2,1,0:T(8,128)(2,1)} %refs_4_.3) | copy-start | bytes 6291460
  11.7 0.8 %copy-start.1 = (bf16[1,128,128]{2,1,0:T(8,128)(2,1)S(1)}, bf16[1,128,128]{2,1,0:T(8,128)(2,1)}, u32[]{:S(2)}) copy-start(bf16[1,128,128]{2,1,0:T(8,128)(2,1)} %refs_0_.3) | copy-start | bytes 98308
  12.4 0.7 copy-start.2
  13.1 0.7 copy-start.4
  13.8 26.9 %copy-start.6 = (f32[400,400]{1,0:T(8,128)S(1)}, f32[400,400]{1,0:T(8,128)}, u32[]{:S(2)}) copy-start(f32[400,400]{1,0:T(8,128)} %coupling_ref.1) | copy-start | bytes 1920004
  13.8 26.9 %copy-start.9 = (s32[256,2]{0,1:T(2,128)S(1)}, s32[256,2]{0,1:T(2,128)}, u32[]{:S(2)}) copy-start(s32[256,2]{0,1:T(2,128)} %param.13) | copy-start | bytes 6148
  13.8 26.9 %copy-start.10 = (f32[4,1,32]{2,1,0:T(1,128)S(1)}, f32[4,1,32]{2,1,0:T(1,128)}, u32[]{:S(2)}) copy-start(f32[4,1,32]{2,1,0:T(1,128)} %gap_ref.1) | copy-start | bytes 1540
  15.3 37.3 %copy-start.3 = (f32[256]{0:T(256)S(1)}, f32[256]{0:T(256)}, u32[]{:S(2)}) copy-start(f32[256]{0:T(256)} %param.17) | copy-start | bytes 3076
  15.4 37.3 %copy-start.5 = (f32[32]{0:T(128)S(1)}, f32[32]{0:T(128)}, u32[]{:S(2)}) copy-start(f32[32]{0:T(128)} %row_ref.3) | copy-start | bytes 388
  15.4 20.8 %collective-permute-start.3 = (bf16[32,16,256]{2,1,0:T(8,128)(2,1)S(1)}, bf16[32,16,256]{2,1,0:T(8,128)(2,1)S(1)}, u32[]{:S(2)}, u32[]{:S(2)}) collective-permute-start(bf16[32,16,256]{2,1,0:T(8,128)(2,1)S(1)} %get-tuple-element.24), channel_id=1, source_target_pairs={{0,8},{4,12},{8,0},{12,4},{1,9},{5,13},{9,1},{13,5},{2,10},{6,14},... | collective-permute-start | bytes 786440 | tf_op jit(solution)/shard_map/ppermute | solution.py:343
  17.4 18.7 %collective-permute-start.5 = (bf16[32,16,256]{2,1,0:T(8,128)(2,1)S(1)}, bf16[32,16,256]{2,1,0:T(8,128)(2,1)S(1)}, u32[]{:S(2)}, u32[]{:S(2)}) collective-permute-start(bf16[32,16,256]{2,1,0:T(8,128)(2,1)S(1)} %get-tuple-element.27), channel_id=1, source_target_pairs={{0,12},{4,8},{8,4},{12,0},{1,13},{5,9},{9,5},{13,1},{2,14},{6,10},... | collective-permute-start | bytes 786440 | tf_op jit(solution)/shard_map/ppermute | solution.py:343
  17.6 23.1 %collective-permute-start.9 = (bf16[32,16,256]{2,1,0:T(8,128)(2,1)S(1)}, bf16[32,16,256]{2,1,0:T(8,128)(2,1)S(1)}, u32[]{:S(2)}, u32[]{:S(2)}) collective-permute-start(bf16[32,16,256]{2,1,0:T(8,128)(2,1)S(1)} %get-tuple-element.32), channel_id=1, source_target_pairs={{0,4},{4,0},{8,12},{12,8},{1,5},{5,1},{9,13},{13,9},{2,6},{6,2},{1... | collective-permute-start | bytes 786440 | tf_op jit(solution)/shard_map/ppermute | solution.py:343
  21.5 0.7 copy-start.7
  22.2 0.7 copy-start.8
  22.9 20.2 %collective-permute-start.7 = (bf16[32,16,256]{2,1,0:T(8,128)(2,1)}, bf16[32,16,256]{2,1,0:T(8,128)(2,1)S(1)}, u32[]{:S(2)}, u32[]{:S(2)}) collective-permute-start(bf16[32,16,256]{2,1,0:T(8,128)(2,1)} %get-tuple-element.29), channel_id=1, source_target_pairs={{0,12},{4,8},{8,4},{12,0},{1,13},{5,9},{9,5},{13,1},{2,14},{6,10},... | collective-permute-start | bytes 786440 | tf_op jit(solution)/shard_map/ppermute | solution.py:343
  36.2 15.0 %collective-permute-start.12 = (bf16[32,16,256]{2,1,0:T(8,128)(2,1)S(1)}, bf16[32,16,256]{2,1,0:T(8,128)(2,1)S(1)}, u32[]{:S(2)}, u32[]{:S(2)}) collective-permute-start(bf16[32,16,256]{2,1,0:T(8,128)(2,1)S(1)} %collective-permute-done.3.refs_2_), channel_id=1, source_target_pairs={{0,1},{1,0},{2,3},{3,2},{4,5},{5,4},{6,7},{7,6},{8,9},{9,8},{10,11... | collective-permute-start | bytes 786440 | tf_op jit(solution)/shard_map/ppermute | solution.py:346
  36.2 16.0 %collective-permute-start.10 = (bf16[32,16,256]{2,1,0:T(8,128)(2,1)S(1)}, bf16[32,16,256]{2,1,0:T(8,128)(2,1)S(1)}, u32[]{:S(2)}, u32[]{:S(2)}) collective-permute-start(bf16[32,16,256]{2,1,0:T(8,128)(2,1)S(1)} %get-tuple-element.33.refs_0_), channel_id=1, source_target_pairs={{0,1},{1,0},{2,3},{3,2},{4,5},{5,4},{6,7},{7,6},{8,9},{9,8},{10,11... | collective-permute-start | bytes 786440 | tf_op jit(solution)/shard_map/ppermute | solution.py:346
  36.7 15.5 %collective-permute-start.13 = (bf16[32,16,256]{2,1,0:T(8,128)(2,1)S(1)}, bf16[32,16,256]{2,1,0:T(8,128)(2,1)S(1)}, u32[]{:S(2)}, u32[]{:S(2)}) collective-permute-start(bf16[32,16,256]{2,1,0:T(8,128)(2,1)S(1)} %collective-permute-done.5.refs_3_), channel_id=1, source_target_pairs={{0,1},{1,0},{2,3},{3,2},{4,5},{5,4},{6,7},{7,6},{8,9},{9,8},{10,11... | collective-permute-start | bytes 786440 | tf_op jit(solution)/shard_map/ppermute | solution.py:346
  40.7 12.0 %collective-permute-start.11 = (bf16[32,16,256]{2,1,0:T(8,128)(2,1)S(1)}, bf16[32,16,256]{2,1,0:T(8,128)(2,1)S(1)}, u32[]{:S(2)}, u32[]{:S(2)}) collective-permute-start(bf16[32,16,256]{2,1,0:T(8,128)(2,1)S(1)} %collective-permute-done.9.refs_1_), channel_id=1, source_target_pairs={{0,1},{1,0},{2,3},{3,2},{4,5},{5,4},{6,7},{7,6},{8,9},{9,8},{10,11... | collective-permute-start | bytes 786440 | tf_op jit(solution)/shard_map/ppermute | solution.py:346
  43.1 19.2 %collective-permute-start.4 = (bf16[32,16,256]{2,1,0:T(8,128)(2,1)}, bf16[32,16,256]{2,1,0:T(8,128)(2,1)S(1)}, u32[]{:S(2)}, u32[]{:S(2)}) collective-permute-start(bf16[32,16,256]{2,1,0:T(8,128)(2,1)} %copy-done.8), channel_id=1, source_target_pairs={{0,4},{4,0},{8,12},{12,8},{1,5},{5,1},{9,13},{13,9},{2,6},{6,2},{1... | collective-permute-start | bytes 786440 | tf_op jit(solution)/shard_map/ppermute | solution.py:343
  51.2 14.7 %collective-permute-start.6 = (bf16[32,16,256]{2,1,0:T(8,128)(2,1)}, bf16[32,16,256]{2,1,0:T(8,128)(2,1)S(1)}, u32[]{:S(2)}, u32[]{:S(2)}) collective-permute-start(bf16[32,16,256]{2,1,0:T(8,128)(2,1)} %copy-done.7), channel_id=1, source_target_pairs={{0,8},{4,12},{8,0},{12,4},{1,9},{5,13},{9,1},{13,5},{2,10},{6,14},... | collective-permute-start | bytes 786440 | tf_op jit(solution)/shard_map/ppermute | solution.py:343
  52.1 14.3 %collective-permute-start.8 = (bf16[32,16,256]{2,1,0:T(8,128)(2,1)S(1)}, bf16[32,16,256]{2,1,0:T(8,128)(2,1)S(1)}, u32[]{:S(2)}, u32[]{:S(2)}) collective-permute-start(bf16[32,16,256]{2,1,0:T(8,128)(2,1)S(1)} %get-tuple-element.30.refs_0_), channel_id=1, source_target_pairs={{0,1},{1,0},{2,3},{3,2},{4,5},{5,4},{6,7},{7,6},{8,9},{9,8},{10,11... | collective-permute-start | bytes 786440 | tf_op jit(solution)/shard_map/ppermute | solution.py:346
  52.2 14.2 %collective-permute-start.16 = (bf16[32,16,256]{2,1,0:T(8,128)(2,1)S(1)}, bf16[32,16,256]{2,1,0:T(8,128)(2,1)S(1)}, u32[]{:S(2)}, u32[]{:S(2)}) collective-permute-start(bf16[32,16,256]{2,1,0:T(8,128)(2,1)S(1)} %collective-permute-done.7.refs_3_), channel_id=1, source_target_pairs={{0,1},{1,0},{2,3},{3,2},{4,5},{5,4},{6,7},{7,6},{8,9},{9,8},{10,11... | collective-permute-start | bytes 786440 | tf_op jit(solution)/shard_map/ppermute | solution.py:346
  65.9 1.5 %collective-permute-start.15 = (bf16[32,16,256]{2,1,0:T(8,128)(2,1)S(1)}, bf16[32,16,256]{2,1,0:T(8,128)(2,1)S(1)}, u32[]{:S(2)}, u32[]{:S(2)}) collective-permute-start(bf16[32,16,256]{2,1,0:T(8,128)(2,1)S(1)} %collective-permute-done.6.refs_2_), channel_id=1, source_target_pairs={{0,1},{1,0},{2,3},{3,2},{4,5},{5,4},{6,7},{7,6},{8,9},{9,8},{10,11... | collective-permute-start | bytes 786440 | tf_op jit(solution)/shard_map/ppermute | solution.py:346
  65.9 1.9 %collective-permute-start.14 = (bf16[32,16,256]{2,1,0:T(8,128)(2,1)S(1)}, bf16[32,16,256]{2,1,0:T(8,128)(2,1)S(1)}, u32[]{:S(2)}, u32[]{:S(2)}) collective-permute-start(bf16[32,16,256]{2,1,0:T(8,128)(2,1)S(1)} %collective-permute-done.4.refs_1_), channel_id=1, source_target_pairs={{0,1},{1,0},{2,3},{3,2},{4,5},{5,4},{6,7},{7,6},{8,9},{9,8},{10,11... | collective-permute-start | bytes 786440 | tf_op jit(solution)/shard_map/ppermute | solution.py:346

commit v3 on v2

v3 whole, which is shorter than its diff:
```python
import functools
import math

import jax
import jax.numpy as jnp
from jax import lax
from jax.experimental import pallas as pl
from jax.experimental.pallas import tpu as pltpu
from jax.sharding import PartitionSpec as P

ROWS = 16
LANES = 128
VMEM_BYTES = 24 * 2**20


def column_tables(coupling, col_pairs):
    left_table = jnp.take(coupling.T, col_pairs[:, 0], axis=0).T
    right_table = jnp.take(coupling.T, col_pairs[:, 1], axis=0).T
    return (left_table, right_table)


def cycle_rows(left_table, right_table, row_pairs):
    left_part = jnp.take(left_table, row_pairs[:, 0], axis=0)
    right_part = jnp.take(right_table, row_pairs[:, 1], axis=0)
    return (left_part * right_part).astype(jnp.bfloat16)


def cycle_all(coupling, pair_list, col_pairs, flat_rhs):
    total_pairs = pair_list.shape[0]
    step_rows = math.gcd(total_pairs, 512)
    row_blocks = pair_list.reshape(total_pairs // step_rows, step_rows, 2)
    left_table, right_table = column_tables(coupling, col_pairs)

    def one_block(row_pairs):
        weights = cycle_rows(left_table, right_table, row_pairs)
        return jnp.dot(weights, flat_rhs, preferred_element_type=jnp.float32)

    return lax.map(one_block, row_blocks).reshape(total_pairs, -1)


def local_general(
    lambda_amps,
    integral_tiles,
    tile_of,
    tile_mask,
    pair_list,
    coupling,
    pair_gap,
    row_energy,
    col_energy,
):
    pair_count = lambda_amps.shape[2]
    tile_rows = lambda_amps.shape[3]
    col_count = lambda_amps.shape[4]
    owners = lax.axis_size("pair")
    sub_count = lax.axis_size("sub")
    wanted = tile_of.reshape(pair_count)
    empty_tiles = jnp.zeros((pair_count, tile_rows, tile_rows), integral_tiles.dtype)
    shard_piece = lax.all_gather(integral_tiles, "pair", axis=0, tiled=True)
    inside = (wanted >= 0) & (wanted < shard_piece.shape[0])
    taken_rows = shard_piece[jnp.clip(wanted, 0, shard_piece.shape[0] - 1)]
    chosen = jnp.where(inside[:, None, None], taken_rows, empty_tiles)
    amplitudes = lambda_amps.reshape(pair_count, tile_rows, col_count)
    ladder = jnp.einsum("pac,pcb->pab", chosen, amplitudes, preferred_element_type=jnp.float32)
    blocks = tile_mask.shape[3]
    keep_mask = tile_mask.reshape(pair_count, 1, blocks, 1).astype(jnp.float32)
    ladder = (
        ladder.reshape(pair_count, tile_rows, blocks, col_count // blocks) * keep_mask
    ).reshape(pair_count, tile_rows, col_count)
    dressed = (amplitudes.astype(jnp.float32) + ladder).astype(jnp.bfloat16)
    dressed = dressed.reshape(1, 1, pair_count, tile_rows, col_count)
    relayed = lax.all_to_all(dressed, "pair", split_axis=3, concat_axis=0, tiled=True)
    sub_index = lax.axis_index("sub")
    block_ids = jnp.arange(owners, dtype=jnp.int32) * sub_count + sub_index
    mine_ids = (
        block_ids[:, None] * pair_count + jnp.arange(pair_count, dtype=jnp.int32)[None, :]
    ).reshape(-1)
    col_pairs = pair_list[mine_ids]
    flat_rhs = relayed.reshape(owners * pair_count, -1)
    partial_value = cycle_all(coupling, pair_list, col_pairs, flat_rhs)
    partial_value = partial_value.reshape(
        owners, sub_count, pair_count, relayed.shape[3], col_count
    )
    cycle_term = lax.psum_scatter(
        partial_value.astype(jnp.bfloat16), "sub", scatter_dimension=1, tiled=True
    ).astype(jnp.float32)
    total_sum = relayed.astype(jnp.float32) + cycle_term
    energy_gap = (
        pair_gap[:, :, :, None, None]
        + row_energy[None, None, None, :, None]
        + col_energy[None, None, None, None, :]
    )
    return (-total_sum / energy_gap).astype(jnp.bfloat16)


def one_hot(hits):
    return jnp.where(hits, 1.0, 0.0).astype(jnp.bfloat16)


def square_iotas(size):
    return (lax.broadcasted_iota(jnp.int32, (size, size), axis) for axis in range(2))


def swap_matrix():
    to, frm = square_iotas(ROWS * ROWS)
    return one_hot(to == (frm % ROWS) * ROWS + frm // ROWS)


def split3(value):
    high = value.astype(jnp.bfloat16)
    rest = value - high.astype(jnp.float32)
    mid = rest.astype(jnp.bfloat16)
    low = (rest - mid.astype(jnp.float32)).astype(jnp.bfloat16)
    return high, mid, low


def pick_columns(value, columns):
    high, mid, low = (
        jnp.dot(part, columns, preferred_element_type=jnp.float32) for part in split3(value)
    )
    return high + (mid + low)


def pick_rows(columns, value):
    dims = (((0,), (0,)), ((), ()))
    high, mid, low = (
        lax.dot_general(columns, part, dims, preferred_element_type=jnp.float32)
        for part in split3(value)
    )
    return high + (mid + low)


def prepare_kernel(pair_ref, coupling_ref, gap_ref, place_ref, lam_ref, w_ref, gaps_ref, held_ref, full, sems):
    halves = sems.shape[0]
    step = lam_ref.shape[2] // halves
    copies = [
        pltpu.make_async_copy(
            lam_ref.at[:, :, pl.ds(i * step, step)], held_ref.at[:, :, pl.ds(i * step, step)], sems.at[i]
        )
        for i in range(halves)
    ]
    for copy in copies:
        copy.start()
    total = pair_ref.shape[1]
    depth = coupling_ref.shape[0]
    owners, _, pairs = gap_ref.shape
    me, sub = place_ref[0], place_ref[1]
    orbital = lax.broadcasted_iota(jnp.int32, (depth, total), 0)
    coupling = coupling_ref[...]
    product = None
    for side in range(2):
        columns = one_hot(orbital == pair_ref[side : side + 1, :])
        picked = pick_rows(columns, pick_columns(coupling, columns))
        product = picked if product is None else product * picked
    frm, to = square_iotas(total)
    block, within = to // pairs, to % pairs
    source = ((me ^ (block % owners)) * 2 + (sub ^ (block // owners))) * pairs + within
    turned = jnp.dot(
        product.astype(jnp.bfloat16), one_hot(frm == source), preferred_element_type=jnp.float32
    )
    full[...] = turned
    row, column = square_iotas(pairs)
    for k in range(owners):
        start = pl.multiple_of(((me ^ k) * 2 + sub) * pairs, pairs)
        rows = pl.ds(k * pairs, pairs)
        w_ref[rows, :] = full[pl.ds(start, pairs), :].astype(jnp.bfloat16)
        gap = jnp.sum(jnp.where(row == column, gap_ref[me ^ k], 0.0), axis=1, keepdims=True)
        gaps_ref[rows, :] = jnp.broadcast_to(gap, (pairs, LANES))
    for copy in copies:
        copy.wait()


def prepare(pair_list, coupling, pair_gap, place, lambda_amps):
    owners, _, pairs = pair_gap.shape
    total = pair_list.shape[0]
    mine = owners * pairs
    vmem = pl.BlockSpec(memory_space=pltpu.VMEM)
    anywhere = pl.BlockSpec(memory_space=pl.ANY)
    fixed = [
        pltpu.with_memory_space_constraint(value, pltpu.HBM)
        for value in (pair_list.T, coupling, pair_gap)
    ]
    return pl.pallas_call(
        prepare_kernel,
        in_specs=[vmem, vmem, vmem, pl.BlockSpec(memory_space=pltpu.SMEM), anywhere],
        out_specs=[vmem, vmem, anywhere],
        out_shape=[
            jax.ShapeDtypeStruct((mine, total), jnp.bfloat16),
            jax.ShapeDtypeStruct((mine, LANES), jnp.float32),
            jax.ShapeDtypeStruct(lambda_amps.shape, lambda_amps.dtype),
        ],
        scratch_shapes=[
            pltpu.VMEM((total, total), jnp.float32),
            pltpu.SemaphoreType.DMA((4,)),
        ],
        compiler_params=pltpu.CompilerParams(vmem_limit_bytes=VMEM_BYTES),
        cost_estimate=pl.CostEstimate(
            flops=12 * total * coupling.size,
            bytes_accessed=4 * coupling.size + 4 * lambda_amps.size,
            transcendentals=0,
        ),
    )(*fixed, place, pltpu.with_memory_space_constraint(lambda_amps, pltpu.HBM))


def dress_kernel(owners, rows, groups, place_ref, tile_of_ref, mask_ref, *refs):
    tile_refs, lam_ref = refs[:owners], refs[owners]
    out_refs = refs[owners + 1 : -2]
    tiles, stage = refs[-2:]
    me = place_ref[0]
    flat = [(k, c, out, j) for out, group in zip(out_refs, groups) for j, (k, c) in enumerate(group)]
    starts = [pl.multiple_of((me ^ k) * rows + c * ROWS, ROWS) for k, c, _, _ in flat]
    for k in range(owners):
        for n, start in enumerate(starts):
            tiles[k, pl.ds(n * ROWS, ROWS), :] = tile_refs[k][0, pl.ds(start, ROWS), :]
    swap = swap_matrix()
    parts = mask_ref.shape[2]
    for g in range(lam_ref.shape[2] // ROWS):
        for i in range(ROWS):
            pair = g * ROWS + i
            ladder = jnp.dot(
                tiles[tile_of_ref[0, 0, pair] ^ me],
                lam_ref[0, 0, pair],
                preferred_element_type=jnp.float32,
            )
            width = ladder.shape[1] // parts
            for part in range(parts):
                keep = mask_ref[0, 0, part, pair].astype(jnp.float32)
                cols = slice(part * width, (part + 1) * width)
                for n, start in enumerate(starts):
                    amps = lam_ref[0, 0, pair, pl.ds(start, ROWS), cols].astype(jnp.float32)
                    kept = keep * ladder[n * ROWS : (n + 1) * ROWS, cols]
                    stage[g, n, pl.ds(i * ROWS, ROWS), cols] = (amps + kept).astype(jnp.bfloat16)
        for n, (_, _, out, j) in enumerate(flat):
            turned = jnp.dot(swap, stage[g, n], preferred_element_type=jnp.float32)
            out[j, :, pl.ds(g * ROWS, ROWS), :] = turned.astype(jnp.bfloat16).reshape(
                ROWS, ROWS, turned.shape[1]
            )


def dress(groups, place, tile_of, tile_mask, tiles, lambda_amps):
    owners = len(tiles)
    pairs, tile_rows, cols = lambda_amps.shape[2:]
    rows = tile_rows // owners
    smem = pl.BlockSpec(memory_space=pltpu.SMEM)
    vmem = pl.BlockSpec(memory_space=pltpu.VMEM)
    count = sum(len(group) for group in groups)
    return pl.pallas_call(
        functools.partial(dress_kernel, owners, rows, groups),
        in_specs=[smem] * 3 + [vmem] * (owners + 1),
        out_specs=[vmem] * len(groups),
        out_shape=[
            jax.ShapeDtypeStruct((len(group), ROWS, pairs, cols), jnp.bfloat16)
            for group in groups
        ],
        scratch_shapes=[
            pltpu.VMEM((owners, count * ROWS, tile_rows), jnp.bfloat16),
            pltpu.VMEM((pairs // ROWS, count, ROWS * ROWS, cols), jnp.bfloat16),
        ],
        compiler_params=pltpu.CompilerParams(vmem_limit_bytes=VMEM_BYTES),
        cost_estimate=pl.CostEstimate(
            flops=2 * pairs * count * ROWS * tile_rows * cols,
            bytes_accessed=3 * pairs * tile_rows * cols,
            transcendentals=0,
        ),
    )(place, tile_of, jnp.swapaxes(tile_mask, 2, 3), *tiles, lambda_amps)


def finish_kernel(pieces, chunk, place_ref, row_ref, w_ref, gap_ref, col_ref, *refs):
    piece_refs = refs[:pieces]
    out_ref, ys, done, sems = refs[-4:]
    _, rows, pairs, cols = piece_refs[0].shape
    owners = pieces // 2
    halves = pairs // ROWS
    mine = owners * pairs
    me = place_ref[0]
    weights = w_ref[...]
    col = col_ref[...]
    for a in range(rows):
        amps = jnp.concatenate([piece_refs[j][0, a] for j in range(pieces)], axis=0)
        cycle = jnp.dot(weights, amps, preferred_element_type=jnp.float32)
        level = gap_ref[...] + row_ref[chunk * rows + a]
        energy = jnp.concatenate([level] * (cols // LANES), axis=1) + col
        value = (-(amps[:mine].astype(jnp.float32) + cycle) / energy).astype(jnp.bfloat16)
        for g in range(owners * halves):
            ys[g, pl.ds(a * ROWS, ROWS), :] = value[g * ROWS : (g + 1) * ROWS]
    swap = swap_matrix()
    leaving = []
    for g in range(owners * halves):
        turned = jnp.dot(swap, ys[g], preferred_element_type=jnp.float32)
        done[g] = turned.astype(jnp.bfloat16).reshape(ROWS, rows, cols)
        k, h = g // halves, g % halves
        copy = pltpu.make_async_copy(
            done.at[g],
            out_ref.at[me ^ k, 0, pl.ds(h * ROWS, ROWS), pl.ds(chunk * rows, rows), :],
            sems.at[g],
        )
        copy.start()
        leaving.append(copy)
    for copy in leaving:
        copy.wait()


def finish(chunk, place, row_energy, weights, gaps, col_energy, pieces, before, shape):
    _, rows, pairs, cols = pieces[0][0].shape
    owners = len(pieces) // 2
    groups = owners * (pairs // ROWS)
    smem = pl.BlockSpec(memory_space=pltpu.SMEM)
    anywhere = pl.BlockSpec(memory_space=pl.ANY)
    args = [place, row_energy, weights, gaps, col_energy] + [piece for piece, _ in pieces]
    in_specs = [smem, smem]
    in_specs += [pl.BlockSpec(value.shape, lambda i: (0, 0)) for value in args[2:5]]
    for _, index in pieces:
        in_specs.append(
            pl.BlockSpec((1, rows, pairs, cols), lambda i, index=index: (index, 0, 0, 0))
        )
    aliases = {}
    if before is not None:
        aliases = {len(args): 0}
        args.append(before)
        in_specs.append(anywhere)
    return pl.pallas_call(
        functools.partial(finish_kernel, len(pieces), chunk),
        grid=(1,),
        in_specs=in_specs,
        out_specs=anywhere,
        out_shape=jax.ShapeDtypeStruct(shape, jnp.bfloat16),
        scratch_shapes=[
            pltpu.VMEM((groups, ROWS * rows, cols), jnp.bfloat16),
            pltpu.VMEM((groups, ROWS, rows, cols), jnp.bfloat16),
            pltpu.SemaphoreType.DMA((groups,)),
        ],
        input_output_aliases=aliases,
        compiler_params=pltpu.CompilerParams(vmem_limit_bytes=VMEM_BYTES),
        cost_estimate=pl.CostEstimate(flops=0, bytes_accessed=0, transcendentals=0),
    )(*args)


def local_chunked(
    lambda_amps,
    integral_tiles,
    tile_of,
    tile_mask,
    pair_list,
    coupling,
    pair_gap,
    row_energy,
    col_energy,
):
    pairs, tile_rows, cols = lambda_amps.shape[2:]
    owners = lax.axis_size("pair")
    rows = tile_rows // owners
    chunks = rows // ROWS
    me = lax.axis_index("pair").astype(jnp.int32)
    sub = lax.axis_index("sub").astype(jnp.int32)
    place = jnp.stack([me, sub])

    def to_owner(value, k):
        return lax.ppermute(value, "pair", [(o, o ^ k) for o in range(owners)])

    def to_sibling(value):
        return lax.ppermute(value, "sub", [(0, 1), (1, 0)])

    def after(value, earlier):
        return value if earlier is None else lax.optimization_barrier((value, earlier))[0]

    tiles = [integral_tiles] + [to_owner(integral_tiles, k) for k in range(1, owners)]
    weights, gaps, held = prepare(pair_list, coupling, pair_gap, place, lambda_amps)

    far = list(range(owners - 1, 1, -1))
    first = [((k, 0),) for k in far]
    near = [tuple((k, c) for c in range(chunks)) for k in (1, 0)]
    rest = near + [((k, c),) for c in range(1, chunks) for k in far]
    direct = {}
    for groups in (first, rest):
        sent = dress(groups, place, tile_of, tile_mask, tiles, held)
        held = after(held, sent[0])
        for group, value in zip(groups, sent):
            k = group[0][0]
            landed = to_owner(value, k) if k else value
            for index, key in enumerate(group):
                direct[key] = (landed, index)

    shape = (owners, 1, pairs, rows, cols)
    col = col_energy.reshape(1, cols)
    result, other = None, {}
    for c in range(chunks):
        for k in far:
            value, index = direct[k, c]
            other[k, c] = (to_sibling(value), index)
        if c == 0:
            for k in (0, 1):
                value, _ = direct[k, 0]
                if k == 0:
                    value = after(value, direct[far[0], 0][0])
                passed = to_sibling(value)
                for index in range(chunks):
                    other[k, index] = (passed, index)
        pieces = [held_by[k, c] for held_by in (direct, other) for k in range(owners)]
        result = finish(c, place, row_energy, weights, gaps, col, pieces, result, shape)
    return result


def solution(mesh):
    placed = (
        P(("mol", "pair"), "sub", None, None, "tile"),
        P(("mol", "pair"), None, None),
        P(("mol", "pair"), "sub", None),
        P(("mol", "pair"), "sub", None, "tile"),
        P("mol", None),
        P("mol", None),
        P("mol", "sub", None),
        P(("mol", "pair")),
        P(("mol", "tile")),
    )
    owners, subs = mesh.shape["pair"], mesh.shape["sub"]

    def local(*args):
        tile_rows, cols = args[0].shape[3:]
        rows = tile_rows // owners
        power = owners & (owners - 1) == 0
        fits = rows % ROWS == 0 and cols % LANES == 0 and args[1].shape[0] == 1
        if power and fits and subs == 2 and args[0].shape[2] % ROWS == 0:
            return local_chunked(*args)
        return local_general(*args)

    return jax.shard_map(
        local,
        mesh=mesh,
        in_specs=placed,
        out_specs=P("mol", "sub", None, "pair", "tile"),
        check_vma=False,
    )
```

time: 72.6 us -> 65.4 us (0.901)
  waiting for transfers between devices: 29.5 us -> 37.7 us
  starting transfers between devices: 22 us -> 15 us
  local copies, waits for them, and re-layouts: 5.13 us -> 0.02 us
  Pallas kernels: 15.6 us -> 11.9 us
    ppermute x9 -> x8, waiting for transfers between devices: 28 us -> 36.7 us  [to_owner(): return lax.ppermute(value, 'pair', [(o, o ^ k) for o in range(owners)])]
    ppermute x9 -> x8, starting transfers between devices: 20.4 us -> 14.4 us  [to_owner(): return lax.ppermute(value, 'pair', [(o, o ^ k) for o in range(owners)])]
    unnamed x22 -> x10, local copies, waits for them, and re-layouts: 5.13 us -> 0.02 us
    pallas_call x5, Pallas kernels: 15.6 us -> 11.9 us  [the longest x2 4.84 us: finish(): pl.pallas_call(functools.partial(finish_kernel, len(pieces), chunk), grid...]
    ppermute x8 -> x6, starting transfers between devices: 1.52 us -> 0.59 us  [to_sibling(): return lax.ppermute(value, 'sub', [(0, 1), (1, 0)])]
  transfers between devices with their start and end apart: 17 -> 14, of which waited for: 8 -> 6; matrix products, arithmetic and copies ran while one was open for 0% -> 0% of each run, Pallas kernels for 13% -> 9%
where the time goes in v3:
time: 65.4 us; the launch traced here: 64.8 us
  waiting for transfers between devices  37.7 us (58%)
  starting transfers between devices  15 us (23%)
  Pallas kernels  11.9 us (18%)
    ppermute x8, waiting for transfers between devices, to_owner(): return lax.ppermute(value, 'pair', [(o, o ^ k) for o in range(owners)])  36.7 us
    ppermute x8, starting transfers between devices, to_owner(): return lax.ppermute(value, 'pair', [(o, o ^ k) for o in range(owners)])  14.4 us
    pallas_call x2, Pallas kernels, finish(): pl.pallas_call(functools.partial(finish_kernel, len(pieces), chunk), grid...  4.84 us
    pallas_call x1, Pallas kernels, prepare(): pl.pallas_call(prepare_kernel, in_specs=[vmem, vmem, vmem, pl.BlockSpec(m...  3.72 us
    pallas_call x2, Pallas kernels, dress(): pl.pallas_call(functools.partial(dress_kernel, owners, rows, groups), in_...  3.34 us
  transfers between devices with their start and end apart: 14, of which 6 were waited for; matrix products, arithmetic and copies ran while one was open for 0% of the time, Pallas kernels for 9%

profile of v3, /device:TPU:0, one launch (start us, length us, event | category | flops | bytes accessed | tf_op | source)
XLA Modules:
  0.0 64.8 jit_solution(9838978669390137033)
XLA Ops:
  0.0 0.0 copy-start
  0.0 0.0 copy-start.3
  0.0 0.0 copy-start.1
  0.0 5.1 %collective-permute-start.2 = (bf16[1,128,128]{2,1,0:T(8,128)(2,1)}, bf16[1,128,128]{2,1,0:T(8,128)(2,1)S(1)}, u32[]{:S(2)}, u32[]{:S(2)}) collective-permute-start(bf16[1,128,128]{2,1,0:T(8,128)(2,1)} %refs_0_.3), channel_id=1, source_target_pairs={{0,12},{4,8},{8,4},{12,0},{1,13},{5,9},{9,5},{13,1},{2,14},{6,10},... | collective-permute-start | bytes 98312 | tf_op jit(solution)/shard_map/ppermute | solution.py:358
  5.1 0.0 collective-permute-start.1
  5.1 0.6 collective-permute-start
  5.8 0.1 pad_add_fusion.place_ref
  5.8 3.7 %shard_map.91 = (bf16[128,256]{1,0:T(8,128)(2,1)S(1)}, f32[128,128]{1,0:T(8,128)S(1)}, bf16[1,1,32,128,256]{4,3,2,1,0:T(8,128)(2,1)S(1)}) custom-call(s32[2,256]{1,0:T(2,128)} %bitcast.9, f32[400,400]{1,0:T(8,128)} %coupling_ref.1, f32[4,1,32]{2,1,0:T(1,128)} %gap_ref.1, s32[2]{0:T(128)S(1)} %pad_add_fusion.place_ref, bf16[1,1,32,128,256]{4,3,2,1,0:T(8,128)(2,1)} %lam_ref.1), custom_call_target="tpu_custom_call" | custom-call | flops 491520000 | bytes 4834304 | tf_op jit(solution)/shard_map/pallas_call | solution.py:183
  9.6 0.0 collective-permute-done.2.refs_3_
  9.6 0.6 collective-permute-done.1.refs_2_
  10.1 0.0 collective-permute-done.refs_1_
  10.2 0.0 copy-done
  10.2 0.0 copy-done.3
  10.2 0.0 copy-done.1
  10.2 0.0 copy-start.2
  10.2 0.0 copy-start.4
  10.2 1.4 %shard_map.92 = (bf16[1,16,32,256]{3,2,1,0:T(8,128)(2,1)S(1)}, bf16[1,16,32,256]{3,2,1,0:T(8,128)(2,1)S(1)}) custom-call(s32[2]{0:T(128)S(1)} %pad_add_fusion.place_ref, s32[1,1,32]{2,1,0:T(1,128)S(1)} %copy-done.3, s32[1,1,2,32]{3,2,1,0:T(2,128)S(1)} %bitcast.5, bf16[1,128,128]{2,1,0:T(8,128)(2,1)S(1)} %copy-done, ...), custom_call_target="tpu_custom_call" | custom-call | flops 67108864 | bytes 3145728 | tf_op jit(solution)/shard_map/pallas_call | solution.py:247
  11.6 1.9 %shard_map.93 = (bf16[2,16,32,256]{3,2,1,0:T(8,128)(2,1)S(1)}, bf16[2,16,32,256]{3,2,1,0:T(8,128)(2,1)S(1)}, bf16[1,16,32,256]{3,2,1,0:T(8,128)(2,1)S(1)}, bf16[1,16,32,256]{3,2,1,0:T(8,128)(2,1)S(1)}) custom-call(s32[2]{0:T(128)S(1)} %pad_add_fusion.place_ref, s32[1,1,32]{2,1,0:T(1,128)S(1)} %copy-done.3, s32[1,1,2,32]{3,2,1,0:T(2,128)S(1)} %bitcast.6, ...), custom_call_target="tpu_custom_call" | custom-call | flops 201326592 | bytes 3145728 | tf_op jit(solution)/shard_map/pallas_call | solution.py:247
  13.6 0.9 %collective-permute-start.3 = (bf16[2,16,32,256]{3,2,1,0:T(8,128)(2,1)S(1)}, bf16[2,16,32,256]{3,2,1,0:T(8,128)(2,1)S(1)}, u32[]{:S(2)}, u32[]{:S(2)}) collective-permute-start(bf16[2,16,32,256]{3,2,1,0:T(8,128)(2,1)S(1)} %get-tuple-element.22), channel_id=1, source_target_pairs={{0,4},{4,0},{8,12},{12,8},{1,5},{5,1},{9,13},{13,9},{2,6},{6,2},{1... | collective-permute-start | bytes 1572872 | tf_op jit(solution)/shard_map/ppermute | solution.py:358
  14.5 2.6 %collective-permute-start.6 = (bf16[1,16,32,256]{3,2,1,0:T(8,128)(2,1)S(1)}, bf16[1,16,32,256]{3,2,1,0:T(8,128)(2,1)S(1)}, u32[]{:S(2)}, u32[]{:S(2)}) collective-permute-start(bf16[1,16,32,256]{3,2,1,0:T(8,128)(2,1)S(1)} %get-tuple-element.19), channel_id=1, source_target_pairs={{0,12},{4,8},{8,4},{12,0},{1,13},{5,9},{9,5},{13,1},{2,14},{6,10},... | collective-permute-start | bytes 786440 | tf_op jit(solution)/shard_map/ppermute | solution.py:358
  17.1 0.3 collective-permute-start.11
  17.4 2.6 %collective-permute-start.4 = (bf16[1,16,32,256]{3,2,1,0:T(8,128)(2,1)S(1)}, bf16[1,16,32,256]{3,2,1,0:T(8,128)(2,1)S(1)}, u32[]{:S(2)}, u32[]{:S(2)}) collective-permute-start(bf16[1,16,32,256]{3,2,1,0:T(8,128)(2,1)S(1)} %get-tuple-element.23), channel_id=1, source_target_pairs={{0,8},{4,12},{8,0},{12,4},{1,9},{5,13},{9,1},{13,5},{2,10},{6,14},... | collective-permute-start | bytes 786440 | tf_op jit(solution)/shard_map/ppermute | solution.py:358
  20.0 15.6 %collective-permute-done.6.refs_3_ = bf16[1,16,32,256]{3,2,1,0:T(8,128)(2,1)S(1)} collective-permute-done((bf16[1,16,32,256]{3,2,1,0:T(8,128)(2,1)S(1)}, bf16[1,16,32,256]{3,2,1,0:T(8,128)(2,1)S(1)}, u32[]{:S(2)}, u32[]{:S(2)}) %collective-permute-start.6) | collective-permute-done | bytes 262176 | tf_op jit(solution)/shard_map/ppermute | solution.py:358
  35.7 0.0 collective-permute-start.7
  35.7 1.5 %collective-permute-done.3.refs_1_ = bf16[2,16,32,256]{3,2,1,0:T(8,128)(2,1)S(1)} collective-permute-done((bf16[2,16,32,256]{3,2,1,0:T(8,128)(2,1)S(1)}, bf16[2,16,32,256]{3,2,1,0:T(8,128)(2,1)S(1)}, u32[]{:S(2)}, u32[]{:S(2)}) %collective-permute-start.3) | collective-permute-done | bytes 524320 | tf_op jit(solution)/shard_map/ppermute | solution.py:358
  37.2 0.0 collective-permute-start.8
  37.2 2.2 %collective-permute-start.5 = (bf16[1,16,32,256]{3,2,1,0:T(8,128)(2,1)S(1)}, bf16[1,16,32,256]{3,2,1,0:T(8,128)(2,1)S(1)}, u32[]{:S(2)}, u32[]{:S(2)}) collective-permute-start(bf16[1,16,32,256]{3,2,1,0:T(8,128)(2,1)S(1)} %get-tuple-element.24), channel_id=1, source_target_pairs={{0,12},{4,8},{8,4},{12,0},{1,13},{5,9},{9,5},{13,1},{2,14},{6,10},... | collective-permute-start | bytes 786440 | tf_op jit(solution)/shard_map/ppermute | solution.py:358
  39.4 13.4 %collective-permute-done.11.refs_2_ = bf16[1,16,32,256]{3,2,1,0:T(8,128)(2,1)S(1)} collective-permute-done((bf16[1,16,32,256]{3,2,1,0:T(8,128)(2,1)S(1)}, bf16[1,16,32,256]{3,2,1,0:T(8,128)(2,1)S(1)}, u32[]{:S(2)}, u32[]{:S(2)}) %collective-permute-start.11) | collective-permute-done | bytes 262176 | tf_op jit(solution)/shard_map/ppermute | solution.py:358
  52.7 0.0 collective-permute-start.12
  52.7 5.6 %collective-permute-done.4.refs_2_ = bf16[1,16,32,256]{3,2,1,0:T(8,128)(2,1)S(1)} collective-permute-done((bf16[1,16,32,256]{3,2,1,0:T(8,128)(2,1)S(1)}, bf16[1,16,32,256]{3,2,1,0:T(8,128)(2,1)S(1)}, u32[]{:S(2)}, u32[]{:S(2)}) %collective-permute-start.4) | collective-permute-done | bytes 262176 | tf_op jit(solution)/shard_map/ppermute | solution.py:358
  58.4 0.0 collective-permute-start.13
  58.4 0.0 collective-permute-done.5.refs_3_
  58.4 0.5 collective-permute-start.9
  58.9 0.0 collective-permute-done.12.refs_6_
  58.9 0.1 collective-permute-start.10
  59.0 0.9 %collective-permute-done.13.refs_7_ = bf16[1,16,32,256]{3,2,1,0:T(8,128)(2,1)S(1)} collective-permute-done((bf16[1,16,32,256]{3,2,1,0:T(8,128)(2,1)S(1)}, bf16[1,16,32,256]{3,2,1,0:T(8,128)(2,1)S(1)}, u32[]{:S(2)}, u32[]{:S(2)}) %collective-permute-start.13) | collective-permute-done | bytes 262176 | tf_op jit(solution)/shard_map/ppermute | solution.py:361
  59.9 0.0 collective-permute-done.7.refs_4_
  59.9 0.0 collective-permute-done.8.refs_5_
  59.9 0.0 copy-done.2
  59.9 0.0 copy-done.4
  59.9 2.4 %shard_map.94.refs_8_ = bf16[4,1,32,32,256]{4,3,2,1,0:T(8,128)(2,1)} custom-call(s32[2]{0:T(128)S(1)} %pad_add_fusion.place_ref, f32[32]{0:T(128)S(1)} %copy-done.4, bf16[128,256]{1,0:T(8,128)(2,1)S(1)} %get-tuple-element.16.w_ref, f32[128,128]{1,0:T(8,128)S(1)} %get-tuple-element.17.gap_ref, f32[1,256]{1,0:T(1,128)S(1)} %bitcast.7, ...), custom_call_target="tpu_custom_call" | custom-call | tf_op jit(solution)/shard_map/pallas_call | solution.py:321
  62.4 0.0 collective-permute-done.9.refs_6_
  62.4 0.0 collective-permute-done.10.refs_7_
  62.4 2.4 %shard_map.95 = bf16[4,1,32,32,256]{4,3,2,1,0:T(8,128)(2,1)} custom-call(s32[2]{0:T(128)S(1)} %pad_add_fusion.place_ref, f32[32]{0:T(128)S(1)} %copy-done.4, bf16[128,256]{1,0:T(8,128)(2,1)S(1)} %get-tuple-element.16.w_ref, f32[128,128]{1,0:T(8,128)S(1)} %get-tuple-element.17.gap_ref, f32[1,256]{1,0:T(1,128)S(1)} %bitcast.8, ...), custom_call_target="tpu_custom_call", output_to_operand_aliasing={{}: (13, {})} | custom-call | tf_op jit(solution)/shard_map/pallas_call | solution.py:321
Async XLA Ops:
  0.0 10.2 %copy-start = (bf16[1,128,128]{2,1,0:T(8,128)(2,1)S(1)}, bf16[1,128,128]{2,1,0:T(8,128)(2,1)}, u32[]{:S(2)}) copy-start(bf16[1,128,128]{2,1,0:T(8,128)(2,1)} %refs_0_.3) | copy-start | bytes 98308
  0.0 10.2 %copy-start.3 = (s32[1,1,32]{2,1,0:T(1,128)S(1)}, s32[1,1,32]{2,1,0:T(1,128)}, u32[]{:S(2)}) copy-start(s32[1,1,32]{2,1,0:T(1,128)} %tile_of_ref.3) | copy-start | bytes 388
  0.0 10.2 %copy-start.1 = (s32[1,1,32,2]{2,3,1,0:T(2,128)S(1)}, s32[1,1,32,2]{2,3,1,0:T(2,128)}, u32[]{:S(2)}) copy-start(s32[1,1,32,2]{2,3,1,0:T(2,128)} %param.12) | copy-start | bytes 772
  0.0 9.6 %collective-permute-start.2 = (bf16[1,128,128]{2,1,0:T(8,128)(2,1)}, bf16[1,128,128]{2,1,0:T(8,128)(2,1)S(1)}, u32[]{:S(2)}, u32[]{:S(2)}) collective-permute-start(bf16[1,128,128]{2,1,0:T(8,128)(2,1)} %refs_0_.3), channel_id=1, source_target_pairs={{0,12},{4,8},{8,4},{12,0},{1,13},{5,9},{9,5},{13,1},{2,14},{6,10},... | collective-permute-start | bytes 98312 | tf_op jit(solution)/shard_map/ppermute | solution.py:358
  5.1 5.0 %collective-permute-start.1 = (bf16[1,128,128]{2,1,0:T(8,128)(2,1)}, bf16[1,128,128]{2,1,0:T(8,128)(2,1)S(1)}, u32[]{:S(2)}, u32[]{:S(2)}) collective-permute-start(bf16[1,128,128]{2,1,0:T(8,128)(2,1)} %refs_0_.3), channel_id=1, source_target_pairs={{0,8},{4,12},{8,0},{12,4},{1,9},{5,13},{9,1},{13,5},{2,10},{6,14},... | collective-permute-start | bytes 98312 | tf_op jit(solution)/shard_map/ppermute | solution.py:358
  5.1 5.0 %collective-permute-start = (bf16[1,128,128]{2,1,0:T(8,128)(2,1)}, bf16[1,128,128]{2,1,0:T(8,128)(2,1)S(1)}, u32[]{:S(2)}, u32[]{:S(2)}) collective-permute-start(bf16[1,128,128]{2,1,0:T(8,128)(2,1)} %refs_0_.3), channel_id=1, source_target_pairs={{0,4},{4,0},{8,12},{12,8},{1,5},{5,1},{9,13},{13,9},{2,6},{6,2},{1... | collective-permute-start | bytes 98312 | tf_op jit(solution)/shard_map/ppermute | solution.py:358
  10.2 49.7 %copy-start.2 = (f32[256]{0:T(256)S(1)}, f32[256]{0:T(256)}, u32[]{:S(2)}) copy-start(f32[256]{0:T(256)} %param.17) | copy-start | bytes 3076
  10.2 49.7 %copy-start.4 = (f32[32]{0:T(128)S(1)}, f32[32]{0:T(128)}, u32[]{:S(2)}) copy-start(f32[32]{0:T(128)} %row_ref.3) | copy-start | bytes 388
  13.6 23.6 %collective-permute-start.3 = (bf16[2,16,32,256]{3,2,1,0:T(8,128)(2,1)S(1)}, bf16[2,16,32,256]{3,2,1,0:T(8,128)(2,1)S(1)}, u32[]{:S(2)}, u32[]{:S(2)}) collective-permute-start(bf16[2,16,32,256]{3,2,1,0:T(8,128)(2,1)S(1)} %get-tuple-element.22), channel_id=1, source_target_pairs={{0,4},{4,0},{8,12},{12,8},{1,5},{5,1},{9,13},{13,9},{2,6},{6,2},{1... | collective-permute-start | bytes 1572872 | tf_op jit(solution)/shard_map/ppermute | solution.py:358
  14.5 21.2 %collective-permute-start.6 = (bf16[1,16,32,256]{3,2,1,0:T(8,128)(2,1)S(1)}, bf16[1,16,32,256]{3,2,1,0:T(8,128)(2,1)S(1)}, u32[]{:S(2)}, u32[]{:S(2)}) collective-permute-start(bf16[1,16,32,256]{3,2,1,0:T(8,128)(2,1)S(1)} %get-tuple-element.19), channel_id=1, source_target_pairs={{0,12},{4,8},{8,4},{12,0},{1,13},{5,9},{9,5},{13,1},{2,14},{6,10},... | collective-permute-start | bytes 786440 | tf_op jit(solution)/shard_map/ppermute | solution.py:358
  17.1 35.6 %collective-permute-start.11 = (bf16[1,16,32,256]{3,2,1,0:T(8,128)(2,1)S(1)}, bf16[1,16,32,256]{3,2,1,0:T(8,128)(2,1)S(1)}, u32[]{:S(2)}, u32[]{:S(2)}) collective-permute-start(bf16[1,16,32,256]{3,2,1,0:T(8,128)(2,1)S(1)} %get-tuple-element.26), channel_id=1, source_target_pairs={{0,8},{4,12},{8,0},{12,4},{1,9},{5,13},{9,1},{13,5},{2,10},{6,14},... | collective-permute-start | bytes 786440 | tf_op jit(solution)/shard_map/ppermute | solution.py:358
  17.4 41.0 %collective-permute-start.4 = (bf16[1,16,32,256]{3,2,1,0:T(8,128)(2,1)S(1)}, bf16[1,16,32,256]{3,2,1,0:T(8,128)(2,1)S(1)}, u32[]{:S(2)}, u32[]{:S(2)}) collective-permute-start(bf16[1,16,32,256]{3,2,1,0:T(8,128)(2,1)S(1)} %get-tuple-element.23), channel_id=1, source_target_pairs={{0,8},{4,12},{8,0},{12,4},{1,9},{5,13},{9,1},{13,5},{2,10},{6,14},... | collective-permute-start | bytes 786440 | tf_op jit(solution)/shard_map/ppermute | solution.py:358
  35.7 24.2 %collective-permute-start.7 = (bf16[2,16,32,256]{3,2,1,0:T(8,128)(2,1)S(1)}, bf16[2,16,32,256]{3,2,1,0:T(8,128)(2,1)S(1)}, u32[]{:S(2)}, u32[]{:S(2)}) collective-permute-start(bf16[2,16,32,256]{3,2,1,0:T(8,128)(2,1)S(1)} %get-tuple-element.25.refs_0_), channel_id=1, source_target_pairs={{0,1},{1,0},{2,3},{3,2},{4,5},{5,4},{6,7},{7,6},{8,9},{9,8},{10,11... | collective-permute-start | bytes 1572872 | tf_op jit(solution)/shard_map/ppermute | solution.py:361
  37.2 22.7 %collective-permute-start.8 = (bf16[2,16,32,256]{3,2,1,0:T(8,128)(2,1)S(1)}, bf16[2,16,32,256]{3,2,1,0:T(8,128)(2,1)S(1)}, u32[]{:S(2)}, u32[]{:S(2)}) collective-permute-start(bf16[2,16,32,256]{3,2,1,0:T(8,128)(2,1)S(1)} %collective-permute-done.3.refs_1_), channel_id=1, source_target_pairs={{0,1},{1,0},{2,3},{3,2},{4,5},{5,4},{6,7},{7,6},{8,9},{9,8},{10,11... | collective-permute-start | bytes 1572872 | tf_op jit(solution)/shard_map/ppermute | solution.py:361
  37.2 21.2 %collective-permute-start.5 = (bf16[1,16,32,256]{3,2,1,0:T(8,128)(2,1)S(1)}, bf16[1,16,32,256]{3,2,1,0:T(8,128)(2,1)S(1)}, u32[]{:S(2)}, u32[]{:S(2)}) collective-permute-start(bf16[1,16,32,256]{3,2,1,0:T(8,128)(2,1)S(1)} %get-tuple-element.24), channel_id=1, source_target_pairs={{0,12},{4,8},{8,4},{12,0},{1,13},{5,9},{9,5},{13,1},{2,14},{6,10},... | collective-permute-start | bytes 786440 | tf_op jit(solution)/shard_map/ppermute | solution.py:358
  52.7 6.1 %collective-permute-start.12 = (bf16[1,16,32,256]{3,2,1,0:T(8,128)(2,1)S(1)}, bf16[1,16,32,256]{3,2,1,0:T(8,128)(2,1)S(1)}, u32[]{:S(2)}, u32[]{:S(2)}) collective-permute-start(bf16[1,16,32,256]{3,2,1,0:T(8,128)(2,1)S(1)} %collective-permute-done.11.refs_2_), channel_id=1, source_target_pairs={{0,1},{1,0},{2,3},{3,2},{4,5},{5,4},{6,7},{7,6},{8,9},{9,8},{10,11... | collective-permute-start | bytes 786440 | tf_op jit(solution)/shard_map/ppermute | solution.py:361
  58.4 1.5 %collective-permute-start.13 = (bf16[1,16,32,256]{3,2,1,0:T(8,128)(2,1)S(1)}, bf16[1,16,32,256]{3,2,1,0:T(8,128)(2,1)S(1)}, u32[]{:S(2)}, u32[]{:S(2)}) collective-permute-start(bf16[1,16,32,256]{3,2,1,0:T(8,128)(2,1)S(1)} %collective-permute-done.6.refs_3_), channel_id=1, source_target_pairs={{0,1},{1,0},{2,3},{3,2},{4,5},{5,4},{6,7},{7,6},{8,9},{9,8},{10,11... | collective-permute-start | bytes 786440 | tf_op jit(solution)/shard_map/ppermute | solution.py:361
  58.4 4.0 %collective-permute-start.9 = (bf16[1,16,32,256]{3,2,1,0:T(8,128)(2,1)S(1)}, bf16[1,16,32,256]{3,2,1,0:T(8,128)(2,1)S(1)}, u32[]{:S(2)}, u32[]{:S(2)}) collective-permute-start(bf16[1,16,32,256]{3,2,1,0:T(8,128)(2,1)S(1)} %collective-permute-done.4.refs_2_), channel_id=1, source_target_pairs={{0,1},{1,0},{2,3},{3,2},{4,5},{5,4},{6,7},{7,6},{8,9},{9,8},{10,11... | collective-permute-start | bytes 786440 | tf_op jit(solution)/shard_map/ppermute | solution.py:361
  58.9 3.5 %collective-permute-start.10 = (bf16[1,16,32,256]{3,2,1,0:T(8,128)(2,1)S(1)}, bf16[1,16,32,256]{3,2,1,0:T(8,128)(2,1)S(1)}, u32[]{:S(2)}, u32[]{:S(2)}) collective-permute-start(bf16[1,16,32,256]{3,2,1,0:T(8,128)(2,1)S(1)} %collective-permute-done.5.refs_3_), channel_id=1, source_target_pairs={{0,1},{1,0},{2,3},{3,2},{4,5},{5,4},{6,7},{7,6},{8,9},{9,8},{10,11... | collective-permute-start | bytes 786440 | tf_op jit(solution)/shard_map/ppermute | solution.py:361

commit v4 on v3

--- a/solution.py
+++ b/solution.py
@@ -93,6 +93,10 @@
     return (-total_sum / energy_gap).astype(jnp.bfloat16)
 
 
+def in_hbm(value):
+    return pltpu.with_memory_space_constraint(value, pltpu.HBM)
+
+
 def one_hot(hits):
     return jnp.where(hits, 1.0, 0.0).astype(jnp.bfloat16)
 
@@ -130,17 +134,7 @@
     return high + (mid + low)
 
 
-def prepare_kernel(pair_ref, coupling_ref, gap_ref, place_ref, lam_ref, w_ref, gaps_ref, held_ref, full, sems):
-    halves = sems.shape[0]
-    step = lam_ref.shape[2] // halves
-    copies = [
-        pltpu.make_async_copy(
-            lam_ref.at[:, :, pl.ds(i * step, step)], held_ref.at[:, :, pl.ds(i * step, step)], sems.at[i]
-        )
-        for i in range(halves)
-    ]
-    for copy in copies:
-        copy.start()
+def weights_kernel(pair_ref, coupling_ref, gap_ref, place_ref, w_ref, gaps_ref, full):
     total = pair_ref.shape[1]
     depth = coupling_ref.shape[0]
     owners, _, pairs = gap_ref.shape
@@ -155,10 +149,9 @@
     frm, to = square_iotas(total)
     block, within = to // pairs, to % pairs
     source = ((me ^ (block % owners)) * 2 + (sub ^ (block // owners))) * pairs + within
-    turned = jnp.dot(
+    full[...] = jnp.dot(
         product.astype(jnp.bfloat16), one_hot(frm == source), preferred_element_type=jnp.float32
     )
-    full[...] = turned
     row, column = square_iotas(pairs)
     for k in range(owners):
         start = pl.multiple_of(((me ^ k) * 2 + sub) * pairs, pairs)
@@ -166,46 +159,40 @@
         w_ref[rows, :] = full[pl.ds(start, pairs), :].astype(jnp.bfloat16)
         gap = jnp.sum(jnp.where(row == column, gap_ref[me ^ k], 0.0), axis=1, keepdims=True)
         gaps_ref[rows, :] = jnp.broadcast_to(gap, (pairs, LANES))
-    for copy in copies:
-        copy.wait()
-
-
-def prepare(pair_list, coupling, pair_gap, place, lambda_amps):
+
+
+def make_weights(pair_list, coupling, pair_gap, place):
     owners, _, pairs = pair_gap.shape
     total = pair_list.shape[0]
     mine = owners * pairs
     vmem = pl.BlockSpec(memory_space=pltpu.VMEM)
-    anywhere = pl.BlockSpec(memory_space=pl.ANY)
-    fixed = [
-        pltpu.with_memory_space_constraint(value, pltpu.HBM)
-        for value in (pair_list.T, coupling, pair_gap)
-    ]
     return pl.pallas_call(
-        prepare_kernel,
-        in_specs=[vmem, vmem, vmem, pl.BlockSpec(memory_space=pltpu.SMEM), anywhere],
-        out_specs=[vmem, vmem, anywhere],
+        weights_kernel,
+        in_specs=[vmem, vmem, vmem, pl.BlockSpec(memory_space=pltpu.SMEM)],
+        out_specs=[vmem, vmem],
         out_shape=[
             jax.ShapeDtypeStruct((mine, total), jnp.bfloat16),
             jax.ShapeDtypeStruct((mine, LANES), jnp.float32),
-            jax.ShapeDtypeStruct(lambda_amps.shape, lambda_amps.dtype),
         ],
-        scratch_shapes=[
-            pltpu.VMEM((total, total), jnp.float32),
-            pltpu.SemaphoreType.DMA((4,)),
-        ],
+        scratch_shapes=[pltpu.VMEM((total, total), jnp.float32)],
         compiler_params=pltpu.CompilerParams(vmem_limit_bytes=VMEM_BYTES),
         cost_estimate=pl.CostEstimate(
-            flops=12 * total * coupling.size,
-            bytes_accessed=4 * coupling.size + 4 * lambda_amps.size,
-            transcendentals=0,
+            flops=12 * total * coupling.size, bytes_accessed=4 * coupling.size, transcendentals=0
         ),
-    )(*fixed, place, pltpu.with_memory_space_constraint(lambda_amps, pltpu.HBM))
+    )(pair_list.T, coupling, pair_gap, place)
 
 
 def dress_kernel(owners, rows, groups, place_ref, tile_of_ref, mask_ref, *refs):
     tile_refs, lam_ref = refs[:owners], refs[owners]
-    out_refs = refs[owners + 1 : -2]
-    tiles, stage = refs[-2:]
+    out_refs = refs[owners + 1 : -4]
+    tiles, stage, amps_ref, sems = refs[-4:]
+    brought = lam_ref.shape[2] // sems.shape[0]
+    copies = []
+    for n in range(sems.shape[0]):
+        block = pl.ds(n * brought, brought)
+        copy = pltpu.make_async_copy(lam_ref.at[0, 0, block], amps_ref.at[block], sems.at[n])
+        copy.start()
+        copies.append(copy)
     me = place_ref[0]
     flat = [(k, c, out, j) for out, group in zip(out_refs, groups) for j, (k, c) in enumerate(group)]
     starts = [pl.multiple_of((me ^ k) * rows + c * ROWS, ROWS) for k, c, _, _ in flat]
@@ -217,9 +204,11 @@
     for g in range(lam_ref.shape[2] // ROWS):
         for i in range(ROWS):
             pair = g * ROWS + i
+            if pair % brought == 0:
+                copies[pair // brought].wait()
             ladder = jnp.dot(
                 tiles[tile_of_ref[0, 0, pair] ^ me],
-                lam_ref[0, 0, pair],
+                amps_ref[pair],
                 preferred_element_type=jnp.float32,
             )
             width = ladder.shape[1] // parts
@@ -227,7 +216,7 @@
                 keep = mask_ref[0, 0, part, pair].astype(jnp.float32)
                 cols = slice(part * width, (part + 1) * width)
                 for n, start in enumerate(starts):
-                    amps = lam_ref[0, 0, pair, pl.ds(start, ROWS), cols].astype(jnp.float32)
+                    amps = amps_ref[pair, pl.ds(start, ROWS), cols].astype(jnp.float32)
                     kept = keep * ladder[n * ROWS : (n + 1) * ROWS, cols]
                     stage[g, n, pl.ds(i * ROWS, ROWS), cols] = (amps + kept).astype(jnp.bfloat16)
         for n, (_, _, out, j) in enumerate(flat):
@@ -246,7 +235,7 @@
     count = sum(len(group) for group in groups)
     return pl.pallas_call(
         functools.partial(dress_kernel, owners, rows, groups),
-        in_specs=[smem] * 3 + [vmem] * (owners + 1),
+        in_specs=[smem] * 3 + [vmem] * owners + [pl.BlockSpec(memory_space=pl.ANY)],
         out_specs=[vmem] * len(groups),
         out_shape=[
             jax.ShapeDtypeStruct((len(group), ROWS, pairs, cols), jnp.bfloat16)
@@ -255,6 +244,8 @@
         scratch_shapes=[
             pltpu.VMEM((owners, count * ROWS, tile_rows), jnp.bfloat16),
             pltpu.VMEM((pairs // ROWS, count, ROWS * ROWS, cols), jnp.bfloat16),
+            pltpu.VMEM((pairs, tile_rows, cols), jnp.bfloat16),
+            pltpu.SemaphoreType.DMA((pairs // 4,)),
         ],
         compiler_params=pltpu.CompilerParams(vmem_limit_bytes=VMEM_BYTES),
         cost_estimate=pl.CostEstimate(
@@ -262,25 +253,51 @@
             bytes_accessed=3 * pairs * tile_rows * cols,
             transcendentals=0,
         ),
-    )(place, tile_of, jnp.swapaxes(tile_mask, 2, 3), *tiles, lambda_amps)
-
-
-def finish_kernel(pieces, chunk, place_ref, row_ref, w_ref, gap_ref, col_ref, *refs):
+    )(
+        place,
+        in_hbm(tile_of),
+        in_hbm(jnp.swapaxes(tile_mask, 2, 3)),
+        in_hbm(tiles[0]),
+        *tiles[1:],
+        in_hbm(lambda_amps),
+    )
+
+
+def finish_kernel(indices, chunk, place_ref, row_ref, w_ref, gap_ref, col_ref, *refs):
+    pieces = len(indices)
     piece_refs = refs[:pieces]
-    out_ref, ys, done, sems = refs[-4:]
+    out_ref, xs, ys, done, in_sems, out_sems = refs[-6:]
     _, rows, pairs, cols = piece_refs[0].shape
     owners = pieces // 2
     halves = pairs // ROWS
     mine = owners * pairs
     me = place_ref[0]
+    steps = in_sems.shape[0]
+    some = rows // steps
+    arriving = []
+    for n in range(steps):
+        block = pl.ds(n * some, some)
+        for j, index in enumerate(indices):
+            copy = pltpu.make_async_copy(
+                piece_refs[j].at[index, block],
+                xs.at[block, pl.ds(j * pairs, pairs), :],
+                in_sems.at[n, j],
+            )
+            copy.start()
+            arriving.append(copy)
     weights = w_ref[...]
     col = col_ref[...]
     for a in range(rows):
-        amps = jnp.concatenate([piece_refs[j][0, a] for j in range(pieces)], axis=0)
+        if a % some == 0:
+            for copy in arriving[a // some * pieces : (a // some + 1) * pieces]:
+                copy.wait()
+        amps = xs[a]
         cycle = jnp.dot(weights, amps, preferred_element_type=jnp.float32)
         level = gap_ref[...] + row_ref[chunk * rows + a]
         energy = jnp.concatenate([level] * (cols // LANES), axis=1) + col
-        value = (-(amps[:mine].astype(jnp.float32) + cycle) / energy).astype(jnp.bfloat16)
+        rough = pl.reciprocal(energy, approx=True)
+        inverse = rough * (energy * rough - 2.0)
+        value = ((amps[:mine].astype(jnp.float32) + cycle) * inverse).astype(jnp.bfloat16)
         for g in range(owners * halves):
             ys[g, pl.ds(a * ROWS, ROWS), :] = value[g * ROWS : (g + 1) * ROWS]
     swap = swap_matrix()
@@ -292,7 +309,7 @@
         copy = pltpu.make_async_copy(
             done.at[g],
             out_ref.at[me ^ k, 0, pl.ds(h * ROWS, ROWS), pl.ds(chunk * rows, rows), :],
-            sems.at[g],
+            out_sems.at[g],
         )
         copy.start()
         leaving.append(copy)
@@ -305,28 +322,25 @@
     owners = len(pieces) // 2
     groups = owners * (pairs // ROWS)
     smem = pl.BlockSpec(memory_space=pltpu.SMEM)
+    vmem = pl.BlockSpec(memory_space=pltpu.VMEM)
     anywhere = pl.BlockSpec(memory_space=pl.ANY)
     args = [place, row_energy, weights, gaps, col_energy] + [piece for piece, _ in pieces]
-    in_specs = [smem, smem]
-    in_specs += [pl.BlockSpec(value.shape, lambda i: (0, 0)) for value in args[2:5]]
-    for _, index in pieces:
-        in_specs.append(
-            pl.BlockSpec((1, rows, pairs, cols), lambda i, index=index: (index, 0, 0, 0))
-        )
+    in_specs = [smem, smem, vmem, vmem, vmem] + [anywhere] * len(pieces)
     aliases = {}
     if before is not None:
         aliases = {len(args): 0}
         args.append(before)
         in_specs.append(anywhere)
     return pl.pallas_call(
-        functools.partial(finish_kernel, len(pieces), chunk),
-        grid=(1,),
+        functools.partial(finish_kernel, [index for _, index in pieces], chunk),
         in_specs=in_specs,
         out_specs=anywhere,
         out_shape=jax.ShapeDtypeStruct(shape, jnp.bfloat16),
         scratch_shapes=[
+            pltpu.VMEM((rows, len(pieces) * pairs, cols), jnp.bfloat16),
             pltpu.VMEM((groups, ROWS * rows, cols), jnp.bfloat16),
             pltpu.VMEM((groups, ROWS, rows, cols), jnp.bfloat16),
+            pltpu.SemaphoreType.DMA((4, len(pieces))),
             pltpu.SemaphoreType.DMA((groups,)),
         ],
         input_output_aliases=aliases,
@@ -364,21 +378,18 @@
         return value if earlier is None else lax.optimization_barrier((value, earlier))[0]
 
     tiles = [integral_tiles] + [to_owner(integral_tiles, k) for k in range(1, owners)]
-    weights, gaps, held = prepare(pair_list, coupling, pair_gap, place, lambda_amps)
 
     far = list(range(owners - 1, 1, -1))
-    first = [((k, 0),) for k in far]
-    near = [tuple((k, c) for c in range(chunks)) for k in (1, 0)]
-    rest = near + [((k, c),) for c in range(1, chunks) for k in far]
+    groups = [((k, c),) for c in range(chunks) for k in far]
+    groups += [tuple((k, c) for c in range(chunks)) for k in (1, 0)]
+    sent = dress(groups, place, tile_of, tile_mask, tiles, lambda_amps)
     direct = {}
-    for groups in (first, rest):
-        sent = dress(groups, place, tile_of, tile_mask, tiles, held)
-        held = after(held, sent[0])
-        for group, value in zip(groups, sent):
-            k = group[0][0]
-            landed = to_owner(value, k) if k else value
-            for index, key in enumerate(group):
-                direct[key] = (landed, index)
+    for group, value in zip(groups, sent):
+        k = group[0][0]
+        landed = to_owner(value, k) if k else value
+        for index, key in enumerate(group):
+            direct[key] = (landed, index)
+    weights, gaps = make_weights(after(pair_list, sent[0]), coupling, pair_gap, place)
 
     shape = (owners, 1, pairs, rows, cols)
     col = col_energy.reshape(1, cols)
@@ -390,8 +401,7 @@
         if c == 0:
             for k in (0, 1):
                 value, _ = direct[k, 0]
-                if k == 0:
-                    value = after(value, direct[far[0], 0][0])
+                value = after(value, weights if k else direct[far[0], 0][0])
                 passed = to_sibling(value)
                 for index in range(chunks):
                     other[k, index] = (passed, index)

time: 65.4 us -> 69.5 us (1.063)
  waiting for transfers between devices: 37.7 us -> 41.8 us
  Pallas kernels: 11.9 us -> 15 us
  starting transfers between devices: 15 us -> 12.4 us
    ppermute x8, waiting for transfers between devices: 36.7 us -> 40.9 us  [to_owner(): return lax.ppermute(value, 'pair', [(o, o ^ k) for o in range(owners)])]
    ppermute x8, starting transfers between devices: 14.4 us -> 11.8 us  [to_owner(): return lax.ppermute(value, 'pair', [(o, o ^ k) for o in range(owners)])]
    pallas_call x3, Pallas kernels: 8.56 us -> 10.6 us  [the longest x2 7.56 us: finish(): pl.pallas_call(functools.partial(finish_kernel, [index for _, index in pi...]
    pallas_call x2 -> x1, Pallas kernels: 3.34 us -> 4.33 us  [dress(): pl.pallas_call(functools.partial(dress_kernel, owners, rows, groups), in_...]
  transfers between devices with their start and end apart: 14 -> 14, of which waited for: 6 -> 8; matrix products, arithmetic and copies ran while one was open for 0% -> 0% of each run, Pallas kernels for 9% -> 10%
where the time goes in v4:
time: 69.5 us; the launch traced here: 69.3 us
  waiting for transfers between devices  41.8 us (60%)
  Pallas kernels  15 us (22%)
  starting transfers between devices  12.4 us (18%)
    ppermute x8, waiting for transfers between devices, to_owner(): return lax.ppermute(value, 'pair', [(o, o ^ k) for o in range(owners)])  40.9 us
    ppermute x8, starting transfers between devices, to_owner(): return lax.ppermute(value, 'pair', [(o, o ^ k) for o in range(owners)])  11.8 us
    pallas_call x2, Pallas kernels, finish(): pl.pallas_call(functools.partial(finish_kernel, [index for _, index in pi...  7.56 us
    pallas_call x1, Pallas kernels, dress(): pl.pallas_call(functools.partial(dress_kernel, owners, rows, groups), in_...  4.33 us
    pallas_call x1, Pallas kernels, make_weights(): pl.pallas_call(weights_kernel, in_specs=[vmem, vmem, vmem, pl.BlockSpec(m...  3.06 us
  transfers between devices with their start and end apart: 14, of which 8 were waited for; matrix products, arithmetic and copies ran while one was open for 0% of the time, Pallas kernels for 10%

profile of v4, /device:TPU:0, one launch (start us, length us, event | category | flops | bytes accessed | tf_op | source)
XLA Modules:
  0.0 69.3 jit_solution(8040145977923459811)
XLA Ops:
  0.0 0.0 copy-start.3
  0.0 0.0 copy-start.4
  0.0 0.0 copy-start.2
  0.0 0.0 copy-start.1
  0.0 0.0 copy-start
  0.0 4.1 %collective-permute-start.1 = (bf16[1,128,128]{2,1,0:T(8,128)(2,1)}, bf16[1,128,128]{2,1,0:T(8,128)(2,1)S(1)}, u32[]{:S(2)}, u32[]{:S(2)}) collective-permute-start(bf16[1,128,128]{2,1,0:T(8,128)(2,1)} %refs_0_.1), channel_id=1, source_target_pairs={{0,8},{4,12},{8,0},{12,4},{1,9},{5,13},{9,1},{13,5},{2,10},{6,14},... | collective-permute-start | bytes 98312 | tf_op jit(solution)/shard_map/ppermute | solution.py:372
  4.1 1.6 %collective-permute-start = (bf16[1,128,128]{2,1,0:T(8,128)(2,1)}, bf16[1,128,128]{2,1,0:T(8,128)(2,1)S(1)}, u32[]{:S(2)}, u32[]{:S(2)}) collective-permute-start(bf16[1,128,128]{2,1,0:T(8,128)(2,1)} %refs_0_.1), channel_id=1, source_target_pairs={{0,4},{4,0},{8,12},{12,8},{1,5},{5,1},{9,13},{13,9},{2,6},{6,2},{1... | collective-permute-start | bytes 98312 | tf_op jit(solution)/shard_map/ppermute | solution.py:372
  5.7 0.0 collective-permute-start.2
  5.7 0.1 pad_add_fusion.place_ref
  5.8 0.9 %collective-permute-done.1.refs_2_ = bf16[1,128,128]{2,1,0:T(8,128)(2,1)S(1)} collective-permute-done((bf16[1,128,128]{2,1,0:T(8,128)(2,1)}, bf16[1,128,128]{2,1,0:T(8,128)(2,1)S(1)}, u32[]{:S(2)}, u32[]{:S(2)}) %collective-permute-start.1) | collective-permute-done | bytes 32800 | tf_op jit(solution)/shard_map/ppermute | solution.py:372
  6.7 1.6 %collective-permute-done.refs_1_ = bf16[1,128,128]{2,1,0:T(8,128)(2,1)S(1)} collective-permute-done((bf16[1,128,128]{2,1,0:T(8,128)(2,1)}, bf16[1,128,128]{2,1,0:T(8,128)(2,1)S(1)}, u32[]{:S(2)}, u32[]{:S(2)}) %collective-permute-start) | collective-permute-done | bytes 32800 | tf_op jit(solution)/shard_map/ppermute | solution.py:372
  8.3 3.4 %collective-permute-done.2.refs_3_ = bf16[1,128,128]{2,1,0:T(8,128)(2,1)S(1)} collective-permute-done((bf16[1,128,128]{2,1,0:T(8,128)(2,1)}, bf16[1,128,128]{2,1,0:T(8,128)(2,1)S(1)}, u32[]{:S(2)}, u32[]{:S(2)}) %collective-permute-start.2) | collective-permute-done | bytes 32800 | tf_op jit(solution)/shard_map/ppermute | solution.py:372
  11.6 4.3 %shard_map.91 = (bf16[1,16,32,256]{3,2,1,0:T(8,128)(2,1)S(1)}, bf16[1,16,32,256]{3,2,1,0:T(8,128)(2,1)S(1)}, bf16[1,16,32,256]{3,2,1,0:T(8,128)(2,1)S(1)}, bf16[...) custom-call(s32[2]{0:T(128)S(1)} %pad_add_fusion.place_ref, ...), custom_call_target="tpu_custom_call" | custom-call | flops 268435456 | bytes 3145728 | tf_op jit(solution)/shard_map/pallas_call | solution.py:236
  16.0 0.1 collective-permute-start.3
  16.0 0.4 collective-permute-start.6
  16.5 3.1 %collective-permute-start.11 = (bf16[1,16,32,256]{3,2,1,0:T(8,128)(2,1)S(1)}, bf16[1,16,32,256]{3,2,1,0:T(8,128)(2,1)S(1)}, u32[]{:S(2)}, u32[]{:S(2)}) collective-permute-start(bf16[1,16,32,256]{3,2,1,0:T(8,128)(2,1)S(1)} %get-tuple-element.26), channel_id=1, source_target_pairs={{0,8},{4,12},{8,0},{12,4},{1,9},{5,13},{9,1},{13,5},{2,10},{6,14},... | collective-permute-start | bytes 786440 | tf_op jit(solution)/shard_map/ppermute | solution.py:372
  19.5 0.0 collective-permute-start.4
  19.6 0.0 copy-done.3
  19.6 0.0 copy-done.4
  19.6 0.0 copy-done.2
  19.6 3.1 %shard_map.92 = (bf16[128,256]{1,0:T(8,128)(2,1)S(1)}, f32[128,128]{1,0:T(8,128)S(1)}) custom-call(s32[2,256]{1,0:T(2,128)S(1)} %bitcast.7, f32[400,400]{1,0:T(8,128)S(1)} %copy-done.2, f32[4,1,32]{2,1,0:T(1,128)S(1)} %copy-done.4, s32[2]{0:T(128)S(1)} %pad_add_fusion.place_ref), custom_call_target="tpu_custom_call" | custom-call | flops 491520000 | bytes 640000 | tf_op jit(solution)/shard_map/pallas_call | solution.py:169
  22.6 12.3 %collective-permute-done.6.refs_3_ = bf16[1,16,32,256]{3,2,1,0:T(8,128)(2,1)S(1)} collective-permute-done((bf16[1,16,32,256]{3,2,1,0:T(8,128)(2,1)S(1)}, bf16[1,16,32,256]{3,2,1,0:T(8,128)(2,1)S(1)}, u32[]{:S(2)}, u32[]{:S(2)}) %collective-permute-start.6) | collective-permute-done | bytes 262176 | tf_op jit(solution)/shard_map/ppermute | solution.py:372
  34.9 0.0 collective-permute-start.7
  34.9 2.3 %collective-permute-done.3.refs_1_ = bf16[2,16,32,256]{3,2,1,0:T(8,128)(2,1)S(1)} collective-permute-done((bf16[2,16,32,256]{3,2,1,0:T(8,128)(2,1)S(1)}, bf16[2,16,32,256]{3,2,1,0:T(8,128)(2,1)S(1)}, u32[]{:S(2)}, u32[]{:S(2)}) %collective-permute-start.3) | collective-permute-done | bytes 524320 | tf_op jit(solution)/shard_map/ppermute | solution.py:372
  37.2 0.0 collective-permute-start.8
  37.2 2.5 %collective-permute-start.5 = (bf16[1,16,32,256]{3,2,1,0:T(8,128)(2,1)S(1)}, bf16[1,16,32,256]{3,2,1,0:T(8,128)(2,1)S(1)}, u32[]{:S(2)}, u32[]{:S(2)}) collective-permute-start(bf16[1,16,32,256]{3,2,1,0:T(8,128)(2,1)S(1)} %get-tuple-element.23), channel_id=1, source_target_pairs={{0,12},{4,8},{8,4},{12,0},{1,13},{5,9},{9,5},{13,1},{2,14},{6,10},... | collective-permute-start | bytes 786440 | tf_op jit(solution)/shard_map/ppermute | solution.py:372
  39.7 15.1 %collective-permute-done.11.refs_2_ = bf16[1,16,32,256]{3,2,1,0:T(8,128)(2,1)S(1)} collective-permute-done((bf16[1,16,32,256]{3,2,1,0:T(8,128)(2,1)S(1)}, bf16[1,16,32,256]{3,2,1,0:T(8,128)(2,1)S(1)}, u32[]{:S(2)}, u32[]{:S(2)}) %collective-permute-start.11) | collective-permute-done | bytes 262176 | tf_op jit(solution)/shard_map/ppermute | solution.py:372
  54.8 0.0 collective-permute-start.12
  54.8 5.3 %collective-permute-done.4.refs_2_ = bf16[1,16,32,256]{3,2,1,0:T(8,128)(2,1)S(1)} collective-permute-done((bf16[1,16,32,256]{3,2,1,0:T(8,128)(2,1)S(1)}, bf16[1,16,32,256]{3,2,1,0:T(8,128)(2,1)S(1)}, u32[]{:S(2)}, u32[]{:S(2)}) %collective-permute-start.4) | collective-permute-done | bytes 262176 | tf_op jit(solution)/shard_map/ppermute | solution.py:372
  60.2 0.0 collective-permute-start.13
  60.2 0.0 collective-permute-done.5.refs_3_
  60.2 0.5 collective-permute-start.9
  60.7 0.0 collective-permute-done.12.refs_6_
  60.7 0.1 collective-permute-start.10
  60.8 0.9 %collective-permute-done.13.refs_7_ = bf16[1,16,32,256]{3,2,1,0:T(8,128)(2,1)S(1)} collective-permute-done((bf16[1,16,32,256]{3,2,1,0:T(8,128)(2,1)S(1)}, bf16[1,16,32,256]{3,2,1,0:T(8,128)(2,1)S(1)}, u32[]{:S(2)}, u32[]{:S(2)}) %collective-permute-start.13) | collective-permute-done | bytes 262176 | tf_op jit(solution)/shard_map/ppermute | solution.py:375
  61.7 0.0 collective-permute-done.7.refs_4_
  61.7 0.0 collective-permute-done.8.refs_5_
  61.7 0.0 copy-done.1
  61.7 0.0 copy-done
  61.7 3.8 %shard_map.93.refs_8_ = bf16[4,1,32,32,256]{4,3,2,1,0:T(8,128)(2,1)} custom-call(s32[2]{0:T(128)S(1)} %pad_add_fusion.place_ref, f32[32]{0:T(128)S(1)} %copy-done.1, bf16[128,256]{1,0:T(8,128)(2,1)S(1)} %get-tuple-element.18.w_ref, f32[128,128]{1,0:T(8,128)S(1)} %get-tuple-element.19.gap_ref, f32[1,256]{1,0:T(1,128)S(1)} %bitcast.5, ...), custom_call_target="tpu_custom_call" | custom-call | tf_op jit(solution)/shard_map/pallas_call | solution.py:334
  65.5 0.0 collective-permute-done.9.refs_6_
  65.5 0.0 collective-permute-done.10.refs_7_
  65.5 3.8 %shard_map.94 = bf16[4,1,32,32,256]{4,3,2,1,0:T(8,128)(2,1)} custom-call(s32[2]{0:T(128)S(1)} %pad_add_fusion.place_ref, f32[32]{0:T(128)S(1)} %copy-done.1, bf16[128,256]{1,0:T(8,128)(2,1)S(1)} %get-tuple-element.18.w_ref, f32[128,128]{1,0:T(8,128)S(1)} %get-tuple-element.19.gap_ref, f32[1,256]{1,0:T(1,128)S(1)} %bitcast.6, ...), custom_call_target="tpu_custom_call", output_to_operand_aliasing={{}: (13, {})} | custom-call | tf_op jit(solution)/shard_map/pallas_call | solution.py:334
Async XLA Ops:
  0.0 19.6 %copy-start.3 = (s32[256,2]{0,1:T(2,128)S(1)}, s32[256,2]{0,1:T(2,128)}, u32[]{:S(2)}) copy-start(s32[256,2]{0,1:T(2,128)} %param.13) | copy-start | bytes 6148
  0.0 19.6 %copy-start.4 = (f32[4,1,32]{2,1,0:T(1,128)S(1)}, f32[4,1,32]{2,1,0:T(1,128)}, u32[]{:S(2)}) copy-start(f32[4,1,32]{2,1,0:T(1,128)} %gap_ref.1) | copy-start | bytes 1540
  0.0 19.6 %copy-start.2 = (f32[400,400]{1,0:T(8,128)S(1)}, f32[400,400]{1,0:T(8,128)}, u32[]{:S(2)}) copy-start(f32[400,400]{1,0:T(8,128)} %coupling_ref.1) | copy-start | bytes 1920004
  0.0 61.7 %copy-start.1 = (f32[32]{0:T(128)S(1)}, f32[32]{0:T(128)}, u32[]{:S(2)}) copy-start(f32[32]{0:T(128)} %row_ref.3) | copy-start | bytes 388
  0.0 61.7 %copy-start = (f32[256]{0:T(256)S(1)}, f32[256]{0:T(256)}, u32[]{:S(2)}) copy-start(f32[256]{0:T(256)} %param.17) | copy-start | bytes 3076
  0.0 6.7 %collective-permute-start.1 = (bf16[1,128,128]{2,1,0:T(8,128)(2,1)}, bf16[1,128,128]{2,1,0:T(8,128)(2,1)S(1)}, u32[]{:S(2)}, u32[]{:S(2)}) collective-permute-start(bf16[1,128,128]{2,1,0:T(8,128)(2,1)} %refs_0_.1), channel_id=1, source_target_pairs={{0,8},{4,12},{8,0},{12,4},{1,9},{5,13},{9,1},{13,5},{2,10},{6,14},... | collective-permute-start | bytes 98312 | tf_op jit(solution)/shard_map/ppermute | solution.py:372
  4.1 4.1 %collective-permute-start = (bf16[1,128,128]{2,1,0:T(8,128)(2,1)}, bf16[1,128,128]{2,1,0:T(8,128)(2,1)S(1)}, u32[]{:S(2)}, u32[]{:S(2)}) collective-permute-start(bf16[1,128,128]{2,1,0:T(8,128)(2,1)} %refs_0_.1), channel_id=1, source_target_pairs={{0,4},{4,0},{8,12},{12,8},{1,5},{5,1},{9,13},{13,9},{2,6},{6,2},{1... | collective-permute-start | bytes 98312 | tf_op jit(solution)/shard_map/ppermute | solution.py:372
  5.7 5.9 %collective-permute-start.2 = (bf16[1,128,128]{2,1,0:T(8,128)(2,1)}, bf16[1,128,128]{2,1,0:T(8,128)(2,1)S(1)}, u32[]{:S(2)}, u32[]{:S(2)}) collective-permute-start(bf16[1,128,128]{2,1,0:T(8,128)(2,1)} %refs_0_.1), channel_id=1, source_target_pairs={{0,12},{4,8},{8,4},{12,0},{1,13},{5,9},{9,5},{13,1},{2,14},{6,10},... | collective-permute-start | bytes 98312 | tf_op jit(solution)/shard_map/ppermute | solution.py:372
  16.0 21.3 %collective-permute-start.3 = (bf16[2,16,32,256]{3,2,1,0:T(8,128)(2,1)S(1)}, bf16[2,16,32,256]{3,2,1,0:T(8,128)(2,1)S(1)}, u32[]{:S(2)}, u32[]{:S(2)}) collective-permute-start(bf16[2,16,32,256]{3,2,1,0:T(8,128)(2,1)S(1)} %get-tuple-element.21), channel_id=1, source_target_pairs={{0,4},{4,0},{8,12},{12,8},{1,5},{5,1},{9,13},{13,9},{2,6},{6,2},{1... | collective-permute-start | bytes 1572872 | tf_op jit(solution)/shard_map/ppermute | solution.py:372
  16.0 18.9 %collective-permute-start.6 = (bf16[1,16,32,256]{3,2,1,0:T(8,128)(2,1)S(1)}, bf16[1,16,32,256]{3,2,1,0:T(8,128)(2,1)S(1)}, u32[]{:S(2)}, u32[]{:S(2)}) collective-permute-start(bf16[1,16,32,256]{3,2,1,0:T(8,128)(2,1)S(1)} %get-tuple-element.16), channel_id=1, source_target_pairs={{0,12},{4,8},{8,4},{12,0},{1,13},{5,9},{9,5},{13,1},{2,14},{6,10},... | collective-permute-start | bytes 786440 | tf_op jit(solution)/shard_map/ppermute | solution.py:372
  16.5 38.4 %collective-permute-start.11 = (bf16[1,16,32,256]{3,2,1,0:T(8,128)(2,1)S(1)}, bf16[1,16,32,256]{3,2,1,0:T(8,128)(2,1)S(1)}, u32[]{:S(2)}, u32[]{:S(2)}) collective-permute-start(bf16[1,16,32,256]{3,2,1,0:T(8,128)(2,1)S(1)} %get-tuple-element.26), channel_id=1, source_target_pairs={{0,8},{4,12},{8,0},{12,4},{1,9},{5,13},{9,1},{13,5},{2,10},{6,14},... | collective-permute-start | bytes 786440 | tf_op jit(solution)/shard_map/ppermute | solution.py:372
  19.5 40.6 %collective-permute-start.4 = (bf16[1,16,32,256]{3,2,1,0:T(8,128)(2,1)S(1)}, bf16[1,16,32,256]{3,2,1,0:T(8,128)(2,1)S(1)}, u32[]{:S(2)}, u32[]{:S(2)}) collective-permute-start(bf16[1,16,32,256]{3,2,1,0:T(8,128)(2,1)S(1)} %get-tuple-element.22), channel_id=1, source_target_pairs={{0,8},{4,12},{8,0},{12,4},{1,9},{5,13},{9,1},{13,5},{2,10},{6,14},... | collective-permute-start | bytes 786440 | tf_op jit(solution)/shard_map/ppermute | solution.py:372
  34.9 26.8 %collective-permute-start.7 = (bf16[2,16,32,256]{3,2,1,0:T(8,128)(2,1)S(1)}, bf16[2,16,32,256]{3,2,1,0:T(8,128)(2,1)S(1)}, u32[]{:S(2)}, u32[]{:S(2)}) collective-permute-start(bf16[2,16,32,256]{3,2,1,0:T(8,128)(2,1)S(1)} %get-tuple-element.24.refs_0_), channel_id=1, source_target_pairs={{0,1},{1,0},{2,3},{3,2},{4,5},{5,4},{6,7},{7,6},{8,9},{9,8},{10,11... | collective-permute-start | bytes 1572872 | tf_op jit(solution)/shard_map/ppermute | solution.py:375
  37.2 24.5 %collective-permute-start.8 = (bf16[2,16,32,256]{3,2,1,0:T(8,128)(2,1)S(1)}, bf16[2,16,32,256]{3,2,1,0:T(8,128)(2,1)S(1)}, u32[]{:S(2)}, u32[]{:S(2)}) collective-permute-start(bf16[2,16,32,256]{3,2,1,0:T(8,128)(2,1)S(1)} %collective-permute-done.3.refs_1_), channel_id=1, source_target_pairs={{0,1},{1,0},{2,3},{3,2},{4,5},{5,4},{6,7},{7,6},{8,9},{9,8},{10,11... | collective-permute-start | bytes 1572872 | tf_op jit(solution)/shard_map/ppermute | solution.py:375
  37.2 23.0 %collective-permute-start.5 = (bf16[1,16,32,256]{3,2,1,0:T(8,128)(2,1)S(1)}, bf16[1,16,32,256]{3,2,1,0:T(8,128)(2,1)S(1)}, u32[]{:S(2)}, u32[]{:S(2)}) collective-permute-start(bf16[1,16,32,256]{3,2,1,0:T(8,128)(2,1)S(1)} %get-tuple-element.23), channel_id=1, source_target_pairs={{0,12},{4,8},{8,4},{12,0},{1,13},{5,9},{9,5},{13,1},{2,14},{6,10},... | collective-permute-start | bytes 786440 | tf_op jit(solution)/shard_map/ppermute | solution.py:372
  54.8 5.9 %collective-permute-start.12 = (bf16[1,16,32,256]{3,2,1,0:T(8,128)(2,1)S(1)}, bf16[1,16,32,256]{3,2,1,0:T(8,128)(2,1)S(1)}, u32[]{:S(2)}, u32[]{:S(2)}) collective-permute-start(bf16[1,16,32,256]{3,2,1,0:T(8,128)(2,1)S(1)} %collective-permute-done.11.refs_2_), channel_id=1, source_target_pairs={{0,1},{1,0},{2,3},{3,2},{4,5},{5,4},{6,7},{7,6},{8,9},{9,8},{10,11... | collective-permute-start | bytes 786440 | tf_op jit(solution)/shard_map/ppermute | solution.py:375
  60.2 1.5 %collective-permute-start.13 = (bf16[1,16,32,256]{3,2,1,0:T(8,128)(2,1)S(1)}, bf16[1,16,32,256]{3,2,1,0:T(8,128)(2,1)S(1)}, u32[]{:S(2)}, u32[]{:S(2)}) collective-permute-start(bf16[1,16,32,256]{3,2,1,0:T(8,128)(2,1)S(1)} %collective-permute-done.6.refs_3_), channel_id=1, source_target_pairs={{0,1},{1,0},{2,3},{3,2},{4,5},{5,4},{6,7},{7,6},{8,9},{9,8},{10,11... | collective-permute-start | bytes 786440 | tf_op jit(solution)/shard_map/ppermute | solution.py:375
  60.2 5.3 %collective-permute-start.9 = (bf16[1,16,32,256]{3,2,1,0:T(8,128)(2,1)S(1)}, bf16[1,16,32,256]{3,2,1,0:T(8,128)(2,1)S(1)}, u32[]{:S(2)}, u32[]{:S(2)}) collective-permute-start(bf16[1,16,32,256]{3,2,1,0:T(8,128)(2,1)S(1)} %collective-permute-done.4.refs_2_), channel_id=1, source_target_pairs={{0,1},{1,0},{2,3},{3,2},{4,5},{5,4},{6,7},{7,6},{8,9},{9,8},{10,11... | collective-permute-start | bytes 786440 | tf_op jit(solution)/shard_map/ppermute | solution.py:375
  60.7 4.8 %collective-permute-start.10 = (bf16[1,16,32,256]{3,2,1,0:T(8,128)(2,1)S(1)}, bf16[1,16,32,256]{3,2,1,0:T(8,128)(2,1)S(1)}, u32[]{:S(2)}, u32[]{:S(2)}) collective-permute-start(bf16[1,16,32,256]{3,2,1,0:T(8,128)(2,1)S(1)} %collective-permute-done.5.refs_3_), channel_id=1, source_target_pairs={{0,1},{1,0},{2,3},{3,2},{4,5},{5,4},{6,7},{7,6},{8,9},{9,8},{10,11... | collective-permute-start | bytes 786440 | tf_op jit(solution)/shard_map/ppermute | solution.py:375

commit v5 on v4

--- a/solution.py
+++ b/solution.py
@@ -105,11 +105,6 @@
     return (lax.broadcasted_iota(jnp.int32, (size, size), axis) for axis in range(2))
 
 
-def swap_matrix():
-    to, frm = square_iotas(ROWS * ROWS)
-    return one_hot(to == (frm % ROWS) * ROWS + frm // ROWS)
-
-
 def split3(value):
     high = value.astype(jnp.bfloat16)
     rest = value - high.astype(jnp.float32)
@@ -134,7 +129,43 @@
     return high + (mid + low)
 
 
-def weights_kernel(pair_ref, coupling_ref, gap_ref, place_ref, w_ref, gaps_ref, full):
+def hold_kernel(lam_ref, held_ref, swap_ref, sems):
+    step = lam_ref.shape[2] // sems.shape[0]
+    copies = []
+    for i in range(sems.shape[0]):
+        block = pl.ds(i * step, step)
+        copy = pltpu.make_async_copy(
+            lam_ref.at[:, :, block], held_ref.at[:, :, block], sems.at[i]
+        )
+        copy.start()
+        copies.append(copy)
+    to, frm = square_iotas(ROWS * ROWS)
+    swap_ref[...] = one_hot(to == (frm % ROWS) * ROWS + frm // ROWS)
+    for copy in copies:
+        copy.wait()
+
+
+def hold(lambda_amps):
+    anywhere = pl.BlockSpec(memory_space=pl.ANY)
+    return pl.pallas_call(
+        hold_kernel,
+        in_specs=[anywhere],
+        out_specs=[anywhere, pl.BlockSpec(memory_space=pltpu.VMEM)],
+        out_shape=[
+            jax.ShapeDtypeStruct(lambda_amps.shape, lambda_amps.dtype),
+            jax.ShapeDtypeStruct((ROWS * ROWS, ROWS * ROWS), jnp.bfloat16),
+        ],
+        scratch_shapes=[pltpu.SemaphoreType.DMA((8,))],
+        compiler_params=pltpu.CompilerParams(vmem_limit_bytes=VMEM_BYTES),
+        cost_estimate=pl.CostEstimate(
+            flops=0, bytes_accessed=4 * lambda_amps.size, transcendentals=0
+        ),
+    )(in_hbm(lambda_amps))
+
+
+def weights_kernel(
+    pair_ref, coupling_ref, gap_ref, place_ref, row_ref, col_ref, w_ref, inverse_ref, full
+):
     total = pair_ref.shape[1]
     depth = coupling_ref.shape[0]
     owners, _, pairs = gap_ref.shape
@@ -158,57 +189,52 @@
         rows = pl.ds(k * pairs, pairs)
         w_ref[rows, :] = full[pl.ds(start, pairs), :].astype(jnp.bfloat16)
         gap = jnp.sum(jnp.where(row == column, gap_ref[me ^ k], 0.0), axis=1, keepdims=True)
-        gaps_ref[rows, :] = jnp.broadcast_to(gap, (pairs, LANES))
-
-
-def make_weights(pair_list, coupling, pair_gap, place):
+        for a in range(inverse_ref.shape[0]):
+            inverse_ref[a, rows, :] = -1.0 / ((gap + row_ref[a]) + col_ref[...])
+
+
+def make_weights(pair_list, coupling, pair_gap, place, row_energy, col_energy):
     owners, _, pairs = pair_gap.shape
     total = pair_list.shape[0]
     mine = owners * pairs
+    rows, cols = row_energy.shape[0], col_energy.shape[0]
+    smem = pl.BlockSpec(memory_space=pltpu.SMEM)
     vmem = pl.BlockSpec(memory_space=pltpu.VMEM)
     return pl.pallas_call(
         weights_kernel,
-        in_specs=[vmem, vmem, vmem, pl.BlockSpec(memory_space=pltpu.SMEM)],
+        in_specs=[vmem, vmem, vmem, smem, smem, vmem],
         out_specs=[vmem, vmem],
         out_shape=[
             jax.ShapeDtypeStruct((mine, total), jnp.bfloat16),
-            jax.ShapeDtypeStruct((mine, LANES), jnp.float32),
+            jax.ShapeDtypeStruct((rows, mine, cols), jnp.float32),
         ],
         scratch_shapes=[pltpu.VMEM((total, total), jnp.float32)],
         compiler_params=pltpu.CompilerParams(vmem_limit_bytes=VMEM_BYTES),
         cost_estimate=pl.CostEstimate(
             flops=12 * total * coupling.size, bytes_accessed=4 * coupling.size, transcendentals=0
         ),
-    )(pair_list.T, coupling, pair_gap, place)
+    )(pair_list.T, coupling, pair_gap, place, row_energy, col_energy.reshape(1, cols))
 
 
 def dress_kernel(owners, rows, groups, place_ref, tile_of_ref, mask_ref, *refs):
-    tile_refs, lam_ref = refs[:owners], refs[owners]
-    out_refs = refs[owners + 1 : -4]
-    tiles, stage, amps_ref, sems = refs[-4:]
-    brought = lam_ref.shape[2] // sems.shape[0]
-    copies = []
-    for n in range(sems.shape[0]):
-        block = pl.ds(n * brought, brought)
-        copy = pltpu.make_async_copy(lam_ref.at[0, 0, block], amps_ref.at[block], sems.at[n])
-        copy.start()
-        copies.append(copy)
+    tile_refs, lam_ref = (refs[0], refs[owners - 1], *refs[1 : owners - 1]), refs[owners]
+    swap_ref = refs[owners + 1]
+    out_refs = refs[owners + 2 : -2]
+    tiles, stage = refs[-2:]
     me = place_ref[0]
     flat = [(k, c, out, j) for out, group in zip(out_refs, groups) for j, (k, c) in enumerate(group)]
     starts = [pl.multiple_of((me ^ k) * rows + c * ROWS, ROWS) for k, c, _, _ in flat]
     for k in range(owners):
         for n, start in enumerate(starts):
             tiles[k, pl.ds(n * ROWS, ROWS), :] = tile_refs[k][0, pl.ds(start, ROWS), :]
-    swap = swap_matrix()
+    swap = swap_ref[...]
     parts = mask_ref.shape[2]
     for g in range(lam_ref.shape[2] // ROWS):
         for i in range(ROWS):
             pair = g * ROWS + i
-            if pair % brought == 0:
-                copies[pair // brought].wait()
             ladder = jnp.dot(
                 tiles[tile_of_ref[0, 0, pair] ^ me],
-                amps_ref[pair],
+                lam_ref[0, 0, pair],
                 preferred_element_type=jnp.float32,
             )
             width = ladder.shape[1] // parts
@@ -216,7 +242,7 @@
                 keep = mask_ref[0, 0, part, pair].astype(jnp.float32)
                 cols = slice(part * width, (part + 1) * width)
                 for n, start in enumerate(starts):
-                    amps = amps_ref[pair, pl.ds(start, ROWS), cols].astype(jnp.float32)
+                    amps = lam_ref[0, 0, pair, pl.ds(start, ROWS), cols].astype(jnp.float32)
                     kept = keep * ladder[n * ROWS : (n + 1) * ROWS, cols]
                     stage[g, n, pl.ds(i * ROWS, ROWS), cols] = (amps + kept).astype(jnp.bfloat16)
         for n, (_, _, out, j) in enumerate(flat):
@@ -226,7 +252,7 @@
             )
 
 
-def dress(groups, place, tile_of, tile_mask, tiles, lambda_amps):
+def dress(groups, place, tile_of, tile_mask, tiles, lambda_amps, swap):
     owners = len(tiles)
     pairs, tile_rows, cols = lambda_amps.shape[2:]
     rows = tile_rows // owners
@@ -235,7 +261,7 @@
     count = sum(len(group) for group in groups)
     return pl.pallas_call(
         functools.partial(dress_kernel, owners, rows, groups),
-        in_specs=[smem] * 3 + [vmem] * owners + [pl.BlockSpec(memory_space=pl.ANY)],
+        in_specs=[smem] * 3 + [vmem] * (owners + 2),
         out_specs=[vmem] * len(groups),
         out_shape=[
             jax.ShapeDtypeStruct((len(group), ROWS, pairs, cols), jnp.bfloat16)
@@ -244,8 +270,6 @@
         scratch_shapes=[
             pltpu.VMEM((owners, count * ROWS, tile_rows), jnp.bfloat16),
             pltpu.VMEM((pairs // ROWS, count, ROWS * ROWS, cols), jnp.bfloat16),
-            pltpu.VMEM((pairs, tile_rows, cols), jnp.bfloat16),
-            pltpu.SemaphoreType.DMA((pairs // 4,)),
         ],
         compiler_params=pltpu.CompilerParams(vmem_limit_bytes=VMEM_BYTES),
         cost_estimate=pl.CostEstimate(
@@ -258,49 +282,30 @@
         in_hbm(tile_of),
         in_hbm(jnp.swapaxes(tile_mask, 2, 3)),
         in_hbm(tiles[0]),
-        *tiles[1:],
-        in_hbm(lambda_amps),
-    )
-
-
-def finish_kernel(indices, chunk, place_ref, row_ref, w_ref, gap_ref, col_ref, *refs):
-    pieces = len(indices)
+        *tiles[2:],
+        tiles[1],
+        lambda_amps,
+        swap,
+    )
+
+
+def finish_kernel(pieces, chunk, place_ref, swap_ref, w_ref, inverse_ref, *refs):
     piece_refs = refs[:pieces]
-    out_ref, xs, ys, done, in_sems, out_sems = refs[-6:]
+    out_ref, ys, done, sems = refs[-4:]
     _, rows, pairs, cols = piece_refs[0].shape
     owners = pieces // 2
     halves = pairs // ROWS
     mine = owners * pairs
     me = place_ref[0]
-    steps = in_sems.shape[0]
-    some = rows // steps
-    arriving = []
-    for n in range(steps):
-        block = pl.ds(n * some, some)
-        for j, index in enumerate(indices):
-            copy = pltpu.make_async_copy(
-                piece_refs[j].at[index, block],
-                xs.at[block, pl.ds(j * pairs, pairs), :],
-                in_sems.at[n, j],
-            )
-            copy.start()
-            arriving.append(copy)
     weights = w_ref[...]
-    col = col_ref[...]
     for a in range(rows):
-        if a % some == 0:
-            for copy in arriving[a // some * pieces : (a // some + 1) * pieces]:
-                copy.wait()
-        amps = xs[a]
+        amps = jnp.concatenate([piece_refs[j][0, a] for j in range(pieces)], axis=0)
         cycle = jnp.dot(weights, amps, preferred_element_type=jnp.float32)
-        level = gap_ref[...] + row_ref[chunk * rows + a]
-        energy = jnp.concatenate([level] * (cols // LANES), axis=1) + col
-        rough = pl.reciprocal(energy, approx=True)
-        inverse = rough * (energy * rough - 2.0)
-        value = ((amps[:mine].astype(jnp.float32) + cycle) * inverse).astype(jnp.bfloat16)
+        total = amps[:mine].astype(jnp.float32) + cycle
+        value = (total * inverse_ref[chunk * rows + a]).astype(jnp.bfloat16)
         for g in range(owners * halves):
             ys[g, pl.ds(a * ROWS, ROWS), :] = value[g * ROWS : (g + 1) * ROWS]
-    swap = swap_matrix()
+    swap = swap_ref[...]
     leaving = []
     for g in range(owners * halves):
         turned = jnp.dot(swap, ys[g], preferred_element_type=jnp.float32)
@@ -309,7 +314,7 @@
         copy = pltpu.make_async_copy(
             done.at[g],
             out_ref.at[me ^ k, 0, pl.ds(h * ROWS, ROWS), pl.ds(chunk * rows, rows), :],
-            out_sems.at[g],
+            sems.at[g],
         )
         copy.start()
         leaving.append(copy)
@@ -317,30 +322,32 @@
         copy.wait()
 
 
-def finish(chunk, place, row_energy, weights, gaps, col_energy, pieces, before, shape):
+def finish(chunk, place, swap, weights, inverse, pieces, before, shape):
     _, rows, pairs, cols = pieces[0][0].shape
     owners = len(pieces) // 2
     groups = owners * (pairs // ROWS)
-    smem = pl.BlockSpec(memory_space=pltpu.SMEM)
-    vmem = pl.BlockSpec(memory_space=pltpu.VMEM)
     anywhere = pl.BlockSpec(memory_space=pl.ANY)
-    args = [place, row_energy, weights, gaps, col_energy] + [piece for piece, _ in pieces]
-    in_specs = [smem, smem, vmem, vmem, vmem] + [anywhere] * len(pieces)
+    args = [place, swap, weights, inverse] + [piece for piece, _ in pieces]
+    in_specs = [pl.BlockSpec(memory_space=pltpu.SMEM)]
+    in_specs += [pl.BlockSpec(memory_space=pltpu.VMEM)] * 3
+    for _, index in pieces:
+        in_specs.append(
+            pl.BlockSpec((1, rows, pairs, cols), lambda i, index=index: (index, 0, 0, 0))
+        )
     aliases = {}
     if before is not None:
         aliases = {len(args): 0}
         args.append(before)
         in_specs.append(anywhere)
     return pl.pallas_call(
-        functools.partial(finish_kernel, [index for _, index in pieces], chunk),
+        functools.partial(finish_kernel, len(pieces), chunk),
+        grid=(1,),
         in_specs=in_specs,
         out_specs=anywhere,
         out_shape=jax.ShapeDtypeStruct(shape, jnp.bfloat16),
         scratch_shapes=[
-            pltpu.VMEM((rows, len(pieces) * pairs, cols), jnp.bfloat16),
             pltpu.VMEM((groups, ROWS * rows, cols), jnp.bfloat16),
             pltpu.VMEM((groups, ROWS, rows, cols), jnp.bfloat16),
-            pltpu.SemaphoreType.DMA((4, len(pieces))),
             pltpu.SemaphoreType.DMA((groups,)),
         ],
         input_output_aliases=aliases,
@@ -382,17 +389,19 @@
     far = list(range(owners - 1, 1, -1))
     groups = [((k, c),) for c in range(chunks) for k in far]
     groups += [tuple((k, c) for c in range(chunks)) for k in (1, 0)]
-    sent = dress(groups, place, tile_of, tile_mask, tiles, lambda_amps)
+    held, swap = hold(lambda_amps)
+    sent = dress(groups, place, tile_of, tile_mask, tiles, held, swap)
+    weights, inverse = make_weights(
+        after(pair_list, sent[0]), coupling, pair_gap, place, row_energy, col_energy
+    )
     direct = {}
     for group, value in zip(groups, sent):
         k = group[0][0]
         landed = to_owner(value, k) if k else value
         for index, key in enumerate(group):
             direct[key] = (landed, index)
-    weights, gaps = make_weights(after(pair_list, sent[0]), coupling, pair_gap, place)
 
     shape = (owners, 1, pairs, rows, cols)
-    col = col_energy.reshape(1, cols)
     result, other = None, {}
     for c in range(chunks):
         for k in far:
@@ -406,7 +415,7 @@
                 for index in range(chunks):
                     other[k, index] = (passed, index)
         pieces = [held_by[k, c] for held_by in (direct, other) for k in range(owners)]
-        result = finish(c, place, row_energy, weights, gaps, col, pieces, result, shape)
+        result = finish(c, place, swap, weights, inverse, pieces, result, shape)
     return result
 
 

time: 69.5 us -> 63 us (0.906)
  waiting for transfers between devices: 41.8 us -> 37.4 us
  Pallas kernels: 15 us -> 11.9 us
  starting transfers between devices: 12.4 us -> 13.3 us
    ppermute x8, waiting for transfers between devices: 40.9 us -> 36.4 us  [to_owner(): return lax.ppermute(value, 'pair', [(o, o ^ k) for o in range(owners)])]
    pallas_call x1, Pallas kernels: 4.33 us -> 2.33 us  [dress(): pl.pallas_call(functools.partial(dress_kernel, owners, rows, groups), in_...]
    pallas_call x3 -> x4, Pallas kernels: 10.6 us -> 9.62 us  [the longest x2 4.45 us: finish(): pl.pallas_call(functools.partial(finish_kernel, len(pieces), chunk), grid...]
    ppermute x8, starting transfers between devices: 11.8 us -> 12.7 us  [to_owner(): return lax.ppermute(value, 'pair', [(o, o ^ k) for o in range(owners)])]
  transfers between devices with their start and end apart: 14 -> 14, of which waited for: 8 -> 6; matrix products, arithmetic and copies ran while one was open for 0% -> 0% of each run, Pallas kernels for 10% -> 12%
where the time goes in v5:
time: 63 us; the launch traced here: 62.8 us
  waiting for transfers between devices  37.4 us (59%)
  starting transfers between devices  13.3 us (21%)
  Pallas kernels  11.9 us (19%)
    ppermute x8, waiting for transfers between devices, to_owner(): return lax.ppermute(value, 'pair', [(o, o ^ k) for o in range(owners)])  36.4 us
    ppermute x8, starting transfers between devices, to_owner(): return lax.ppermute(value, 'pair', [(o, o ^ k) for o in range(owners)])  12.7 us
    pallas_call x2, Pallas kernels, finish(): pl.pallas_call(functools.partial(finish_kernel, len(pieces), chunk), grid...  4.45 us
    pallas_call x1, Pallas kernels, make_weights(): pl.pallas_call(weights_kernel, in_specs=[vmem, vmem, vmem, smem, smem, vm...  3.52 us
    pallas_call x1, Pallas kernels, dress(): pl.pallas_call(functools.partial(dress_kernel, owners, rows, groups), in_...  2.33 us
    pallas_call x1, Pallas kernels, hold(): pl.pallas_call(hold_kernel, in_specs=[anywhere], out_specs=[anywhere, pl....  1.64 us
  transfers between devices with their start and end apart: 14, of which 6 were waited for; matrix products, arithmetic and copies ran while one was open for 0% of the time, Pallas kernels for 12%

profile of v5, /device:TPU:0, one launch (start us, length us, event | category | flops | bytes accessed | tf_op | source)
XLA Modules:
  0.0 62.8 jit_solution(13741431686356311564)
XLA Ops:
  0.0 5.0 %collective-permute-start.1 = (bf16[1,128,128]{2,1,0:T(8,128)(2,1)}, bf16[1,128,128]{2,1,0:T(8,128)(2,1)S(1)}, u32[]{:S(2)}, u32[]{:S(2)}) collective-permute-start(bf16[1,128,128]{2,1,0:T(8,128)(2,1)} %refs_0_.1), channel_id=1, source_target_pairs={{0,12},{4,8},{8,4},{12,0},{1,13},{5,9},{9,5},{13,1},{2,14},{6,10},... | collective-permute-start | bytes 98312 | tf_op jit(solution)/shard_map/ppermute | solution.py:379
  5.0 0.0 collective-permute-start
  5.1 0.6 collective-permute-start.2
  5.6 0.1 pad_add_fusion.place_ref
  5.7 0.0 copy-start
  5.7 0.0 copy-start.1
  5.7 0.0 copy-start.2
  5.7 0.0 copy-start.3
  5.7 0.0 copy-start.4
  5.7 1.6 %shard_map.91 = (bf16[1,1,32,128,256]{4,3,2,1,0:T(8,128)(2,1)S(1)}, bf16[256,256]{1,0:T(8,128)(2,1)S(1)}) custom-call(bf16[1,1,32,128,256]{4,3,2,1,0:T(8,128)(2,1)} %lam_ref.1), custom_call_target="tpu_custom_call" | custom-call | bytes 4194304 | tf_op jit(solution)/shard_map/pallas_call | solution.py:150
  7.4 0.0 collective-permute-done.1.refs_2_
  7.4 2.7 %collective-permute-done.refs_1_ = bf16[1,128,128]{2,1,0:T(8,128)(2,1)S(1)} collective-permute-done((bf16[1,128,128]{2,1,0:T(8,128)(2,1)}, bf16[1,128,128]{2,1,0:T(8,128)(2,1)S(1)}, u32[]{:S(2)}, u32[]{:S(2)}) %collective-permute-start) | collective-permute-done | bytes 32800 | tf_op jit(solution)/shard_map/ppermute | solution.py:379
  10.1 0.0 collective-permute-done.2.refs_3_
  10.1 2.3 %shard_map.92 = (bf16[1,16,32,256]{3,2,1,0:T(8,128)(2,1)S(1)}, bf16[1,16,32,256]{3,2,1,0:T(8,128)(2,1)S(1)}, bf16[1,16,32,256]{3,2,1,0:T(8,128)(2,1)S(1)}, bf16[...) custom-call(s32[2]{0:T(128)S(1)} %pad_add_fusion.place_ref, ...), custom_call_target="tpu_custom_call" | custom-call | flops 268435456 | bytes 3145728 | tf_op jit(solution)/shard_map/pallas_call | solution.py:262
  12.4 0.1 collective-permute-start.3
  12.5 3.5 %collective-permute-start.6 = (bf16[1,16,32,256]{3,2,1,0:T(8,128)(2,1)S(1)}, bf16[1,16,32,256]{3,2,1,0:T(8,128)(2,1)S(1)}, u32[]{:S(2)}, u32[]{:S(2)}) collective-permute-start(bf16[1,16,32,256]{3,2,1,0:T(8,128)(2,1)S(1)} %get-tuple-element.20), channel_id=1, source_target_pairs={{0,12},{4,8},{8,4},{12,0},{1,13},{5,9},{9,5},{13,1},{2,14},{6,10},... | collective-permute-start | bytes 786440 | tf_op jit(solution)/shard_map/ppermute | solution.py:379
  16.0 0.0 collective-permute-start.11
  16.0 2.9 %collective-permute-start.4 = (bf16[1,16,32,256]{3,2,1,0:T(8,128)(2,1)S(1)}, bf16[1,16,32,256]{3,2,1,0:T(8,128)(2,1)S(1)}, u32[]{:S(2)}, u32[]{:S(2)}) collective-permute-start(bf16[1,16,32,256]{3,2,1,0:T(8,128)(2,1)S(1)} %get-tuple-element.26), channel_id=1, source_target_pairs={{0,8},{4,12},{8,0},{12,4},{1,9},{5,13},{9,1},{13,5},{2,10},{6,14},... | collective-permute-start | bytes 786440 | tf_op jit(solution)/shard_map/ppermute | solution.py:379
  18.9 0.0 copy-done
  18.9 0.0 copy-done.1
  18.9 0.0 copy-done.2
  18.9 0.0 copy-done.3
  18.9 0.0 copy-done.4
  18.9 3.5 %shard_map.93 = (bf16[128,256]{1,0:T(8,128)(2,1)S(1)}, f32[32,128,256]{2,1,0:T(8,128)S(1)}) custom-call(s32[2,256]{1,0:T(2,128)S(1)} %bitcast.5, f32[400,400]{1,0:T(8,128)S(1)} %copy-done, f32[4,1,32]{2,1,0:T(1,128)S(1)} %copy-done.2, s32[2]{0:T(128)S(1)} %pad_add_fusion.place_ref, f32[32]{0:T(128)S(1)} %copy-done.4, f32[1,256]{1,0:T(1,128)S(1)} %bitcast.6), custom_call_target="tpu_custom_call" | custom-call | flops 491520000 | bytes 640000 | tf_op jit(solution)/shard_map/pallas_call | solution.py:203
  22.4 12.1 %collective-permute-done.6.refs_3_ = bf16[1,16,32,256]{3,2,1,0:T(8,128)(2,1)S(1)} collective-permute-done((bf16[1,16,32,256]{3,2,1,0:T(8,128)(2,1)S(1)}, bf16[1,16,32,256]{3,2,1,0:T(8,128)(2,1)S(1)}, u32[]{:S(2)}, u32[]{:S(2)}) %collective-permute-start.6) | collective-permute-done | bytes 262176 | tf_op jit(solution)/shard_map/ppermute | solution.py:379
  34.5 0.0 collective-permute-start.7
  34.5 1.8 %collective-permute-done.3.refs_1_ = bf16[2,16,32,256]{3,2,1,0:T(8,128)(2,1)S(1)} collective-permute-done((bf16[2,16,32,256]{3,2,1,0:T(8,128)(2,1)S(1)}, bf16[2,16,32,256]{3,2,1,0:T(8,128)(2,1)S(1)}, u32[]{:S(2)}, u32[]{:S(2)}) %collective-permute-start.3) | collective-permute-done | bytes 524320 | tf_op jit(solution)/shard_map/ppermute | solution.py:379
  36.3 0.0 collective-permute-start.8
  36.3 0.6 collective-permute-start.5
  37.0 14.3 %collective-permute-done.11.refs_2_ = bf16[1,16,32,256]{3,2,1,0:T(8,128)(2,1)S(1)} collective-permute-done((bf16[1,16,32,256]{3,2,1,0:T(8,128)(2,1)S(1)}, bf16[1,16,32,256]{3,2,1,0:T(8,128)(2,1)S(1)}, u32[]{:S(2)}, u32[]{:S(2)}) %collective-permute-start.11) | collective-permute-done | bytes 262176 | tf_op jit(solution)/shard_map/ppermute | solution.py:379
  51.3 0.0 collective-permute-start.12
  51.3 5.5 %collective-permute-done.4.refs_2_ = bf16[1,16,32,256]{3,2,1,0:T(8,128)(2,1)S(1)} collective-permute-done((bf16[1,16,32,256]{3,2,1,0:T(8,128)(2,1)S(1)}, bf16[1,16,32,256]{3,2,1,0:T(8,128)(2,1)S(1)}, u32[]{:S(2)}, u32[]{:S(2)}) %collective-permute-start.4) | collective-permute-done | bytes 262176 | tf_op jit(solution)/shard_map/ppermute | solution.py:379
  56.8 0.0 collective-permute-start.13
  56.8 0.0 collective-permute-done.5.refs_3_
  56.8 0.5 collective-permute-start.9
  57.3 0.0 collective-permute-done.12.refs_6_
  57.3 0.1 collective-permute-start.10
  57.4 0.9 %collective-permute-done.13.refs_7_ = bf16[1,16,32,256]{3,2,1,0:T(8,128)(2,1)S(1)} collective-permute-done((bf16[1,16,32,256]{3,2,1,0:T(8,128)(2,1)S(1)}, bf16[1,16,32,256]{3,2,1,0:T(8,128)(2,1)S(1)}, u32[]{:S(2)}, u32[]{:S(2)}) %collective-permute-start.13) | collective-permute-done | bytes 262176 | tf_op jit(solution)/shard_map/ppermute | solution.py:382
  58.3 0.0 collective-permute-done.7.refs_4_
  58.3 0.0 collective-permute-done.8.refs_5_
  58.3 2.2 %shard_map.94.refs_8_ = bf16[4,1,32,32,256]{4,3,2,1,0:T(8,128)(2,1)} custom-call(s32[2]{0:T(128)S(1)} %pad_add_fusion.place_ref, bf16[256,256]{1,0:T(8,128)(2,1)S(1)} %get-tuple-element.18.refs_5_.swap_ref, bf16[128,256]{1,0:T(8,128)(2,1)S(1)} %get-tuple-element.22.w_ref, f32[32,128,256]{2,1,0:T(8,128)S(1)} %get-tuple-element.23.inverse_ref, ...), custom_call_target="tpu_custom_call" | custom-call | tf_op jit(solution)/shard_map/pallas_call | solution.py:342
  60.6 0.0 collective-permute-done.9.refs_6_
  60.6 0.0 collective-permute-done.10.refs_7_
  60.6 2.2 %shard_map.95 = bf16[4,1,32,32,256]{4,3,2,1,0:T(8,128)(2,1)} custom-call(s32[2]{0:T(128)S(1)} %pad_add_fusion.place_ref, bf16[256,256]{1,0:T(8,128)(2,1)S(1)} %get-tuple-element.18.refs_5_.swap_ref, bf16[128,256]{1,0:T(8,128)(2,1)S(1)} %get-tuple-element.22.w_ref, ...), custom_call_target="tpu_custom_call", output_to_operand_aliasing={{}: (12, {})} | custom-call | tf_op jit(solution)/shard_map/pallas_call | solution.py:342
Async XLA Ops:
  0.0 7.4 %collective-permute-start.1 = (bf16[1,128,128]{2,1,0:T(8,128)(2,1)}, bf16[1,128,128]{2,1,0:T(8,128)(2,1)S(1)}, u32[]{:S(2)}, u32[]{:S(2)}) collective-permute-start(bf16[1,128,128]{2,1,0:T(8,128)(2,1)} %refs_0_.1), channel_id=1, source_target_pairs={{0,12},{4,8},{8,4},{12,0},{1,13},{5,9},{9,5},{13,1},{2,14},{6,10},... | collective-permute-start | bytes 98312 | tf_op jit(solution)/shard_map/ppermute | solution.py:379
  5.0 5.0 %collective-permute-start = (bf16[1,128,128]{2,1,0:T(8,128)(2,1)}, bf16[1,128,128]{2,1,0:T(8,128)(2,1)S(1)}, u32[]{:S(2)}, u32[]{:S(2)}) collective-permute-start(bf16[1,128,128]{2,1,0:T(8,128)(2,1)} %refs_0_.1), channel_id=1, source_target_pairs={{0,8},{4,12},{8,0},{12,4},{1,9},{5,13},{9,1},{13,5},{2,10},{6,14},... | collective-permute-start | bytes 98312 | tf_op jit(solution)/shard_map/ppermute | solution.py:379
  5.1 5.0 %collective-permute-start.2 = (bf16[1,128,128]{2,1,0:T(8,128)(2,1)}, bf16[1,128,128]{2,1,0:T(8,128)(2,1)S(1)}, u32[]{:S(2)}, u32[]{:S(2)}) collective-permute-start(bf16[1,128,128]{2,1,0:T(8,128)(2,1)} %refs_0_.1), channel_id=1, source_target_pairs={{0,4},{4,0},{8,12},{12,8},{1,5},{5,1},{9,13},{13,9},{2,6},{6,2},{1... | collective-permute-start | bytes 98312 | tf_op jit(solution)/shard_map/ppermute | solution.py:379
  5.7 13.2 %copy-start = (f32[400,400]{1,0:T(8,128)S(1)}, f32[400,400]{1,0:T(8,128)}, u32[]{:S(2)}) copy-start(f32[400,400]{1,0:T(8,128)} %coupling_ref.1) | copy-start | bytes 1920004
  5.7 13.2 %copy-start.1 = (s32[256,2]{0,1:T(2,128)S(1)}, s32[256,2]{0,1:T(2,128)}, u32[]{:S(2)}) copy-start(s32[256,2]{0,1:T(2,128)} %param.13) | copy-start | bytes 6148
  5.7 13.2 %copy-start.2 = (f32[4,1,32]{2,1,0:T(1,128)S(1)}, f32[4,1,32]{2,1,0:T(1,128)}, u32[]{:S(2)}) copy-start(f32[4,1,32]{2,1,0:T(1,128)} %gap_ref.1) | copy-start | bytes 1540
  5.7 13.2 %copy-start.3 = (f32[256]{0:T(256)S(1)}, f32[256]{0:T(256)}, u32[]{:S(2)}) copy-start(f32[256]{0:T(256)} %param.17) | copy-start | bytes 3076
  5.7 13.2 %copy-start.4 = (f32[32]{0:T(128)S(1)}, f32[32]{0:T(128)}, u32[]{:S(2)}) copy-start(f32[32]{0:T(128)} %row_ref.1) | copy-start | bytes 388
  12.4 23.9 %collective-permute-start.3 = (bf16[2,16,32,256]{3,2,1,0:T(8,128)(2,1)S(1)}, bf16[2,16,32,256]{3,2,1,0:T(8,128)(2,1)S(1)}, u32[]{:S(2)}, u32[]{:S(2)}) collective-permute-start(bf16[2,16,32,256]{3,2,1,0:T(8,128)(2,1)S(1)} %get-tuple-element.25), channel_id=1, source_target_pairs={{0,4},{4,0},{8,12},{12,8},{1,5},{5,1},{9,13},{13,9},{2,6},{6,2},{1... | collective-permute-start | bytes 1572872 | tf_op jit(solution)/shard_map/ppermute | solution.py:379
  12.5 22.0 %collective-permute-start.6 = (bf16[1,16,32,256]{3,2,1,0:T(8,128)(2,1)S(1)}, bf16[1,16,32,256]{3,2,1,0:T(8,128)(2,1)S(1)}, u32[]{:S(2)}, u32[]{:S(2)}) collective-permute-start(bf16[1,16,32,256]{3,2,1,0:T(8,128)(2,1)S(1)} %get-tuple-element.20), channel_id=1, source_target_pairs={{0,12},{4,8},{8,4},{12,0},{1,13},{5,9},{9,5},{13,1},{2,14},{6,10},... | collective-permute-start | bytes 786440 | tf_op jit(solution)/shard_map/ppermute | solution.py:379
  16.0 35.3 %collective-permute-start.11 = (bf16[1,16,32,256]{3,2,1,0:T(8,128)(2,1)S(1)}, bf16[1,16,32,256]{3,2,1,0:T(8,128)(2,1)S(1)}, u32[]{:S(2)}, u32[]{:S(2)}) collective-permute-start(bf16[1,16,32,256]{3,2,1,0:T(8,128)(2,1)S(1)} %get-tuple-element.30), channel_id=1, source_target_pairs={{0,8},{4,12},{8,0},{12,4},{1,9},{5,13},{9,1},{13,5},{2,10},{6,14},... | collective-permute-start | bytes 786440 | tf_op jit(solution)/shard_map/ppermute | solution.py:379
  16.0 40.8 %collective-permute-start.4 = (bf16[1,16,32,256]{3,2,1,0:T(8,128)(2,1)S(1)}, bf16[1,16,32,256]{3,2,1,0:T(8,128)(2,1)S(1)}, u32[]{:S(2)}, u32[]{:S(2)}) collective-permute-start(bf16[1,16,32,256]{3,2,1,0:T(8,128)(2,1)S(1)} %get-tuple-element.26), channel_id=1, source_target_pairs={{0,8},{4,12},{8,0},{12,4},{1,9},{5,13},{9,1},{13,5},{2,10},{6,14},... | collective-permute-start | bytes 786440 | tf_op jit(solution)/shard_map/ppermute | solution.py:379
  34.5 23.8 %collective-permute-start.7 = (bf16[2,16,32,256]{3,2,1,0:T(8,128)(2,1)S(1)}, bf16[2,16,32,256]{3,2,1,0:T(8,128)(2,1)S(1)}, u32[]{:S(2)}, u32[]{:S(2)}) collective-permute-start(bf16[2,16,32,256]{3,2,1,0:T(8,128)(2,1)S(1)} %get-tuple-element.28.refs_0_), channel_id=1, source_target_pairs={{0,1},{1,0},{2,3},{3,2},{4,5},{5,4},{6,7},{7,6},{8,9},{9,8},{10,11... | collective-permute-start | bytes 1572872 | tf_op jit(solution)/shard_map/ppermute | solution.py:382
  36.3 22.0 %collective-permute-start.8 = (bf16[2,16,32,256]{3,2,1,0:T(8,128)(2,1)S(1)}, bf16[2,16,32,256]{3,2,1,0:T(8,128)(2,1)S(1)}, u32[]{:S(2)}, u32[]{:S(2)}) collective-permute-start(bf16[2,16,32,256]{3,2,1,0:T(8,128)(2,1)S(1)} %collective-permute-done.3.refs_1_), channel_id=1, source_target_pairs={{0,1},{1,0},{2,3},{3,2},{4,5},{5,4},{6,7},{7,6},{8,9},{9,8},{10,11... | collective-permute-start | bytes 1572872 | tf_op jit(solution)/shard_map/ppermute | solution.py:382
  36.3 20.5 %collective-permute-start.5 = (bf16[1,16,32,256]{3,2,1,0:T(8,128)(2,1)S(1)}, bf16[1,16,32,256]{3,2,1,0:T(8,128)(2,1)S(1)}, u32[]{:S(2)}, u32[]{:S(2)}) collective-permute-start(bf16[1,16,32,256]{3,2,1,0:T(8,128)(2,1)S(1)} %get-tuple-element.27), channel_id=1, source_target_pairs={{0,12},{4,8},{8,4},{12,0},{1,13},{5,9},{9,5},{13,1},{2,14},{6,10},... | collective-permute-start | bytes 786440 | tf_op jit(solution)/shard_map/ppermute | solution.py:379
  51.3 6.0 %collective-permute-start.12 = (bf16[1,16,32,256]{3,2,1,0:T(8,128)(2,1)S(1)}, bf16[1,16,32,256]{3,2,1,0:T(8,128)(2,1)S(1)}, u32[]{:S(2)}, u32[]{:S(2)}) collective-permute-start(bf16[1,16,32,256]{3,2,1,0:T(8,128)(2,1)S(1)} %collective-permute-done.11.refs_2_), channel_id=1, source_target_pairs={{0,1},{1,0},{2,3},{3,2},{4,5},{5,4},{6,7},{7,6},{8,9},{9,8},{10,11... | collective-permute-start | bytes 786440 | tf_op jit(solution)/shard_map/ppermute | solution.py:382
  56.8 1.5 %collective-permute-start.13 = (bf16[1,16,32,256]{3,2,1,0:T(8,128)(2,1)S(1)}, bf16[1,16,32,256]{3,2,1,0:T(8,128)(2,1)S(1)}, u32[]{:S(2)}, u32[]{:S(2)}) collective-permute-start(bf16[1,16,32,256]{3,2,1,0:T(8,128)(2,1)S(1)} %collective-permute-done.6.refs_3_), channel_id=1, source_target_pairs={{0,1},{1,0},{2,3},{3,2},{4,5},{5,4},{6,7},{7,6},{8,9},{9,8},{10,11... | collective-permute-start | bytes 786440 | tf_op jit(solution)/shard_map/ppermute | solution.py:382
  56.8 3.8 %collective-permute-start.9 = (bf16[1,16,32,256]{3,2,1,0:T(8,128)(2,1)S(1)}, bf16[1,16,32,256]{3,2,1,0:T(8,128)(2,1)S(1)}, u32[]{:S(2)}, u32[]{:S(2)}) collective-permute-start(bf16[1,16,32,256]{3,2,1,0:T(8,128)(2,1)S(1)} %collective-permute-done.4.refs_2_), channel_id=1, source_target_pairs={{0,1},{1,0},{2,3},{3,2},{4,5},{5,4},{6,7},{7,6},{8,9},{9,8},{10,11... | collective-permute-start | bytes 786440 | tf_op jit(solution)/shard_map/ppermute | solution.py:382
  57.3 3.3 %collective-permute-start.10 = (bf16[1,16,32,256]{3,2,1,0:T(8,128)(2,1)S(1)}, bf16[1,16,32,256]{3,2,1,0:T(8,128)(2,1)S(1)}, u32[]{:S(2)}, u32[]{:S(2)}) collective-permute-start(bf16[1,16,32,256]{3,2,1,0:T(8,128)(2,1)S(1)} %collective-permute-done.5.refs_3_), channel_id=1, source_target_pairs={{0,1},{1,0},{2,3},{3,2},{4,5},{5,4},{6,7},{7,6},{8,9},{9,8},{10,11... | collective-permute-start | bytes 786440 | tf_op jit(solution)/shard_map/ppermute | solution.py:382

commit v6 on v5

--- a/solution.py
+++ b/solution.py
@@ -289,7 +289,8 @@
     )
 
 
-def finish_kernel(pieces, chunk, place_ref, swap_ref, w_ref, inverse_ref, *refs):
+def finish_kernel(indices, chunk, place_ref, swap_ref, w_ref, inverse_ref, *refs):
+    pieces = len(indices)
     piece_refs = refs[:pieces]
     out_ref, ys, done, sems = refs[-4:]
     _, rows, pairs, cols = piece_refs[0].shape
@@ -299,7 +300,7 @@
     me = place_ref[0]
     weights = w_ref[...]
     for a in range(rows):
-        amps = jnp.concatenate([piece_refs[j][0, a] for j in range(pieces)], axis=0)
+        amps = jnp.concatenate([ref[index, a] for ref, index in zip(piece_refs, indices)], axis=0)
         cycle = jnp.dot(weights, amps, preferred_element_type=jnp.float32)
         total = amps[:mine].astype(jnp.float32) + cycle
         value = (total * inverse_ref[chunk * rows + a]).astype(jnp.bfloat16)
@@ -329,19 +330,14 @@
     anywhere = pl.BlockSpec(memory_space=pl.ANY)
     args = [place, swap, weights, inverse] + [piece for piece, _ in pieces]
     in_specs = [pl.BlockSpec(memory_space=pltpu.SMEM)]
-    in_specs += [pl.BlockSpec(memory_space=pltpu.VMEM)] * 3
-    for _, index in pieces:
-        in_specs.append(
-            pl.BlockSpec((1, rows, pairs, cols), lambda i, index=index: (index, 0, 0, 0))
-        )
+    in_specs += [pl.BlockSpec(memory_space=pltpu.VMEM)] * (3 + len(pieces))
     aliases = {}
     if before is not None:
         aliases = {len(args): 0}
         args.append(before)
         in_specs.append(anywhere)
     return pl.pallas_call(
-        functools.partial(finish_kernel, len(pieces), chunk),
-        grid=(1,),
+        functools.partial(finish_kernel, [index for _, index in pieces], chunk),
         in_specs=in_specs,
         out_specs=anywhere,
         out_shape=jax.ShapeDtypeStruct(shape, jnp.bfloat16),
@@ -391,6 +387,7 @@
     groups += [tuple((k, c) for c in range(chunks)) for k in (1, 0)]
     held, swap = hold(lambda_amps)
     sent = dress(groups, place, tile_of, tile_mask, tiles, held, swap)
+    own = to_sibling(sent[-1])
     weights, inverse = make_weights(
         after(pair_list, sent[0]), coupling, pair_gap, place, row_energy, col_energy
     )
@@ -406,14 +403,11 @@
     for c in range(chunks):
         for k in far:
             value, index = direct[k, c]
-            other[k, c] = (to_sibling(value), index)
+            other[k, c] = (to_sibling(after(value, result if k == far[-1] else None)), index)
         if c == 0:
-            for k in (0, 1):
-                value, _ = direct[k, 0]
-                value = after(value, weights if k else direct[far[0], 0][0])
-                passed = to_sibling(value)
-                for index in range(chunks):
-                    other[k, index] = (passed, index)
+            near = to_sibling(after(direct[1, 0][0], (weights, own)))
+            for index in range(chunks):
+                other[0, index], other[1, index] = (own, index), (near, index)
         pieces = [held_by[k, c] for held_by in (direct, other) for k in range(owners)]
         result = finish(c, place, swap, weights, inverse, pieces, result, shape)
     return result
@@ -436,7 +430,7 @@
     def local(*args):
         tile_rows, cols = args[0].shape[3:]
         rows = tile_rows // owners
-        power = owners & (owners - 1) == 0
+        power = owners >= 4 and owners & (owners - 1) == 0
         fits = rows % ROWS == 0 and cols % LANES == 0 and args[1].shape[0] == 1
         if power and fits and subs == 2 and args[0].shape[2] % ROWS == 0:
             return local_chunked(*args)

time: 63 us -> 66 us (1.048)
  waiting for transfers between devices: 37.4 us -> 42.2 us
  starting transfers between devices: 13.3 us -> 11.4 us
    ppermute x8, waiting for transfers between devices: 36.4 us -> 39.4 us  [to_owner(): return lax.ppermute(value, 'pair', [(o, o ^ k) for o in range(owners)])]
    ppermute x8, starting transfers between devices: 12.7 us -> 10.8 us  [to_owner(): return lax.ppermute(value, 'pair', [(o, o ^ k) for o in range(owners)])]
    ppermute x6, waiting for transfers between devices: 0.96 us -> 2.85 us  [to_sibling(): return lax.ppermute(value, 'sub', [(0, 1), (1, 0)])]
  transfers between devices with their start and end apart: 14 -> 14, of which waited for: 6 -> 7; matrix products, arithmetic and copies ran while one was open for 0% -> 0% of each run, Pallas kernels for 12% -> 11%
where the time goes in v6:
time: 66 us; the launch traced here: 65.8 us
  waiting for transfers between devices  42.2 us (64%)
  Pallas kernels  11.9 us (18%)
  starting transfers between devices  11.4 us (17%)
    ppermute x8, waiting for transfers between devices, to_owner(): return lax.ppermute(value, 'pair', [(o, o ^ k) for o in range(owners)])  39.4 us
    ppermute x8, starting transfers between devices, to_owner(): return lax.ppermute(value, 'pair', [(o, o ^ k) for o in range(owners)])  10.8 us
    pallas_call x2, Pallas kernels, finish(): pl.pallas_call(functools.partial(finish_kernel, [index for _, index in pi...  4.43 us
    pallas_call x1, Pallas kernels, make_weights(): pl.pallas_call(weights_kernel, in_specs=[vmem, vmem, vmem, smem, smem, vm...  3.52 us
    ppermute x6, waiting for transfers between devices, to_sibling(): return lax.ppermute(value, 'sub', [(0, 1), (1, 0)])  2.85 us
    pallas_call x1, Pallas kernels, dress(): pl.pallas_call(functools.partial(dress_kernel, owners, rows, groups), in_...  2.33 us
    pallas_call x1, Pallas kernels, hold(): pl.pallas_call(hold_kernel, in_specs=[anywhere], out_specs=[anywhere, pl....  1.64 us
  transfers between devices with their start and end apart: 14, of which 7 were waited for; matrix products, arithmetic and copies ran while one was open for 0% of the time, Pallas kernels for 11%

profile of v6, /device:TPU:0, one launch (start us, length us, event | category | flops | bytes accessed | tf_op | source)
XLA Modules:
  0.0 65.8 jit_solution(18321616898228967770)
XLA Ops:
  0.0 5.0 %collective-permute-start.1 = (bf16[1,128,128]{2,1,0:T(8,128)(2,1)}, bf16[1,128,128]{2,1,0:T(8,128)(2,1)S(1)}, u32[]{:S(2)}, u32[]{:S(2)}) collective-permute-start(bf16[1,128,128]{2,1,0:T(8,128)(2,1)} %refs_0_.1), channel_id=1, source_target_pairs={{0,12},{4,8},{8,4},{12,0},{1,13},{5,9},{9,5},{13,1},{2,14},{6,10},... | collective-permute-start | bytes 98312 | tf_op jit(solution)/shard_map/ppermute | solution.py:375
  5.0 0.0 collective-permute-start
  5.1 0.6 collective-permute-start.2
  5.6 0.1 pad_add_fusion.place_ref
  5.7 0.0 copy-start
  5.7 0.0 copy-start.1
  5.7 0.0 copy-start.2
  5.7 0.0 copy-start.3
  5.7 0.0 copy-start.4
  5.7 1.6 %shard_map.91 = (bf16[1,1,32,128,256]{4,3,2,1,0:T(8,128)(2,1)S(1)}, bf16[256,256]{1,0:T(8,128)(2,1)S(1)}) custom-call(bf16[1,1,32,128,256]{4,3,2,1,0:T(8,128)(2,1)} %lam_ref.1), custom_call_target="tpu_custom_call" | custom-call | bytes 4194304 | tf_op jit(solution)/shard_map/pallas_call | solution.py:150
  7.4 0.0 collective-permute-done.1.refs_2_
  7.4 2.7 %collective-permute-done.refs_1_ = bf16[1,128,128]{2,1,0:T(8,128)(2,1)S(1)} collective-permute-done((bf16[1,128,128]{2,1,0:T(8,128)(2,1)}, bf16[1,128,128]{2,1,0:T(8,128)(2,1)S(1)}, u32[]{:S(2)}, u32[]{:S(2)}) %collective-permute-start) | collective-permute-done | bytes 32800 | tf_op jit(solution)/shard_map/ppermute | solution.py:375
  10.1 0.0 collective-permute-done.2.refs_3_
  10.1 2.3 %shard_map.92 = (bf16[1,16,32,256]{3,2,1,0:T(8,128)(2,1)S(1)}, bf16[1,16,32,256]{3,2,1,0:T(8,128)(2,1)S(1)}, bf16[1,16,32,256]{3,2,1,0:T(8,128)(2,1)S(1)}, bf16[...) custom-call(s32[2]{0:T(128)S(1)} %pad_add_fusion.place_ref, ...), custom_call_target="tpu_custom_call" | custom-call | flops 268435456 | bytes 3145728 | tf_op jit(solution)/shard_map/pallas_call | solution.py:262
  12.4 0.1 collective-permute-start.3
  12.5 0.1 collective-permute-start.6
  12.6 3.4 %collective-permute-start.9 = (bf16[1,16,32,256]{3,2,1,0:T(8,128)(2,1)S(1)}, bf16[1,16,32,256]{3,2,1,0:T(8,128)(2,1)S(1)}, u32[]{:S(2)}, u32[]{:S(2)}) collective-permute-start(bf16[1,16,32,256]{3,2,1,0:T(8,128)(2,1)S(1)} %get-tuple-element.20), channel_id=1, source_target_pairs={{0,12},{4,8},{8,4},{12,0},{1,13},{5,9},{9,5},{13,1},{2,14},{6,10},... | collective-permute-start | bytes 786440 | tf_op jit(solution)/shard_map/ppermute | solution.py:375
  16.0 0.0 collective-permute-start.8
  16.0 0.0 copy-done
  16.0 0.0 copy-done.1
  16.0 0.0 copy-done.2
  16.0 0.0 copy-done.3
  16.0 0.0 copy-done.4
  16.0 3.5 %shard_map.93 = (bf16[128,256]{1,0:T(8,128)(2,1)S(1)}, f32[32,128,256]{2,1,0:T(8,128)S(1)}) custom-call(s32[2,256]{1,0:T(2,128)S(1)} %bitcast.5, f32[400,400]{1,0:T(8,128)S(1)} %copy-done, f32[4,1,32]{2,1,0:T(1,128)S(1)} %copy-done.2, s32[2]{0:T(128)S(1)} %pad_add_fusion.place_ref, f32[32]{0:T(128)S(1)} %copy-done.4, f32[1,256]{1,0:T(1,128)S(1)} %bitcast.6), custom_call_target="tpu_custom_call" | custom-call | flops 491520000 | bytes 640000 | tf_op jit(solution)/shard_map/pallas_call | solution.py:203
  19.5 13.6 %collective-permute-done.3.refs_1_ = bf16[2,16,32,256]{3,2,1,0:T(8,128)(2,1)S(1)} collective-permute-done((bf16[2,16,32,256]{3,2,1,0:T(8,128)(2,1)S(1)}, bf16[2,16,32,256]{3,2,1,0:T(8,128)(2,1)S(1)}, u32[]{:S(2)}, u32[]{:S(2)}) %collective-permute-start.3) | collective-permute-done | bytes 524320 | tf_op jit(solution)/shard_map/ppermute | solution.py:375
  33.2 0.0 collective-permute-done.6.refs_4_
  33.2 0.0 collective-permute-start.7
  33.2 1.7 %collective-permute-start.5 = (bf16[1,16,32,256]{3,2,1,0:T(8,128)(2,1)S(1)}, bf16[1,16,32,256]{3,2,1,0:T(8,128)(2,1)S(1)}, u32[]{:S(2)}, u32[]{:S(2)}) collective-permute-start(bf16[1,16,32,256]{3,2,1,0:T(8,128)(2,1)S(1)} %get-tuple-element.27), channel_id=1, source_target_pairs={{0,12},{4,8},{8,4},{12,0},{1,13},{5,9},{9,5},{13,1},{2,14},{6,10},... | collective-permute-start | bytes 786440 | tf_op jit(solution)/shard_map/ppermute | solution.py:375
  34.9 10.7 %collective-permute-done.8.refs_2_ = bf16[1,16,32,256]{3,2,1,0:T(8,128)(2,1)S(1)} collective-permute-done((bf16[1,16,32,256]{3,2,1,0:T(8,128)(2,1)S(1)}, bf16[1,16,32,256]{3,2,1,0:T(8,128)(2,1)S(1)}, u32[]{:S(2)}, u32[]{:S(2)}) %collective-permute-start.8) | collective-permute-done | bytes 262176 | tf_op jit(solution)/shard_map/ppermute | solution.py:375
  45.6 0.0 collective-permute-start.10
  45.6 0.0 collective-permute-done.9.refs_3_
  45.6 0.5 collective-permute-start.11
  46.1 0.0 collective-permute-start.4
  46.1 0.0 collective-permute-done.5.refs_3_
  46.1 0.1 collective-permute-start.13
  46.2 0.9 %collective-permute-done.10.refs_6_ = bf16[1,16,32,256]{3,2,1,0:T(8,128)(2,1)S(1)} collective-permute-done((bf16[1,16,32,256]{3,2,1,0:T(8,128)(2,1)S(1)}, bf16[1,16,32,256]{3,2,1,0:T(8,128)(2,1)S(1)}, u32[]{:S(2)}, u32[]{:S(2)}) %collective-permute-start.10) | collective-permute-done | bytes 262176 | tf_op jit(solution)/shard_map/ppermute | solution.py:378
  47.1 0.4 collective-permute-done.11.refs_7_
  47.5 0.0 collective-permute-done.7.refs_5_
  47.5 2.2 %shard_map.94.refs_8_ = bf16[4,1,32,32,256]{4,3,2,1,0:T(8,128)(2,1)} custom-call(s32[2]{0:T(128)S(1)} %pad_add_fusion.place_ref, bf16[256,256]{1,0:T(8,128)(2,1)S(1)} %get-tuple-element.18.refs_5_.swap_ref, bf16[128,256]{1,0:T(8,128)(2,1)S(1)} %get-tuple-element.22.w_ref, f32[32,128,256]{2,1,0:T(8,128)S(1)} %get-tuple-element.23.inverse_ref, ...), custom_call_target="tpu_custom_call" | custom-call | tf_op jit(solution)/shard_map/pallas_call | solution.py:339
  49.7 12.3 %collective-permute-done.4.refs_2_ = bf16[1,16,32,256]{3,2,1,0:T(8,128)(2,1)S(1)} collective-permute-done((bf16[1,16,32,256]{3,2,1,0:T(8,128)(2,1)S(1)}, bf16[1,16,32,256]{3,2,1,0:T(8,128)(2,1)S(1)}, u32[]{:S(2)}, u32[]{:S(2)}) %collective-permute-start.4) | collective-permute-done | bytes 262176 | tf_op jit(solution)/shard_map/ppermute | solution.py:375
  62.0 0.0 collective-permute-start.12
  62.0 0.0 collective-permute-done.13.refs_7_
  62.0 1.5 %collective-permute-done.12.refs_6_ = bf16[1,16,32,256]{3,2,1,0:T(8,128)(2,1)S(1)} collective-permute-done((bf16[1,16,32,256]{3,2,1,0:T(8,128)(2,1)S(1)}, bf16[1,16,32,256]{3,2,1,0:T(8,128)(2,1)S(1)}, u32[]{:S(2)}, u32[]{:S(2)}) %collective-permute-start.12) | collective-permute-done | bytes 262176 | tf_op jit(solution)/shard_map/ppermute | solution.py:378
  63.6 2.2 %shard_map.95 = bf16[4,1,32,32,256]{4,3,2,1,0:T(8,128)(2,1)} custom-call(s32[2]{0:T(128)S(1)} %pad_add_fusion.place_ref, bf16[256,256]{1,0:T(8,128)(2,1)S(1)} %get-tuple-element.18.refs_5_.swap_ref, bf16[128,256]{1,0:T(8,128)(2,1)S(1)} %get-tuple-element.22.w_ref, ...), custom_call_target="tpu_custom_call", output_to_operand_aliasing={{}: (12, {})} | custom-call | tf_op jit(solution)/shard_map/pallas_call | solution.py:339
Async XLA Ops:
  0.0 7.4 %collective-permute-start.1 = (bf16[1,128,128]{2,1,0:T(8,128)(2,1)}, bf16[1,128,128]{2,1,0:T(8,128)(2,1)S(1)}, u32[]{:S(2)}, u32[]{:S(2)}) collective-permute-start(bf16[1,128,128]{2,1,0:T(8,128)(2,1)} %refs_0_.1), channel_id=1, source_target_pairs={{0,12},{4,8},{8,4},{12,0},{1,13},{5,9},{9,5},{13,1},{2,14},{6,10},... | collective-permute-start | bytes 98312 | tf_op jit(solution)/shard_map/ppermute | solution.py:375
  5.0 5.0 %collective-permute-start = (bf16[1,128,128]{2,1,0:T(8,128)(2,1)}, bf16[1,128,128]{2,1,0:T(8,128)(2,1)S(1)}, u32[]{:S(2)}, u32[]{:S(2)}) collective-permute-start(bf16[1,128,128]{2,1,0:T(8,128)(2,1)} %refs_0_.1), channel_id=1, source_target_pairs={{0,8},{4,12},{8,0},{12,4},{1,9},{5,13},{9,1},{13,5},{2,10},{6,14},... | collective-permute-start | bytes 98312 | tf_op jit(solution)/shard_map/ppermute | solution.py:375
  5.1 5.0 %collective-permute-start.2 = (bf16[1,128,128]{2,1,0:T(8,128)(2,1)}, bf16[1,128,128]{2,1,0:T(8,128)(2,1)S(1)}, u32[]{:S(2)}, u32[]{:S(2)}) collective-permute-start(bf16[1,128,128]{2,1,0:T(8,128)(2,1)} %refs_0_.1), channel_id=1, source_target_pairs={{0,4},{4,0},{8,12},{12,8},{1,5},{5,1},{9,13},{13,9},{2,6},{6,2},{1... | collective-permute-start | bytes 98312 | tf_op jit(solution)/shard_map/ppermute | solution.py:375
  5.7 10.3 %copy-start = (f32[400,400]{1,0:T(8,128)S(1)}, f32[400,400]{1,0:T(8,128)}, u32[]{:S(2)}) copy-start(f32[400,400]{1,0:T(8,128)} %coupling_ref.1) | copy-start | bytes 1920004
  5.7 10.3 %copy-start.1 = (s32[256,2]{0,1:T(2,128)S(1)}, s32[256,2]{0,1:T(2,128)}, u32[]{:S(2)}) copy-start(s32[256,2]{0,1:T(2,128)} %param.13) | copy-start | bytes 6148
  5.7 10.3 %copy-start.2 = (f32[4,1,32]{2,1,0:T(1,128)S(1)}, f32[4,1,32]{2,1,0:T(1,128)}, u32[]{:S(2)}) copy-start(f32[4,1,32]{2,1,0:T(1,128)} %gap_ref.1) | copy-start | bytes 1540
  5.7 10.3 %copy-start.3 = (f32[256]{0:T(256)S(1)}, f32[256]{0:T(256)}, u32[]{:S(2)}) copy-start(f32[256]{0:T(256)} %param.17) | copy-start | bytes 3076
  5.7 10.3 %copy-start.4 = (f32[32]{0:T(128)S(1)}, f32[32]{0:T(128)}, u32[]{:S(2)}) copy-start(f32[32]{0:T(128)} %row_ref.1) | copy-start | bytes 388
  12.4 20.8 %collective-permute-start.3 = (bf16[2,16,32,256]{3,2,1,0:T(8,128)(2,1)S(1)}, bf16[2,16,32,256]{3,2,1,0:T(8,128)(2,1)S(1)}, u32[]{:S(2)}, u32[]{:S(2)}) collective-permute-start(bf16[2,16,32,256]{3,2,1,0:T(8,128)(2,1)S(1)} %get-tuple-element.25), channel_id=1, source_target_pairs={{0,4},{4,0},{8,12},{12,8},{1,5},{5,1},{9,13},{13,9},{2,6},{6,2},{1... | collective-permute-start | bytes 1572872 | tf_op jit(solution)/shard_map/ppermute | solution.py:375
  12.5 20.7 %collective-permute-start.6 = (bf16[2,16,32,256]{3,2,1,0:T(8,128)(2,1)S(1)}, bf16[2,16,32,256]{3,2,1,0:T(8,128)(2,1)S(1)}, u32[]{:S(2)}, u32[]{:S(2)}) collective-permute-start(bf16[2,16,32,256]{3,2,1,0:T(8,128)(2,1)S(1)} %get-tuple-element.24.refs_0_), channel_id=1, source_target_pairs={{0,1},{1,0},{2,3},{3,2},{4,5},{5,4},{6,7},{7,6},{8,9},{9,8},{10,11... | collective-permute-start | bytes 1572872 | tf_op jit(solution)/shard_map/ppermute | solution.py:378
  12.6 33.0 %collective-permute-start.9 = (bf16[1,16,32,256]{3,2,1,0:T(8,128)(2,1)S(1)}, bf16[1,16,32,256]{3,2,1,0:T(8,128)(2,1)S(1)}, u32[]{:S(2)}, u32[]{:S(2)}) collective-permute-start(bf16[1,16,32,256]{3,2,1,0:T(8,128)(2,1)S(1)} %get-tuple-element.20), channel_id=1, source_target_pairs={{0,12},{4,8},{8,4},{12,0},{1,13},{5,9},{9,5},{13,1},{2,14},{6,10},... | collective-permute-start | bytes 786440 | tf_op jit(solution)/shard_map/ppermute | solution.py:375
  16.0 29.6 %collective-permute-start.8 = (bf16[1,16,32,256]{3,2,1,0:T(8,128)(2,1)S(1)}, bf16[1,16,32,256]{3,2,1,0:T(8,128)(2,1)S(1)}, u32[]{:S(2)}, u32[]{:S(2)}) collective-permute-start(bf16[1,16,32,256]{3,2,1,0:T(8,128)(2,1)S(1)} %get-tuple-element.29), channel_id=1, source_target_pairs={{0,8},{4,12},{8,0},{12,4},{1,9},{5,13},{9,1},{13,5},{2,10},{6,14},... | collective-permute-start | bytes 786440 | tf_op jit(solution)/shard_map/ppermute | solution.py:375
  33.2 14.3 %collective-permute-start.7 = (bf16[2,16,32,256]{3,2,1,0:T(8,128)(2,1)S(1)}, bf16[2,16,32,256]{3,2,1,0:T(8,128)(2,1)S(1)}, u32[]{:S(2)}, u32[]{:S(2)}) collective-permute-start(bf16[2,16,32,256]{3,2,1,0:T(8,128)(2,1)S(1)} %collective-permute-done.3.refs_1_), channel_id=1, source_target_pairs={{0,1},{1,0},{2,3},{3,2},{4,5},{5,4},{6,7},{7,6},{8,9},{9,8},{10,11... | collective-permute-start | bytes 1572872 | tf_op jit(solution)/shard_map/ppermute | solution.py:378
  33.2 12.9 %collective-permute-start.5 = (bf16[1,16,32,256]{3,2,1,0:T(8,128)(2,1)S(1)}, bf16[1,16,32,256]{3,2,1,0:T(8,128)(2,1)S(1)}, u32[]{:S(2)}, u32[]{:S(2)}) collective-permute-start(bf16[1,16,32,256]{3,2,1,0:T(8,128)(2,1)S(1)} %get-tuple-element.27), channel_id=1, source_target_pairs={{0,12},{4,8},{8,4},{12,0},{1,13},{5,9},{9,5},{13,1},{2,14},{6,10},... | collective-permute-start | bytes 786440 | tf_op jit(solution)/shard_map/ppermute | solution.py:375
  45.6 1.5 %collective-permute-start.10 = (bf16[1,16,32,256]{3,2,1,0:T(8,128)(2,1)S(1)}, bf16[1,16,32,256]{3,2,1,0:T(8,128)(2,1)S(1)}, u32[]{:S(2)}, u32[]{:S(2)}) collective-permute-start(bf16[1,16,32,256]{3,2,1,0:T(8,128)(2,1)S(1)} %collective-permute-done.8.refs_2_), channel_id=1, source_target_pairs={{0,1},{1,0},{2,3},{3,2},{4,5},{5,4},{6,7},{7,6},{8,9},{9,8},{10,11... | collective-permute-start | bytes 786440 | tf_op jit(solution)/shard_map/ppermute | solution.py:378
  45.6 1.9 %collective-permute-start.11 = (bf16[1,16,32,256]{3,2,1,0:T(8,128)(2,1)S(1)}, bf16[1,16,32,256]{3,2,1,0:T(8,128)(2,1)S(1)}, u32[]{:S(2)}, u32[]{:S(2)}) collective-permute-start(bf16[1,16,32,256]{3,2,1,0:T(8,128)(2,1)S(1)} %collective-permute-done.9.refs_3_), channel_id=1, source_target_pairs={{0,1},{1,0},{2,3},{3,2},{4,5},{5,4},{6,7},{7,6},{8,9},{9,8},{10,11... | collective-permute-start | bytes 786440 | tf_op jit(solution)/shard_map/ppermute | solution.py:378
  46.1 16.0 %collective-permute-start.4 = (bf16[1,16,32,256]{3,2,1,0:T(8,128)(2,1)S(1)}, bf16[1,16,32,256]{3,2,1,0:T(8,128)(2,1)S(1)}, u32[]{:S(2)}, u32[]{:S(2)}) collective-permute-start(bf16[1,16,32,256]{3,2,1,0:T(8,128)(2,1)S(1)} %get-tuple-element.26), channel_id=1, source_target_pairs={{0,8},{4,12},{8,0},{12,4},{1,9},{5,13},{9,1},{13,5},{2,10},{6,14},... | collective-permute-start | bytes 786440 | tf_op jit(solution)/shard_map/ppermute | solution.py:375
  46.1 16.0 %collective-permute-start.13 = (bf16[1,16,32,256]{3,2,1,0:T(8,128)(2,1)S(1)}, bf16[1,16,32,256]{3,2,1,0:T(8,128)(2,1)S(1)}, u32[]{:S(2)}, u32[]{:S(2)}) collective-permute-start(bf16[1,16,32,256]{3,2,1,0:T(8,128)(2,1)S(1)} %collective-permute-done.5.refs_3_), channel_id=1, source_target_pairs={{0,1},{1,0},{2,3},{3,2},{4,5},{5,4},{6,7},{7,6},{8,9},{9,8},{10,11... | collective-permute-start | bytes 786440 | tf_op jit(solution)/shard_map/ppermute | solution.py:378
  62.0 1.5 %collective-permute-start.12 = (bf16[1,16,32,256]{3,2,1,0:T(8,128)(2,1)S(1)}, bf16[1,16,32,256]{3,2,1,0:T(8,128)(2,1)S(1)}, u32[]{:S(2)}, u32[]{:S(2)}) collective-permute-start(bf16[1,16,32,256]{3,2,1,0:T(8,128)(2,1)S(1)} %collective-permute-done.4.refs_2_), channel_id=1, source_target_pairs={{0,1},{1,0},{2,3},{3,2},{4,5},{5,4},{6,7},{7,6},{8,9},{9,8},{10,11... | collective-permute-start | bytes 786440 | tf_op jit(solution)/shard_map/ppermute | solution.py:378

commit v7 on v6

--- a/solution.py
+++ b/solution.py
@@ -224,27 +224,33 @@
     me = place_ref[0]
     flat = [(k, c, out, j) for out, group in zip(out_refs, groups) for j, (k, c) in enumerate(group)]
     starts = [pl.multiple_of((me ^ k) * rows + c * ROWS, ROWS) for k, c, _, _ in flat]
-    for k in range(owners):
-        for n, start in enumerate(starts):
-            tiles[k, pl.ds(n * ROWS, ROWS), :] = tile_refs[k][0, pl.ds(start, ROWS), :]
+    tile_rows, cols = lam_ref.shape[3:]
+    row = lax.broadcasted_iota(jnp.int32, (ROWS, tile_rows), 0)
+    column = lax.broadcasted_iota(jnp.int32, (ROWS, tile_rows), 1)
+    for n, start in enumerate(starts):
+        block = pl.ds(n * ROWS, ROWS)
+        own_row = one_hot(column == row + start)
+        for k in range(owners):
+            tiles[k, block, :tile_rows] = tile_refs[k][0, pl.ds(start, ROWS), :]
+            tiles[k, block, tile_rows:] = own_row
     swap = swap_ref[...]
     parts = mask_ref.shape[2]
+    width = cols // parts
     for g in range(lam_ref.shape[2] // ROWS):
         for i in range(ROWS):
             pair = g * ROWS + i
-            ladder = jnp.dot(
-                tiles[tile_of_ref[0, 0, pair] ^ me],
-                lam_ref[0, 0, pair],
-                preferred_element_type=jnp.float32,
-            )
-            width = ladder.shape[1] // parts
-            for part in range(parts):
-                keep = mask_ref[0, 0, part, pair].astype(jnp.float32)
-                cols = slice(part * width, (part + 1) * width)
-                for n, start in enumerate(starts):
-                    amps = lam_ref[0, 0, pair, pl.ds(start, ROWS), cols].astype(jnp.float32)
-                    kept = keep * ladder[n * ROWS : (n + 1) * ROWS, cols]
-                    stage[g, n, pl.ds(i * ROWS, ROWS), cols] = (amps + kept).astype(jnp.bfloat16)
+            amps = lam_ref[0, 0, pair]
+            kept = [
+                amps[:, part * width : (part + 1) * width]
+                * mask_ref[0, 0, part, pair].astype(jnp.float32).astype(jnp.bfloat16)
+                for part in range(parts)
+            ]
+            both = jnp.concatenate([jnp.concatenate(kept, axis=1), amps], axis=0)
+            full = jnp.dot(
+                tiles[tile_of_ref[0, 0, pair] ^ me], both, preferred_element_type=jnp.float32
+            ).astype(jnp.bfloat16)
+            for n in range(len(flat)):
+                stage[g, n, pl.ds(i * ROWS, ROWS), :] = full[n * ROWS : (n + 1) * ROWS]
         for n, (_, _, out, j) in enumerate(flat):
             turned = jnp.dot(swap, stage[g, n], preferred_element_type=jnp.float32)
             out[j, :, pl.ds(g * ROWS, ROWS), :] = turned.astype(jnp.bfloat16).reshape(
@@ -268,7 +274,7 @@
             for group in groups
         ],
         scratch_shapes=[
-            pltpu.VMEM((owners, count * ROWS, tile_rows), jnp.bfloat16),
+            pltpu.VMEM((owners, count * ROWS, 2 * tile_rows), jnp.bfloat16),
             pltpu.VMEM((pairs // ROWS, count, ROWS * ROWS, cols), jnp.bfloat16),
         ],
         compiler_params=pltpu.CompilerParams(vmem_limit_bytes=VMEM_BYTES),
@@ -382,33 +388,33 @@
 
     tiles = [integral_tiles] + [to_owner(integral_tiles, k) for k in range(1, owners)]
 
-    far = list(range(owners - 1, 1, -1))
-    groups = [((k, c),) for c in range(chunks) for k in far]
+    far = list(range(2, owners))
+    last = far[-1]
+    groups = [((k, c),) for c in range(chunks) for k in far[::-1]]
     groups += [tuple((k, c) for c in range(chunks)) for k in (1, 0)]
     held, swap = hold(lambda_amps)
-    sent = dress(groups, place, tile_of, tile_mask, tiles, held, swap)
-    own = to_sibling(sent[-1])
+    sent = dict(zip(groups, dress(groups, place, tile_of, tile_mask, tiles, held, swap)))
     weights, inverse = make_weights(
-        after(pair_list, sent[0]), coupling, pair_gap, place, row_energy, col_energy
-    )
-    direct = {}
-    for group, value in zip(groups, sent):
-        k = group[0][0]
-        landed = to_owner(value, k) if k else value
-        for index, key in enumerate(group):
-            direct[key] = (landed, index)
-
-    shape = (owners, 1, pairs, rows, cols)
-    result, other = None, {}
+        after(pair_list, sent[groups[0]]), coupling, pair_gap, place, row_energy, col_energy
+    )
+    own, near = sent[groups[-1]], to_owner(sent[groups[-2]], 1)
+    direct, other = {}, {}
+    for k in far:
+        for c in range(chunks):
+            earlier = direct[k, c - 1] if c and k == last else None
+            direct[k, c] = to_owner(after(sent[((k, c),)], earlier), k)
+    own_passed = to_sibling(after(own, direct[last, 0]))
+    near_passed = to_sibling(after(near, (weights, direct[far[0], 0])))
+    for k in far:
+        for c in range(chunks):
+            earlier = other[k, c - 1] if c else None
+            other[k, c] = to_sibling(after(direct[k, c], earlier))
+
+    result = None
     for c in range(chunks):
-        for k in far:
-            value, index = direct[k, c]
-            other[k, c] = (to_sibling(after(value, result if k == far[-1] else None)), index)
-        if c == 0:
-            near = to_sibling(after(direct[1, 0][0], (weights, own)))
-            for index in range(chunks):
-                other[0, index], other[1, index] = (own, index), (near, index)
-        pieces = [held_by[k, c] for held_by in (direct, other) for k in range(owners)]
+        pieces = [(own, c), (near, c)] + [(direct[k, c], 0) for k in far]
+        pieces += [(own_passed, c), (near_passed, c)] + [(other[k, c], 0) for k in far]
+        shape = (owners, 1, pairs, rows, cols)
         result = finish(c, place, swap, weights, inverse, pieces, result, shape)
     return result
 

time: 66 us -> 63.4 us (0.961)
  waiting for transfers between devices: 42.2 us -> 37.5 us
  starting transfers between devices: 11.4 us -> 13.5 us
    ppermute x8, waiting for transfers between devices: 39.4 us -> 36.2 us  [to_owner(): return lax.ppermute(value, 'pair', [(o, o ^ k) for o in range(owners)])]
    ppermute x8, starting transfers between devices: 10.8 us -> 12.4 us  [to_owner(): return lax.ppermute(value, 'pair', [(o, o ^ k) for o in range(owners)])]
    ppermute x6, waiting for transfers between devices: 2.85 us -> 1.32 us  [to_sibling(): return lax.ppermute(value, 'sub', [(0, 1), (1, 0)])]
  transfers between devices with their start and end apart: 14 -> 14, of which waited for: 7 -> 5; matrix products, arithmetic and copies ran while one was open for 0% -> 0% of each run, Pallas kernels for 11% -> 12%
where the time goes in v7:
time: 63.4 us; the launch traced here: 63.1 us
  waiting for transfers between devices  37.5 us (59%)
  starting transfers between devices  13.5 us (21%)
  Pallas kernels  11.9 us (19%)
    ppermute x8, waiting for transfers between devices, to_owner(): return lax.ppermute(value, 'pair', [(o, o ^ k) for o in range(owners)])  36.2 us
    ppermute x8, starting transfers between devices, to_owner(): return lax.ppermute(value, 'pair', [(o, o ^ k) for o in range(owners)])  12.4 us
    pallas_call x2, Pallas kernels, finish(): pl.pallas_call(functools.partial(finish_kernel, [index for _, index in pi...  4.44 us
    pallas_call x1, Pallas kernels, make_weights(): pl.pallas_call(weights_kernel, in_specs=[vmem, vmem, vmem, smem, smem, vm...  3.52 us
    pallas_call x1, Pallas kernels, dress(): pl.pallas_call(functools.partial(dress_kernel, owners, rows, groups), in_...  2.31 us
    pallas_call x1, Pallas kernels, hold(): pl.pallas_call(hold_kernel, in_specs=[anywhere], out_specs=[anywhere, pl....  1.64 us
    ppermute x6, waiting for transfers between devices, to_sibling(): return lax.ppermute(value, 'sub', [(0, 1), (1, 0)])  1.32 us
  transfers between devices with their start and end apart: 14, of which 5 were waited for; matrix products, arithmetic and copies ran while one was open for 0% of the time, Pallas kernels for 12%

profile of v7, /device:TPU:0, one launch (start us, length us, event | category | flops | bytes accessed | tf_op | source)
XLA Modules:
  0.0 63.1 jit_solution(5937097347080778808)
XLA Ops:
  0.0 5.0 %collective-permute-start.1 = (bf16[1,128,128]{2,1,0:T(8,128)(2,1)}, bf16[1,128,128]{2,1,0:T(8,128)(2,1)S(1)}, u32[]{:S(2)}, u32[]{:S(2)}) collective-permute-start(bf16[1,128,128]{2,1,0:T(8,128)(2,1)} %refs_0_.1), channel_id=1, source_target_pairs={{0,12},{4,8},{8,4},{12,0},{1,13},{5,9},{9,5},{13,1},{2,14},{6,10},... | collective-permute-start | bytes 98312 | tf_op jit(solution)/shard_map/ppermute | solution.py:381
  5.0 0.0 collective-permute-start
  5.1 0.6 collective-permute-start.2
  5.6 0.1 pad_add_fusion.place_ref
  5.7 0.0 copy-start
  5.7 0.0 copy-start.1
  5.7 0.0 copy-start.2
  5.7 0.0 copy-start.3
  5.7 0.0 copy-start.4
  5.7 1.6 %shard_map.91 = (bf16[1,1,32,128,256]{4,3,2,1,0:T(8,128)(2,1)S(1)}, bf16[256,256]{1,0:T(8,128)(2,1)S(1)}) custom-call(bf16[1,1,32,128,256]{4,3,2,1,0:T(8,128)(2,1)} %lam_ref.1), custom_call_target="tpu_custom_call" | custom-call | bytes 4194304 | tf_op jit(solution)/shard_map/pallas_call | solution.py:150
  7.4 0.0 collective-permute-done.1.refs_2_
  7.4 2.7 %collective-permute-done.refs_1_ = bf16[1,128,128]{2,1,0:T(8,128)(2,1)S(1)} collective-permute-done((bf16[1,128,128]{2,1,0:T(8,128)(2,1)}, bf16[1,128,128]{2,1,0:T(8,128)(2,1)S(1)}, u32[]{:S(2)}, u32[]{:S(2)}) %collective-permute-start) | collective-permute-done | bytes 32800 | tf_op jit(solution)/shard_map/ppermute | solution.py:381
  10.1 0.0 collective-permute-done.2.refs_3_
  10.1 2.3 %shard_map.92 = (bf16[1,16,32,256]{3,2,1,0:T(8,128)(2,1)S(1)}, bf16[1,16,32,256]{3,2,1,0:T(8,128)(2,1)S(1)}, bf16[1,16,32,256]{3,2,1,0:T(8,128)(2,1)S(1)}, bf16[...) custom-call(s32[2]{0:T(128)S(1)} %pad_add_fusion.place_ref, ...), custom_call_target="tpu_custom_call" | custom-call | flops 268435456 | bytes 3145728 | tf_op jit(solution)/shard_map/pallas_call | solution.py:268
  12.4 0.1 collective-permute-start.3
  12.5 3.5 %collective-permute-start.5 = (bf16[1,16,32,256]{3,2,1,0:T(8,128)(2,1)S(1)}, bf16[1,16,32,256]{3,2,1,0:T(8,128)(2,1)S(1)}, u32[]{:S(2)}, u32[]{:S(2)}) collective-permute-start(bf16[1,16,32,256]{3,2,1,0:T(8,128)(2,1)S(1)} %get-tuple-element.23), channel_id=1, source_target_pairs={{0,12},{4,8},{8,4},{12,0},{1,13},{5,9},{9,5},{13,1},{2,14},{6,10},... | collective-permute-start | bytes 786440 | tf_op jit(solution)/shard_map/ppermute | solution.py:381
  15.9 0.0 collective-permute-start.8
  15.9 2.9 %collective-permute-start.4 = (bf16[1,16,32,256]{3,2,1,0:T(8,128)(2,1)S(1)}, bf16[1,16,32,256]{3,2,1,0:T(8,128)(2,1)S(1)}, u32[]{:S(2)}, u32[]{:S(2)}) collective-permute-start(bf16[1,16,32,256]{3,2,1,0:T(8,128)(2,1)S(1)} %get-tuple-element.29), channel_id=1, source_target_pairs={{0,8},{4,12},{8,0},{12,4},{1,9},{5,13},{9,1},{13,5},{2,10},{6,14},... | collective-permute-start | bytes 786440 | tf_op jit(solution)/shard_map/ppermute | solution.py:381
  18.9 0.0 copy-done
  18.9 0.0 copy-done.1
  18.9 0.0 copy-done.2
  18.9 0.0 copy-done.3
  18.9 0.0 copy-done.4
  18.9 3.5 %shard_map.93 = (bf16[128,256]{1,0:T(8,128)(2,1)S(1)}, f32[32,128,256]{2,1,0:T(8,128)S(1)}) custom-call(s32[2,256]{1,0:T(2,128)S(1)} %bitcast.5, f32[400,400]{1,0:T(8,128)S(1)} %copy-done, f32[4,1,32]{2,1,0:T(1,128)S(1)} %copy-done.2, s32[2]{0:T(128)S(1)} %pad_add_fusion.place_ref, f32[32]{0:T(128)S(1)} %copy-done.4, f32[1,256]{1,0:T(1,128)S(1)} %bitcast.6), custom_call_target="tpu_custom_call" | custom-call | flops 491520000 | bytes 640000 | tf_op jit(solution)/shard_map/pallas_call | solution.py:203
  22.4 12.1 %collective-permute-done.5.refs_3_ = bf16[1,16,32,256]{3,2,1,0:T(8,128)(2,1)S(1)} collective-permute-done((bf16[1,16,32,256]{3,2,1,0:T(8,128)(2,1)S(1)}, bf16[1,16,32,256]{3,2,1,0:T(8,128)(2,1)S(1)}, u32[]{:S(2)}, u32[]{:S(2)}) %collective-permute-start.5) | collective-permute-done | bytes 262176 | tf_op jit(solution)/shard_map/ppermute | solution.py:381
  34.5 0.3 collective-permute-start.6
  34.8 0.0 collective-permute-start.7
  34.8 16.4 %collective-permute-done.8.refs_2_ = bf16[1,16,32,256]{3,2,1,0:T(8,128)(2,1)S(1)} collective-permute-done((bf16[1,16,32,256]{3,2,1,0:T(8,128)(2,1)S(1)}, bf16[1,16,32,256]{3,2,1,0:T(8,128)(2,1)S(1)}, u32[]{:S(2)}, u32[]{:S(2)}) %collective-permute-start.8) | collective-permute-done | bytes 262176 | tf_op jit(solution)/shard_map/ppermute | solution.py:381
  51.2 0.0 collective-permute-start.12
  51.3 0.0 collective-permute-done.3.refs_1_
  51.3 0.5 collective-permute-start.10
  51.8 5.0 %collective-permute-done.4.refs_2_ = bf16[1,16,32,256]{3,2,1,0:T(8,128)(2,1)S(1)} collective-permute-done((bf16[1,16,32,256]{3,2,1,0:T(8,128)(2,1)S(1)}, bf16[1,16,32,256]{3,2,1,0:T(8,128)(2,1)S(1)}, u32[]{:S(2)}, u32[]{:S(2)}) %collective-permute-start.4) | collective-permute-done | bytes 262176 | tf_op jit(solution)/shard_map/ppermute | solution.py:381
  56.8 0.0 collective-permute-start.9
  56.8 0.0 collective-permute-done.10.refs_6_
  56.8 0.5 collective-permute-start.11
  57.3 0.0 collective-permute-done.6.refs_3_
  57.3 0.0 collective-permute-done.12.refs_7_
  57.3 0.1 collective-permute-start.13
  57.4 0.0 collective-permute-done.7.refs_4_
  57.4 1.3 %collective-permute-done.9.refs_5_ = bf16[2,16,32,256]{3,2,1,0:T(8,128)(2,1)S(1)} collective-permute-done((bf16[2,16,32,256]{3,2,1,0:T(8,128)(2,1)S(1)}, bf16[2,16,32,256]{3,2,1,0:T(8,128)(2,1)S(1)}, u32[]{:S(2)}, u32[]{:S(2)}) %collective-permute-start.9) | collective-permute-done | bytes 524320 | tf_op jit(solution)/shard_map/ppermute | solution.py:384
  58.7 2.2 %shard_map.94.refs_8_ = bf16[4,1,32,32,256]{4,3,2,1,0:T(8,128)(2,1)} custom-call(s32[2]{0:T(128)S(1)} %pad_add_fusion.place_ref, bf16[256,256]{1,0:T(8,128)(2,1)S(1)} %get-tuple-element.21.refs_5_.swap_ref, bf16[128,256]{1,0:T(8,128)(2,1)S(1)} %get-tuple-element.25.w_ref, f32[32,128,256]{2,1,0:T(8,128)S(1)} %get-tuple-element.26.inverse_ref, ...), custom_call_target="tpu_custom_call" | custom-call | tf_op jit(solution)/shard_map/pallas_call | solution.py:345
  60.9 0.0 collective-permute-done.11.refs_6_
  60.9 0.0 collective-permute-done.13.refs_7_
  60.9 2.2 %shard_map.95 = bf16[4,1,32,32,256]{4,3,2,1,0:T(8,128)(2,1)} custom-call(s32[2]{0:T(128)S(1)} %pad_add_fusion.place_ref, bf16[256,256]{1,0:T(8,128)(2,1)S(1)} %get-tuple-element.21.refs_5_.swap_ref, bf16[128,256]{1,0:T(8,128)(2,1)S(1)} %get-tuple-element.25.w_ref, ...), custom_call_target="tpu_custom_call", output_to_operand_aliasing={{}: (12, {})} | custom-call | tf_op jit(solution)/shard_map/pallas_call | solution.py:345
Async XLA Ops:
  0.0 7.4 %collective-permute-start.1 = (bf16[1,128,128]{2,1,0:T(8,128)(2,1)}, bf16[1,128,128]{2,1,0:T(8,128)(2,1)S(1)}, u32[]{:S(2)}, u32[]{:S(2)}) collective-permute-start(bf16[1,128,128]{2,1,0:T(8,128)(2,1)} %refs_0_.1), channel_id=1, source_target_pairs={{0,12},{4,8},{8,4},{12,0},{1,13},{5,9},{9,5},{13,1},{2,14},{6,10},... | collective-permute-start | bytes 98312 | tf_op jit(solution)/shard_map/ppermute | solution.py:381
  5.0 5.0 %collective-permute-start = (bf16[1,128,128]{2,1,0:T(8,128)(2,1)}, bf16[1,128,128]{2,1,0:T(8,128)(2,1)S(1)}, u32[]{:S(2)}, u32[]{:S(2)}) collective-permute-start(bf16[1,128,128]{2,1,0:T(8,128)(2,1)} %refs_0_.1), channel_id=1, source_target_pairs={{0,8},{4,12},{8,0},{12,4},{1,9},{5,13},{9,1},{13,5},{2,10},{6,14},... | collective-permute-start | bytes 98312 | tf_op jit(solution)/shard_map/ppermute | solution.py:381
  5.1 5.0 %collective-permute-start.2 = (bf16[1,128,128]{2,1,0:T(8,128)(2,1)}, bf16[1,128,128]{2,1,0:T(8,128)(2,1)S(1)}, u32[]{:S(2)}, u32[]{:S(2)}) collective-permute-start(bf16[1,128,128]{2,1,0:T(8,128)(2,1)} %refs_0_.1), channel_id=1, source_target_pairs={{0,4},{4,0},{8,12},{12,8},{1,5},{5,1},{9,13},{13,9},{2,6},{6,2},{1... | collective-permute-start | bytes 98312 | tf_op jit(solution)/shard_map/ppermute | solution.py:381
  5.7 13.2 %copy-start = (f32[400,400]{1,0:T(8,128)S(1)}, f32[400,400]{1,0:T(8,128)}, u32[]{:S(2)}) copy-start(f32[400,400]{1,0:T(8,128)} %coupling_ref.1) | copy-start | bytes 1920004
  5.7 13.2 %copy-start.1 = (s32[256,2]{0,1:T(2,128)S(1)}, s32[256,2]{0,1:T(2,128)}, u32[]{:S(2)}) copy-start(s32[256,2]{0,1:T(2,128)} %param.13) | copy-start | bytes 6148
  5.7 13.2 %copy-start.2 = (f32[4,1,32]{2,1,0:T(1,128)S(1)}, f32[4,1,32]{2,1,0:T(1,128)}, u32[]{:S(2)}) copy-start(f32[4,1,32]{2,1,0:T(1,128)} %gap_ref.1) | copy-start | bytes 1540
  5.7 13.2 %copy-start.3 = (f32[256]{0:T(256)S(1)}, f32[256]{0:T(256)}, u32[]{:S(2)}) copy-start(f32[256]{0:T(256)} %param.17) | copy-start | bytes 3076
  5.7 13.2 %copy-start.4 = (f32[32]{0:T(128)S(1)}, f32[32]{0:T(128)}, u32[]{:S(2)}) copy-start(f32[32]{0:T(128)} %row_ref.1) | copy-start | bytes 388
  12.4 38.9 %collective-permute-start.3 = (bf16[2,16,32,256]{3,2,1,0:T(8,128)(2,1)S(1)}, bf16[2,16,32,256]{3,2,1,0:T(8,128)(2,1)S(1)}, u32[]{:S(2)}, u32[]{:S(2)}) collective-permute-start(bf16[2,16,32,256]{3,2,1,0:T(8,128)(2,1)S(1)} %get-tuple-element.28), channel_id=1, source_target_pairs={{0,4},{4,0},{8,12},{12,8},{1,5},{5,1},{9,13},{13,9},{2,6},{6,2},{1... | collective-permute-start | bytes 1572872 | tf_op jit(solution)/shard_map/ppermute | solution.py:381
  12.5 22.0 %collective-permute-start.5 = (bf16[1,16,32,256]{3,2,1,0:T(8,128)(2,1)S(1)}, bf16[1,16,32,256]{3,2,1,0:T(8,128)(2,1)S(1)}, u32[]{:S(2)}, u32[]{:S(2)}) collective-permute-start(bf16[1,16,32,256]{3,2,1,0:T(8,128)(2,1)S(1)} %get-tuple-element.23), channel_id=1, source_target_pairs={{0,12},{4,8},{8,4},{12,0},{1,13},{5,9},{9,5},{13,1},{2,14},{6,10},... | collective-permute-start | bytes 786440 | tf_op jit(solution)/shard_map/ppermute | solution.py:381
  15.9 35.3 %collective-permute-start.8 = (bf16[1,16,32,256]{3,2,1,0:T(8,128)(2,1)S(1)}, bf16[1,16,32,256]{3,2,1,0:T(8,128)(2,1)S(1)}, u32[]{:S(2)}, u32[]{:S(2)}) collective-permute-start(bf16[1,16,32,256]{3,2,1,0:T(8,128)(2,1)S(1)} %get-tuple-element.33), channel_id=1, source_target_pairs={{0,8},{4,12},{8,0},{12,4},{1,9},{5,13},{9,1},{13,5},{2,10},{6,14},... | collective-permute-start | bytes 786440 | tf_op jit(solution)/shard_map/ppermute | solution.py:381
  15.9 40.8 %collective-permute-start.4 = (bf16[1,16,32,256]{3,2,1,0:T(8,128)(2,1)S(1)}, bf16[1,16,32,256]{3,2,1,0:T(8,128)(2,1)S(1)}, u32[]{:S(2)}, u32[]{:S(2)}) collective-permute-start(bf16[1,16,32,256]{3,2,1,0:T(8,128)(2,1)S(1)} %get-tuple-element.29), channel_id=1, source_target_pairs={{0,8},{4,12},{8,0},{12,4},{1,9},{5,13},{9,1},{13,5},{2,10},{6,14},... | collective-permute-start | bytes 786440 | tf_op jit(solution)/shard_map/ppermute | solution.py:381
  34.5 22.8 %collective-permute-start.6 = (bf16[1,16,32,256]{3,2,1,0:T(8,128)(2,1)S(1)}, bf16[1,16,32,256]{3,2,1,0:T(8,128)(2,1)S(1)}, u32[]{:S(2)}, u32[]{:S(2)}) collective-permute-start(bf16[1,16,32,256]{3,2,1,0:T(8,128)(2,1)S(1)} %get-tuple-element.31), channel_id=1, source_target_pairs={{0,12},{4,8},{8,4},{12,0},{1,13},{5,9},{9,5},{13,1},{2,14},{6,10},... | collective-permute-start | bytes 786440 | tf_op jit(solution)/shard_map/ppermute | solution.py:381
  34.8 22.5 %collective-permute-start.7 = (bf16[2,16,32,256]{3,2,1,0:T(8,128)(2,1)S(1)}, bf16[2,16,32,256]{3,2,1,0:T(8,128)(2,1)S(1)}, u32[]{:S(2)}, u32[]{:S(2)}) collective-permute-start(bf16[2,16,32,256]{3,2,1,0:T(8,128)(2,1)S(1)} %get-tuple-element.32.refs_0_), channel_id=1, source_target_pairs={{0,1},{1,0},{2,3},{3,2},{4,5},{5,4},{6,7},{7,6},{8,9},{9,8},{10,11... | collective-permute-start | bytes 1572872 | tf_op jit(solution)/shard_map/ppermute | solution.py:384
  51.2 6.0 %collective-permute-start.12 = (bf16[1,16,32,256]{3,2,1,0:T(8,128)(2,1)S(1)}, bf16[1,16,32,256]{3,2,1,0:T(8,128)(2,1)S(1)}, u32[]{:S(2)}, u32[]{:S(2)}) collective-permute-start(bf16[1,16,32,256]{3,2,1,0:T(8,128)(2,1)S(1)} %collective-permute-done.5.refs_3_), channel_id=1, source_target_pairs={{0,1},{1,0},{2,3},{3,2},{4,5},{5,4},{6,7},{7,6},{8,9},{9,8},{10,11... | collective-permute-start | bytes 786440 | tf_op jit(solution)/shard_map/ppermute | solution.py:384
  51.3 5.5 %collective-permute-start.10 = (bf16[1,16,32,256]{3,2,1,0:T(8,128)(2,1)S(1)}, bf16[1,16,32,256]{3,2,1,0:T(8,128)(2,1)S(1)}, u32[]{:S(2)}, u32[]{:S(2)}) collective-permute-start(bf16[1,16,32,256]{3,2,1,0:T(8,128)(2,1)S(1)} %collective-permute-done.8.refs_2_), channel_id=1, source_target_pairs={{0,1},{1,0},{2,3},{3,2},{4,5},{5,4},{6,7},{7,6},{8,9},{9,8},{10,11... | collective-permute-start | bytes 786440 | tf_op jit(solution)/shard_map/ppermute | solution.py:384
  56.8 1.9 %collective-permute-start.9 = (bf16[2,16,32,256]{3,2,1,0:T(8,128)(2,1)S(1)}, bf16[2,16,32,256]{3,2,1,0:T(8,128)(2,1)S(1)}, u32[]{:S(2)}, u32[]{:S(2)}) collective-permute-start(bf16[2,16,32,256]{3,2,1,0:T(8,128)(2,1)S(1)} %collective-permute-done.3.refs_1_), channel_id=1, source_target_pairs={{0,1},{1,0},{2,3},{3,2},{4,5},{5,4},{6,7},{7,6},{8,9},{9,8},{10,11... | collective-permute-start | bytes 1572872 | tf_op jit(solution)/shard_map/ppermute | solution.py:384
  56.8 4.1 %collective-permute-start.11 = (bf16[1,16,32,256]{3,2,1,0:T(8,128)(2,1)S(1)}, bf16[1,16,32,256]{3,2,1,0:T(8,128)(2,1)S(1)}, u32[]{:S(2)}, u32[]{:S(2)}) collective-permute-start(bf16[1,16,32,256]{3,2,1,0:T(8,128)(2,1)S(1)} %collective-permute-done.4.refs_2_), channel_id=1, source_target_pairs={{0,1},{1,0},{2,3},{3,2},{4,5},{5,4},{6,7},{7,6},{8,9},{9,8},{10,11... | collective-permute-start | bytes 786440 | tf_op jit(solution)/shard_map/ppermute | solution.py:384
  57.3 3.6 %collective-permute-start.13 = (bf16[1,16,32,256]{3,2,1,0:T(8,128)(2,1)S(1)}, bf16[1,16,32,256]{3,2,1,0:T(8,128)(2,1)S(1)}, u32[]{:S(2)}, u32[]{:S(2)}) collective-permute-start(bf16[1,16,32,256]{3,2,1,0:T(8,128)(2,1)S(1)} %collective-permute-done.6.refs_3_), channel_id=1, source_target_pairs={{0,1},{1,0},{2,3},{3,2},{4,5},{5,4},{6,7},{7,6},{8,9},{9,8},{10,11... | collective-permute-start | bytes 786440 | tf_op jit(solution)/shard_map/ppermute | solution.py:384

commit v8 on v7

--- a/solution.py
+++ b/solution.py
@@ -295,67 +295,94 @@
     )
 
 
-def finish_kernel(indices, chunk, place_ref, swap_ref, w_ref, inverse_ref, *refs):
-    pieces = len(indices)
-    piece_refs = refs[:pieces]
-    out_ref, ys, done, sems = refs[-4:]
-    _, rows, pairs, cols = piece_refs[0].shape
-    owners = pieces // 2
-    halves = pairs // ROWS
-    mine = owners * pairs
-    me = place_ref[0]
+def finish_blocks(indices, chunk, swap_ref, w_ref, inverse_ref, piece_refs, done, ys, then):
+    groups, _, rows, _ = done.shape
+    mine = groups * ROWS
     weights = w_ref[...]
     for a in range(rows):
         amps = jnp.concatenate([ref[index, a] for ref, index in zip(piece_refs, indices)], axis=0)
         cycle = jnp.dot(weights, amps, preferred_element_type=jnp.float32)
         total = amps[:mine].astype(jnp.float32) + cycle
         value = (total * inverse_ref[chunk * rows + a]).astype(jnp.bfloat16)
-        for g in range(owners * halves):
+        for g in range(groups):
             ys[g, pl.ds(a * ROWS, ROWS), :] = value[g * ROWS : (g + 1) * ROWS]
     swap = swap_ref[...]
+    for g in range(groups):
+        turned = jnp.dot(swap, ys[g], preferred_element_type=jnp.float32)
+        done[g] = turned.astype(jnp.bfloat16).reshape(done.shape[1:])
+        then(g)
+
+
+def early_kernel(indices, chunk, swap_ref, w_ref, inverse_ref, *refs):
+    piece_refs, (done, ys) = refs[:-2], refs[-2:]
+    finish_blocks(
+        indices, chunk, swap_ref, w_ref, inverse_ref, piece_refs, done, ys, lambda g: None
+    )
+
+
+def last_kernel(indices, chunk, swap_ref, w_ref, inverse_ref, place_ref, *refs):
+    ready_refs, piece_refs, (out_ref, done, ys, sems) = refs[:chunk], refs[chunk:-4], refs[-4:]
+    groups, _, rows, _ = done.shape
+    halves = 2 * groups // len(indices)
+    me = place_ref[0]
     leaving = []
-    for g in range(owners * halves):
-        turned = jnp.dot(swap, ys[g], preferred_element_type=jnp.float32)
-        done[g] = turned.astype(jnp.bfloat16).reshape(ROWS, rows, cols)
+
+    def write(source, c, g):
         k, h = g // halves, g % halves
         copy = pltpu.make_async_copy(
-            done.at[g],
-            out_ref.at[me ^ k, 0, pl.ds(h * ROWS, ROWS), pl.ds(chunk * rows, rows), :],
-            sems.at[g],
+            source.at[g],
+            out_ref.at[me ^ k, 0, pl.ds(h * ROWS, ROWS), pl.ds(c * rows, rows), :],
+            sems.at[c, g],
         )
         copy.start()
         leaving.append(copy)
+
+    for c, ref in enumerate(ready_refs):
+        for g in range(groups):
+            write(ref, c, g)
+    finish_blocks(
+        indices,
+        chunk,
+        swap_ref,
+        w_ref,
+        inverse_ref,
+        piece_refs,
+        done,
+        ys,
+        lambda g: write(done, chunk, g),
+    )
     for copy in leaving:
         copy.wait()
 
 
-def finish(chunk, place, swap, weights, inverse, pieces, before, shape):
+def finish(chunk, swap, weights, inverse, pieces, place=None, ready=(), shape=None):
     _, rows, pairs, cols = pieces[0][0].shape
-    owners = len(pieces) // 2
-    groups = owners * (pairs // ROWS)
-    anywhere = pl.BlockSpec(memory_space=pl.ANY)
-    args = [place, swap, weights, inverse] + [piece for piece, _ in pieces]
-    in_specs = [pl.BlockSpec(memory_space=pltpu.SMEM)]
-    in_specs += [pl.BlockSpec(memory_space=pltpu.VMEM)] * (3 + len(pieces))
-    aliases = {}
-    if before is not None:
-        aliases = {len(args): 0}
-        args.append(before)
-        in_specs.append(anywhere)
+    groups = len(pieces) // 2 * (pairs // ROWS)
+    indices = [index for _, index in pieces]
+    vmem, anywhere = pl.BlockSpec(memory_space=pltpu.VMEM), pl.BlockSpec(memory_space=pl.ANY)
+    block = (groups, ROWS, rows, cols)
+    ys = pltpu.VMEM((groups, ROWS * rows, cols), jnp.bfloat16)
+    args, in_specs = [swap, weights, inverse], [vmem] * 3
+    if shape is None:
+        kernel = functools.partial(early_kernel, indices, chunk)
+        out_spec, out_shape = vmem, jax.ShapeDtypeStruct(block, jnp.bfloat16)
+        scratch = [ys]
+    else:
+        kernel = functools.partial(last_kernel, indices, chunk)
+        out_spec, out_shape = anywhere, jax.ShapeDtypeStruct(shape, jnp.bfloat16)
+        scratch = [pltpu.VMEM(block, jnp.bfloat16), ys]
+        scratch += [pltpu.SemaphoreType.DMA((chunk + 1, groups))]
+        args += [place, *ready]
+        in_specs += [pl.BlockSpec(memory_space=pltpu.SMEM)] + [anywhere] * len(ready)
     return pl.pallas_call(
-        functools.partial(finish_kernel, [index for _, index in pieces], chunk),
-        in_specs=in_specs,
-        out_specs=anywhere,
-        out_shape=jax.ShapeDtypeStruct(shape, jnp.bfloat16),
-        scratch_shapes=[
-            pltpu.VMEM((groups, ROWS * rows, cols), jnp.bfloat16),
-            pltpu.VMEM((groups, ROWS, rows, cols), jnp.bfloat16),
-            pltpu.SemaphoreType.DMA((groups,)),
-        ],
-        input_output_aliases=aliases,
+        kernel,
+        in_specs=in_specs + [vmem] * len(pieces),
+        out_specs=out_spec,
+        out_shape=out_shape,
+        scratch_shapes=scratch,
         compiler_params=pltpu.CompilerParams(vmem_limit_bytes=VMEM_BYTES),
         cost_estimate=pl.CostEstimate(flops=0, bytes_accessed=0, transcendentals=0),
-    )(*args)
+    )(*args, *[piece for piece, _ in pieces])
 
 
 def local_chunked(
@@ -410,13 +437,14 @@
             earlier = other[k, c - 1] if c else None
             other[k, c] = to_sibling(after(direct[k, c], earlier))
 
-    result = None
+    ready = []
     for c in range(chunks):
         pieces = [(own, c), (near, c)] + [(direct[k, c], 0) for k in far]
         pieces += [(own_passed, c), (near_passed, c)] + [(other[k, c], 0) for k in far]
-        shape = (owners, 1, pairs, rows, cols)
-        result = finish(c, place, swap, weights, inverse, pieces, result, shape)
-    return result
+        if c + 1 < chunks:
+            ready.append(finish(c, swap, weights, inverse, pieces))
+    shape = (owners, 1, pairs, rows, cols)
+    return finish(c, swap, weights, inverse, pieces, place, ready, shape)
 
 
 def solution(mesh):

time: 63.4 us -> 62.3 us (0.983)
  Pallas kernels: 11.9 us -> 10.8 us
    pallas_call x2, Pallas kernels: 4.44 us -> 3.35 us  [finish(): pl.pallas_call(kernel, in_specs=in_specs + [vmem] * len(pieces), out_spec...]
  transfers between devices with their start and end apart: 14 -> 14, of which waited for: 5 -> 5; matrix products, arithmetic and copies ran while one was open for 0% -> 0% of each run, Pallas kernels for 12% -> 10%
where the time goes in v8:
time: 62.3 us; the launch traced here: 62.1 us
  waiting for transfers between devices  37.5 us (60%)
  starting transfers between devices  13.5 us (22%)
  Pallas kernels  10.8 us (17%)
    ppermute x8, waiting for transfers between devices, to_owner(): return lax.ppermute(value, 'pair', [(o, o ^ k) for o in range(owners)])  36.2 us
    ppermute x8, starting transfers between devices, to_owner(): return lax.ppermute(value, 'pair', [(o, o ^ k) for o in range(owners)])  12.4 us
    pallas_call x1, Pallas kernels, make_weights(): pl.pallas_call(weights_kernel, in_specs=[vmem, vmem, vmem, smem, smem, vm...  3.52 us
    pallas_call x2, Pallas kernels, finish(): pl.pallas_call(kernel, in_specs=in_specs + [vmem] * len(pieces), out_spec...  3.35 us
    pallas_call x1, Pallas kernels, dress(): pl.pallas_call(functools.partial(dress_kernel, owners, rows, groups), in_...  2.31 us
    pallas_call x1, Pallas kernels, hold(): pl.pallas_call(hold_kernel, in_specs=[anywhere], out_specs=[anywhere, pl....  1.64 us
    ppermute x6, waiting for transfers between devices, to_sibling(): return lax.ppermute(value, 'sub', [(0, 1), (1, 0)])  1.32 us
  transfers between devices with their start and end apart: 14, of which 5 were waited for; matrix products, arithmetic and copies ran while one was open for 0% of the time, Pallas kernels for 10%

profile of v8, /device:TPU:0, one launch (start us, length us, event | category | flops | bytes accessed | tf_op | source)
XLA Modules:
  0.0 62.1 jit_solution(17358968641035122008)
XLA Ops:
  0.0 5.0 %collective-permute-start.1 = (bf16[1,128,128]{2,1,0:T(8,128)(2,1)}, bf16[1,128,128]{2,1,0:T(8,128)(2,1)S(1)}, u32[]{:S(2)}, u32[]{:S(2)}) collective-permute-start(bf16[1,128,128]{2,1,0:T(8,128)(2,1)} %refs_0_.1), channel_id=1, source_target_pairs={{0,12},{4,8},{8,4},{12,0},{1,13},{5,9},{9,5},{13,1},{2,14},{6,10},... | collective-permute-start | bytes 98312 | tf_op jit(solution)/shard_map/ppermute | solution.py:408
  5.0 0.0 collective-permute-start
  5.1 0.6 collective-permute-start.2
  5.6 0.1 pad_add_fusion.place_ref
  5.7 0.0 copy-start
  5.7 0.0 copy-start.1
  5.7 0.0 copy-start.2
  5.7 0.0 copy-start.3
  5.7 0.0 copy-start.4
  5.7 1.6 %shard_map.91 = (bf16[1,1,32,128,256]{4,3,2,1,0:T(8,128)(2,1)S(1)}, bf16[256,256]{1,0:T(8,128)(2,1)S(1)}) custom-call(bf16[1,1,32,128,256]{4,3,2,1,0:T(8,128)(2,1)} %lam_ref.1), custom_call_target="tpu_custom_call" | custom-call | bytes 4194304 | tf_op jit(solution)/shard_map/pallas_call | solution.py:150
  7.4 0.0 collective-permute-done.1.refs_2_
  7.4 2.7 %collective-permute-done.refs_1_ = bf16[1,128,128]{2,1,0:T(8,128)(2,1)S(1)} collective-permute-done((bf16[1,128,128]{2,1,0:T(8,128)(2,1)}, bf16[1,128,128]{2,1,0:T(8,128)(2,1)S(1)}, u32[]{:S(2)}, u32[]{:S(2)}) %collective-permute-start) | collective-permute-done | bytes 32800 | tf_op jit(solution)/shard_map/ppermute | solution.py:408
  10.1 0.0 collective-permute-done.2.refs_3_
  10.1 2.3 %shard_map.92 = (bf16[1,16,32,256]{3,2,1,0:T(8,128)(2,1)S(1)}, bf16[1,16,32,256]{3,2,1,0:T(8,128)(2,1)S(1)}, bf16[1,16,32,256]{3,2,1,0:T(8,128)(2,1)S(1)}, bf16[...) custom-call(s32[2]{0:T(128)S(1)} %pad_add_fusion.place_ref, ...), custom_call_target="tpu_custom_call" | custom-call | flops 268435456 | bytes 3145728 | tf_op jit(solution)/shard_map/pallas_call | solution.py:268
  12.4 0.1 collective-permute-start.3
  12.5 3.5 %collective-permute-start.5 = (bf16[1,16,32,256]{3,2,1,0:T(8,128)(2,1)S(1)}, bf16[1,16,32,256]{3,2,1,0:T(8,128)(2,1)S(1)}, u32[]{:S(2)}, u32[]{:S(2)}) collective-permute-start(bf16[1,16,32,256]{3,2,1,0:T(8,128)(2,1)S(1)} %get-tuple-element.23), channel_id=1, source_target_pairs={{0,12},{4,8},{8,4},{12,0},{1,13},{5,9},{9,5},{13,1},{2,14},{6,10},... | collective-permute-start | bytes 786440 | tf_op jit(solution)/shard_map/ppermute | solution.py:408
  15.9 0.0 collective-permute-start.4
  15.9 2.9 %collective-permute-start.10 = (bf16[1,16,32,256]{3,2,1,0:T(8,128)(2,1)S(1)}, bf16[1,16,32,256]{3,2,1,0:T(8,128)(2,1)S(1)}, u32[]{:S(2)}, u32[]{:S(2)}) collective-permute-start(bf16[1,16,32,256]{3,2,1,0:T(8,128)(2,1)S(1)} %get-tuple-element.32), channel_id=1, source_target_pairs={{0,8},{4,12},{8,0},{12,4},{1,9},{5,13},{9,1},{13,5},{2,10},{6,14},... | collective-permute-start | bytes 786440 | tf_op jit(solution)/shard_map/ppermute | solution.py:408
  18.9 0.0 copy-done
  18.9 0.0 copy-done.1
  18.9 0.0 copy-done.2
  18.9 0.0 copy-done.3
  18.9 0.0 copy-done.4
  18.9 3.5 %shard_map.93 = (bf16[128,256]{1,0:T(8,128)(2,1)S(1)}, f32[32,128,256]{2,1,0:T(8,128)S(1)}) custom-call(s32[2,256]{1,0:T(2,128)S(1)} %bitcast.5, f32[400,400]{1,0:T(8,128)S(1)} %copy-done, f32[4,1,32]{2,1,0:T(1,128)S(1)} %copy-done.2, s32[2]{0:T(128)S(1)} %pad_add_fusion.place_ref, f32[32]{0:T(128)S(1)} %copy-done.4, f32[1,256]{1,0:T(1,128)S(1)} %bitcast.6), custom_call_target="tpu_custom_call" | custom-call | flops 491520000 | bytes 640000 | tf_op jit(solution)/shard_map/pallas_call | solution.py:203
  22.4 12.1 %collective-permute-done.5.refs_3_ = bf16[1,16,32,256]{3,2,1,0:T(8,128)(2,1)S(1)} collective-permute-done((bf16[1,16,32,256]{3,2,1,0:T(8,128)(2,1)S(1)}, bf16[1,16,32,256]{3,2,1,0:T(8,128)(2,1)S(1)}, u32[]{:S(2)}, u32[]{:S(2)}) %collective-permute-start.5) | collective-permute-done | bytes 262176 | tf_op jit(solution)/shard_map/ppermute | solution.py:408
  34.5 0.3 collective-permute-start.11
  34.8 0.0 collective-permute-start.6
  34.8 16.4 %collective-permute-done.4.refs_2_ = bf16[1,16,32,256]{3,2,1,0:T(8,128)(2,1)S(1)} collective-permute-done((bf16[1,16,32,256]{3,2,1,0:T(8,128)(2,1)S(1)}, bf16[1,16,32,256]{3,2,1,0:T(8,128)(2,1)S(1)}, u32[]{:S(2)}, u32[]{:S(2)}) %collective-permute-start.4) | collective-permute-done | bytes 262176 | tf_op jit(solution)/shard_map/ppermute | solution.py:408
  51.2 0.0 collective-permute-start.9
  51.3 0.0 collective-permute-done.3.refs_1_.refs_2_
  51.3 0.5 collective-permute-start.8
  51.8 5.0 %collective-permute-done.10.refs_3_ = bf16[1,16,32,256]{3,2,1,0:T(8,128)(2,1)S(1)} collective-permute-done((bf16[1,16,32,256]{3,2,1,0:T(8,128)(2,1)S(1)}, bf16[1,16,32,256]{3,2,1,0:T(8,128)(2,1)S(1)}, u32[]{:S(2)}, u32[]{:S(2)}) %collective-permute-start.10) | collective-permute-done | bytes 262176 | tf_op jit(solution)/shard_map/ppermute | solution.py:408
  56.8 0.0 collective-permute-start.7
  56.8 0.0 collective-permute-done.8.refs_6_
  56.8 0.5 collective-permute-start.12
  57.3 0.0 collective-permute-done.11.refs_4_
  57.3 0.0 collective-permute-done.9.refs_7_
  57.3 0.1 collective-permute-start.13
  57.4 0.0 collective-permute-done.6.refs_4_.refs_5_
  57.4 1.3 %collective-permute-done.7.refs_5_.refs_6_ = bf16[2,16,32,256]{3,2,1,0:T(8,128)(2,1)S(1)} collective-permute-done((bf16[2,16,32,256]{3,2,1,0:T(8,128)(2,1)S(1)}, bf16[2,16,32,256]{3,2,1,0:T(8,128)(2,1)S(1)}, u32[]{:S(2)}, u32[]{:S(2)}) %collective-permute-start.7) | collective-permute-done | bytes 524320 | tf_op jit(solution)/shard_map/ppermute | solution.py:411
  58.7 0.9 %shard_map.94.refs_0_ = bf16[8,16,16,256]{3,2,1,0:T(8,128)(2,1)S(1)} custom-call(bf16[256,256]{1,0:T(8,128)(2,1)S(1)} %get-tuple-element.21.refs_5_.swap_ref, bf16[128,256]{1,0:T(8,128)(2,1)S(1)} %get-tuple-element.25.w_ref, f32[32,128,256]{2,1,0:T(8,128)S(1)} %get-tuple-element.26.inverse_ref, ...), custom_call_target="tpu_custom_call" | custom-call | tf_op jit(solution)/shard_map/pallas_call | solution.py:377
  59.6 0.0 collective-permute-done.12.refs_7_
  59.6 0.0 collective-permute-done.13.refs_8_
  59.6 2.5 %shard_map.95 = bf16[4,1,32,32,256]{4,3,2,1,0:T(8,128)(2,1)} custom-call(bf16[256,256]{1,0:T(8,128)(2,1)S(1)} %get-tuple-element.21.refs_5_.swap_ref, bf16[128,256]{1,0:T(8,128)(2,1)S(1)} %get-tuple-element.25.w_ref, f32[32,128,256]{2,1,0:T(8,128)S(1)} %get-tuple-element.26.inverse_ref, s32[2]{0:T(128)S(1)} %pad_add_fusion.place_ref, ...), custom_call_target="tpu_custom_call" | custom-call | tf_op jit(solution)/shard_map/pallas_call | solution.py:377
Async XLA Ops:
  0.0 7.4 %collective-permute-start.1 = (bf16[1,128,128]{2,1,0:T(8,128)(2,1)}, bf16[1,128,128]{2,1,0:T(8,128)(2,1)S(1)}, u32[]{:S(2)}, u32[]{:S(2)}) collective-permute-start(bf16[1,128,128]{2,1,0:T(8,128)(2,1)} %refs_0_.1), channel_id=1, source_target_pairs={{0,12},{4,8},{8,4},{12,0},{1,13},{5,9},{9,5},{13,1},{2,14},{6,10},... | collective-permute-start | bytes 98312 | tf_op jit(solution)/shard_map/ppermute | solution.py:408
  5.0 5.0 %collective-permute-start = (bf16[1,128,128]{2,1,0:T(8,128)(2,1)}, bf16[1,128,128]{2,1,0:T(8,128)(2,1)S(1)}, u32[]{:S(2)}, u32[]{:S(2)}) collective-permute-start(bf16[1,128,128]{2,1,0:T(8,128)(2,1)} %refs_0_.1), channel_id=1, source_target_pairs={{0,8},{4,12},{8,0},{12,4},{1,9},{5,13},{9,1},{13,5},{2,10},{6,14},... | collective-permute-start | bytes 98312 | tf_op jit(solution)/shard_map/ppermute | solution.py:408
  5.1 5.0 %collective-permute-start.2 = (bf16[1,128,128]{2,1,0:T(8,128)(2,1)}, bf16[1,128,128]{2,1,0:T(8,128)(2,1)S(1)}, u32[]{:S(2)}, u32[]{:S(2)}) collective-permute-start(bf16[1,128,128]{2,1,0:T(8,128)(2,1)} %refs_0_.1), channel_id=1, source_target_pairs={{0,4},{4,0},{8,12},{12,8},{1,5},{5,1},{9,13},{13,9},{2,6},{6,2},{1... | collective-permute-start | bytes 98312 | tf_op jit(solution)/shard_map/ppermute | solution.py:408
  5.7 13.2 %copy-start = (f32[400,400]{1,0:T(8,128)S(1)}, f32[400,400]{1,0:T(8,128)}, u32[]{:S(2)}) copy-start(f32[400,400]{1,0:T(8,128)} %coupling_ref.1) | copy-start | bytes 1920004
  5.7 13.2 %copy-start.1 = (s32[256,2]{0,1:T(2,128)S(1)}, s32[256,2]{0,1:T(2,128)}, u32[]{:S(2)}) copy-start(s32[256,2]{0,1:T(2,128)} %param.13) | copy-start | bytes 6148
  5.7 13.2 %copy-start.2 = (f32[4,1,32]{2,1,0:T(1,128)S(1)}, f32[4,1,32]{2,1,0:T(1,128)}, u32[]{:S(2)}) copy-start(f32[4,1,32]{2,1,0:T(1,128)} %gap_ref.1) | copy-start | bytes 1540
  5.7 13.2 %copy-start.3 = (f32[256]{0:T(256)S(1)}, f32[256]{0:T(256)}, u32[]{:S(2)}) copy-start(f32[256]{0:T(256)} %param.17) | copy-start | bytes 3076
  5.7 13.2 %copy-start.4 = (f32[32]{0:T(128)S(1)}, f32[32]{0:T(128)}, u32[]{:S(2)}) copy-start(f32[32]{0:T(128)} %row_ref.1) | copy-start | bytes 388
  12.4 38.9 %collective-permute-start.3 = (bf16[2,16,32,256]{3,2,1,0:T(8,128)(2,1)S(1)}, bf16[2,16,32,256]{3,2,1,0:T(8,128)(2,1)S(1)}, u32[]{:S(2)}, u32[]{:S(2)}) collective-permute-start(bf16[2,16,32,256]{3,2,1,0:T(8,128)(2,1)S(1)} %get-tuple-element.28), channel_id=1, source_target_pairs={{0,4},{4,0},{8,12},{12,8},{1,5},{5,1},{9,13},{13,9},{2,6},{6,2},{1... | collective-permute-start | bytes 1572872 | tf_op jit(solution)/shard_map/ppermute | solution.py:408
  12.5 22.0 %collective-permute-start.5 = (bf16[1,16,32,256]{3,2,1,0:T(8,128)(2,1)S(1)}, bf16[1,16,32,256]{3,2,1,0:T(8,128)(2,1)S(1)}, u32[]{:S(2)}, u32[]{:S(2)}) collective-permute-start(bf16[1,16,32,256]{3,2,1,0:T(8,128)(2,1)S(1)} %get-tuple-element.23), channel_id=1, source_target_pairs={{0,12},{4,8},{8,4},{12,0},{1,13},{5,9},{9,5},{13,1},{2,14},{6,10},... | collective-permute-start | bytes 786440 | tf_op jit(solution)/shard_map/ppermute | solution.py:408
  15.9 35.3 %collective-permute-start.4 = (bf16[1,16,32,256]{3,2,1,0:T(8,128)(2,1)S(1)}, bf16[1,16,32,256]{3,2,1,0:T(8,128)(2,1)S(1)}, u32[]{:S(2)}, u32[]{:S(2)}) collective-permute-start(bf16[1,16,32,256]{3,2,1,0:T(8,128)(2,1)S(1)} %get-tuple-element.29), channel_id=1, source_target_pairs={{0,8},{4,12},{8,0},{12,4},{1,9},{5,13},{9,1},{13,5},{2,10},{6,14},... | collective-permute-start | bytes 786440 | tf_op jit(solution)/shard_map/ppermute | solution.py:408
  15.9 40.8 %collective-permute-start.10 = (bf16[1,16,32,256]{3,2,1,0:T(8,128)(2,1)S(1)}, bf16[1,16,32,256]{3,2,1,0:T(8,128)(2,1)S(1)}, u32[]{:S(2)}, u32[]{:S(2)}) collective-permute-start(bf16[1,16,32,256]{3,2,1,0:T(8,128)(2,1)S(1)} %get-tuple-element.32), channel_id=1, source_target_pairs={{0,8},{4,12},{8,0},{12,4},{1,9},{5,13},{9,1},{13,5},{2,10},{6,14},... | collective-permute-start | bytes 786440 | tf_op jit(solution)/shard_map/ppermute | solution.py:408
  34.5 22.8 %collective-permute-start.11 = (bf16[1,16,32,256]{3,2,1,0:T(8,128)(2,1)S(1)}, bf16[1,16,32,256]{3,2,1,0:T(8,128)(2,1)S(1)}, u32[]{:S(2)}, u32[]{:S(2)}) collective-permute-start(bf16[1,16,32,256]{3,2,1,0:T(8,128)(2,1)S(1)} %get-tuple-element.34), channel_id=1, source_target_pairs={{0,12},{4,8},{8,4},{12,0},{1,13},{5,9},{9,5},{13,1},{2,14},{6,10},... | collective-permute-start | bytes 786440 | tf_op jit(solution)/shard_map/ppermute | solution.py:408
  34.8 22.5 %collective-permute-start.6 = (bf16[2,16,32,256]{3,2,1,0:T(8,128)(2,1)S(1)}, bf16[2,16,32,256]{3,2,1,0:T(8,128)(2,1)S(1)}, u32[]{:S(2)}, u32[]{:S(2)}) collective-permute-start(bf16[2,16,32,256]{3,2,1,0:T(8,128)(2,1)S(1)} %get-tuple-element.30.refs_0_.refs_1_), channel_id=1, source_target_pairs={{0,1},{1,0},{2,3},{3,2},{4,5},{5,4},{6,7},{7,6},{8,9},{9,8},{10,11... | collective-permute-start | bytes 1572872 | tf_op jit(solution)/shard_map/ppermute | solution.py:411
  51.2 6.0 %collective-permute-start.9 = (bf16[1,16,32,256]{3,2,1,0:T(8,128)(2,1)S(1)}, bf16[1,16,32,256]{3,2,1,0:T(8,128)(2,1)S(1)}, u32[]{:S(2)}, u32[]{:S(2)}) collective-permute-start(bf16[1,16,32,256]{3,2,1,0:T(8,128)(2,1)S(1)} %collective-permute-done.5.refs_3_), channel_id=1, source_target_pairs={{0,1},{1,0},{2,3},{3,2},{4,5},{5,4},{6,7},{7,6},{8,9},{9,8},{10,11... | collective-permute-start | bytes 786440 | tf_op jit(solution)/shard_map/ppermute | solution.py:411
  51.3 5.5 %collective-permute-start.8 = (bf16[1,16,32,256]{3,2,1,0:T(8,128)(2,1)S(1)}, bf16[1,16,32,256]{3,2,1,0:T(8,128)(2,1)S(1)}, u32[]{:S(2)}, u32[]{:S(2)}) collective-permute-start(bf16[1,16,32,256]{3,2,1,0:T(8,128)(2,1)S(1)} %collective-permute-done.4.refs_2_), channel_id=1, source_target_pairs={{0,1},{1,0},{2,3},{3,2},{4,5},{5,4},{6,7},{7,6},{8,9},{9,8},{10,11... | collective-permute-start | bytes 786440 | tf_op jit(solution)/shard_map/ppermute | solution.py:411
  56.8 1.9 %collective-permute-start.7 = (bf16[2,16,32,256]{3,2,1,0:T(8,128)(2,1)S(1)}, bf16[2,16,32,256]{3,2,1,0:T(8,128)(2,1)S(1)}, u32[]{:S(2)}, u32[]{:S(2)}) collective-permute-start(bf16[2,16,32,256]{3,2,1,0:T(8,128)(2,1)S(1)} %collective-permute-done.3.refs_1_.refs_2_), channel_id=1, source_target_pairs={{0,1},{1,0},{2,3},{3,2},{4,5},{5,4},{6,7},{7,6},{8,9},{9,8},{10,11... | collective-permute-start | bytes 1572872 | tf_op jit(solution)/shard_map/ppermute | solution.py:411
  56.8 2.8 %collective-permute-start.12 = (bf16[1,16,32,256]{3,2,1,0:T(8,128)(2,1)S(1)}, bf16[1,16,32,256]{3,2,1,0:T(8,128)(2,1)S(1)}, u32[]{:S(2)}, u32[]{:S(2)}) collective-permute-start(bf16[1,16,32,256]{3,2,1,0:T(8,128)(2,1)S(1)} %collective-permute-done.10.refs_3_), channel_id=1, source_target_pairs={{0,1},{1,0},{2,3},{3,2},{4,5},{5,4},{6,7},{7,6},{8,9},{9,8},{10,11... | collective-permute-start | bytes 786440 | tf_op jit(solution)/shard_map/ppermute | solution.py:411
  57.3 2.3 %collective-permute-start.13 = (bf16[1,16,32,256]{3,2,1,0:T(8,128)(2,1)S(1)}, bf16[1,16,32,256]{3,2,1,0:T(8,128)(2,1)S(1)}, u32[]{:S(2)}, u32[]{:S(2)}) collective-permute-start(bf16[1,16,32,256]{3,2,1,0:T(8,128)(2,1)S(1)} %collective-permute-done.11.refs_4_), channel_id=1, source_target_pairs={{0,1},{1,0},{2,3},{3,2},{4,5},{5,4},{6,7},{7,6},{8,9},{9,8},{10,11... | collective-permute-start | bytes 786440 | tf_op jit(solution)/shard_map/ppermute | solution.py:411

commit v9 on v8

--- a/solution.py
+++ b/solution.py
@@ -97,6 +97,10 @@
     return pltpu.with_memory_space_constraint(value, pltpu.HBM)
 
 
+def in_smem(value):
+    return pltpu.with_memory_space_constraint(value, pltpu.SMEM)
+
+
 def one_hot(hits):
     return jnp.where(hits, 1.0, 0.0).astype(jnp.bfloat16)
 
@@ -217,7 +221,7 @@
 
 
 def dress_kernel(owners, rows, groups, place_ref, tile_of_ref, mask_ref, *refs):
-    tile_refs, lam_ref = (refs[0], refs[owners - 1], *refs[1 : owners - 1]), refs[owners]
+    tile_refs, lam_ref = (refs[0], *refs[2:owners], refs[1]), refs[owners]
     swap_ref = refs[owners + 1]
     out_refs = refs[owners + 2 : -2]
     tiles, stage = refs[-2:]
@@ -284,12 +288,12 @@
             transcendentals=0,
         ),
     )(
-        place,
-        in_hbm(tile_of),
-        in_hbm(jnp.swapaxes(tile_mask, 2, 3)),
-        in_hbm(tiles[0]),
-        *tiles[2:],
-        tiles[1],
+        in_smem(place),
+        in_smem(tile_of),
+        in_smem(jnp.swapaxes(tile_mask, 2, 3)),
+        tiles[0],
+        tiles[-1],
+        *tiles[1:-1],
         lambda_amps,
         swap,
     )

time: 62.3 us -> 63 us (1.011)
  transfers between devices with their start and end apart: 14 -> 14, of which waited for: 5 -> 6; matrix products, arithmetic and copies ran while one was open for 0% -> 0% of each run, Pallas kernels for 10% -> 10%
where the time goes in v9:
time: 63 us; the launch traced here: 62.8 us
  waiting for transfers between devices  38.1 us (60%)
  starting transfers between devices  13.9 us (22%)
  Pallas kernels  10.6 us (17%)
    ppermute x8, waiting for transfers between devices, to_owner(): return lax.ppermute(value, 'pair', [(o, o ^ k) for o in range(owners)])  36.8 us
    ppermute x8, starting transfers between devices, to_owner(): return lax.ppermute(value, 'pair', [(o, o ^ k) for o in range(owners)])  12.8 us
    pallas_call x1, Pallas kernels, make_weights(): pl.pallas_call(weights_kernel, in_specs=[vmem, vmem, vmem, smem, smem, vm...  3.52 us
    pallas_call x2, Pallas kernels, finish(): pl.pallas_call(kernel, in_specs=in_specs + [vmem] * len(pieces), out_spec...  3.35 us
    pallas_call x1, Pallas kernels, dress(): pl.pallas_call(functools.partial(dress_kernel, owners, rows, groups), in_...  2.1 us
    pallas_call x1, Pallas kernels, hold(): pl.pallas_call(hold_kernel, in_specs=[anywhere], out_specs=[anywhere, pl....  1.64 us
    ppermute x6, waiting for transfers between devices, to_sibling(): return lax.ppermute(value, 'sub', [(0, 1), (1, 0)])  1.32 us
  transfers between devices with their start and end apart: 14, of which 6 were waited for; matrix products, arithmetic and copies ran while one was open for 0% of the time, Pallas kernels for 10%

profile of v9, /device:TPU:0, one launch (start us, length us, event | category | flops | bytes accessed | tf_op | source)
XLA Modules:
  0.0 62.8 jit_solution(10653191202576321080)
XLA Ops:
  0.0 0.0 copy-start
  0.0 0.0 copy-start.1
  0.0 0.0 copy-start.2
  0.0 3.1 %collective-permute-start.1 = (bf16[1,128,128]{2,1,0:T(8,128)(2,1)}, bf16[1,128,128]{2,1,0:T(8,128)(2,1)S(1)}, u32[]{:S(2)}, u32[]{:S(2)}) collective-permute-start(bf16[1,128,128]{2,1,0:T(8,128)(2,1)} %refs_0_.1), channel_id=1, source_target_pairs={{0,4},{4,0},{8,12},{12,8},{1,5},{5,1},{9,13},{13,9},{2,6},{6,2},{1... | collective-permute-start | bytes 98312 | tf_op jit(solution)/shard_map/ppermute | solution.py:412
  3.1 2.5 %collective-permute-start = (bf16[1,128,128]{2,1,0:T(8,128)(2,1)}, bf16[1,128,128]{2,1,0:T(8,128)(2,1)S(1)}, u32[]{:S(2)}, u32[]{:S(2)}) collective-permute-start(bf16[1,128,128]{2,1,0:T(8,128)(2,1)} %refs_0_.1), channel_id=1, source_target_pairs={{0,12},{4,8},{8,4},{12,0},{1,13},{5,9},{9,5},{13,1},{2,14},{6,10},... | collective-permute-start | bytes 98312 | tf_op jit(solution)/shard_map/ppermute | solution.py:412
  5.6 0.1 collective-permute-start.2
  5.7 0.1 pad_add_fusion.place_ref
  5.8 0.0 copy-start.3
  5.8 0.0 copy-start.4
  5.8 0.0 copy-start.7
  5.8 1.6 %shard_map.91 = (bf16[1,1,32,128,256]{4,3,2,1,0:T(8,128)(2,1)S(1)}, bf16[256,256]{1,0:T(8,128)(2,1)S(1)}) custom-call(bf16[1,1,32,128,256]{4,3,2,1,0:T(8,128)(2,1)} %lam_ref.1), custom_call_target="tpu_custom_call" | custom-call | bytes 4194304 | tf_op jit(solution)/shard_map/pallas_call | solution.py:154
  7.4 0.0 collective-permute-done.1.refs_2_
  7.5 2.0 %collective-permute-done.refs_1_ = bf16[1,128,128]{2,1,0:T(8,128)(2,1)S(1)} collective-permute-done((bf16[1,128,128]{2,1,0:T(8,128)(2,1)}, bf16[1,128,128]{2,1,0:T(8,128)(2,1)S(1)}, u32[]{:S(2)}, u32[]{:S(2)}) %collective-permute-start) | collective-permute-done | bytes 32800 | tf_op jit(solution)/shard_map/ppermute | solution.py:412
  9.5 1.5 %collective-permute-done.2.refs_3_ = bf16[1,128,128]{2,1,0:T(8,128)(2,1)S(1)} collective-permute-done((bf16[1,128,128]{2,1,0:T(8,128)(2,1)}, bf16[1,128,128]{2,1,0:T(8,128)(2,1)S(1)}, u32[]{:S(2)}, u32[]{:S(2)}) %collective-permute-start.2) | collective-permute-done | bytes 32800 | tf_op jit(solution)/shard_map/ppermute | solution.py:412
  10.9 0.0 copy-done
  11.0 0.0 copy-done.1
  11.0 0.0 copy-done.2
  11.0 2.1 %shard_map.92 = (bf16[1,16,32,256]{3,2,1,0:T(8,128)(2,1)S(1)}, bf16[1,16,32,256]{3,2,1,0:T(8,128)(2,1)S(1)}, bf16[1,16,32,256]{3,2,1,0:T(8,128)(2,1)S(1)}, bf16[...) custom-call(s32[2]{0:T(128)S(1)} %pad_add_fusion.place_ref, ...), custom_call_target="tpu_custom_call" | custom-call | flops 268435456 | bytes 3145728 | tf_op jit(solution)/shard_map/pallas_call | solution.py:272
  13.1 0.5 collective-permute-start.3
  13.6 1.0 %collective-permute-start.5 = (bf16[1,16,32,256]{3,2,1,0:T(8,128)(2,1)S(1)}, bf16[1,16,32,256]{3,2,1,0:T(8,128)(2,1)S(1)}, u32[]{:S(2)}, u32[]{:S(2)}) collective-permute-start(bf16[1,16,32,256]{3,2,1,0:T(8,128)(2,1)S(1)} %get-tuple-element.23), channel_id=1, source_target_pairs={{0,12},{4,8},{8,4},{12,0},{1,13},{5,9},{9,5},{13,1},{2,14},{6,10},... | collective-permute-start | bytes 786440 | tf_op jit(solution)/shard_map/ppermute | solution.py:412
  14.6 2.0 %collective-permute-start.4 = (bf16[1,16,32,256]{3,2,1,0:T(8,128)(2,1)S(1)}, bf16[1,16,32,256]{3,2,1,0:T(8,128)(2,1)S(1)}, u32[]{:S(2)}, u32[]{:S(2)}) collective-permute-start(bf16[1,16,32,256]{3,2,1,0:T(8,128)(2,1)S(1)} %get-tuple-element.29), channel_id=1, source_target_pairs={{0,8},{4,12},{8,0},{12,4},{1,9},{5,13},{9,1},{13,5},{2,10},{6,14},... | collective-permute-start | bytes 786440 | tf_op jit(solution)/shard_map/ppermute | solution.py:412
  16.6 0.9 %collective-permute-start.10 = (bf16[1,16,32,256]{3,2,1,0:T(8,128)(2,1)S(1)}, bf16[1,16,32,256]{3,2,1,0:T(8,128)(2,1)S(1)}, u32[]{:S(2)}, u32[]{:S(2)}) collective-permute-start(bf16[1,16,32,256]{3,2,1,0:T(8,128)(2,1)S(1)} %get-tuple-element.32), channel_id=1, source_target_pairs={{0,8},{4,12},{8,0},{12,4},{1,9},{5,13},{9,1},{13,5},{2,10},{6,14},... | collective-permute-start | bytes 786440 | tf_op jit(solution)/shard_map/ppermute | solution.py:412
  17.5 0.0 copy-done.3
  17.5 0.0 copy-done.4
  17.5 0.0 copy-done.5
  17.6 0.0 copy-done.6
  17.6 0.0 copy-done.7
  17.6 3.5 %shard_map.93 = (bf16[128,256]{1,0:T(8,128)(2,1)S(1)}, f32[32,128,256]{2,1,0:T(8,128)S(1)}) custom-call(s32[2,256]{1,0:T(2,128)S(1)} %bitcast.6, f32[400,400]{1,0:T(8,128)S(1)} %copy-done.3, f32[4,1,32]{2,1,0:T(1,128)S(1)} %copy-done.5, s32[2]{0:T(128)S(1)} %pad_add_fusion.place_ref, f32[32]{0:T(128)S(1)} %copy-done.7, f32[1,256]{1,0:T(1,128)S(1)} %bitcast.7), custom_call_target="tpu_custom_call" | custom-call | flops 491520000 | bytes 640000 | tf_op jit(solution)/shard_map/pallas_call | solution.py:207
  21.1 12.1 %collective-permute-done.5.refs_3_ = bf16[1,16,32,256]{3,2,1,0:T(8,128)(2,1)S(1)} collective-permute-done((bf16[1,16,32,256]{3,2,1,0:T(8,128)(2,1)S(1)}, bf16[1,16,32,256]{3,2,1,0:T(8,128)(2,1)S(1)}, u32[]{:S(2)}, u32[]{:S(2)}) %collective-permute-start.5) | collective-permute-done | bytes 262176 | tf_op jit(solution)/shard_map/ppermute | solution.py:412
  33.2 2.7 %collective-permute-start.11 = (bf16[1,16,32,256]{3,2,1,0:T(8,128)(2,1)S(1)}, bf16[1,16,32,256]{3,2,1,0:T(8,128)(2,1)S(1)}, u32[]{:S(2)}, u32[]{:S(2)}) collective-permute-start(bf16[1,16,32,256]{3,2,1,0:T(8,128)(2,1)S(1)} %get-tuple-element.34), channel_id=1, source_target_pairs={{0,12},{4,8},{8,4},{12,0},{1,13},{5,9},{9,5},{13,1},{2,14},{6,10},... | collective-permute-start | bytes 786440 | tf_op jit(solution)/shard_map/ppermute | solution.py:412
  35.8 0.0 collective-permute-start.6
  35.9 16.1 %collective-permute-done.4.refs_2_ = bf16[1,16,32,256]{3,2,1,0:T(8,128)(2,1)S(1)} collective-permute-done((bf16[1,16,32,256]{3,2,1,0:T(8,128)(2,1)S(1)}, bf16[1,16,32,256]{3,2,1,0:T(8,128)(2,1)S(1)}, u32[]{:S(2)}, u32[]{:S(2)}) %collective-permute-start.4) | collective-permute-done | bytes 262176 | tf_op jit(solution)/shard_map/ppermute | solution.py:412
  51.9 0.0 collective-permute-start.9
  51.9 0.0 collective-permute-done.3.refs_1_.refs_2_
  51.9 0.5 collective-permute-start.8
  52.4 5.1 %collective-permute-done.10.refs_3_ = bf16[1,16,32,256]{3,2,1,0:T(8,128)(2,1)S(1)} collective-permute-done((bf16[1,16,32,256]{3,2,1,0:T(8,128)(2,1)S(1)}, bf16[1,16,32,256]{3,2,1,0:T(8,128)(2,1)S(1)}, u32[]{:S(2)}, u32[]{:S(2)}) %collective-permute-start.10) | collective-permute-done | bytes 262176 | tf_op jit(solution)/shard_map/ppermute | solution.py:412
  57.5 0.0 collective-permute-start.7
  57.6 0.0 collective-permute-done.8.refs_6_
  57.6 0.5 collective-permute-start.12
  58.1 0.0 collective-permute-done.11.refs_4_
  58.1 0.0 collective-permute-done.9.refs_7_
  58.1 0.1 collective-permute-start.13
  58.1 0.0 collective-permute-done.6.refs_4_.refs_5_
  58.2 1.3 %collective-permute-done.7.refs_5_.refs_6_ = bf16[2,16,32,256]{3,2,1,0:T(8,128)(2,1)S(1)} collective-permute-done((bf16[2,16,32,256]{3,2,1,0:T(8,128)(2,1)S(1)}, bf16[2,16,32,256]{3,2,1,0:T(8,128)(2,1)S(1)}, u32[]{:S(2)}, u32[]{:S(2)}) %collective-permute-start.7) | collective-permute-done | bytes 524320 | tf_op jit(solution)/shard_map/ppermute | solution.py:415
  59.5 0.9 %shard_map.94.refs_0_ = bf16[8,16,16,256]{3,2,1,0:T(8,128)(2,1)S(1)} custom-call(bf16[256,256]{1,0:T(8,128)(2,1)S(1)} %get-tuple-element.21.refs_5_.swap_ref, bf16[128,256]{1,0:T(8,128)(2,1)S(1)} %get-tuple-element.25.w_ref, f32[32,128,256]{2,1,0:T(8,128)S(1)} %get-tuple-element.26.inverse_ref, ...), custom_call_target="tpu_custom_call" | custom-call | tf_op jit(solution)/shard_map/pallas_call | solution.py:381
  60.4 0.0 collective-permute-done.12.refs_7_
  60.4 0.0 collective-permute-done.13.refs_8_
  60.4 2.5 %shard_map.95 = bf16[4,1,32,32,256]{4,3,2,1,0:T(8,128)(2,1)} custom-call(bf16[256,256]{1,0:T(8,128)(2,1)S(1)} %get-tuple-element.21.refs_5_.swap_ref, bf16[128,256]{1,0:T(8,128)(2,1)S(1)} %get-tuple-element.25.w_ref, f32[32,128,256]{2,1,0:T(8,128)S(1)} %get-tuple-element.26.inverse_ref, s32[2]{0:T(128)S(1)} %pad_add_fusion.place_ref, ...), custom_call_target="tpu_custom_call" | custom-call | tf_op jit(solution)/shard_map/pallas_call | solution.py:381
  (2 shorter events, 0.0 us)
Async XLA Ops:
  0.0 11.0 %copy-start = (bf16[1,128,128]{2,1,0:T(8,128)(2,1)S(1)}, bf16[1,128,128]{2,1,0:T(8,128)(2,1)}, u32[]{:S(2)}) copy-start(bf16[1,128,128]{2,1,0:T(8,128)(2,1)} %refs_0_.1) | copy-start | bytes 98308
  0.0 11.0 %copy-start.1 = (s32[1,1,32,2]{2,3,1,0:T(2,128)S(1)}, s32[1,1,32,2]{2,3,1,0:T(2,128)}, u32[]{:S(2)}) copy-start(s32[1,1,32,2]{2,3,1,0:T(2,128)} %param.12) | copy-start | bytes 772
  0.0 11.0 %copy-start.2 = (s32[1,1,32]{2,1,0:T(1,128)S(1)}, s32[1,1,32]{2,1,0:T(1,128)}, u32[]{:S(2)}) copy-start(s32[1,1,32]{2,1,0:T(1,128)} %tile_of_ref.1) | copy-start | bytes 388
  0.0 7.4 %collective-permute-start.1 = (bf16[1,128,128]{2,1,0:T(8,128)(2,1)}, bf16[1,128,128]{2,1,0:T(8,128)(2,1)S(1)}, u32[]{:S(2)}, u32[]{:S(2)}) collective-permute-start(bf16[1,128,128]{2,1,0:T(8,128)(2,1)} %refs_0_.1), channel_id=1, source_target_pairs={{0,4},{4,0},{8,12},{12,8},{1,5},{5,1},{9,13},{13,9},{2,6},{6,2},{1... | collective-permute-start | bytes 98312 | tf_op jit(solution)/shard_map/ppermute | solution.py:412
  3.1 6.4 %collective-permute-start = (bf16[1,128,128]{2,1,0:T(8,128)(2,1)}, bf16[1,128,128]{2,1,0:T(8,128)(2,1)S(1)}, u32[]{:S(2)}, u32[]{:S(2)}) collective-permute-start(bf16[1,128,128]{2,1,0:T(8,128)(2,1)} %refs_0_.1), channel_id=1, source_target_pairs={{0,12},{4,8},{8,4},{12,0},{1,13},{5,9},{9,5},{13,1},{2,14},{6,10},... | collective-permute-start | bytes 98312 | tf_op jit(solution)/shard_map/ppermute | solution.py:412
  5.6 5.4 %collective-permute-start.2 = (bf16[1,128,128]{2,1,0:T(8,128)(2,1)}, bf16[1,128,128]{2,1,0:T(8,128)(2,1)S(1)}, u32[]{:S(2)}, u32[]{:S(2)}) collective-permute-start(bf16[1,128,128]{2,1,0:T(8,128)(2,1)} %refs_0_.1), channel_id=1, source_target_pairs={{0,8},{4,12},{8,0},{12,4},{1,9},{5,13},{9,1},{13,5},{2,10},{6,14},... | collective-permute-start | bytes 98312 | tf_op jit(solution)/shard_map/ppermute | solution.py:412
  5.8 11.8 %copy-start.3 = (f32[400,400]{1,0:T(8,128)S(1)}, f32[400,400]{1,0:T(8,128)}, u32[]{:S(2)}) copy-start(f32[400,400]{1,0:T(8,128)} %coupling_ref.1) | copy-start | bytes 1920004
  5.8 11.8 %copy-start.4 = (s32[256,2]{0,1:T(2,128)S(1)}, s32[256,2]{0,1:T(2,128)}, u32[]{:S(2)}) copy-start(s32[256,2]{0,1:T(2,128)} %param.13) | copy-start | bytes 6148
  5.8 11.8 %copy-start.5 = (f32[4,1,32]{2,1,0:T(1,128)S(1)}, f32[4,1,32]{2,1,0:T(1,128)}, u32[]{:S(2)}) copy-start(f32[4,1,32]{2,1,0:T(1,128)} %gap_ref.1) | copy-start | bytes 1540
  5.8 11.8 %copy-start.6 = (f32[256]{0:T(256)S(1)}, f32[256]{0:T(256)}, u32[]{:S(2)}) copy-start(f32[256]{0:T(256)} %param.17) | copy-start | bytes 3076
  5.8 11.8 %copy-start.7 = (f32[32]{0:T(128)S(1)}, f32[32]{0:T(128)}, u32[]{:S(2)}) copy-start(f32[32]{0:T(128)} %row_ref.1) | copy-start | bytes 388
  13.1 38.9 %collective-permute-start.3 = (bf16[2,16,32,256]{3,2,1,0:T(8,128)(2,1)S(1)}, bf16[2,16,32,256]{3,2,1,0:T(8,128)(2,1)S(1)}, u32[]{:S(2)}, u32[]{:S(2)}) collective-permute-start(bf16[2,16,32,256]{3,2,1,0:T(8,128)(2,1)S(1)} %get-tuple-element.28), channel_id=1, source_target_pairs={{0,4},{4,0},{8,12},{12,8},{1,5},{5,1},{9,13},{13,9},{2,6},{6,2},{1... | collective-permute-start | bytes 1572872 | tf_op jit(solution)/shard_map/ppermute | solution.py:412
  13.6 19.6 %collective-permute-start.5 = (bf16[1,16,32,256]{3,2,1,0:T(8,128)(2,1)S(1)}, bf16[1,16,32,256]{3,2,1,0:T(8,128)(2,1)S(1)}, u32[]{:S(2)}, u32[]{:S(2)}) collective-permute-start(bf16[1,16,32,256]{3,2,1,0:T(8,128)(2,1)S(1)} %get-tuple-element.23), channel_id=1, source_target_pairs={{0,12},{4,8},{8,4},{12,0},{1,13},{5,9},{9,5},{13,1},{2,14},{6,10},... | collective-permute-start | bytes 786440 | tf_op jit(solution)/shard_map/ppermute | solution.py:412
  14.6 37.3 %collective-permute-start.4 = (bf16[1,16,32,256]{3,2,1,0:T(8,128)(2,1)S(1)}, bf16[1,16,32,256]{3,2,1,0:T(8,128)(2,1)S(1)}, u32[]{:S(2)}, u32[]{:S(2)}) collective-permute-start(bf16[1,16,32,256]{3,2,1,0:T(8,128)(2,1)S(1)} %get-tuple-element.29), channel_id=1, source_target_pairs={{0,8},{4,12},{8,0},{12,4},{1,9},{5,13},{9,1},{13,5},{2,10},{6,14},... | collective-permute-start | bytes 786440 | tf_op jit(solution)/shard_map/ppermute | solution.py:412
  16.6 40.9 %collective-permute-start.10 = (bf16[1,16,32,256]{3,2,1,0:T(8,128)(2,1)S(1)}, bf16[1,16,32,256]{3,2,1,0:T(8,128)(2,1)S(1)}, u32[]{:S(2)}, u32[]{:S(2)}) collective-permute-start(bf16[1,16,32,256]{3,2,1,0:T(8,128)(2,1)S(1)} %get-tuple-element.32), channel_id=1, source_target_pairs={{0,8},{4,12},{8,0},{12,4},{1,9},{5,13},{9,1},{13,5},{2,10},{6,14},... | collective-permute-start | bytes 786440 | tf_op jit(solution)/shard_map/ppermute | solution.py:412
  33.2 24.9 %collective-permute-start.11 = (bf16[1,16,32,256]{3,2,1,0:T(8,128)(2,1)S(1)}, bf16[1,16,32,256]{3,2,1,0:T(8,128)(2,1)S(1)}, u32[]{:S(2)}, u32[]{:S(2)}) collective-permute-start(bf16[1,16,32,256]{3,2,1,0:T(8,128)(2,1)S(1)} %get-tuple-element.34), channel_id=1, source_target_pairs={{0,12},{4,8},{8,4},{12,0},{1,13},{5,9},{9,5},{13,1},{2,14},{6,10},... | collective-permute-start | bytes 786440 | tf_op jit(solution)/shard_map/ppermute | solution.py:412
  35.8 22.3 %collective-permute-start.6 = (bf16[2,16,32,256]{3,2,1,0:T(8,128)(2,1)S(1)}, bf16[2,16,32,256]{3,2,1,0:T(8,128)(2,1)S(1)}, u32[]{:S(2)}, u32[]{:S(2)}) collective-permute-start(bf16[2,16,32,256]{3,2,1,0:T(8,128)(2,1)S(1)} %get-tuple-element.30.refs_0_.refs_1_), channel_id=1, source_target_pairs={{0,1},{1,0},{2,3},{3,2},{4,5},{5,4},{6,7},{7,6},{8,9},{9,8},{10,11... | collective-permute-start | bytes 1572872 | tf_op jit(solution)/shard_map/ppermute | solution.py:415
  51.9 6.1 %collective-permute-start.9 = (bf16[1,16,32,256]{3,2,1,0:T(8,128)(2,1)S(1)}, bf16[1,16,32,256]{3,2,1,0:T(8,128)(2,1)S(1)}, u32[]{:S(2)}, u32[]{:S(2)}) collective-permute-start(bf16[1,16,32,256]{3,2,1,0:T(8,128)(2,1)S(1)} %collective-permute-done.5.refs_3_), channel_id=1, source_target_pairs={{0,1},{1,0},{2,3},{3,2},{4,5},{5,4},{6,7},{7,6},{8,9},{9,8},{10,11... | collective-permute-start | bytes 786440 | tf_op jit(solution)/shard_map/ppermute | solution.py:415
  51.9 5.6 %collective-permute-start.8 = (bf16[1,16,32,256]{3,2,1,0:T(8,128)(2,1)S(1)}, bf16[1,16,32,256]{3,2,1,0:T(8,128)(2,1)S(1)}, u32[]{:S(2)}, u32[]{:S(2)}) collective-permute-start(bf16[1,16,32,256]{3,2,1,0:T(8,128)(2,1)S(1)} %collective-permute-done.4.refs_2_), channel_id=1, source_target_pairs={{0,1},{1,0},{2,3},{3,2},{4,5},{5,4},{6,7},{7,6},{8,9},{9,8},{10,11... | collective-permute-start | bytes 786440 | tf_op jit(solution)/shard_map/ppermute | solution.py:415
  57.5 1.9 %collective-permute-start.7 = (bf16[2,16,32,256]{3,2,1,0:T(8,128)(2,1)S(1)}, bf16[2,16,32,256]{3,2,1,0:T(8,128)(2,1)S(1)}, u32[]{:S(2)}, u32[]{:S(2)}) collective-permute-start(bf16[2,16,32,256]{3,2,1,0:T(8,128)(2,1)S(1)} %collective-permute-done.3.refs_1_.refs_2_), channel_id=1, source_target_pairs={{0,1},{1,0},{2,3},{3,2},{4,5},{5,4},{6,7},{7,6},{8,9},{9,8},{10,11... | collective-permute-start | bytes 1572872 | tf_op jit(solution)/shard_map/ppermute | solution.py:415
  57.6 2.8 %collective-permute-start.12 = (bf16[1,16,32,256]{3,2,1,0:T(8,128)(2,1)S(1)}, bf16[1,16,32,256]{3,2,1,0:T(8,128)(2,1)S(1)}, u32[]{:S(2)}, u32[]{:S(2)}) collective-permute-start(bf16[1,16,32,256]{3,2,1,0:T(8,128)(2,1)S(1)} %collective-permute-done.10.refs_3_), channel_id=1, source_target_pairs={{0,1},{1,0},{2,3},{3,2},{4,5},{5,4},{6,7},{7,6},{8,9},{9,8},{10,11... | collective-permute-start | bytes 786440 | tf_op jit(solution)/shard_map/ppermute | solution.py:415
  58.1 2.3 %collective-permute-start.13 = (bf16[1,16,32,256]{3,2,1,0:T(8,128)(2,1)S(1)}, bf16[1,16,32,256]{3,2,1,0:T(8,128)(2,1)S(1)}, u32[]{:S(2)}, u32[]{:S(2)}) collective-permute-start(bf16[1,16,32,256]{3,2,1,0:T(8,128)(2,1)S(1)} %collective-permute-done.11.refs_4_), channel_id=1, source_target_pairs={{0,1},{1,0},{2,3},{3,2},{4,5},{5,4},{6,7},{7,6},{8,9},{9,8},{10,11... | collective-permute-start | bytes 786440 | tf_op jit(solution)/shard_map/ppermute | solution.py:415

commit v10 on v9

--- a/solution.py
+++ b/solution.py
@@ -221,7 +221,7 @@
 
 
 def dress_kernel(owners, rows, groups, place_ref, tile_of_ref, mask_ref, *refs):
-    tile_refs, lam_ref = (refs[0], *refs[2:owners], refs[1]), refs[owners]
+    tile_refs, lam_ref = (refs[0], refs[owners - 1], *refs[1 : owners - 1]), refs[owners]
     swap_ref = refs[owners + 1]
     out_refs = refs[owners + 2 : -2]
     tiles, stage = refs[-2:]
@@ -292,8 +292,8 @@
         in_smem(tile_of),
         in_smem(jnp.swapaxes(tile_mask, 2, 3)),
         tiles[0],
-        tiles[-1],
-        *tiles[1:-1],
+        *tiles[2:],
+        tiles[1],
         lambda_amps,
         swap,
     )

time: 63 us -> 62.1 us (0.986)
  waiting for transfers between devices: 38.1 us -> 37.4 us
    ppermute x8, waiting for transfers between devices: 36.8 us -> 36.1 us  [to_owner(): return lax.ppermute(value, 'pair', [(o, o ^ k) for o in range(owners)])]
  transfers between devices with their start and end apart: 14 -> 14, of which waited for: 6 -> 5; matrix products, arithmetic and copies ran while one was open for 0% -> 0% of each run, Pallas kernels for 10% -> 10%
where the time goes in v10:
time: 62.1 us; the launch traced here: 62 us
  waiting for transfers between devices  37.4 us (60%)
  starting transfers between devices  13.7 us (22%)
  Pallas kernels  10.6 us (17%)
    ppermute x8, waiting for transfers between devices, to_owner(): return lax.ppermute(value, 'pair', [(o, o ^ k) for o in range(owners)])  36.1 us
    ppermute x8, starting transfers between devices, to_owner(): return lax.ppermute(value, 'pair', [(o, o ^ k) for o in range(owners)])  12.6 us
    pallas_call x1, Pallas kernels, make_weights(): pl.pallas_call(weights_kernel, in_specs=[vmem, vmem, vmem, smem, smem, vm...  3.52 us
    pallas_call x2, Pallas kernels, finish(): pl.pallas_call(kernel, in_specs=in_specs + [vmem] * len(pieces), out_spec...  3.35 us
    pallas_call x1, Pallas kernels, dress(): pl.pallas_call(functools.partial(dress_kernel, owners, rows, groups), in_...  2.11 us
    pallas_call x1, Pallas kernels, hold(): pl.pallas_call(hold_kernel, in_specs=[anywhere], out_specs=[anywhere, pl....  1.64 us
    ppermute x6, waiting for transfers between devices, to_sibling(): return lax.ppermute(value, 'sub', [(0, 1), (1, 0)])  1.32 us
  transfers between devices with their start and end apart: 14, of which 5 were waited for; matrix products, arithmetic and copies ran while one was open for 0% of the time, Pallas kernels for 10%

profile of v10, /device:TPU:0, one launch (start us, length us, event | category | flops | bytes accessed | tf_op | source)
XLA Modules:
  0.0 62.0 jit_solution(1032136861697858907)
XLA Ops:
  0.0 0.0 copy-start
  0.0 0.0 copy-start.1
  0.0 0.0 copy-start.2
  0.0 5.1 %collective-permute-start.1 = (bf16[1,128,128]{2,1,0:T(8,128)(2,1)}, bf16[1,128,128]{2,1,0:T(8,128)(2,1)S(1)}, u32[]{:S(2)}, u32[]{:S(2)}) collective-permute-start(bf16[1,128,128]{2,1,0:T(8,128)(2,1)} %refs_0_.1), channel_id=1, source_target_pairs={{0,12},{4,8},{8,4},{12,0},{1,13},{5,9},{9,5},{13,1},{2,14},{6,10},... | collective-permute-start | bytes 98312 | tf_op jit(solution)/shard_map/ppermute | solution.py:412
  5.1 0.0 collective-permute-start
  5.1 0.6 %collective-permute-start.2 = (bf16[1,128,128]{2,1,0:T(8,128)(2,1)}, bf16[1,128,128]{2,1,0:T(8,128)(2,1)S(1)}, u32[]{:S(2)}, u32[]{:S(2)}) collective-permute-start(bf16[1,128,128]{2,1,0:T(8,128)(2,1)} %refs_0_.1), channel_id=1, source_target_pairs={{0,4},{4,0},{8,12},{12,8},{1,5},{5,1},{9,13},{13,9},{2,6},{6,2},{1... | collective-permute-start | bytes 98312 | tf_op jit(solution)/shard_map/ppermute | solution.py:412
  5.8 0.1 pad_add_fusion.place_ref
  5.8 0.0 copy-start.3
  5.8 0.0 copy-start.4
  5.9 0.0 copy-start.7
  5.9 1.6 %shard_map.91 = (bf16[1,1,32,128,256]{4,3,2,1,0:T(8,128)(2,1)S(1)}, bf16[256,256]{1,0:T(8,128)(2,1)S(1)}) custom-call(bf16[1,1,32,128,256]{4,3,2,1,0:T(8,128)(2,1)} %lam_ref.1), custom_call_target="tpu_custom_call" | custom-call | bytes 4194304 | tf_op jit(solution)/shard_map/pallas_call | solution.py:154
  7.5 0.0 collective-permute-done.1.refs_2_
  7.5 2.6 %collective-permute-done.refs_1_ = bf16[1,128,128]{2,1,0:T(8,128)(2,1)S(1)} collective-permute-done((bf16[1,128,128]{2,1,0:T(8,128)(2,1)}, bf16[1,128,128]{2,1,0:T(8,128)(2,1)S(1)}, u32[]{:S(2)}, u32[]{:S(2)}) %collective-permute-start) | collective-permute-done | bytes 32800 | tf_op jit(solution)/shard_map/ppermute | solution.py:412
  10.1 0.0 collective-permute-done.2.refs_3_
  10.2 0.0 copy-done
  10.2 0.0 copy-done.1
  10.2 0.0 copy-done.2
  10.2 2.1 %shard_map.92 = (bf16[1,16,32,256]{3,2,1,0:T(8,128)(2,1)S(1)}, bf16[1,16,32,256]{3,2,1,0:T(8,128)(2,1)S(1)}, bf16[1,16,32,256]{3,2,1,0:T(8,128)(2,1)S(1)}, bf16[...) custom-call(s32[2]{0:T(128)S(1)} %pad_add_fusion.place_ref, ...), custom_call_target="tpu_custom_call" | custom-call | flops 268435456 | bytes 3145728 | tf_op jit(solution)/shard_map/pallas_call | solution.py:272
  12.3 0.1 collective-permute-start.3
  12.4 3.5 %collective-permute-start.5 = (bf16[1,16,32,256]{3,2,1,0:T(8,128)(2,1)S(1)}, bf16[1,16,32,256]{3,2,1,0:T(8,128)(2,1)S(1)}, u32[]{:S(2)}, u32[]{:S(2)}) collective-permute-start(bf16[1,16,32,256]{3,2,1,0:T(8,128)(2,1)S(1)} %get-tuple-element.23), channel_id=1, source_target_pairs={{0,12},{4,8},{8,4},{12,0},{1,13},{5,9},{9,5},{13,1},{2,14},{6,10},... | collective-permute-start | bytes 786440 | tf_op jit(solution)/shard_map/ppermute | solution.py:412
  15.8 0.0 collective-permute-start.4
  15.8 2.9 %collective-permute-start.10 = (bf16[1,16,32,256]{3,2,1,0:T(8,128)(2,1)S(1)}, bf16[1,16,32,256]{3,2,1,0:T(8,128)(2,1)S(1)}, u32[]{:S(2)}, u32[]{:S(2)}) collective-permute-start(bf16[1,16,32,256]{3,2,1,0:T(8,128)(2,1)S(1)} %get-tuple-element.32), channel_id=1, source_target_pairs={{0,8},{4,12},{8,0},{12,4},{1,9},{5,13},{9,1},{13,5},{2,10},{6,14},... | collective-permute-start | bytes 786440 | tf_op jit(solution)/shard_map/ppermute | solution.py:412
  18.7 0.0 copy-done.3
  18.7 0.0 copy-done.4
  18.8 0.0 copy-done.5
  18.8 0.0 copy-done.6
  18.8 0.0 copy-done.7
  18.8 3.5 %shard_map.93 = (bf16[128,256]{1,0:T(8,128)(2,1)S(1)}, f32[32,128,256]{2,1,0:T(8,128)S(1)}) custom-call(s32[2,256]{1,0:T(2,128)S(1)} %bitcast.6, f32[400,400]{1,0:T(8,128)S(1)} %copy-done.3, f32[4,1,32]{2,1,0:T(1,128)S(1)} %copy-done.5, s32[2]{0:T(128)S(1)} %pad_add_fusion.place_ref, f32[32]{0:T(128)S(1)} %copy-done.7, f32[1,256]{1,0:T(1,128)S(1)} %bitcast.7), custom_call_target="tpu_custom_call" | custom-call | flops 491520000 | bytes 640000 | tf_op jit(solution)/shard_map/pallas_call | solution.py:207
  22.3 12.1 %collective-permute-done.5.refs_3_ = bf16[1,16,32,256]{3,2,1,0:T(8,128)(2,1)S(1)} collective-permute-done((bf16[1,16,32,256]{3,2,1,0:T(8,128)(2,1)S(1)}, bf16[1,16,32,256]{3,2,1,0:T(8,128)(2,1)S(1)}, u32[]{:S(2)}, u32[]{:S(2)}) %collective-permute-start.5) | collective-permute-done | bytes 262176 | tf_op jit(solution)/shard_map/ppermute | solution.py:412
  34.4 0.4 collective-permute-start.11
  34.7 0.0 collective-permute-start.6
  34.7 16.4 %collective-permute-done.4.refs_2_ = bf16[1,16,32,256]{3,2,1,0:T(8,128)(2,1)S(1)} collective-permute-done((bf16[1,16,32,256]{3,2,1,0:T(8,128)(2,1)S(1)}, bf16[1,16,32,256]{3,2,1,0:T(8,128)(2,1)S(1)}, u32[]{:S(2)}, u32[]{:S(2)}) %collective-permute-start.4) | collective-permute-done | bytes 262176 | tf_op jit(solution)/shard_map/ppermute | solution.py:412
  51.1 0.0 collective-permute-start.9
  51.1 0.0 collective-permute-done.3.refs_1_.refs_2_
  51.2 0.5 collective-permute-start.8
  51.7 5.0 %collective-permute-done.10.refs_3_ = bf16[1,16,32,256]{3,2,1,0:T(8,128)(2,1)S(1)} collective-permute-done((bf16[1,16,32,256]{3,2,1,0:T(8,128)(2,1)S(1)}, bf16[1,16,32,256]{3,2,1,0:T(8,128)(2,1)S(1)}, u32[]{:S(2)}, u32[]{:S(2)}) %collective-permute-start.10) | collective-permute-done | bytes 262176 | tf_op jit(solution)/shard_map/ppermute | solution.py:412
  56.7 0.0 collective-permute-start.7
  56.7 0.0 collective-permute-done.8.refs_6_
  56.7 0.5 collective-permute-start.12
  57.2 0.0 collective-permute-done.11.refs_4_
  57.2 0.0 collective-permute-done.9.refs_7_
  57.2 0.1 collective-permute-start.13
  57.3 0.0 collective-permute-done.6.refs_4_.refs_5_
  57.3 1.3 %collective-permute-done.7.refs_5_.refs_6_ = bf16[2,16,32,256]{3,2,1,0:T(8,128)(2,1)S(1)} collective-permute-done((bf16[2,16,32,256]{3,2,1,0:T(8,128)(2,1)S(1)}, bf16[2,16,32,256]{3,2,1,0:T(8,128)(2,1)S(1)}, u32[]{:S(2)}, u32[]{:S(2)}) %collective-permute-start.7) | collective-permute-done | bytes 524320 | tf_op jit(solution)/shard_map/ppermute | solution.py:415
  58.6 0.9 %shard_map.94.refs_0_ = bf16[8,16,16,256]{3,2,1,0:T(8,128)(2,1)S(1)} custom-call(bf16[256,256]{1,0:T(8,128)(2,1)S(1)} %get-tuple-element.21.refs_5_.swap_ref, bf16[128,256]{1,0:T(8,128)(2,1)S(1)} %get-tuple-element.25.w_ref, f32[32,128,256]{2,1,0:T(8,128)S(1)} %get-tuple-element.26.inverse_ref, ...), custom_call_target="tpu_custom_call" | custom-call | tf_op jit(solution)/shard_map/pallas_call | solution.py:381
  59.5 0.0 collective-permute-done.12.refs_7_
  59.5 0.0 collective-permute-done.13.refs_8_
  59.5 2.5 %shard_map.95 = bf16[4,1,32,32,256]{4,3,2,1,0:T(8,128)(2,1)} custom-call(bf16[256,256]{1,0:T(8,128)(2,1)S(1)} %get-tuple-element.21.refs_5_.swap_ref, bf16[128,256]{1,0:T(8,128)(2,1)S(1)} %get-tuple-element.25.w_ref, f32[32,128,256]{2,1,0:T(8,128)S(1)} %get-tuple-element.26.inverse_ref, s32[2]{0:T(128)S(1)} %pad_add_fusion.place_ref, ...), custom_call_target="tpu_custom_call" | custom-call | tf_op jit(solution)/shard_map/pallas_call | solution.py:381
  (2 shorter events, 0.0 us)
Async XLA Ops:
  0.0 10.2 %copy-start = (bf16[1,128,128]{2,1,0:T(8,128)(2,1)S(1)}, bf16[1,128,128]{2,1,0:T(8,128)(2,1)}, u32[]{:S(2)}) copy-start(bf16[1,128,128]{2,1,0:T(8,128)(2,1)} %refs_0_.1) | copy-start | bytes 98308
  0.0 10.2 %copy-start.1 = (s32[1,1,32,2]{2,3,1,0:T(2,128)S(1)}, s32[1,1,32,2]{2,3,1,0:T(2,128)}, u32[]{:S(2)}) copy-start(s32[1,1,32,2]{2,3,1,0:T(2,128)} %param.12) | copy-start | bytes 772
  0.0 10.2 %copy-start.2 = (s32[1,1,32]{2,1,0:T(1,128)S(1)}, s32[1,1,32]{2,1,0:T(1,128)}, u32[]{:S(2)}) copy-start(s32[1,1,32]{2,1,0:T(1,128)} %tile_of_ref.1) | copy-start | bytes 388
  0.0 7.5 %collective-permute-start.1 = (bf16[1,128,128]{2,1,0:T(8,128)(2,1)}, bf16[1,128,128]{2,1,0:T(8,128)(2,1)S(1)}, u32[]{:S(2)}, u32[]{:S(2)}) collective-permute-start(bf16[1,128,128]{2,1,0:T(8,128)(2,1)} %refs_0_.1), channel_id=1, source_target_pairs={{0,12},{4,8},{8,4},{12,0},{1,13},{5,9},{9,5},{13,1},{2,14},{6,10},... | collective-permute-start | bytes 98312 | tf_op jit(solution)/shard_map/ppermute | solution.py:412
  5.1 5.0 %collective-permute-start = (bf16[1,128,128]{2,1,0:T(8,128)(2,1)}, bf16[1,128,128]{2,1,0:T(8,128)(2,1)S(1)}, u32[]{:S(2)}, u32[]{:S(2)}) collective-permute-start(bf16[1,128,128]{2,1,0:T(8,128)(2,1)} %refs_0_.1), channel_id=1, source_target_pairs={{0,8},{4,12},{8,0},{12,4},{1,9},{5,13},{9,1},{13,5},{2,10},{6,14},... | collective-permute-start | bytes 98312 | tf_op jit(solution)/shard_map/ppermute | solution.py:412
  5.1 5.0 %collective-permute-start.2 = (bf16[1,128,128]{2,1,0:T(8,128)(2,1)}, bf16[1,128,128]{2,1,0:T(8,128)(2,1)S(1)}, u32[]{:S(2)}, u32[]{:S(2)}) collective-permute-start(bf16[1,128,128]{2,1,0:T(8,128)(2,1)} %refs_0_.1), channel_id=1, source_target_pairs={{0,4},{4,0},{8,12},{12,8},{1,5},{5,1},{9,13},{13,9},{2,6},{6,2},{1... | collective-permute-start | bytes 98312 | tf_op jit(solution)/shard_map/ppermute | solution.py:412
  5.8 12.9 %copy-start.3 = (f32[400,400]{1,0:T(8,128)S(1)}, f32[400,400]{1,0:T(8,128)}, u32[]{:S(2)}) copy-start(f32[400,400]{1,0:T(8,128)} %coupling_ref.1) | copy-start | bytes 1920004
  5.8 12.9 %copy-start.4 = (s32[256,2]{0,1:T(2,128)S(1)}, s32[256,2]{0,1:T(2,128)}, u32[]{:S(2)}) copy-start(s32[256,2]{0,1:T(2,128)} %param.13) | copy-start | bytes 6148
  5.8 12.9 %copy-start.5 = (f32[4,1,32]{2,1,0:T(1,128)S(1)}, f32[4,1,32]{2,1,0:T(1,128)}, u32[]{:S(2)}) copy-start(f32[4,1,32]{2,1,0:T(1,128)} %gap_ref.1) | copy-start | bytes 1540
  5.8 12.9 %copy-start.6 = (f32[256]{0:T(256)S(1)}, f32[256]{0:T(256)}, u32[]{:S(2)}) copy-start(f32[256]{0:T(256)} %param.17) | copy-start | bytes 3076
  5.9 12.9 %copy-start.7 = (f32[32]{0:T(128)S(1)}, f32[32]{0:T(128)}, u32[]{:S(2)}) copy-start(f32[32]{0:T(128)} %row_ref.1) | copy-start | bytes 388
  12.3 38.9 %collective-permute-start.3 = (bf16[2,16,32,256]{3,2,1,0:T(8,128)(2,1)S(1)}, bf16[2,16,32,256]{3,2,1,0:T(8,128)(2,1)S(1)}, u32[]{:S(2)}, u32[]{:S(2)}) collective-permute-start(bf16[2,16,32,256]{3,2,1,0:T(8,128)(2,1)S(1)} %get-tuple-element.28), channel_id=1, source_target_pairs={{0,4},{4,0},{8,12},{12,8},{1,5},{5,1},{9,13},{13,9},{2,6},{6,2},{1... | collective-permute-start | bytes 1572872 | tf_op jit(solution)/shard_map/ppermute | solution.py:412
  12.4 22.0 %collective-permute-start.5 = (bf16[1,16,32,256]{3,2,1,0:T(8,128)(2,1)S(1)}, bf16[1,16,32,256]{3,2,1,0:T(8,128)(2,1)S(1)}, u32[]{:S(2)}, u32[]{:S(2)}) collective-permute-start(bf16[1,16,32,256]{3,2,1,0:T(8,128)(2,1)S(1)} %get-tuple-element.23), channel_id=1, source_target_pairs={{0,12},{4,8},{8,4},{12,0},{1,13},{5,9},{9,5},{13,1},{2,14},{6,10},... | collective-permute-start | bytes 786440 | tf_op jit(solution)/shard_map/ppermute | solution.py:412
  15.8 35.3 %collective-permute-start.4 = (bf16[1,16,32,256]{3,2,1,0:T(8,128)(2,1)S(1)}, bf16[1,16,32,256]{3,2,1,0:T(8,128)(2,1)S(1)}, u32[]{:S(2)}, u32[]{:S(2)}) collective-permute-start(bf16[1,16,32,256]{3,2,1,0:T(8,128)(2,1)S(1)} %get-tuple-element.29), channel_id=1, source_target_pairs={{0,8},{4,12},{8,0},{12,4},{1,9},{5,13},{9,1},{13,5},{2,10},{6,14},... | collective-permute-start | bytes 786440 | tf_op jit(solution)/shard_map/ppermute | solution.py:412
  15.8 40.8 %collective-permute-start.10 = (bf16[1,16,32,256]{3,2,1,0:T(8,128)(2,1)S(1)}, bf16[1,16,32,256]{3,2,1,0:T(8,128)(2,1)S(1)}, u32[]{:S(2)}, u32[]{:S(2)}) collective-permute-start(bf16[1,16,32,256]{3,2,1,0:T(8,128)(2,1)S(1)} %get-tuple-element.32), channel_id=1, source_target_pairs={{0,8},{4,12},{8,0},{12,4},{1,9},{5,13},{9,1},{13,5},{2,10},{6,14},... | collective-permute-start | bytes 786440 | tf_op jit(solution)/shard_map/ppermute | solution.py:412
  34.4 22.8 %collective-permute-start.11 = (bf16[1,16,32,256]{3,2,1,0:T(8,128)(2,1)S(1)}, bf16[1,16,32,256]{3,2,1,0:T(8,128)(2,1)S(1)}, u32[]{:S(2)}, u32[]{:S(2)}) collective-permute-start(bf16[1,16,32,256]{3,2,1,0:T(8,128)(2,1)S(1)} %get-tuple-element.34), channel_id=1, source_target_pairs={{0,12},{4,8},{8,4},{12,0},{1,13},{5,9},{9,5},{13,1},{2,14},{6,10},... | collective-permute-start | bytes 786440 | tf_op jit(solution)/shard_map/ppermute | solution.py:412
  34.7 22.5 %collective-permute-start.6 = (bf16[2,16,32,256]{3,2,1,0:T(8,128)(2,1)S(1)}, bf16[2,16,32,256]{3,2,1,0:T(8,128)(2,1)S(1)}, u32[]{:S(2)}, u32[]{:S(2)}) collective-permute-start(bf16[2,16,32,256]{3,2,1,0:T(8,128)(2,1)S(1)} %get-tuple-element.30.refs_0_.refs_1_), channel_id=1, source_target_pairs={{0,1},{1,0},{2,3},{3,2},{4,5},{5,4},{6,7},{7,6},{8,9},{9,8},{10,11... | collective-permute-start | bytes 1572872 | tf_op jit(solution)/shard_map/ppermute | solution.py:415
  51.1 6.0 %collective-permute-start.9 = (bf16[1,16,32,256]{3,2,1,0:T(8,128)(2,1)S(1)}, bf16[1,16,32,256]{3,2,1,0:T(8,128)(2,1)S(1)}, u32[]{:S(2)}, u32[]{:S(2)}) collective-permute-start(bf16[1,16,32,256]{3,2,1,0:T(8,128)(2,1)S(1)} %collective-permute-done.5.refs_3_), channel_id=1, source_target_pairs={{0,1},{1,0},{2,3},{3,2},{4,5},{5,4},{6,7},{7,6},{8,9},{9,8},{10,11... | collective-permute-start | bytes 786440 | tf_op jit(solution)/shard_map/ppermute | solution.py:415
  51.2 5.5 %collective-permute-start.8 = (bf16[1,16,32,256]{3,2,1,0:T(8,128)(2,1)S(1)}, bf16[1,16,32,256]{3,2,1,0:T(8,128)(2,1)S(1)}, u32[]{:S(2)}, u32[]{:S(2)}) collective-permute-start(bf16[1,16,32,256]{3,2,1,0:T(8,128)(2,1)S(1)} %collective-permute-done.4.refs_2_), channel_id=1, source_target_pairs={{0,1},{1,0},{2,3},{3,2},{4,5},{5,4},{6,7},{7,6},{8,9},{9,8},{10,11... | collective-permute-start | bytes 786440 | tf_op jit(solution)/shard_map/ppermute | solution.py:415
  56.7 1.9 %collective-permute-start.7 = (bf16[2,16,32,256]{3,2,1,0:T(8,128)(2,1)S(1)}, bf16[2,16,32,256]{3,2,1,0:T(8,128)(2,1)S(1)}, u32[]{:S(2)}, u32[]{:S(2)}) collective-permute-start(bf16[2,16,32,256]{3,2,1,0:T(8,128)(2,1)S(1)} %collective-permute-done.3.refs_1_.refs_2_), channel_id=1, source_target_pairs={{0,1},{1,0},{2,3},{3,2},{4,5},{5,4},{6,7},{7,6},{8,9},{9,8},{10,11... | collective-permute-start | bytes 1572872 | tf_op jit(solution)/shard_map/ppermute | solution.py:415
  56.7 2.8 %collective-permute-start.12 = (bf16[1,16,32,256]{3,2,1,0:T(8,128)(2,1)S(1)}, bf16[1,16,32,256]{3,2,1,0:T(8,128)(2,1)S(1)}, u32[]{:S(2)}, u32[]{:S(2)}) collective-permute-start(bf16[1,16,32,256]{3,2,1,0:T(8,128)(2,1)S(1)} %collective-permute-done.10.refs_3_), channel_id=1, source_target_pairs={{0,1},{1,0},{2,3},{3,2},{4,5},{5,4},{6,7},{7,6},{8,9},{9,8},{10,11... | collective-permute-start | bytes 786440 | tf_op jit(solution)/shard_map/ppermute | solution.py:415
  57.2 2.3 %collective-permute-start.13 = (bf16[1,16,32,256]{3,2,1,0:T(8,128)(2,1)S(1)}, bf16[1,16,32,256]{3,2,1,0:T(8,128)(2,1)S(1)}, u32[]{:S(2)}, u32[]{:S(2)}) collective-permute-start(bf16[1,16,32,256]{3,2,1,0:T(8,128)(2,1)S(1)} %collective-permute-done.11.refs_4_), channel_id=1, source_target_pairs={{0,1},{1,0},{2,3},{3,2},{4,5},{5,4},{6,7},{7,6},{8,9},{9,8},{10,11... | collective-permute-start | bytes 786440 | tf_op jit(solution)/shard_map/ppermute | solution.py:415

commit v11 on v7

--- a/solution.py
+++ b/solution.py
@@ -97,6 +97,10 @@
     return pltpu.with_memory_space_constraint(value, pltpu.HBM)
 
 
+def in_smem(value):
+    return pltpu.with_memory_space_constraint(value, pltpu.SMEM)
+
+
 def one_hot(hits):
     return jnp.where(hits, 1.0, 0.0).astype(jnp.bfloat16)
 
@@ -284,10 +288,10 @@
             transcendentals=0,
         ),
     )(
-        place,
-        in_hbm(tile_of),
-        in_hbm(jnp.swapaxes(tile_mask, 2, 3)),
-        in_hbm(tiles[0]),
+        in_smem(place),
+        in_smem(tile_of),
+        in_smem(jnp.swapaxes(tile_mask, 2, 3)),
+        tiles[0],
         *tiles[2:],
         tiles[1],
         lambda_amps,
@@ -295,62 +299,80 @@
     )
 
 
-def finish_kernel(indices, chunk, place_ref, swap_ref, w_ref, inverse_ref, *refs):
+def finish_kernel(indices, chunk, kept, last, swap_ref, w_ref, inverse_ref, place_ref, *refs):
     pieces = len(indices)
-    piece_refs = refs[:pieces]
-    out_ref, ys, done, sems = refs[-4:]
-    _, rows, pairs, cols = piece_refs[0].shape
-    owners = pieces // 2
-    halves = pairs // ROWS
-    mine = owners * pairs
+    piece_refs, refs = refs[:pieces], refs[pieces:]
+    ready_refs, refs = (refs[:chunk], refs[chunk:]) if last else ((), refs)
+    out_ref, *left_ref, done, ys, sems = refs[1 if chunk else 0 :]
+    groups, _, rows, _ = done.shape
+    halves = 2 * groups // pieces
+    mine = groups * ROWS
     me = place_ref[0]
+    leaving = []
+
+    def write(source, c, g, at):
+        k, h = g // halves, g % halves
+        copy = pltpu.make_async_copy(
+            source.at[at],
+            out_ref.at[me ^ k, 0, pl.ds(h * ROWS, ROWS), pl.ds(c * rows, rows), :],
+            sems.at[c, g],
+        )
+        copy.start()
+        leaving.append(copy)
+
+    for c, ref in enumerate(ready_refs):
+        for at in range(kept):
+            write(ref, c, groups - kept + at, at)
     weights = w_ref[...]
     for a in range(rows):
         amps = jnp.concatenate([ref[index, a] for ref, index in zip(piece_refs, indices)], axis=0)
         cycle = jnp.dot(weights, amps, preferred_element_type=jnp.float32)
         total = amps[:mine].astype(jnp.float32) + cycle
         value = (total * inverse_ref[chunk * rows + a]).astype(jnp.bfloat16)
-        for g in range(owners * halves):
+        for g in range(groups):
             ys[g, pl.ds(a * ROWS, ROWS), :] = value[g * ROWS : (g + 1) * ROWS]
     swap = swap_ref[...]
-    leaving = []
-    for g in range(owners * halves):
+    for g in range(groups):
         turned = jnp.dot(swap, ys[g], preferred_element_type=jnp.float32)
-        done[g] = turned.astype(jnp.bfloat16).reshape(ROWS, rows, cols)
-        k, h = g // halves, g % halves
-        copy = pltpu.make_async_copy(
-            done.at[g],
-            out_ref.at[me ^ k, 0, pl.ds(h * ROWS, ROWS), pl.ds(chunk * rows, rows), :],
-            sems.at[g],
-        )
-        copy.start()
-        leaving.append(copy)
+        turned = turned.astype(jnp.bfloat16).reshape(done.shape[1:])
+        if last or g < groups - kept:
+            done[g] = turned
+            write(done, chunk, g, g)
+        else:
+            left_ref[0][g - (groups - kept)] = turned
     for copy in leaving:
         copy.wait()
 
 
-def finish(chunk, place, swap, weights, inverse, pieces, before, shape):
+def finish(chunk, place, swap, weights, inverse, pieces, before, ready, shape):
     _, rows, pairs, cols = pieces[0][0].shape
-    owners = len(pieces) // 2
-    groups = owners * (pairs // ROWS)
-    anywhere = pl.BlockSpec(memory_space=pl.ANY)
-    args = [place, swap, weights, inverse] + [piece for piece, _ in pieces]
-    in_specs = [pl.BlockSpec(memory_space=pltpu.SMEM)]
-    in_specs += [pl.BlockSpec(memory_space=pltpu.VMEM)] * (3 + len(pieces))
+    groups = len(pieces) // 2 * (pairs // ROWS)
+    kept = groups // 2
+    last = chunk + 1 == shape[3] // rows
+    vmem, anywhere = pl.BlockSpec(memory_space=pltpu.VMEM), pl.BlockSpec(memory_space=pl.ANY)
+    args = [swap, weights, inverse, place, *[piece for piece, _ in pieces]]
+    in_specs = [vmem] * 3 + [pl.BlockSpec(memory_space=pltpu.SMEM)] + [vmem] * len(pieces)
+    if last:
+        args += ready
+        in_specs += [anywhere] * len(ready)
     aliases = {}
     if before is not None:
         aliases = {len(args): 0}
         args.append(before)
         in_specs.append(anywhere)
+    out_specs, out_shape = [anywhere], [jax.ShapeDtypeStruct(shape, jnp.bfloat16)]
+    if not last:
+        out_specs.append(vmem)
+        out_shape.append(jax.ShapeDtypeStruct((kept, ROWS, rows, cols), jnp.bfloat16))
     return pl.pallas_call(
-        functools.partial(finish_kernel, [index for _, index in pieces], chunk),
+        functools.partial(finish_kernel, [index for _, index in pieces], chunk, kept, last),
         in_specs=in_specs,
-        out_specs=anywhere,
-        out_shape=jax.ShapeDtypeStruct(shape, jnp.bfloat16),
+        out_specs=out_specs,
+        out_shape=out_shape,
         scratch_shapes=[
+            pltpu.VMEM((groups, ROWS, rows, cols), jnp.bfloat16),
             pltpu.VMEM((groups, ROWS * rows, cols), jnp.bfloat16),
-            pltpu.VMEM((groups, ROWS, rows, cols), jnp.bfloat16),
-            pltpu.SemaphoreType.DMA((groups,)),
+            pltpu.SemaphoreType.DMA((chunk + 1, groups)),
         ],
         input_output_aliases=aliases,
         compiler_params=pltpu.CompilerParams(vmem_limit_bytes=VMEM_BYTES),
@@ -403,19 +425,22 @@
         for c in range(chunks):
             earlier = direct[k, c - 1] if c and k == last else None
             direct[k, c] = to_owner(after(sent[((k, c),)], earlier), k)
-    own_passed = to_sibling(after(own, direct[last, 0]))
+    own_passed = to_sibling(after(own, weights))
     near_passed = to_sibling(after(near, (weights, direct[far[0], 0])))
     for k in far:
         for c in range(chunks):
-            earlier = other[k, c - 1] if c else None
+            earlier = None
+            if k == last:
+                earlier = other[far[0], c - 1] if c else weights
             other[k, c] = to_sibling(after(direct[k, c], earlier))
 
-    result = None
+    result, ready = None, []
     for c in range(chunks):
         pieces = [(own, c), (near, c)] + [(direct[k, c], 0) for k in far]
         pieces += [(own_passed, c), (near_passed, c)] + [(other[k, c], 0) for k in far]
         shape = (owners, 1, pairs, rows, cols)
-        result = finish(c, place, swap, weights, inverse, pieces, result, shape)
+        result, *left = finish(c, place, swap, weights, inverse, pieces, result, ready, shape)
+        ready += left
     return result
 
 

time: 63.4 us -> 62.8 us (level)
  no operation moved by 1% of the time
where the time goes in v11:
time: 62.8 us; the launch traced here: 62.6 us
  waiting for transfers between devices  37 us (59%)
  starting transfers between devices  13.7 us (22%)
  Pallas kernels  11.7 us (19%)
    ppermute x8, waiting for transfers between devices, to_owner(): return lax.ppermute(value, 'pair', [(o, o ^ k) for o in range(owners)])  36 us
    ppermute x8, starting transfers between devices, to_owner(): return lax.ppermute(value, 'pair', [(o, o ^ k) for o in range(owners)])  12.6 us
    pallas_call x2, Pallas kernels, finish(): pl.pallas_call(functools.partial(finish_kernel, [index for _, index in pi...  4.39 us
    pallas_call x1, Pallas kernels, make_weights(): pl.pallas_call(weights_kernel, in_specs=[vmem, vmem, vmem, smem, smem, vm...  3.52 us
    pallas_call x1, Pallas kernels, dress(): pl.pallas_call(functools.partial(dress_kernel, owners, rows, groups), in_...  2.11 us
    pallas_call x1, Pallas kernels, hold(): pl.pallas_call(hold_kernel, in_specs=[anywhere], out_specs=[anywhere, pl....  1.64 us
  transfers between devices with their start and end apart: 14, of which 5 were waited for; matrix products, arithmetic and copies ran while one was open for 0% of the time, Pallas kernels for 12%

profile of v11, /device:TPU:0, one launch (start us, length us, event | category | flops | bytes accessed | tf_op | source)
XLA Modules:
  0.0 62.6 jit_solution(3944108916339516078)
XLA Ops:
  0.0 0.0 copy-start
  0.0 0.0 copy-start.1
  0.0 0.0 copy-start.2
  0.0 5.1 %collective-permute-start.1 = (bf16[1,128,128]{2,1,0:T(8,128)(2,1)}, bf16[1,128,128]{2,1,0:T(8,128)(2,1)S(1)}, u32[]{:S(2)}, u32[]{:S(2)}) collective-permute-start(bf16[1,128,128]{2,1,0:T(8,128)(2,1)} %refs_0_.1), channel_id=1, source_target_pairs={{0,12},{4,8},{8,4},{12,0},{1,13},{5,9},{9,5},{13,1},{2,14},{6,10},... | collective-permute-start | bytes 98312 | tf_op jit(solution)/shard_map/ppermute | solution.py:403
  5.1 0.0 collective-permute-start
  5.1 0.6 %collective-permute-start.2 = (bf16[1,128,128]{2,1,0:T(8,128)(2,1)}, bf16[1,128,128]{2,1,0:T(8,128)(2,1)S(1)}, u32[]{:S(2)}, u32[]{:S(2)}) collective-permute-start(bf16[1,128,128]{2,1,0:T(8,128)(2,1)} %refs_0_.1), channel_id=1, source_target_pairs={{0,4},{4,0},{8,12},{12,8},{1,5},{5,1},{9,13},{13,9},{2,6},{6,2},{1... | collective-permute-start | bytes 98312 | tf_op jit(solution)/shard_map/ppermute | solution.py:403
  5.8 0.1 pad_add_fusion.place_ref
  5.8 0.0 copy-start.3
  5.8 0.0 copy-start.4
  5.9 0.0 copy-start.7
  5.9 1.6 %shard_map.91 = (bf16[1,1,32,128,256]{4,3,2,1,0:T(8,128)(2,1)S(1)}, bf16[256,256]{1,0:T(8,128)(2,1)S(1)}) custom-call(bf16[1,1,32,128,256]{4,3,2,1,0:T(8,128)(2,1)} %lam_ref.1), custom_call_target="tpu_custom_call" | custom-call | bytes 4194304 | tf_op jit(solution)/shard_map/pallas_call | solution.py:154
  7.5 0.0 collective-permute-done.1.refs_2_
  7.5 2.6 %collective-permute-done.refs_1_ = bf16[1,128,128]{2,1,0:T(8,128)(2,1)S(1)} collective-permute-done((bf16[1,128,128]{2,1,0:T(8,128)(2,1)}, bf16[1,128,128]{2,1,0:T(8,128)(2,1)S(1)}, u32[]{:S(2)}, u32[]{:S(2)}) %collective-permute-start) | collective-permute-done | bytes 32800 | tf_op jit(solution)/shard_map/ppermute | solution.py:403
  10.1 0.0 collective-permute-done.2.refs_3_
  10.2 0.0 copy-done
  10.2 0.0 copy-done.1
  10.2 0.0 copy-done.2
  10.2 2.1 %shard_map.92 = (bf16[1,16,32,256]{3,2,1,0:T(8,128)(2,1)S(1)}, bf16[1,16,32,256]{3,2,1,0:T(8,128)(2,1)S(1)}, bf16[1,16,32,256]{3,2,1,0:T(8,128)(2,1)S(1)}, bf16[...) custom-call(s32[2]{0:T(128)S(1)} %pad_add_fusion.place_ref, ...), custom_call_target="tpu_custom_call" | custom-call | flops 268435456 | bytes 3145728 | tf_op jit(solution)/shard_map/pallas_call | solution.py:272
  12.3 0.1 collective-permute-start.3
  12.4 3.5 %collective-permute-start.5 = (bf16[1,16,32,256]{3,2,1,0:T(8,128)(2,1)S(1)}, bf16[1,16,32,256]{3,2,1,0:T(8,128)(2,1)S(1)}, u32[]{:S(2)}, u32[]{:S(2)}) collective-permute-start(bf16[1,16,32,256]{3,2,1,0:T(8,128)(2,1)S(1)} %get-tuple-element.25), channel_id=1, source_target_pairs={{0,12},{4,8},{8,4},{12,0},{1,13},{5,9},{9,5},{13,1},{2,14},{6,10},... | collective-permute-start | bytes 786440 | tf_op jit(solution)/shard_map/ppermute | solution.py:403
  15.8 0.0 collective-permute-start.8
  15.8 2.9 %collective-permute-start.4 = (bf16[1,16,32,256]{3,2,1,0:T(8,128)(2,1)S(1)}, bf16[1,16,32,256]{3,2,1,0:T(8,128)(2,1)S(1)}, u32[]{:S(2)}, u32[]{:S(2)}) collective-permute-start(bf16[1,16,32,256]{3,2,1,0:T(8,128)(2,1)S(1)} %get-tuple-element.31), channel_id=1, source_target_pairs={{0,8},{4,12},{8,0},{12,4},{1,9},{5,13},{9,1},{13,5},{2,10},{6,14},... | collective-permute-start | bytes 786440 | tf_op jit(solution)/shard_map/ppermute | solution.py:403
  18.7 0.0 copy-done.3
  18.7 0.0 copy-done.4
  18.8 0.0 copy-done.5
  18.8 0.0 copy-done.6
  18.8 0.0 copy-done.7
  18.8 3.5 %shard_map.93 = (bf16[128,256]{1,0:T(8,128)(2,1)S(1)}, f32[32,128,256]{2,1,0:T(8,128)S(1)}) custom-call(s32[2,256]{1,0:T(2,128)S(1)} %bitcast.6, f32[400,400]{1,0:T(8,128)S(1)} %copy-done.3, f32[4,1,32]{2,1,0:T(1,128)S(1)} %copy-done.5, s32[2]{0:T(128)S(1)} %pad_add_fusion.place_ref, f32[32]{0:T(128)S(1)} %copy-done.7, f32[1,256]{1,0:T(1,128)S(1)} %bitcast.7), custom_call_target="tpu_custom_call" | custom-call | flops 491520000 | bytes 640000 | tf_op jit(solution)/shard_map/pallas_call | solution.py:207
  22.3 0.1 collective-permute-start.7
  22.4 12.0 %collective-permute-done.5.refs_3_ = bf16[1,16,32,256]{3,2,1,0:T(8,128)(2,1)S(1)} collective-permute-done((bf16[1,16,32,256]{3,2,1,0:T(8,128)(2,1)S(1)}, bf16[1,16,32,256]{3,2,1,0:T(8,128)(2,1)S(1)}, u32[]{:S(2)}, u32[]{:S(2)}) %collective-permute-start.5) | collective-permute-done | bytes 262176 | tf_op jit(solution)/shard_map/ppermute | solution.py:403
  34.4 0.4 collective-permute-start.6
  34.7 16.4 %collective-permute-done.8.refs_2_ = bf16[1,16,32,256]{3,2,1,0:T(8,128)(2,1)S(1)} collective-permute-done((bf16[1,16,32,256]{3,2,1,0:T(8,128)(2,1)S(1)}, bf16[1,16,32,256]{3,2,1,0:T(8,128)(2,1)S(1)}, u32[]{:S(2)}, u32[]{:S(2)}) %collective-permute-start.8) | collective-permute-done | bytes 262176 | tf_op jit(solution)/shard_map/ppermute | solution.py:403
  51.1 0.0 collective-permute-start.11
  51.1 0.0 collective-permute-done.3.refs_1_
  51.2 0.5 collective-permute-start.9
  51.7 5.0 %collective-permute-done.4.refs_2_ = bf16[1,16,32,256]{3,2,1,0:T(8,128)(2,1)S(1)} collective-permute-done((bf16[1,16,32,256]{3,2,1,0:T(8,128)(2,1)S(1)}, bf16[1,16,32,256]{3,2,1,0:T(8,128)(2,1)S(1)}, u32[]{:S(2)}, u32[]{:S(2)}) %collective-permute-start.4) | collective-permute-done | bytes 262176 | tf_op jit(solution)/shard_map/ppermute | solution.py:403
  56.7 0.0 collective-permute-start.13
  56.7 0.0 collective-permute-done.11.refs_6_
  56.7 0.5 collective-permute-start.10
  57.2 0.0 collective-permute-done.6.refs_3_
  57.2 0.1 collective-permute-start.12
  57.3 0.9 %collective-permute-done.13.refs_7_ = bf16[1,16,32,256]{3,2,1,0:T(8,128)(2,1)S(1)} collective-permute-done((bf16[1,16,32,256]{3,2,1,0:T(8,128)(2,1)S(1)}, bf16[1,16,32,256]{3,2,1,0:T(8,128)(2,1)S(1)}, u32[]{:S(2)}, u32[]{:S(2)}) %collective-permute-start.13) | collective-permute-done | bytes 262176 | tf_op jit(solution)/shard_map/ppermute | solution.py:406
  58.2 0.0 collective-permute-done.7.refs_4_
  58.2 0.0 collective-permute-done.9.refs_5_
  58.2 2.1 %shard_map.94 = (bf16[4,1,32,32,256]{4,3,2,1,0:T(8,128)(2,1)}, bf16[4,16,16,256]{3,2,1,0:T(8,128)(2,1)S(1)}) custom-call(bf16[256,256]{1,0:T(8,128)(2,1)S(1)} %get-tuple-element.23.refs_5_.swap_ref, bf16[128,256]{1,0:T(8,128)(2,1)S(1)} %get-tuple-element.27.w_ref, f32[32,128,256]{2,1,0:T(8,128)S(1)} %get-tuple-element.28.inverse_ref, ...), custom_call_target="tpu_custom_call" | custom-call | tf_op jit(solution)/shard_map/pallas_call | solution.py:367
  60.3 0.0 collective-permute-done.10.refs_6_
  60.3 0.0 collective-permute-done.12.refs_7_
  60.3 2.3 %shard_map.95 = bf16[4,1,32,32,256]{4,3,2,1,0:T(8,128)(2,1)} custom-call(bf16[256,256]{1,0:T(8,128)(2,1)S(1)} %get-tuple-element.23.refs_5_.swap_ref, bf16[128,256]{1,0:T(8,128)(2,1)S(1)} %get-tuple-element.27.w_ref, f32[32,128,256]{2,1,0:T(8,128)S(1)} %get-tuple-element.28.inverse_ref, ...), custom_call_target="tpu_custom_call", output_to_operand_aliasing={{}: (13, {})} | custom-call | tf_op jit(solution)/shard_map/pallas_call | solution.py:367
  (2 shorter events, 0.0 us)
Async XLA Ops:
  0.0 10.2 %copy-start = (bf16[1,128,128]{2,1,0:T(8,128)(2,1)S(1)}, bf16[1,128,128]{2,1,0:T(8,128)(2,1)}, u32[]{:S(2)}) copy-start(bf16[1,128,128]{2,1,0:T(8,128)(2,1)} %refs_0_.1) | copy-start | bytes 98308
  0.0 10.2 %copy-start.1 = (s32[1,1,32,2]{2,3,1,0:T(2,128)S(1)}, s32[1,1,32,2]{2,3,1,0:T(2,128)}, u32[]{:S(2)}) copy-start(s32[1,1,32,2]{2,3,1,0:T(2,128)} %param.12) | copy-start | bytes 772
  0.0 10.2 %copy-start.2 = (s32[1,1,32]{2,1,0:T(1,128)S(1)}, s32[1,1,32]{2,1,0:T(1,128)}, u32[]{:S(2)}) copy-start(s32[1,1,32]{2,1,0:T(1,128)} %tile_of_ref.1) | copy-start | bytes 388
  0.0 7.5 %collective-permute-start.1 = (bf16[1,128,128]{2,1,0:T(8,128)(2,1)}, bf16[1,128,128]{2,1,0:T(8,128)(2,1)S(1)}, u32[]{:S(2)}, u32[]{:S(2)}) collective-permute-start(bf16[1,128,128]{2,1,0:T(8,128)(2,1)} %refs_0_.1), channel_id=1, source_target_pairs={{0,12},{4,8},{8,4},{12,0},{1,13},{5,9},{9,5},{13,1},{2,14},{6,10},... | collective-permute-start | bytes 98312 | tf_op jit(solution)/shard_map/ppermute | solution.py:403
  5.1 5.0 %collective-permute-start = (bf16[1,128,128]{2,1,0:T(8,128)(2,1)}, bf16[1,128,128]{2,1,0:T(8,128)(2,1)S(1)}, u32[]{:S(2)}, u32[]{:S(2)}) collective-permute-start(bf16[1,128,128]{2,1,0:T(8,128)(2,1)} %refs_0_.1), channel_id=1, source_target_pairs={{0,8},{4,12},{8,0},{12,4},{1,9},{5,13},{9,1},{13,5},{2,10},{6,14},... | collective-permute-start | bytes 98312 | tf_op jit(solution)/shard_map/ppermute | solution.py:403
  5.1 5.0 %collective-permute-start.2 = (bf16[1,128,128]{2,1,0:T(8,128)(2,1)}, bf16[1,128,128]{2,1,0:T(8,128)(2,1)S(1)}, u32[]{:S(2)}, u32[]{:S(2)}) collective-permute-start(bf16[1,128,128]{2,1,0:T(8,128)(2,1)} %refs_0_.1), channel_id=1, source_target_pairs={{0,4},{4,0},{8,12},{12,8},{1,5},{5,1},{9,13},{13,9},{2,6},{6,2},{1... | collective-permute-start | bytes 98312 | tf_op jit(solution)/shard_map/ppermute | solution.py:403
  5.8 12.9 %copy-start.3 = (f32[400,400]{1,0:T(8,128)S(1)}, f32[400,400]{1,0:T(8,128)}, u32[]{:S(2)}) copy-start(f32[400,400]{1,0:T(8,128)} %coupling_ref.1) | copy-start | bytes 1920004
  5.8 12.9 %copy-start.4 = (s32[256,2]{0,1:T(2,128)S(1)}, s32[256,2]{0,1:T(2,128)}, u32[]{:S(2)}) copy-start(s32[256,2]{0,1:T(2,128)} %param.13) | copy-start | bytes 6148
  5.8 12.9 %copy-start.5 = (f32[4,1,32]{2,1,0:T(1,128)S(1)}, f32[4,1,32]{2,1,0:T(1,128)}, u32[]{:S(2)}) copy-start(f32[4,1,32]{2,1,0:T(1,128)} %gap_ref.1) | copy-start | bytes 1540
  5.8 12.9 %copy-start.6 = (f32[256]{0:T(256)S(1)}, f32[256]{0:T(256)}, u32[]{:S(2)}) copy-start(f32[256]{0:T(256)} %param.17) | copy-start | bytes 3076
  5.9 12.9 %copy-start.7 = (f32[32]{0:T(128)S(1)}, f32[32]{0:T(128)}, u32[]{:S(2)}) copy-start(f32[32]{0:T(128)} %row_ref.1) | copy-start | bytes 388
  12.3 38.9 %collective-permute-start.3 = (bf16[2,16,32,256]{3,2,1,0:T(8,128)(2,1)S(1)}, bf16[2,16,32,256]{3,2,1,0:T(8,128)(2,1)S(1)}, u32[]{:S(2)}, u32[]{:S(2)}) collective-permute-start(bf16[2,16,32,256]{3,2,1,0:T(8,128)(2,1)S(1)} %get-tuple-element.30), channel_id=1, source_target_pairs={{0,4},{4,0},{8,12},{12,8},{1,5},{5,1},{9,13},{13,9},{2,6},{6,2},{1... | collective-permute-start | bytes 1572872 | tf_op jit(solution)/shard_map/ppermute | solution.py:403
  12.4 22.0 %collective-permute-start.5 = (bf16[1,16,32,256]{3,2,1,0:T(8,128)(2,1)S(1)}, bf16[1,16,32,256]{3,2,1,0:T(8,128)(2,1)S(1)}, u32[]{:S(2)}, u32[]{:S(2)}) collective-permute-start(bf16[1,16,32,256]{3,2,1,0:T(8,128)(2,1)S(1)} %get-tuple-element.25), channel_id=1, source_target_pairs={{0,12},{4,8},{8,4},{12,0},{1,13},{5,9},{9,5},{13,1},{2,14},{6,10},... | collective-permute-start | bytes 786440 | tf_op jit(solution)/shard_map/ppermute | solution.py:403
  15.8 35.3 %collective-permute-start.8 = (bf16[1,16,32,256]{3,2,1,0:T(8,128)(2,1)S(1)}, bf16[1,16,32,256]{3,2,1,0:T(8,128)(2,1)S(1)}, u32[]{:S(2)}, u32[]{:S(2)}) collective-permute-start(bf16[1,16,32,256]{3,2,1,0:T(8,128)(2,1)S(1)} %get-tuple-element.35), channel_id=1, source_target_pairs={{0,8},{4,12},{8,0},{12,4},{1,9},{5,13},{9,1},{13,5},{2,10},{6,14},... | collective-permute-start | bytes 786440 | tf_op jit(solution)/shard_map/ppermute | solution.py:403
  15.8 40.8 %collective-permute-start.4 = (bf16[1,16,32,256]{3,2,1,0:T(8,128)(2,1)S(1)}, bf16[1,16,32,256]{3,2,1,0:T(8,128)(2,1)S(1)}, u32[]{:S(2)}, u32[]{:S(2)}) collective-permute-start(bf16[1,16,32,256]{3,2,1,0:T(8,128)(2,1)S(1)} %get-tuple-element.31), channel_id=1, source_target_pairs={{0,8},{4,12},{8,0},{12,4},{1,9},{5,13},{9,1},{13,5},{2,10},{6,14},... | collective-permute-start | bytes 786440 | tf_op jit(solution)/shard_map/ppermute | solution.py:403
  22.3 35.9 %collective-permute-start.7 = (bf16[2,16,32,256]{3,2,1,0:T(8,128)(2,1)S(1)}, bf16[2,16,32,256]{3,2,1,0:T(8,128)(2,1)S(1)}, u32[]{:S(2)}, u32[]{:S(2)}) collective-permute-start(bf16[2,16,32,256]{3,2,1,0:T(8,128)(2,1)S(1)} %get-tuple-element.34.refs_0_), channel_id=1, source_target_pairs={{0,1},{1,0},{2,3},{3,2},{4,5},{5,4},{6,7},{7,6},{8,9},{9,8},{10,11... | collective-permute-start | bytes 1572872 | tf_op jit(solution)/shard_map/ppermute | solution.py:406
  34.4 22.8 %collective-permute-start.6 = (bf16[1,16,32,256]{3,2,1,0:T(8,128)(2,1)S(1)}, bf16[1,16,32,256]{3,2,1,0:T(8,128)(2,1)S(1)}, u32[]{:S(2)}, u32[]{:S(2)}) collective-permute-start(bf16[1,16,32,256]{3,2,1,0:T(8,128)(2,1)S(1)} %get-tuple-element.33), channel_id=1, source_target_pairs={{0,12},{4,8},{8,4},{12,0},{1,13},{5,9},{9,5},{13,1},{2,14},{6,10},... | collective-permute-start | bytes 786440 | tf_op jit(solution)/shard_map/ppermute | solution.py:403
  51.1 5.5 %collective-permute-start.11 = (bf16[1,16,32,256]{3,2,1,0:T(8,128)(2,1)S(1)}, bf16[1,16,32,256]{3,2,1,0:T(8,128)(2,1)S(1)}, u32[]{:S(2)}, u32[]{:S(2)}) collective-permute-start(bf16[1,16,32,256]{3,2,1,0:T(8,128)(2,1)S(1)} %collective-permute-done.8.refs_2_), channel_id=1, source_target_pairs={{0,1},{1,0},{2,3},{3,2},{4,5},{5,4},{6,7},{7,6},{8,9},{9,8},{10,11... | collective-permute-start | bytes 786440 | tf_op jit(solution)/shard_map/ppermute | solution.py:406
  51.2 7.1 %collective-permute-start.9 = (bf16[2,16,32,256]{3,2,1,0:T(8,128)(2,1)S(1)}, bf16[2,16,32,256]{3,2,1,0:T(8,128)(2,1)S(1)}, u32[]{:S(2)}, u32[]{:S(2)}) collective-permute-start(bf16[2,16,32,256]{3,2,1,0:T(8,128)(2,1)S(1)} %collective-permute-done.3.refs_1_), channel_id=1, source_target_pairs={{0,1},{1,0},{2,3},{3,2},{4,5},{5,4},{6,7},{7,6},{8,9},{9,8},{10,11... | collective-permute-start | bytes 1572872 | tf_op jit(solution)/shard_map/ppermute | solution.py:406
  56.7 1.5 %collective-permute-start.13 = (bf16[1,16,32,256]{3,2,1,0:T(8,128)(2,1)S(1)}, bf16[1,16,32,256]{3,2,1,0:T(8,128)(2,1)S(1)}, u32[]{:S(2)}, u32[]{:S(2)}) collective-permute-start(bf16[1,16,32,256]{3,2,1,0:T(8,128)(2,1)S(1)} %collective-permute-done.5.refs_3_), channel_id=1, source_target_pairs={{0,1},{1,0},{2,3},{3,2},{4,5},{5,4},{6,7},{7,6},{8,9},{9,8},{10,11... | collective-permute-start | bytes 786440 | tf_op jit(solution)/shard_map/ppermute | solution.py:406
  56.7 3.6 %collective-permute-start.10 = (bf16[1,16,32,256]{3,2,1,0:T(8,128)(2,1)S(1)}, bf16[1,16,32,256]{3,2,1,0:T(8,128)(2,1)S(1)}, u32[]{:S(2)}, u32[]{:S(2)}) collective-permute-start(bf16[1,16,32,256]{3,2,1,0:T(8,128)(2,1)S(1)} %collective-permute-done.4.refs_2_), channel_id=1, source_target_pairs={{0,1},{1,0},{2,3},{3,2},{4,5},{5,4},{6,7},{7,6},{8,9},{9,8},{10,11... | collective-permute-start | bytes 786440 | tf_op jit(solution)/shard_map/ppermute | solution.py:406
  57.2 3.1 %collective-permute-start.12 = (bf16[1,16,32,256]{3,2,1,0:T(8,128)(2,1)S(1)}, bf16[1,16,32,256]{3,2,1,0:T(8,128)(2,1)S(1)}, u32[]{:S(2)}, u32[]{:S(2)}) collective-permute-start(bf16[1,16,32,256]{3,2,1,0:T(8,128)(2,1)S(1)} %collective-permute-done.6.refs_3_), channel_id=1, source_target_pairs={{0,1},{1,0},{2,3},{3,2},{4,5},{5,4},{6,7},{7,6},{8,9},{9,8},{10,11... | collective-permute-start | bytes 786440 | tf_op jit(solution)/shard_map/ppermute | solution.py:406

commit v12 on v10

--- a/solution.py
+++ b/solution.py
@@ -434,11 +434,13 @@
         for c in range(chunks):
             earlier = direct[k, c - 1] if c and k == last else None
             direct[k, c] = to_owner(after(sent[((k, c),)], earlier), k)
-    own_passed = to_sibling(after(own, direct[last, 0]))
+    own_passed = to_sibling(after(own, weights))
     near_passed = to_sibling(after(near, (weights, direct[far[0], 0])))
     for k in far:
         for c in range(chunks):
-            earlier = other[k, c - 1] if c else None
+            earlier = None
+            if k == last:
+                earlier = other[far[0], c - 1] if c else weights
             other[k, c] = to_sibling(after(direct[k, c], earlier))
 
     ready = []

time: 62.1 us -> 61.7 us (level)
  no operation moved by 1% of the time
where the time goes in v12:
time: 61.7 us; the launch traced here: 61.6 us
  waiting for transfers between devices  37 us (60%)
  starting transfers between devices  13.7 us (22%)
  Pallas kernels  10.6 us (17%)
    ppermute x8, waiting for transfers between devices, to_owner(): return lax.ppermute(value, 'pair', [(o, o ^ k) for o in range(owners)])  36 us
    ppermute x8, starting transfers between devices, to_owner(): return lax.ppermute(value, 'pair', [(o, o ^ k) for o in range(owners)])  12.6 us
    pallas_call x1, Pallas kernels, make_weights(): pl.pallas_call(weights_kernel, in_specs=[vmem, vmem, vmem, smem, smem, vm...  3.52 us
    pallas_call x2, Pallas kernels, finish(): pl.pallas_call(kernel, in_specs=in_specs + [vmem] * len(pieces), out_spec...  3.35 us
    pallas_call x1, Pallas kernels, dress(): pl.pallas_call(functools.partial(dress_kernel, owners, rows, groups), in_...  2.11 us
    pallas_call x1, Pallas kernels, hold(): pl.pallas_call(hold_kernel, in_specs=[anywhere], out_specs=[anywhere, pl....  1.64 us
  transfers between devices with their start and end apart: 14, of which 5 were waited for; matrix products, arithmetic and copies ran while one was open for 0% of the time, Pallas kernels for 10%

profile of v12, /device:TPU:0, one launch (start us, length us, event | category | flops | bytes accessed | tf_op | source)
XLA Modules:
  0.0 61.6 jit_solution(13303955445379075087)
XLA Ops:
  0.0 0.0 copy-start
  0.0 0.0 copy-start.1
  0.0 0.0 copy-start.2
  0.0 5.1 %collective-permute-start.1 = (bf16[1,128,128]{2,1,0:T(8,128)(2,1)}, bf16[1,128,128]{2,1,0:T(8,128)(2,1)S(1)}, u32[]{:S(2)}, u32[]{:S(2)}) collective-permute-start(bf16[1,128,128]{2,1,0:T(8,128)(2,1)} %refs_0_.1), channel_id=1, source_target_pairs={{0,12},{4,8},{8,4},{12,0},{1,13},{5,9},{9,5},{13,1},{2,14},{6,10},... | collective-permute-start | bytes 98312 | tf_op jit(solution)/shard_map/ppermute | solution.py:412
  5.1 0.0 collective-permute-start
  5.1 0.6 %collective-permute-start.2 = (bf16[1,128,128]{2,1,0:T(8,128)(2,1)}, bf16[1,128,128]{2,1,0:T(8,128)(2,1)S(1)}, u32[]{:S(2)}, u32[]{:S(2)}) collective-permute-start(bf16[1,128,128]{2,1,0:T(8,128)(2,1)} %refs_0_.1), channel_id=1, source_target_pairs={{0,4},{4,0},{8,12},{12,8},{1,5},{5,1},{9,13},{13,9},{2,6},{6,2},{1... | collective-permute-start | bytes 98312 | tf_op jit(solution)/shard_map/ppermute | solution.py:412
  5.8 0.1 pad_add_fusion.place_ref
  5.8 0.0 copy-start.3
  5.8 0.0 copy-start.4
  5.9 0.0 copy-start.7
  5.9 1.6 %shard_map.91 = (bf16[1,1,32,128,256]{4,3,2,1,0:T(8,128)(2,1)S(1)}, bf16[256,256]{1,0:T(8,128)(2,1)S(1)}) custom-call(bf16[1,1,32,128,256]{4,3,2,1,0:T(8,128)(2,1)} %lam_ref.1), custom_call_target="tpu_custom_call" | custom-call | bytes 4194304 | tf_op jit(solution)/shard_map/pallas_call | solution.py:154
  7.5 0.0 collective-permute-done.1.refs_2_
  7.5 2.6 %collective-permute-done.refs_1_ = bf16[1,128,128]{2,1,0:T(8,128)(2,1)S(1)} collective-permute-done((bf16[1,128,128]{2,1,0:T(8,128)(2,1)}, bf16[1,128,128]{2,1,0:T(8,128)(2,1)S(1)}, u32[]{:S(2)}, u32[]{:S(2)}) %collective-permute-start) | collective-permute-done | bytes 32800 | tf_op jit(solution)/shard_map/ppermute | solution.py:412
  10.1 0.0 collective-permute-done.2.refs_3_
  10.2 0.0 copy-done
  10.2 0.0 copy-done.1
  10.2 0.0 copy-done.2
  10.2 2.1 %shard_map.92 = (bf16[1,16,32,256]{3,2,1,0:T(8,128)(2,1)S(1)}, bf16[1,16,32,256]{3,2,1,0:T(8,128)(2,1)S(1)}, bf16[1,16,32,256]{3,2,1,0:T(8,128)(2,1)S(1)}, bf16[...) custom-call(s32[2]{0:T(128)S(1)} %pad_add_fusion.place_ref, ...), custom_call_target="tpu_custom_call" | custom-call | flops 268435456 | bytes 3145728 | tf_op jit(solution)/shard_map/pallas_call | solution.py:272
  12.3 0.1 collective-permute-start.3
  12.4 3.5 %collective-permute-start.5 = (bf16[1,16,32,256]{3,2,1,0:T(8,128)(2,1)S(1)}, bf16[1,16,32,256]{3,2,1,0:T(8,128)(2,1)S(1)}, u32[]{:S(2)}, u32[]{:S(2)}) collective-permute-start(bf16[1,16,32,256]{3,2,1,0:T(8,128)(2,1)S(1)} %get-tuple-element.23), channel_id=1, source_target_pairs={{0,12},{4,8},{8,4},{12,0},{1,13},{5,9},{9,5},{13,1},{2,14},{6,10},... | collective-permute-start | bytes 786440 | tf_op jit(solution)/shard_map/ppermute | solution.py:412
  15.8 0.0 collective-permute-start.4
  15.8 2.9 %collective-permute-start.10 = (bf16[1,16,32,256]{3,2,1,0:T(8,128)(2,1)S(1)}, bf16[1,16,32,256]{3,2,1,0:T(8,128)(2,1)S(1)}, u32[]{:S(2)}, u32[]{:S(2)}) collective-permute-start(bf16[1,16,32,256]{3,2,1,0:T(8,128)(2,1)S(1)} %get-tuple-element.33), channel_id=1, source_target_pairs={{0,8},{4,12},{8,0},{12,4},{1,9},{5,13},{9,1},{13,5},{2,10},{6,14},... | collective-permute-start | bytes 786440 | tf_op jit(solution)/shard_map/ppermute | solution.py:412
  18.7 0.0 copy-done.3
  18.7 0.0 copy-done.4
  18.8 0.0 copy-done.5
  18.8 0.0 copy-done.6
  18.8 0.0 copy-done.7
  18.8 3.5 %shard_map.93 = (bf16[128,256]{1,0:T(8,128)(2,1)S(1)}, f32[32,128,256]{2,1,0:T(8,128)S(1)}) custom-call(s32[2,256]{1,0:T(2,128)S(1)} %bitcast.6, f32[400,400]{1,0:T(8,128)S(1)} %copy-done.3, f32[4,1,32]{2,1,0:T(1,128)S(1)} %copy-done.5, s32[2]{0:T(128)S(1)} %pad_add_fusion.place_ref, f32[32]{0:T(128)S(1)} %copy-done.7, f32[1,256]{1,0:T(1,128)S(1)} %bitcast.7), custom_call_target="tpu_custom_call" | custom-call | flops 491520000 | bytes 640000 | tf_op jit(solution)/shard_map/pallas_call | solution.py:207
  22.3 0.1 collective-permute-start.6
  22.4 12.0 %collective-permute-done.5.refs_3_ = bf16[1,16,32,256]{3,2,1,0:T(8,128)(2,1)S(1)} collective-permute-done((bf16[1,16,32,256]{3,2,1,0:T(8,128)(2,1)S(1)}, bf16[1,16,32,256]{3,2,1,0:T(8,128)(2,1)S(1)}, u32[]{:S(2)}, u32[]{:S(2)}) %collective-permute-start.5) | collective-permute-done | bytes 262176 | tf_op jit(solution)/shard_map/ppermute | solution.py:412
  34.4 0.4 collective-permute-start.11
  34.7 16.4 %collective-permute-done.4.refs_2_ = bf16[1,16,32,256]{3,2,1,0:T(8,128)(2,1)S(1)} collective-permute-done((bf16[1,16,32,256]{3,2,1,0:T(8,128)(2,1)S(1)}, bf16[1,16,32,256]{3,2,1,0:T(8,128)(2,1)S(1)}, u32[]{:S(2)}, u32[]{:S(2)}) %collective-permute-start.4) | collective-permute-done | bytes 262176 | tf_op jit(solution)/shard_map/ppermute | solution.py:412
  51.1 0.0 collective-permute-start.8
  51.1 0.0 collective-permute-done.3.refs_1_.refs_2_
  51.2 0.5 collective-permute-start.7
  51.7 5.0 %collective-permute-done.10.refs_3_ = bf16[1,16,32,256]{3,2,1,0:T(8,128)(2,1)S(1)} collective-permute-done((bf16[1,16,32,256]{3,2,1,0:T(8,128)(2,1)S(1)}, bf16[1,16,32,256]{3,2,1,0:T(8,128)(2,1)S(1)}, u32[]{:S(2)}, u32[]{:S(2)}) %collective-permute-start.10) | collective-permute-done | bytes 262176 | tf_op jit(solution)/shard_map/ppermute | solution.py:412
  56.7 0.0 collective-permute-start.9
  56.7 0.0 collective-permute-done.8.refs_6_
  56.7 0.5 collective-permute-start.12
  57.2 0.0 collective-permute-done.11.refs_4_
  57.2 0.1 collective-permute-start.13
  57.3 0.9 %collective-permute-done.9.refs_7_ = bf16[1,16,32,256]{3,2,1,0:T(8,128)(2,1)S(1)} collective-permute-done((bf16[1,16,32,256]{3,2,1,0:T(8,128)(2,1)S(1)}, bf16[1,16,32,256]{3,2,1,0:T(8,128)(2,1)S(1)}, u32[]{:S(2)}, u32[]{:S(2)}) %collective-permute-start.9) | collective-permute-done | bytes 262176 | tf_op jit(solution)/shard_map/ppermute | solution.py:415
  58.2 0.0 collective-permute-done.6.refs_4_.refs_5_
  58.2 0.0 collective-permute-done.7.refs_5_.refs_6_
  58.2 0.9 %shard_map.94.refs_0_ = bf16[8,16,16,256]{3,2,1,0:T(8,128)(2,1)S(1)} custom-call(bf16[256,256]{1,0:T(8,128)(2,1)S(1)} %get-tuple-element.21.refs_5_.swap_ref, bf16[128,256]{1,0:T(8,128)(2,1)S(1)} %get-tuple-element.25.w_ref, f32[32,128,256]{2,1,0:T(8,128)S(1)} %get-tuple-element.26.inverse_ref, ...), custom_call_target="tpu_custom_call" | custom-call | tf_op jit(solution)/shard_map/pallas_call | solution.py:381
  59.1 0.0 collective-permute-done.12.refs_7_
  59.1 0.0 collective-permute-done.13.refs_8_
  59.1 2.5 %shard_map.95 = bf16[4,1,32,32,256]{4,3,2,1,0:T(8,128)(2,1)} custom-call(bf16[256,256]{1,0:T(8,128)(2,1)S(1)} %get-tuple-element.21.refs_5_.swap_ref, bf16[128,256]{1,0:T(8,128)(2,1)S(1)} %get-tuple-element.25.w_ref, f32[32,128,256]{2,1,0:T(8,128)S(1)} %get-tuple-element.26.inverse_ref, s32[2]{0:T(128)S(1)} %pad_add_fusion.place_ref, ...), custom_call_target="tpu_custom_call" | custom-call | tf_op jit(solution)/shard_map/pallas_call | solution.py:381
  (2 shorter events, 0.0 us)
Async XLA Ops:
  0.0 10.2 %copy-start = (bf16[1,128,128]{2,1,0:T(8,128)(2,1)S(1)}, bf16[1,128,128]{2,1,0:T(8,128)(2,1)}, u32[]{:S(2)}) copy-start(bf16[1,128,128]{2,1,0:T(8,128)(2,1)} %refs_0_.1) | copy-start | bytes 98308
  0.0 10.2 %copy-start.1 = (s32[1,1,32,2]{2,3,1,0:T(2,128)S(1)}, s32[1,1,32,2]{2,3,1,0:T(2,128)}, u32[]{:S(2)}) copy-start(s32[1,1,32,2]{2,3,1,0:T(2,128)} %param.12) | copy-start | bytes 772
  0.0 10.2 %copy-start.2 = (s32[1,1,32]{2,1,0:T(1,128)S(1)}, s32[1,1,32]{2,1,0:T(1,128)}, u32[]{:S(2)}) copy-start(s32[1,1,32]{2,1,0:T(1,128)} %tile_of_ref.1) | copy-start | bytes 388
  0.0 7.5 %collective-permute-start.1 = (bf16[1,128,128]{2,1,0:T(8,128)(2,1)}, bf16[1,128,128]{2,1,0:T(8,128)(2,1)S(1)}, u32[]{:S(2)}, u32[]{:S(2)}) collective-permute-start(bf16[1,128,128]{2,1,0:T(8,128)(2,1)} %refs_0_.1), channel_id=1, source_target_pairs={{0,12},{4,8},{8,4},{12,0},{1,13},{5,9},{9,5},{13,1},{2,14},{6,10},... | collective-permute-start | bytes 98312 | tf_op jit(solution)/shard_map/ppermute | solution.py:412
  5.1 5.0 %collective-permute-start = (bf16[1,128,128]{2,1,0:T(8,128)(2,1)}, bf16[1,128,128]{2,1,0:T(8,128)(2,1)S(1)}, u32[]{:S(2)}, u32[]{:S(2)}) collective-permute-start(bf16[1,128,128]{2,1,0:T(8,128)(2,1)} %refs_0_.1), channel_id=1, source_target_pairs={{0,8},{4,12},{8,0},{12,4},{1,9},{5,13},{9,1},{13,5},{2,10},{6,14},... | collective-permute-start | bytes 98312 | tf_op jit(solution)/shard_map/ppermute | solution.py:412
  5.1 5.0 %collective-permute-start.2 = (bf16[1,128,128]{2,1,0:T(8,128)(2,1)}, bf16[1,128,128]{2,1,0:T(8,128)(2,1)S(1)}, u32[]{:S(2)}, u32[]{:S(2)}) collective-permute-start(bf16[1,128,128]{2,1,0:T(8,128)(2,1)} %refs_0_.1), channel_id=1, source_target_pairs={{0,4},{4,0},{8,12},{12,8},{1,5},{5,1},{9,13},{13,9},{2,6},{6,2},{1... | collective-permute-start | bytes 98312 | tf_op jit(solution)/shard_map/ppermute | solution.py:412
  5.8 12.9 %copy-start.3 = (f32[400,400]{1,0:T(8,128)S(1)}, f32[400,400]{1,0:T(8,128)}, u32[]{:S(2)}) copy-start(f32[400,400]{1,0:T(8,128)} %coupling_ref.1) | copy-start | bytes 1920004
  5.8 12.9 %copy-start.4 = (s32[256,2]{0,1:T(2,128)S(1)}, s32[256,2]{0,1:T(2,128)}, u32[]{:S(2)}) copy-start(s32[256,2]{0,1:T(2,128)} %param.13) | copy-start | bytes 6148
  5.8 12.9 %copy-start.5 = (f32[4,1,32]{2,1,0:T(1,128)S(1)}, f32[4,1,32]{2,1,0:T(1,128)}, u32[]{:S(2)}) copy-start(f32[4,1,32]{2,1,0:T(1,128)} %gap_ref.1) | copy-start | bytes 1540
  5.8 12.9 %copy-start.6 = (f32[256]{0:T(256)S(1)}, f32[256]{0:T(256)}, u32[]{:S(2)}) copy-start(f32[256]{0:T(256)} %param.17) | copy-start | bytes 3076
  5.9 12.9 %copy-start.7 = (f32[32]{0:T(128)S(1)}, f32[32]{0:T(128)}, u32[]{:S(2)}) copy-start(f32[32]{0:T(128)} %row_ref.1) | copy-start | bytes 388
  12.3 38.9 %collective-permute-start.3 = (bf16[2,16,32,256]{3,2,1,0:T(8,128)(2,1)S(1)}, bf16[2,16,32,256]{3,2,1,0:T(8,128)(2,1)S(1)}, u32[]{:S(2)}, u32[]{:S(2)}) collective-permute-start(bf16[2,16,32,256]{3,2,1,0:T(8,128)(2,1)S(1)} %get-tuple-element.28), channel_id=1, source_target_pairs={{0,4},{4,0},{8,12},{12,8},{1,5},{5,1},{9,13},{13,9},{2,6},{6,2},{1... | collective-permute-start | bytes 1572872 | tf_op jit(solution)/shard_map/ppermute | solution.py:412
  12.4 22.0 %collective-permute-start.5 = (bf16[1,16,32,256]{3,2,1,0:T(8,128)(2,1)S(1)}, bf16[1,16,32,256]{3,2,1,0:T(8,128)(2,1)S(1)}, u32[]{:S(2)}, u32[]{:S(2)}) collective-permute-start(bf16[1,16,32,256]{3,2,1,0:T(8,128)(2,1)S(1)} %get-tuple-element.23), channel_id=1, source_target_pairs={{0,12},{4,8},{8,4},{12,0},{1,13},{5,9},{9,5},{13,1},{2,14},{6,10},... | collective-permute-start | bytes 786440 | tf_op jit(solution)/shard_map/ppermute | solution.py:412
  15.8 35.3 %collective-permute-start.4 = (bf16[1,16,32,256]{3,2,1,0:T(8,128)(2,1)S(1)}, bf16[1,16,32,256]{3,2,1,0:T(8,128)(2,1)S(1)}, u32[]{:S(2)}, u32[]{:S(2)}) collective-permute-start(bf16[1,16,32,256]{3,2,1,0:T(8,128)(2,1)S(1)} %get-tuple-element.29), channel_id=1, source_target_pairs={{0,8},{4,12},{8,0},{12,4},{1,9},{5,13},{9,1},{13,5},{2,10},{6,14},... | collective-permute-start | bytes 786440 | tf_op jit(solution)/shard_map/ppermute | solution.py:412
  15.8 40.8 %collective-permute-start.10 = (bf16[1,16,32,256]{3,2,1,0:T(8,128)(2,1)S(1)}, bf16[1,16,32,256]{3,2,1,0:T(8,128)(2,1)S(1)}, u32[]{:S(2)}, u32[]{:S(2)}) collective-permute-start(bf16[1,16,32,256]{3,2,1,0:T(8,128)(2,1)S(1)} %get-tuple-element.33), channel_id=1, source_target_pairs={{0,8},{4,12},{8,0},{12,4},{1,9},{5,13},{9,1},{13,5},{2,10},{6,14},... | collective-permute-start | bytes 786440 | tf_op jit(solution)/shard_map/ppermute | solution.py:412
  22.3 35.9 %collective-permute-start.6 = (bf16[2,16,32,256]{3,2,1,0:T(8,128)(2,1)S(1)}, bf16[2,16,32,256]{3,2,1,0:T(8,128)(2,1)S(1)}, u32[]{:S(2)}, u32[]{:S(2)}) collective-permute-start(bf16[2,16,32,256]{3,2,1,0:T(8,128)(2,1)S(1)} %get-tuple-element.30.refs_0_.refs_1_), channel_id=1, source_target_pairs={{0,1},{1,0},{2,3},{3,2},{4,5},{5,4},{6,7},{7,6},{8,9},{9,8},{10,11... | collective-permute-start | bytes 1572872 | tf_op jit(solution)/shard_map/ppermute | solution.py:415
  34.4 22.8 %collective-permute-start.11 = (bf16[1,16,32,256]{3,2,1,0:T(8,128)(2,1)S(1)}, bf16[1,16,32,256]{3,2,1,0:T(8,128)(2,1)S(1)}, u32[]{:S(2)}, u32[]{:S(2)}) collective-permute-start(bf16[1,16,32,256]{3,2,1,0:T(8,128)(2,1)S(1)} %get-tuple-element.35), channel_id=1, source_target_pairs={{0,12},{4,8},{8,4},{12,0},{1,13},{5,9},{9,5},{13,1},{2,14},{6,10},... | collective-permute-start | bytes 786440 | tf_op jit(solution)/shard_map/ppermute | solution.py:412
  51.1 5.5 %collective-permute-start.8 = (bf16[1,16,32,256]{3,2,1,0:T(8,128)(2,1)S(1)}, bf16[1,16,32,256]{3,2,1,0:T(8,128)(2,1)S(1)}, u32[]{:S(2)}, u32[]{:S(2)}) collective-permute-start(bf16[1,16,32,256]{3,2,1,0:T(8,128)(2,1)S(1)} %collective-permute-done.4.refs_2_), channel_id=1, source_target_pairs={{0,1},{1,0},{2,3},{3,2},{4,5},{5,4},{6,7},{7,6},{8,9},{9,8},{10,11... | collective-permute-start | bytes 786440 | tf_op jit(solution)/shard_map/ppermute | solution.py:415
  51.2 7.1 %collective-permute-start.7 = (bf16[2,16,32,256]{3,2,1,0:T(8,128)(2,1)S(1)}, bf16[2,16,32,256]{3,2,1,0:T(8,128)(2,1)S(1)}, u32[]{:S(2)}, u32[]{:S(2)}) collective-permute-start(bf16[2,16,32,256]{3,2,1,0:T(8,128)(2,1)S(1)} %collective-permute-done.3.refs_1_.refs_2_), channel_id=1, source_target_pairs={{0,1},{1,0},{2,3},{3,2},{4,5},{5,4},{6,7},{7,6},{8,9},{9,8},{10,11... | collective-permute-start | bytes 1572872 | tf_op jit(solution)/shard_map/ppermute | solution.py:415
  56.7 1.5 %collective-permute-start.9 = (bf16[1,16,32,256]{3,2,1,0:T(8,128)(2,1)S(1)}, bf16[1,16,32,256]{3,2,1,0:T(8,128)(2,1)S(1)}, u32[]{:S(2)}, u32[]{:S(2)}) collective-permute-start(bf16[1,16,32,256]{3,2,1,0:T(8,128)(2,1)S(1)} %collective-permute-done.5.refs_3_), channel_id=1, source_target_pairs={{0,1},{1,0},{2,3},{3,2},{4,5},{5,4},{6,7},{7,6},{8,9},{9,8},{10,11... | collective-permute-start | bytes 786440 | tf_op jit(solution)/shard_map/ppermute | solution.py:415
  56.7 2.4 %collective-permute-start.12 = (bf16[1,16,32,256]{3,2,1,0:T(8,128)(2,1)S(1)}, bf16[1,16,32,256]{3,2,1,0:T(8,128)(2,1)S(1)}, u32[]{:S(2)}, u32[]{:S(2)}) collective-permute-start(bf16[1,16,32,256]{3,2,1,0:T(8,128)(2,1)S(1)} %collective-permute-done.10.refs_3_), channel_id=1, source_target_pairs={{0,1},{1,0},{2,3},{3,2},{4,5},{5,4},{6,7},{7,6},{8,9},{9,8},{10,11... | collective-permute-start | bytes 786440 | tf_op jit(solution)/shard_map/ppermute | solution.py:415
  57.2 1.9 %collective-permute-start.13 = (bf16[1,16,32,256]{3,2,1,0:T(8,128)(2,1)S(1)}, bf16[1,16,32,256]{3,2,1,0:T(8,128)(2,1)S(1)}, u32[]{:S(2)}, u32[]{:S(2)}) collective-permute-start(bf16[1,16,32,256]{3,2,1,0:T(8,128)(2,1)S(1)} %collective-permute-done.11.refs_4_), channel_id=1, source_target_pairs={{0,1},{1,0},{2,3},{3,2},{4,5},{5,4},{6,7},{7,6},{8,9},{9,8},{10,11... | collective-permute-start | bytes 786440 | tf_op jit(solution)/shard_map/ppermute | solution.py:415

commit v13 on v10

--- a/solution.py
+++ b/solution.py
@@ -429,26 +429,29 @@
         after(pair_list, sent[groups[0]]), coupling, pair_gap, place, row_energy, col_energy
     )
     own, near = sent[groups[-1]], to_owner(sent[groups[-2]], 1)
-    direct, other = {}, {}
-    for k in far:
-        for c in range(chunks):
-            earlier = direct[k, c - 1] if c and k == last else None
-            direct[k, c] = to_owner(after(sent[((k, c),)], earlier), k)
-    own_passed = to_sibling(after(own, direct[last, 0]))
-    near_passed = to_sibling(after(near, (weights, direct[far[0], 0])))
-    for k in far:
-        for c in range(chunks):
-            earlier = other[k, c - 1] if c else None
-            other[k, c] = to_sibling(after(direct[k, c], earlier))
-
-    ready = []
-    for c in range(chunks):
-        pieces = [(own, c), (near, c)] + [(direct[k, c], 0) for k in far]
-        pieces += [(own_passed, c), (near_passed, c)] + [(other[k, c], 0) for k in far]
-        if c + 1 < chunks:
-            ready.append(finish(c, swap, weights, inverse, pieces))
+
+    @functools.cache
+    def landed(k, c):
+        earlier = landed(k, c - 1) if c and k == last else None
+        return to_owner(after(sent[((k, c),)], earlier), k)
+
+    @functools.cache
+    def passed(k, c):
+        earlier = passed(far[0], c - 1) if c else (weights, inverse) if k == last else None
+        return to_sibling(after(landed(k, c), earlier))
+
+    @functools.cache
+    def passed_whole(k):
+        return to_sibling(after(near, (weights, inverse, passed(last, 0))) if k else after(own, near))
+
+    chunk_pieces = []
+    for c in range(chunks - 1, -1, -1):
+        pieces = [(own, c), (near, c)] + [(landed(k, c), 0) for k in far]
+        pieces += [(passed_whole(k), c) for k in (0, 1)] + [(passed(k, c), 0) for k in far]
+        chunk_pieces.insert(0, pieces)
+    ready = [finish(c, swap, weights, inverse, chunk_pieces[c]) for c in range(chunks - 1)]
     shape = (owners, 1, pairs, rows, cols)
-    return finish(c, swap, weights, inverse, pieces, place, ready, shape)
+    return finish(chunks - 1, swap, weights, inverse, chunk_pieces[-1], place, ready, shape)
 
 
 def solution(mesh):

time: 62.1 us -> 60.8 us (0.979)
  the two profiles are of different devices: /device:TPU:0 before, /device:TPU:23 now
where the time goes in v13:
time: 60.8 us; the launch traced here: 60.6 us
  waiting for transfers between devices  30.4 us (50%)
  starting transfers between devices  19.3 us (32%)
  Pallas kernels  10.6 us (17%)
    ppermute x8, waiting for transfers between devices, to_owner(): return lax.ppermute(value, 'pair', [(o, o ^ k) for o in range(owners)])  30.2 us
    ppermute x6, starting transfers between devices, to_sibling(): return lax.ppermute(value, 'sub', [(0, 1), (1, 0)])  12.4 us
    ppermute x8, starting transfers between devices, to_owner(): return lax.ppermute(value, 'pair', [(o, o ^ k) for o in range(owners)])  6.95 us
    pallas_call x1, Pallas kernels, make_weights(): pl.pallas_call(weights_kernel, in_specs=[vmem, vmem, vmem, smem, smem, vm...  3.52 us
    pallas_call x2, Pallas kernels, finish(): pl.pallas_call(kernel, in_specs=in_specs + [vmem] * len(pieces), out_spec...  3.36 us
    pallas_call x1, Pallas kernels, dress(): pl.pallas_call(functools.partial(dress_kernel, owners, rows, groups), in_...  2.1 us
    pallas_call x1, Pallas kernels, hold(): pl.pallas_call(hold_kernel, in_specs=[anywhere], out_specs=[anywhere, pl....  1.64 us
  transfers between devices with their start and end apart: 14, of which 7 were waited for; matrix products, arithmetic and copies ran while one was open for 0% of the time, Pallas kernels for 10%

profile of v13, /device:TPU:23, one launch (start us, length us, event | category | flops | bytes accessed | tf_op | source)
XLA Modules:
  0.0 60.6 jit_solution(10954248490904052301)
XLA Ops:
  0.0 0.0 copy-start
  0.0 0.0 copy-start.1
  0.0 0.0 copy-start.2
  0.0 0.2 collective-permute-start.1
  0.2 3.2 %collective-permute-start = (bf16[1,128,128]{2,1,0:T(8,128)(2,1)}, bf16[1,128,128]{2,1,0:T(8,128)(2,1)S(1)}, u32[]{:S(2)}, u32[]{:S(2)}) collective-permute-start(bf16[1,128,128]{2,1,0:T(8,128)(2,1)} %refs_0_.1), channel_id=1, source_target_pairs={{0,8},{4,12},{8,0},{12,4},{1,9},{5,13},{9,1},{13,5},{2,10},{6,14},... | collective-permute-start | bytes 98312 | tf_op jit(solution)/shard_map/ppermute | solution.py:412
  3.5 0.0 collective-permute-start.2
  3.5 0.1 pad_add_fusion.place_ref
  3.5 0.0 copy-start.3
  3.5 0.0 copy-start.4
  3.5 0.0 copy-start.7
  3.6 1.6 %shard_map.91 = (bf16[1,1,32,128,256]{4,3,2,1,0:T(8,128)(2,1)S(1)}, bf16[256,256]{1,0:T(8,128)(2,1)S(1)}) custom-call(bf16[1,1,32,128,256]{4,3,2,1,0:T(8,128)(2,1)} %lam_ref.1), custom_call_target="tpu_custom_call" | custom-call | bytes 4194304 | tf_op jit(solution)/shard_map/pallas_call | solution.py:154
  5.2 0.0 collective-permute-done.1.refs_2_
  5.2 0.1 collective-permute-done.refs_1_
  5.3 1.4 %collective-permute-done.2.refs_3_ = bf16[1,128,128]{2,1,0:T(8,128)(2,1)S(1)} collective-permute-done((bf16[1,128,128]{2,1,0:T(8,128)(2,1)}, bf16[1,128,128]{2,1,0:T(8,128)(2,1)S(1)}, u32[]{:S(2)}, u32[]{:S(2)}) %collective-permute-start.2) | collective-permute-done | bytes 32800 | tf_op jit(solution)/shard_map/ppermute | solution.py:412
  6.7 0.0 copy-done
  6.7 0.0 copy-done.1
  6.7 0.0 copy-done.2
  6.7 2.1 %shard_map.92 = (bf16[1,16,32,256]{3,2,1,0:T(8,128)(2,1)S(1)}, bf16[1,16,32,256]{3,2,1,0:T(8,128)(2,1)S(1)}, bf16[1,16,32,256]{3,2,1,0:T(8,128)(2,1)S(1)}, bf16[...) custom-call(s32[2]{0:T(128)S(1)} %pad_add_fusion.place_ref, ...), custom_call_target="tpu_custom_call" | custom-call | flops 268435456 | bytes 3145728 | tf_op jit(solution)/shard_map/pallas_call | solution.py:272
  8.8 0.1 collective-permute-start.5
  8.9 1.8 %collective-permute-start.3 = (bf16[2,16,32,256]{3,2,1,0:T(8,128)(2,1)S(1)}, bf16[2,16,32,256]{3,2,1,0:T(8,128)(2,1)S(1)}, u32[]{:S(2)}, u32[]{:S(2)}) collective-permute-start(bf16[2,16,32,256]{3,2,1,0:T(8,128)(2,1)S(1)} %get-tuple-element.29), channel_id=1, source_target_pairs={{0,4},{4,0},{8,12},{12,8},{1,5},{5,1},{9,13},{13,9},{2,6},{6,2},{1... | collective-permute-start | bytes 1572872 | tf_op jit(solution)/shard_map/ppermute | solution.py:412
  10.7 0.9 %collective-permute-start.4 = (bf16[1,16,32,256]{3,2,1,0:T(8,128)(2,1)S(1)}, bf16[1,16,32,256]{3,2,1,0:T(8,128)(2,1)S(1)}, u32[]{:S(2)}, u32[]{:S(2)}) collective-permute-start(bf16[1,16,32,256]{3,2,1,0:T(8,128)(2,1)S(1)} %get-tuple-element.30), channel_id=1, source_target_pairs={{0,8},{4,12},{8,0},{12,4},{1,9},{5,13},{9,1},{13,5},{2,10},{6,14},... | collective-permute-start | bytes 786440 | tf_op jit(solution)/shard_map/ppermute | solution.py:412
  11.6 0.0 copy-done.3
  11.6 0.0 copy-done.4
  11.6 0.0 copy-done.5
  11.6 0.0 copy-done.6
  11.6 0.0 copy-done.7
  11.6 3.5 %shard_map.93 = (bf16[128,256]{1,0:T(8,128)(2,1)S(1)}, f32[32,128,256]{2,1,0:T(8,128)S(1)}) custom-call(s32[2,256]{1,0:T(2,128)S(1)} %bitcast.6, f32[400,400]{1,0:T(8,128)S(1)} %copy-done.3, f32[4,1,32]{2,1,0:T(1,128)S(1)} %copy-done.5, s32[2]{0:T(128)S(1)} %pad_add_fusion.place_ref, f32[32]{0:T(128)S(1)} %copy-done.7, f32[1,256]{1,0:T(1,128)S(1)} %bitcast.7), custom_call_target="tpu_custom_call" | custom-call | flops 491520000 | bytes 640000 | tf_op jit(solution)/shard_map/pallas_call | solution.py:207
  15.1 6.9 %collective-permute-done.5.refs_3_ = bf16[1,16,32,256]{3,2,1,0:T(8,128)(2,1)S(1)} collective-permute-done((bf16[1,16,32,256]{3,2,1,0:T(8,128)(2,1)S(1)}, bf16[1,16,32,256]{3,2,1,0:T(8,128)(2,1)S(1)}, u32[]{:S(2)}, u32[]{:S(2)}) %collective-permute-start.5) | collective-permute-done | bytes 262176 | tf_op jit(solution)/shard_map/ppermute | solution.py:412
  22.0 2.1 %collective-permute-start.7 = (bf16[1,16,32,256]{3,2,1,0:T(8,128)(2,1)S(1)}, bf16[1,16,32,256]{3,2,1,0:T(8,128)(2,1)S(1)}, u32[]{:S(2)}, u32[]{:S(2)}) collective-permute-start(bf16[1,16,32,256]{3,2,1,0:T(8,128)(2,1)S(1)} %collective-permute-done.5.refs_3_), channel_id=1, source_target_pairs={{0,1},{1,0},{2,3},{3,2},{4,5},{5,4},{6,7},{7,6},{8,9},{9,8},{10,11... | collective-permute-start | bytes 786440 | tf_op jit(solution)/shard_map/ppermute | solution.py:415
  24.1 0.0 collective-permute-start.10
  24.1 0.8 %collective-permute-start.11 = (bf16[1,16,32,256]{3,2,1,0:T(8,128)(2,1)S(1)}, bf16[1,16,32,256]{3,2,1,0:T(8,128)(2,1)S(1)}, u32[]{:S(2)}, u32[]{:S(2)}) collective-permute-start(bf16[1,16,32,256]{3,2,1,0:T(8,128)(2,1)S(1)} %get-tuple-element.36), channel_id=1, source_target_pairs={{0,12},{4,8},{8,4},{12,0},{1,13},{5,9},{9,5},{13,1},{2,14},{6,10},... | collective-permute-start | bytes 786440 | tf_op jit(solution)/shard_map/ppermute | solution.py:412
  24.9 7.7 %collective-permute-done.4.refs_2_ = bf16[1,16,32,256]{3,2,1,0:T(8,128)(2,1)S(1)} collective-permute-done((bf16[1,16,32,256]{3,2,1,0:T(8,128)(2,1)S(1)}, bf16[1,16,32,256]{3,2,1,0:T(8,128)(2,1)S(1)}, u32[]{:S(2)}, u32[]{:S(2)}) %collective-permute-start.4) | collective-permute-done | bytes 262176 | tf_op jit(solution)/shard_map/ppermute | solution.py:412
  32.7 4.9 %collective-permute-start.9 = (bf16[1,16,32,256]{3,2,1,0:T(8,128)(2,1)S(1)}, bf16[1,16,32,256]{3,2,1,0:T(8,128)(2,1)S(1)}, u32[]{:S(2)}, u32[]{:S(2)}) collective-permute-start(bf16[1,16,32,256]{3,2,1,0:T(8,128)(2,1)S(1)} %collective-permute-done.4.refs_2_), channel_id=1, source_target_pairs={{0,1},{1,0},{2,3},{3,2},{4,5},{5,4},{6,7},{7,6},{8,9},{9,8},{10,11... | collective-permute-start | bytes 786440 | tf_op jit(solution)/shard_map/ppermute | solution.py:415
  37.6 0.0 collective-permute-done.3.refs_1_.refs_2_
  37.6 0.0 collective-permute-start.6
  37.6 0.0 collective-permute-done.7.refs_7_
  37.6 0.5 collective-permute-start.8
  38.1 9.1 %collective-permute-done.10.refs_3_ = bf16[1,16,32,256]{3,2,1,0:T(8,128)(2,1)S(1)} collective-permute-done((bf16[1,16,32,256]{3,2,1,0:T(8,128)(2,1)S(1)}, bf16[1,16,32,256]{3,2,1,0:T(8,128)(2,1)S(1)}, u32[]{:S(2)}, u32[]{:S(2)}) %collective-permute-start.10) | collective-permute-done | bytes 262176 | tf_op jit(solution)/shard_map/ppermute | solution.py:412
  47.2 0.0 collective-permute-done.9.refs_6_
  47.2 3.5 %collective-permute-start.12 = (bf16[1,16,32,256]{3,2,1,0:T(8,128)(2,1)S(1)}, bf16[1,16,32,256]{3,2,1,0:T(8,128)(2,1)S(1)}, u32[]{:S(2)}, u32[]{:S(2)}) collective-permute-start(bf16[1,16,32,256]{3,2,1,0:T(8,128)(2,1)S(1)} %collective-permute-done.10.refs_3_), channel_id=1, source_target_pairs={{0,1},{1,0},{2,3},{3,2},{4,5},{5,4},{6,7},{7,6},{8,9},{9,8},{10,11... | collective-permute-start | bytes 786440 | tf_op jit(solution)/shard_map/ppermute | solution.py:415
  50.7 5.0 %collective-permute-done.11.refs_4_ = bf16[1,16,32,256]{3,2,1,0:T(8,128)(2,1)S(1)} collective-permute-done((bf16[1,16,32,256]{3,2,1,0:T(8,128)(2,1)S(1)}, bf16[1,16,32,256]{3,2,1,0:T(8,128)(2,1)S(1)}, u32[]{:S(2)}, u32[]{:S(2)}) %collective-permute-start.11) | collective-permute-done | bytes 262176 | tf_op jit(solution)/shard_map/ppermute | solution.py:412
  55.7 1.3 %collective-permute-start.13 = (bf16[1,16,32,256]{3,2,1,0:T(8,128)(2,1)S(1)}, bf16[1,16,32,256]{3,2,1,0:T(8,128)(2,1)S(1)}, u32[]{:S(2)}, u32[]{:S(2)}) collective-permute-start(bf16[1,16,32,256]{3,2,1,0:T(8,128)(2,1)S(1)} %collective-permute-done.11.refs_4_), channel_id=1, source_target_pairs={{0,1},{1,0},{2,3},{3,2},{4,5},{5,4},{6,7},{7,6},{8,9},{9,8},{10,11... | collective-permute-start | bytes 786440 | tf_op jit(solution)/shard_map/ppermute | solution.py:415
  57.0 0.0 collective-permute-done.6.refs_4_.refs_5_
  57.0 0.0 collective-permute-done.8.refs_5_.refs_6_
  57.0 0.9 %shard_map.94.refs_0_ = bf16[8,16,16,256]{3,2,1,0:T(8,128)(2,1)S(1)} custom-call(bf16[256,256]{1,0:T(8,128)(2,1)S(1)} %get-tuple-element.22.refs_5_.swap_ref, bf16[128,256]{1,0:T(8,128)(2,1)S(1)} %get-tuple-element.26.w_ref, f32[32,128,256]{2,1,0:T(8,128)S(1)} %get-tuple-element.27.inverse_ref, ...), custom_call_target="tpu_custom_call" | custom-call | tf_op jit(solution)/shard_map/pallas_call | solution.py:381
  57.9 0.0 collective-permute-done.12.refs_7_
  57.9 0.2 collective-permute-done.13.refs_8_
  58.2 2.5 %shard_map.95 = bf16[4,1,32,32,256]{4,3,2,1,0:T(8,128)(2,1)} custom-call(bf16[256,256]{1,0:T(8,128)(2,1)S(1)} %get-tuple-element.22.refs_5_.swap_ref, bf16[128,256]{1,0:T(8,128)(2,1)S(1)} %get-tuple-element.26.w_ref, f32[32,128,256]{2,1,0:T(8,128)S(1)} %get-tuple-element.27.inverse_ref, s32[2]{0:T(128)S(1)} %pad_add_fusion.place_ref, ...), custom_call_target="tpu_custom_call" | custom-call | tf_op jit(solution)/shard_map/pallas_call | solution.py:381
  (2 shorter events, 0.0 us)
Async XLA Ops:
  0.0 6.7 %copy-start = (bf16[1,128,128]{2,1,0:T(8,128)(2,1)S(1)}, bf16[1,128,128]{2,1,0:T(8,128)(2,1)}, u32[]{:S(2)}) copy-start(bf16[1,128,128]{2,1,0:T(8,128)(2,1)} %refs_0_.1) | copy-start | bytes 98308
  0.0 6.7 %copy-start.1 = (s32[1,1,32,2]{2,3,1,0:T(2,128)S(1)}, s32[1,1,32,2]{2,3,1,0:T(2,128)}, u32[]{:S(2)}) copy-start(s32[1,1,32,2]{2,3,1,0:T(2,128)} %param.12) | copy-start | bytes 772
  0.0 6.7 %copy-start.2 = (s32[1,1,32]{2,1,0:T(1,128)S(1)}, s32[1,1,32]{2,1,0:T(1,128)}, u32[]{:S(2)}) copy-start(s32[1,1,32]{2,1,0:T(1,128)} %tile_of_ref.1) | copy-start | bytes 388
  0.0 5.2 %collective-permute-start.1 = (bf16[1,128,128]{2,1,0:T(8,128)(2,1)}, bf16[1,128,128]{2,1,0:T(8,128)(2,1)S(1)}, u32[]{:S(2)}, u32[]{:S(2)}) collective-permute-start(bf16[1,128,128]{2,1,0:T(8,128)(2,1)} %refs_0_.1), channel_id=1, source_target_pairs={{0,12},{4,8},{8,4},{12,0},{1,13},{5,9},{9,5},{13,1},{2,14},{6,10},... | collective-permute-start | bytes 98312 | tf_op jit(solution)/shard_map/ppermute | solution.py:412
  0.2 5.1 %collective-permute-start = (bf16[1,128,128]{2,1,0:T(8,128)(2,1)}, bf16[1,128,128]{2,1,0:T(8,128)(2,1)S(1)}, u32[]{:S(2)}, u32[]{:S(2)}) collective-permute-start(bf16[1,128,128]{2,1,0:T(8,128)(2,1)} %refs_0_.1), channel_id=1, source_target_pairs={{0,8},{4,12},{8,0},{12,4},{1,9},{5,13},{9,1},{13,5},{2,10},{6,14},... | collective-permute-start | bytes 98312 | tf_op jit(solution)/shard_map/ppermute | solution.py:412
  3.5 3.3 %collective-permute-start.2 = (bf16[1,128,128]{2,1,0:T(8,128)(2,1)}, bf16[1,128,128]{2,1,0:T(8,128)(2,1)S(1)}, u32[]{:S(2)}, u32[]{:S(2)}) collective-permute-start(bf16[1,128,128]{2,1,0:T(8,128)(2,1)} %refs_0_.1), channel_id=1, source_target_pairs={{0,4},{4,0},{8,12},{12,8},{1,5},{5,1},{9,13},{13,9},{2,6},{6,2},{1... | collective-permute-start | bytes 98312 | tf_op jit(solution)/shard_map/ppermute | solution.py:412
  3.5 8.0 %copy-start.3 = (f32[400,400]{1,0:T(8,128)S(1)}, f32[400,400]{1,0:T(8,128)}, u32[]{:S(2)}) copy-start(f32[400,400]{1,0:T(8,128)} %coupling_ref.1) | copy-start | bytes 1920004
  3.5 8.0 %copy-start.4 = (s32[256,2]{0,1:T(2,128)S(1)}, s32[256,2]{0,1:T(2,128)}, u32[]{:S(2)}) copy-start(s32[256,2]{0,1:T(2,128)} %param.13) | copy-start | bytes 6148
  3.5 8.0 %copy-start.5 = (f32[4,1,32]{2,1,0:T(1,128)S(1)}, f32[4,1,32]{2,1,0:T(1,128)}, u32[]{:S(2)}) copy-start(f32[4,1,32]{2,1,0:T(1,128)} %gap_ref.1) | copy-start | bytes 1540
  3.5 8.0 %copy-start.6 = (f32[256]{0:T(256)S(1)}, f32[256]{0:T(256)}, u32[]{:S(2)}) copy-start(f32[256]{0:T(256)} %param.17) | copy-start | bytes 3076
  3.5 8.0 %copy-start.7 = (f32[32]{0:T(128)S(1)}, f32[32]{0:T(128)}, u32[]{:S(2)}) copy-start(f32[32]{0:T(128)} %row_ref.1) | copy-start | bytes 388
  8.8 13.1 %collective-permute-start.5 = (bf16[1,16,32,256]{3,2,1,0:T(8,128)(2,1)S(1)}, bf16[1,16,32,256]{3,2,1,0:T(8,128)(2,1)S(1)}, u32[]{:S(2)}, u32[]{:S(2)}) collective-permute-start(bf16[1,16,32,256]{3,2,1,0:T(8,128)(2,1)S(1)} %get-tuple-element.24), channel_id=1, source_target_pairs={{0,12},{4,8},{8,4},{12,0},{1,13},{5,9},{9,5},{13,1},{2,14},{6,10},... | collective-permute-start | bytes 786440 | tf_op jit(solution)/shard_map/ppermute | solution.py:412
  8.9 28.7 %collective-permute-start.3 = (bf16[2,16,32,256]{3,2,1,0:T(8,128)(2,1)S(1)}, bf16[2,16,32,256]{3,2,1,0:T(8,128)(2,1)S(1)}, u32[]{:S(2)}, u32[]{:S(2)}) collective-permute-start(bf16[2,16,32,256]{3,2,1,0:T(8,128)(2,1)S(1)} %get-tuple-element.29), channel_id=1, source_target_pairs={{0,4},{4,0},{8,12},{12,8},{1,5},{5,1},{9,13},{13,9},{2,6},{6,2},{1... | collective-permute-start | bytes 1572872 | tf_op jit(solution)/shard_map/ppermute | solution.py:412
  10.7 21.9 %collective-permute-start.4 = (bf16[1,16,32,256]{3,2,1,0:T(8,128)(2,1)S(1)}, bf16[1,16,32,256]{3,2,1,0:T(8,128)(2,1)S(1)}, u32[]{:S(2)}, u32[]{:S(2)}) collective-permute-start(bf16[1,16,32,256]{3,2,1,0:T(8,128)(2,1)S(1)} %get-tuple-element.30), channel_id=1, source_target_pairs={{0,8},{4,12},{8,0},{12,4},{1,9},{5,13},{9,1},{13,5},{2,10},{6,14},... | collective-permute-start | bytes 786440 | tf_op jit(solution)/shard_map/ppermute | solution.py:412
  22.0 15.6 %collective-permute-start.7 = (bf16[1,16,32,256]{3,2,1,0:T(8,128)(2,1)S(1)}, bf16[1,16,32,256]{3,2,1,0:T(8,128)(2,1)S(1)}, u32[]{:S(2)}, u32[]{:S(2)}) collective-permute-start(bf16[1,16,32,256]{3,2,1,0:T(8,128)(2,1)S(1)} %collective-permute-done.5.refs_3_), channel_id=1, source_target_pairs={{0,1},{1,0},{2,3},{3,2},{4,5},{5,4},{6,7},{7,6},{8,9},{9,8},{10,11... | collective-permute-start | bytes 786440 | tf_op jit(solution)/shard_map/ppermute | solution.py:415
  24.1 23.0 %collective-permute-start.10 = (bf16[1,16,32,256]{3,2,1,0:T(8,128)(2,1)S(1)}, bf16[1,16,32,256]{3,2,1,0:T(8,128)(2,1)S(1)}, u32[]{:S(2)}, u32[]{:S(2)}) collective-permute-start(bf16[1,16,32,256]{3,2,1,0:T(8,128)(2,1)S(1)} %get-tuple-element.34), channel_id=1, source_target_pairs={{0,8},{4,12},{8,0},{12,4},{1,9},{5,13},{9,1},{13,5},{2,10},{6,14},... | collective-permute-start | bytes 786440 | tf_op jit(solution)/shard_map/ppermute | solution.py:412
  24.1 31.6 %collective-permute-start.11 = (bf16[1,16,32,256]{3,2,1,0:T(8,128)(2,1)S(1)}, bf16[1,16,32,256]{3,2,1,0:T(8,128)(2,1)S(1)}, u32[]{:S(2)}, u32[]{:S(2)}) collective-permute-start(bf16[1,16,32,256]{3,2,1,0:T(8,128)(2,1)S(1)} %get-tuple-element.36), channel_id=1, source_target_pairs={{0,12},{4,8},{8,4},{12,0},{1,13},{5,9},{9,5},{13,1},{2,14},{6,10},... | collective-permute-start | bytes 786440 | tf_op jit(solution)/shard_map/ppermute | solution.py:412
  32.7 14.5 %collective-permute-start.9 = (bf16[1,16,32,256]{3,2,1,0:T(8,128)(2,1)S(1)}, bf16[1,16,32,256]{3,2,1,0:T(8,128)(2,1)S(1)}, u32[]{:S(2)}, u32[]{:S(2)}) collective-permute-start(bf16[1,16,32,256]{3,2,1,0:T(8,128)(2,1)S(1)} %collective-permute-done.4.refs_2_), channel_id=1, source_target_pairs={{0,1},{1,0},{2,3},{3,2},{4,5},{5,4},{6,7},{7,6},{8,9},{9,8},{10,11... | collective-permute-start | bytes 786440 | tf_op jit(solution)/shard_map/ppermute | solution.py:415
  37.6 19.4 %collective-permute-start.6 = (bf16[2,16,32,256]{3,2,1,0:T(8,128)(2,1)S(1)}, bf16[2,16,32,256]{3,2,1,0:T(8,128)(2,1)S(1)}, u32[]{:S(2)}, u32[]{:S(2)}) collective-permute-start(bf16[2,16,32,256]{3,2,1,0:T(8,128)(2,1)S(1)} %get-tuple-element.31.refs_0_.refs_1_), channel_id=1, source_target_pairs={{0,1},{1,0},{2,3},{3,2},{4,5},{5,4},{6,7},{7,6},{8,9},{9,8},{10,11... | collective-permute-start | bytes 1572872 | tf_op jit(solution)/shard_map/ppermute | solution.py:415
  37.6 19.4 %collective-permute-start.8 = (bf16[2,16,32,256]{3,2,1,0:T(8,128)(2,1)S(1)}, bf16[2,16,32,256]{3,2,1,0:T(8,128)(2,1)S(1)}, u32[]{:S(2)}, u32[]{:S(2)}) collective-permute-start(bf16[2,16,32,256]{3,2,1,0:T(8,128)(2,1)S(1)} %collective-permute-done.3.refs_1_.refs_2_), channel_id=1, source_target_pairs={{0,1},{1,0},{2,3},{3,2},{4,5},{5,4},{6,7},{7,6},{8,9},{9,8},{10,11... | collective-permute-start | bytes 1572872 | tf_op jit(solution)/shard_map/ppermute | solution.py:415
  47.2 10.7 %collective-permute-start.12 = (bf16[1,16,32,256]{3,2,1,0:T(8,128)(2,1)S(1)}, bf16[1,16,32,256]{3,2,1,0:T(8,128)(2,1)S(1)}, u32[]{:S(2)}, u32[]{:S(2)}) collective-permute-start(bf16[1,16,32,256]{3,2,1,0:T(8,128)(2,1)S(1)} %collective-permute-done.10.refs_3_), channel_id=1, source_target_pairs={{0,1},{1,0},{2,3},{3,2},{4,5},{5,4},{6,7},{7,6},{8,9},{9,8},{10,11... | collective-permute-start | bytes 786440 | tf_op jit(solution)/shard_map/ppermute | solution.py:415
  55.7 2.4 %collective-permute-start.13 = (bf16[1,16,32,256]{3,2,1,0:T(8,128)(2,1)S(1)}, bf16[1,16,32,256]{3,2,1,0:T(8,128)(2,1)S(1)}, u32[]{:S(2)}, u32[]{:S(2)}) collective-permute-start(bf16[1,16,32,256]{3,2,1,0:T(8,128)(2,1)S(1)} %collective-permute-done.11.refs_4_), channel_id=1, source_target_pairs={{0,1},{1,0},{2,3},{3,2},{4,5},{5,4},{6,7},{7,6},{8,9},{9,8},{10,11... | collective-permute-start | bytes 786440 | tf_op jit(solution)/shard_map/ppermute | solution.py:415

commit v14 on v13

--- a/solution.py
+++ b/solution.py
@@ -420,7 +420,7 @@
     tiles = [integral_tiles] + [to_owner(integral_tiles, k) for k in range(1, owners)]
 
     far = list(range(2, owners))
-    last = far[-1]
+    lead, last = far[0], far[-1]
     groups = [((k, c),) for c in range(chunks) for k in far[::-1]]
     groups += [tuple((k, c) for c in range(chunks)) for k in (1, 0)]
     held, swap = hold(lambda_amps)
@@ -432,17 +432,17 @@
 
     @functools.cache
     def landed(k, c):
-        earlier = landed(k, c - 1) if c and k == last else None
+        earlier = landed(k, c - 1) if c and k == lead else None
         return to_owner(after(sent[((k, c),)], earlier), k)
 
     @functools.cache
     def passed(k, c):
-        earlier = passed(far[0], c - 1) if c else (weights, inverse) if k == last else None
+        earlier = passed(last, c - 1) if c else (weights, inverse) if k == lead else None
         return to_sibling(after(landed(k, c), earlier))
 
     @functools.cache
     def passed_whole(k):
-        return to_sibling(after(near, (weights, inverse, passed(last, 0))) if k else after(own, near))
+        return to_sibling(after(near, (weights, inverse, passed(lead, 0))) if k else after(own, near))
 
     chunk_pieces = []
     for c in range(chunks - 1, -1, -1):

time: 60.8 us -> 63.2 us (1.039)
  the two profiles are of different devices: /device:TPU:23 before, /device:TPU:0 now
where the time goes in v14:
time: 63.2 us; the launch traced here: 63.1 us
  waiting for transfers between devices  37.6 us (59%)
  starting transfers between devices  14.7 us (23%)
  Pallas kernels  10.6 us (17%)
    ppermute x8, waiting for transfers between devices, to_owner(): return lax.ppermute(value, 'pair', [(o, o ^ k) for o in range(owners)])  37.1 us
    ppermute x8, starting transfers between devices, to_owner(): return lax.ppermute(value, 'pair', [(o, o ^ k) for o in range(owners)])  13.7 us
    pallas_call x1, Pallas kernels, make_weights(): pl.pallas_call(weights_kernel, in_specs=[vmem, vmem, vmem, smem, smem, vm...  3.52 us
    pallas_call x2, Pallas kernels, finish(): pl.pallas_call(kernel, in_specs=in_specs + [vmem] * len(pieces), out_spec...  3.34 us
    pallas_call x1, Pallas kernels, dress(): pl.pallas_call(functools.partial(dress_kernel, owners, rows, groups), in_...  2.11 us
    pallas_call x1, Pallas kernels, hold(): pl.pallas_call(hold_kernel, in_specs=[anywhere], out_specs=[anywhere, pl....  1.64 us
  transfers between devices with their start and end apart: 14, of which 8 were waited for; matrix products, arithmetic and copies ran while one was open for 0% of the time, Pallas kernels for 10%

profile of v14, /device:TPU:0, one launch (start us, length us, event | category | flops | bytes accessed | tf_op | source)
XLA Modules:
  0.0 63.1 jit_solution(7498592187641950427)
XLA Ops:
  0.0 0.0 copy-start
  0.0 0.0 copy-start.1
  0.0 0.0 copy-start.2
  0.0 5.1 %collective-permute-start.1 = (bf16[1,128,128]{2,1,0:T(8,128)(2,1)}, bf16[1,128,128]{2,1,0:T(8,128)(2,1)S(1)}, u32[]{:S(2)}, u32[]{:S(2)}) collective-permute-start(bf16[1,128,128]{2,1,0:T(8,128)(2,1)} %refs_0_.1), channel_id=1, source_target_pairs={{0,12},{4,8},{8,4},{12,0},{1,13},{5,9},{9,5},{13,1},{2,14},{6,10},... | collective-permute-start | bytes 98312 | tf_op jit(solution)/shard_map/ppermute | solution.py:412
  5.1 0.0 collective-permute-start
  5.1 0.6 %collective-permute-start.2 = (bf16[1,128,128]{2,1,0:T(8,128)(2,1)}, bf16[1,128,128]{2,1,0:T(8,128)(2,1)S(1)}, u32[]{:S(2)}, u32[]{:S(2)}) collective-permute-start(bf16[1,128,128]{2,1,0:T(8,128)(2,1)} %refs_0_.1), channel_id=1, source_target_pairs={{0,4},{4,0},{8,12},{12,8},{1,5},{5,1},{9,13},{13,9},{2,6},{6,2},{1... | collective-permute-start | bytes 98312 | tf_op jit(solution)/shard_map/ppermute | solution.py:412
  5.8 0.1 pad_add_fusion.place_ref
  5.8 0.0 copy-start.3
  5.8 0.0 copy-start.4
  5.9 0.0 copy-start.7
  5.9 1.6 %shard_map.91 = (bf16[1,1,32,128,256]{4,3,2,1,0:T(8,128)(2,1)S(1)}, bf16[256,256]{1,0:T(8,128)(2,1)S(1)}) custom-call(bf16[1,1,32,128,256]{4,3,2,1,0:T(8,128)(2,1)} %lam_ref.1), custom_call_target="tpu_custom_call" | custom-call | bytes 4194304 | tf_op jit(solution)/shard_map/pallas_call | solution.py:154
  7.5 0.0 collective-permute-done.1.refs_2_
  7.5 2.6 %collective-permute-done.refs_1_ = bf16[1,128,128]{2,1,0:T(8,128)(2,1)S(1)} collective-permute-done((bf16[1,128,128]{2,1,0:T(8,128)(2,1)}, bf16[1,128,128]{2,1,0:T(8,128)(2,1)S(1)}, u32[]{:S(2)}, u32[]{:S(2)}) %collective-permute-start) | collective-permute-done | bytes 32800 | tf_op jit(solution)/shard_map/ppermute | solution.py:412
  10.1 0.0 collective-permute-done.2.refs_3_
  10.2 0.0 copy-done
  10.2 0.0 copy-done.1
  10.2 0.0 copy-done.2
  10.2 2.1 %shard_map.92 = (bf16[1,16,32,256]{3,2,1,0:T(8,128)(2,1)S(1)}, bf16[1,16,32,256]{3,2,1,0:T(8,128)(2,1)S(1)}, bf16[1,16,32,256]{3,2,1,0:T(8,128)(2,1)S(1)}, bf16[...) custom-call(s32[2]{0:T(128)S(1)} %pad_add_fusion.place_ref, ...), custom_call_target="tpu_custom_call" | custom-call | flops 268435456 | bytes 3145728 | tf_op jit(solution)/shard_map/pallas_call | solution.py:272
  12.3 2.1 %collective-permute-start.4 = (bf16[1,16,32,256]{3,2,1,0:T(8,128)(2,1)S(1)}, bf16[1,16,32,256]{3,2,1,0:T(8,128)(2,1)S(1)}, u32[]{:S(2)}, u32[]{:S(2)}) collective-permute-start(bf16[1,16,32,256]{3,2,1,0:T(8,128)(2,1)S(1)} %get-tuple-element.30), channel_id=1, source_target_pairs={{0,8},{4,12},{8,0},{12,4},{1,9},{5,13},{9,1},{13,5},{2,10},{6,14},... | collective-permute-start | bytes 786440 | tf_op jit(solution)/shard_map/ppermute | solution.py:412
  14.4 0.0 collective-permute-start.3
  14.4 2.3 %collective-permute-start.5 = (bf16[1,16,32,256]{3,2,1,0:T(8,128)(2,1)S(1)}, bf16[1,16,32,256]{3,2,1,0:T(8,128)(2,1)S(1)}, u32[]{:S(2)}, u32[]{:S(2)}) collective-permute-start(bf16[1,16,32,256]{3,2,1,0:T(8,128)(2,1)S(1)} %get-tuple-element.24), channel_id=1, source_target_pairs={{0,12},{4,8},{8,4},{12,0},{1,13},{5,9},{9,5},{13,1},{2,14},{6,10},... | collective-permute-start | bytes 786440 | tf_op jit(solution)/shard_map/ppermute | solution.py:412
  16.7 0.0 copy-done.3
  16.7 0.0 copy-done.4
  16.7 0.0 copy-done.5
  16.7 0.0 copy-done.6
  16.8 0.0 copy-done.7
  16.8 3.5 %shard_map.93 = (bf16[128,256]{1,0:T(8,128)(2,1)S(1)}, f32[32,128,256]{2,1,0:T(8,128)S(1)}) custom-call(s32[2,256]{1,0:T(2,128)S(1)} %bitcast.6, f32[400,400]{1,0:T(8,128)S(1)} %copy-done.3, f32[4,1,32]{2,1,0:T(1,128)S(1)} %copy-done.5, s32[2]{0:T(128)S(1)} %pad_add_fusion.place_ref, f32[32]{0:T(128)S(1)} %copy-done.7, f32[1,256]{1,0:T(1,128)S(1)} %bitcast.7), custom_call_target="tpu_custom_call" | custom-call | flops 491520000 | bytes 640000 | tf_op jit(solution)/shard_map/pallas_call | solution.py:207
  20.3 4.8 %collective-permute-done.4.refs_2_ = bf16[1,16,32,256]{3,2,1,0:T(8,128)(2,1)S(1)} collective-permute-done((bf16[1,16,32,256]{3,2,1,0:T(8,128)(2,1)S(1)}, bf16[1,16,32,256]{3,2,1,0:T(8,128)(2,1)S(1)}, u32[]{:S(2)}, u32[]{:S(2)}) %collective-permute-start.4) | collective-permute-done | bytes 262176 | tf_op jit(solution)/shard_map/ppermute | solution.py:412
  25.1 0.0 collective-permute-start.7
  25.1 3.4 %collective-permute-start.11 = (bf16[1,16,32,256]{3,2,1,0:T(8,128)(2,1)S(1)}, bf16[1,16,32,256]{3,2,1,0:T(8,128)(2,1)S(1)}, u32[]{:S(2)}, u32[]{:S(2)}) collective-permute-start(bf16[1,16,32,256]{3,2,1,0:T(8,128)(2,1)S(1)} %get-tuple-element.36), channel_id=1, source_target_pairs={{0,12},{4,8},{8,4},{12,0},{1,13},{5,9},{9,5},{13,1},{2,14},{6,10},... | collective-permute-start | bytes 786440 | tf_op jit(solution)/shard_map/ppermute | solution.py:412
  28.6 0.0 collective-permute-start.10
  28.6 10.2 %collective-permute-done.5.refs_3_ = bf16[1,16,32,256]{3,2,1,0:T(8,128)(2,1)S(1)} collective-permute-done((bf16[1,16,32,256]{3,2,1,0:T(8,128)(2,1)S(1)}, bf16[1,16,32,256]{3,2,1,0:T(8,128)(2,1)S(1)}, u32[]{:S(2)}, u32[]{:S(2)}) %collective-permute-start.5) | collective-permute-done | bytes 262176 | tf_op jit(solution)/shard_map/ppermute | solution.py:412
  38.7 0.0 collective-permute-start.9
  38.7 3.1 %collective-permute-done.3.refs_1_.refs_2_ = bf16[2,16,32,256]{3,2,1,0:T(8,128)(2,1)S(1)} collective-permute-done((bf16[2,16,32,256]{3,2,1,0:T(8,128)(2,1)S(1)}, bf16[2,16,32,256]{3,2,1,0:T(8,128)(2,1)S(1)}, u32[]{:S(2)}, u32[]{:S(2)}) %collective-permute-start.3) | collective-permute-done | bytes 524320 | tf_op jit(solution)/shard_map/ppermute | solution.py:412
  41.9 0.0 collective-permute-start.6
  41.9 0.0 collective-permute-done.7.refs_6_
  41.9 0.5 collective-permute-start.8
  42.4 1.9 %collective-permute-done.11.refs_4_ = bf16[1,16,32,256]{3,2,1,0:T(8,128)(2,1)S(1)} collective-permute-done((bf16[1,16,32,256]{3,2,1,0:T(8,128)(2,1)S(1)}, bf16[1,16,32,256]{3,2,1,0:T(8,128)(2,1)S(1)}, u32[]{:S(2)}, u32[]{:S(2)}) %collective-permute-start.11) | collective-permute-done | bytes 262176 | tf_op jit(solution)/shard_map/ppermute | solution.py:412
  44.3 0.0 collective-permute-done.9.refs_7_
  44.3 14.4 %collective-permute-done.10.refs_3_ = bf16[1,16,32,256]{3,2,1,0:T(8,128)(2,1)S(1)} collective-permute-done((bf16[1,16,32,256]{3,2,1,0:T(8,128)(2,1)S(1)}, bf16[1,16,32,256]{3,2,1,0:T(8,128)(2,1)S(1)}, u32[]{:S(2)}, u32[]{:S(2)}) %collective-permute-start.10) | collective-permute-done | bytes 262176 | tf_op jit(solution)/shard_map/ppermute | solution.py:412
  58.7 0.0 collective-permute-start.12
  58.8 0.5 collective-permute-start.13
  59.3 0.0 collective-permute-done.6.refs_4_.refs_5_
  59.3 0.0 collective-permute-done.8.refs_5_.refs_6_
  59.3 0.9 %shard_map.94.refs_0_ = bf16[8,16,16,256]{3,2,1,0:T(8,128)(2,1)S(1)} custom-call(bf16[256,256]{1,0:T(8,128)(2,1)S(1)} %get-tuple-element.22.refs_5_.swap_ref, bf16[128,256]{1,0:T(8,128)(2,1)S(1)} %get-tuple-element.26.w_ref, f32[32,128,256]{2,1,0:T(8,128)S(1)} %get-tuple-element.27.inverse_ref, ...), custom_call_target="tpu_custom_call" | custom-call | tf_op jit(solution)/shard_map/pallas_call | solution.py:381
  60.2 0.1 collective-permute-done.12.refs_7_
  60.3 0.4 collective-permute-done.13.refs_8_
  60.7 2.4 %shard_map.95 = bf16[4,1,32,32,256]{4,3,2,1,0:T(8,128)(2,1)} custom-call(bf16[256,256]{1,0:T(8,128)(2,1)S(1)} %get-tuple-element.22.refs_5_.swap_ref, bf16[128,256]{1,0:T(8,128)(2,1)S(1)} %get-tuple-element.26.w_ref, f32[32,128,256]{2,1,0:T(8,128)S(1)} %get-tuple-element.27.inverse_ref, s32[2]{0:T(128)S(1)} %pad_add_fusion.place_ref, ...), custom_call_target="tpu_custom_call" | custom-call | tf_op jit(solution)/shard_map/pallas_call | solution.py:381
  (2 shorter events, 0.0 us)
Async XLA Ops:
  0.0 10.2 %copy-start = (bf16[1,128,128]{2,1,0:T(8,128)(2,1)S(1)}, bf16[1,128,128]{2,1,0:T(8,128)(2,1)}, u32[]{:S(2)}) copy-start(bf16[1,128,128]{2,1,0:T(8,128)(2,1)} %refs_0_.1) | copy-start | bytes 98308
  0.0 10.2 %copy-start.1 = (s32[1,1,32,2]{2,3,1,0:T(2,128)S(1)}, s32[1,1,32,2]{2,3,1,0:T(2,128)}, u32[]{:S(2)}) copy-start(s32[1,1,32,2]{2,3,1,0:T(2,128)} %param.12) | copy-start | bytes 772
  0.0 10.2 %copy-start.2 = (s32[1,1,32]{2,1,0:T(1,128)S(1)}, s32[1,1,32]{2,1,0:T(1,128)}, u32[]{:S(2)}) copy-start(s32[1,1,32]{2,1,0:T(1,128)} %tile_of_ref.1) | copy-start | bytes 388
  0.0 7.5 %collective-permute-start.1 = (bf16[1,128,128]{2,1,0:T(8,128)(2,1)}, bf16[1,128,128]{2,1,0:T(8,128)(2,1)S(1)}, u32[]{:S(2)}, u32[]{:S(2)}) collective-permute-start(bf16[1,128,128]{2,1,0:T(8,128)(2,1)} %refs_0_.1), channel_id=1, source_target_pairs={{0,12},{4,8},{8,4},{12,0},{1,13},{5,9},{9,5},{13,1},{2,14},{6,10},... | collective-permute-start | bytes 98312 | tf_op jit(solution)/shard_map/ppermute | solution.py:412
  5.1 5.0 %collective-permute-start = (bf16[1,128,128]{2,1,0:T(8,128)(2,1)}, bf16[1,128,128]{2,1,0:T(8,128)(2,1)S(1)}, u32[]{:S(2)}, u32[]{:S(2)}) collective-permute-start(bf16[1,128,128]{2,1,0:T(8,128)(2,1)} %refs_0_.1), channel_id=1, source_target_pairs={{0,8},{4,12},{8,0},{12,4},{1,9},{5,13},{9,1},{13,5},{2,10},{6,14},... | collective-permute-start | bytes 98312 | tf_op jit(solution)/shard_map/ppermute | solution.py:412
  5.1 5.0 %collective-permute-start.2 = (bf16[1,128,128]{2,1,0:T(8,128)(2,1)}, bf16[1,128,128]{2,1,0:T(8,128)(2,1)S(1)}, u32[]{:S(2)}, u32[]{:S(2)}) collective-permute-start(bf16[1,128,128]{2,1,0:T(8,128)(2,1)} %refs_0_.1), channel_id=1, source_target_pairs={{0,4},{4,0},{8,12},{12,8},{1,5},{5,1},{9,13},{13,9},{2,6},{6,2},{1... | collective-permute-start | bytes 98312 | tf_op jit(solution)/shard_map/ppermute | solution.py:412
  5.8 10.9 %copy-start.3 = (f32[400,400]{1,0:T(8,128)S(1)}, f32[400,400]{1,0:T(8,128)}, u32[]{:S(2)}) copy-start(f32[400,400]{1,0:T(8,128)} %coupling_ref.1) | copy-start | bytes 1920004
  5.8 10.9 %copy-start.4 = (s32[256,2]{0,1:T(2,128)S(1)}, s32[256,2]{0,1:T(2,128)}, u32[]{:S(2)}) copy-start(s32[256,2]{0,1:T(2,128)} %param.13) | copy-start | bytes 6148
  5.8 10.9 %copy-start.5 = (f32[4,1,32]{2,1,0:T(1,128)S(1)}, f32[4,1,32]{2,1,0:T(1,128)}, u32[]{:S(2)}) copy-start(f32[4,1,32]{2,1,0:T(1,128)} %gap_ref.1) | copy-start | bytes 1540
  5.8 10.9 %copy-start.6 = (f32[256]{0:T(256)S(1)}, f32[256]{0:T(256)}, u32[]{:S(2)}) copy-start(f32[256]{0:T(256)} %param.17) | copy-start | bytes 3076
  5.9 10.9 %copy-start.7 = (f32[32]{0:T(128)S(1)}, f32[32]{0:T(128)}, u32[]{:S(2)}) copy-start(f32[32]{0:T(128)} %row_ref.1) | copy-start | bytes 388
  12.3 12.8 %collective-permute-start.4 = (bf16[1,16,32,256]{3,2,1,0:T(8,128)(2,1)S(1)}, bf16[1,16,32,256]{3,2,1,0:T(8,128)(2,1)S(1)}, u32[]{:S(2)}, u32[]{:S(2)}) collective-permute-start(bf16[1,16,32,256]{3,2,1,0:T(8,128)(2,1)S(1)} %get-tuple-element.30), channel_id=1, source_target_pairs={{0,8},{4,12},{8,0},{12,4},{1,9},{5,13},{9,1},{13,5},{2,10},{6,14},... | collective-permute-start | bytes 786440 | tf_op jit(solution)/shard_map/ppermute | solution.py:412
  14.4 27.5 %collective-permute-start.3 = (bf16[2,16,32,256]{3,2,1,0:T(8,128)(2,1)S(1)}, bf16[2,16,32,256]{3,2,1,0:T(8,128)(2,1)S(1)}, u32[]{:S(2)}, u32[]{:S(2)}) collective-permute-start(bf16[2,16,32,256]{3,2,1,0:T(8,128)(2,1)S(1)} %get-tuple-element.29), channel_id=1, source_target_pairs={{0,4},{4,0},{8,12},{12,8},{1,5},{5,1},{9,13},{13,9},{2,6},{6,2},{1... | collective-permute-start | bytes 1572872 | tf_op jit(solution)/shard_map/ppermute | solution.py:412
  14.4 24.3 %collective-permute-start.5 = (bf16[1,16,32,256]{3,2,1,0:T(8,128)(2,1)S(1)}, bf16[1,16,32,256]{3,2,1,0:T(8,128)(2,1)S(1)}, u32[]{:S(2)}, u32[]{:S(2)}) collective-permute-start(bf16[1,16,32,256]{3,2,1,0:T(8,128)(2,1)S(1)} %get-tuple-element.24), channel_id=1, source_target_pairs={{0,12},{4,8},{8,4},{12,0},{1,13},{5,9},{9,5},{13,1},{2,14},{6,10},... | collective-permute-start | bytes 786440 | tf_op jit(solution)/shard_map/ppermute | solution.py:412
  25.1 16.8 %collective-permute-start.7 = (bf16[1,16,32,256]{3,2,1,0:T(8,128)(2,1)S(1)}, bf16[1,16,32,256]{3,2,1,0:T(8,128)(2,1)S(1)}, u32[]{:S(2)}, u32[]{:S(2)}) collective-permute-start(bf16[1,16,32,256]{3,2,1,0:T(8,128)(2,1)S(1)} %collective-permute-done.4.refs_2_), channel_id=1, source_target_pairs={{0,1},{1,0},{2,3},{3,2},{4,5},{5,4},{6,7},{7,6},{8,9},{9,8},{10,11... | collective-permute-start | bytes 786440 | tf_op jit(solution)/shard_map/ppermute | solution.py:415
  25.1 19.2 %collective-permute-start.11 = (bf16[1,16,32,256]{3,2,1,0:T(8,128)(2,1)S(1)}, bf16[1,16,32,256]{3,2,1,0:T(8,128)(2,1)S(1)}, u32[]{:S(2)}, u32[]{:S(2)}) collective-permute-start(bf16[1,16,32,256]{3,2,1,0:T(8,128)(2,1)S(1)} %get-tuple-element.36), channel_id=1, source_target_pairs={{0,12},{4,8},{8,4},{12,0},{1,13},{5,9},{9,5},{13,1},{2,14},{6,10},... | collective-permute-start | bytes 786440 | tf_op jit(solution)/shard_map/ppermute | solution.py:412
  28.6 30.2 %collective-permute-start.10 = (bf16[1,16,32,256]{3,2,1,0:T(8,128)(2,1)S(1)}, bf16[1,16,32,256]{3,2,1,0:T(8,128)(2,1)S(1)}, u32[]{:S(2)}, u32[]{:S(2)}) collective-permute-start(bf16[1,16,32,256]{3,2,1,0:T(8,128)(2,1)S(1)} %get-tuple-element.35), channel_id=1, source_target_pairs={{0,8},{4,12},{8,0},{12,4},{1,9},{5,13},{9,1},{13,5},{2,10},{6,14},... | collective-permute-start | bytes 786440 | tf_op jit(solution)/shard_map/ppermute | solution.py:412
  38.7 5.6 %collective-permute-start.9 = (bf16[1,16,32,256]{3,2,1,0:T(8,128)(2,1)S(1)}, bf16[1,16,32,256]{3,2,1,0:T(8,128)(2,1)S(1)}, u32[]{:S(2)}, u32[]{:S(2)}) collective-permute-start(bf16[1,16,32,256]{3,2,1,0:T(8,128)(2,1)S(1)} %collective-permute-done.5.refs_3_), channel_id=1, source_target_pairs={{0,1},{1,0},{2,3},{3,2},{4,5},{5,4},{6,7},{7,6},{8,9},{9,8},{10,11... | collective-permute-start | bytes 786440 | tf_op jit(solution)/shard_map/ppermute | solution.py:415
  41.9 17.4 %collective-permute-start.6 = (bf16[2,16,32,256]{3,2,1,0:T(8,128)(2,1)S(1)}, bf16[2,16,32,256]{3,2,1,0:T(8,128)(2,1)S(1)}, u32[]{:S(2)}, u32[]{:S(2)}) collective-permute-start(bf16[2,16,32,256]{3,2,1,0:T(8,128)(2,1)S(1)} %get-tuple-element.31.refs_0_.refs_1_), channel_id=1, source_target_pairs={{0,1},{1,0},{2,3},{3,2},{4,5},{5,4},{6,7},{7,6},{8,9},{9,8},{10,11... | collective-permute-start | bytes 1572872 | tf_op jit(solution)/shard_map/ppermute | solution.py:415
  41.9 17.4 %collective-permute-start.8 = (bf16[2,16,32,256]{3,2,1,0:T(8,128)(2,1)S(1)}, bf16[2,16,32,256]{3,2,1,0:T(8,128)(2,1)S(1)}, u32[]{:S(2)}, u32[]{:S(2)}) collective-permute-start(bf16[2,16,32,256]{3,2,1,0:T(8,128)(2,1)S(1)} %collective-permute-done.3.refs_1_.refs_2_), channel_id=1, source_target_pairs={{0,1},{1,0},{2,3},{3,2},{4,5},{5,4},{6,7},{7,6},{8,9},{9,8},{10,11... | collective-permute-start | bytes 1572872 | tf_op jit(solution)/shard_map/ppermute | solution.py:415
  58.7 1.5 %collective-permute-start.12 = (bf16[1,16,32,256]{3,2,1,0:T(8,128)(2,1)S(1)}, bf16[1,16,32,256]{3,2,1,0:T(8,128)(2,1)S(1)}, u32[]{:S(2)}, u32[]{:S(2)}) collective-permute-start(bf16[1,16,32,256]{3,2,1,0:T(8,128)(2,1)S(1)} %collective-permute-done.10.refs_3_), channel_id=1, source_target_pairs={{0,1},{1,0},{2,3},{3,2},{4,5},{5,4},{6,7},{7,6},{8,9},{9,8},{10,11... | collective-permute-start | bytes 786440 | tf_op jit(solution)/shard_map/ppermute | solution.py:415
  58.8 1.9 %collective-permute-start.13 = (bf16[1,16,32,256]{3,2,1,0:T(8,128)(2,1)S(1)}, bf16[1,16,32,256]{3,2,1,0:T(8,128)(2,1)S(1)}, u32[]{:S(2)}, u32[]{:S(2)}) collective-permute-start(bf16[1,16,32,256]{3,2,1,0:T(8,128)(2,1)S(1)} %collective-permute-done.11.refs_4_), channel_id=1, source_target_pairs={{0,1},{1,0},{2,3},{3,2},{4,5},{5,4},{6,7},{7,6},{8,9},{9,8},{10,11... | collective-permute-start | bytes 786440 | tf_op jit(solution)/shard_map/ppermute | solution.py:415

commit v15 on v13

--- a/solution.py
+++ b/solution.py
@@ -432,7 +432,9 @@
 
     @functools.cache
     def landed(k, c):
-        earlier = landed(k, c - 1) if c and k == last else None
+        earlier = None
+        if c:
+            earlier = landed(k, c - 1) if k == last else passed(last, c - 1)
         return to_owner(after(sent[((k, c),)], earlier), k)
 
     @functools.cache

time: 60.8 us -> 62.7 us (1.031)
  the two profiles are of different devices: /device:TPU:23 before, /device:TPU:0 now
where the time goes in v15:
time: 62.7 us; the launch traced here: 62.6 us
  waiting for transfers between devices  36.1 us (58%)
  starting transfers between devices  15.6 us (25%)
  Pallas kernels  10.6 us (17%)
    ppermute x8, waiting for transfers between devices, to_owner(): return lax.ppermute(value, 'pair', [(o, o ^ k) for o in range(owners)])  35.5 us
    ppermute x8, starting transfers between devices, to_owner(): return lax.ppermute(value, 'pair', [(o, o ^ k) for o in range(owners)])  15.1 us
    pallas_call x1, Pallas kernels, make_weights(): pl.pallas_call(weights_kernel, in_specs=[vmem, vmem, vmem, smem, smem, vm...  3.52 us
    pallas_call x2, Pallas kernels, finish(): pl.pallas_call(kernel, in_specs=in_specs + [vmem] * len(pieces), out_spec...  3.34 us
    pallas_call x1, Pallas kernels, dress(): pl.pallas_call(functools.partial(dress_kernel, owners, rows, groups), in_...  2.11 us
    pallas_call x1, Pallas kernels, hold(): pl.pallas_call(hold_kernel, in_specs=[anywhere], out_specs=[anywhere, pl....  1.64 us
  transfers between devices with their start and end apart: 14, of which 6 were waited for; matrix products, arithmetic and copies ran while one was open for 0% of the time, Pallas kernels for 10%

profile of v15, /device:TPU:0, one launch (start us, length us, event | category | flops | bytes accessed | tf_op | source)
XLA Modules:
  0.0 62.6 jit_solution(14114180833464108911)
XLA Ops:
  0.0 0.0 copy-start
  0.0 0.0 copy-start.1
  0.0 0.0 copy-start.2
  0.0 5.1 %collective-permute-start.1 = (bf16[1,128,128]{2,1,0:T(8,128)(2,1)}, bf16[1,128,128]{2,1,0:T(8,128)(2,1)S(1)}, u32[]{:S(2)}, u32[]{:S(2)}) collective-permute-start(bf16[1,128,128]{2,1,0:T(8,128)(2,1)} %refs_0_.1), channel_id=1, source_target_pairs={{0,12},{4,8},{8,4},{12,0},{1,13},{5,9},{9,5},{13,1},{2,14},{6,10},... | collective-permute-start | bytes 98312 | tf_op jit(solution)/shard_map/ppermute | solution.py:412
  5.1 0.0 collective-permute-start
  5.1 0.6 %collective-permute-start.2 = (bf16[1,128,128]{2,1,0:T(8,128)(2,1)}, bf16[1,128,128]{2,1,0:T(8,128)(2,1)S(1)}, u32[]{:S(2)}, u32[]{:S(2)}) collective-permute-start(bf16[1,128,128]{2,1,0:T(8,128)(2,1)} %refs_0_.1), channel_id=1, source_target_pairs={{0,4},{4,0},{8,12},{12,8},{1,5},{5,1},{9,13},{13,9},{2,6},{6,2},{1... | collective-permute-start | bytes 98312 | tf_op jit(solution)/shard_map/ppermute | solution.py:412
  5.8 0.1 pad_add_fusion.place_ref
  5.8 0.0 copy-start.3
  5.8 0.0 copy-start.4
  5.9 0.0 copy-start.7
  5.9 1.6 %shard_map.91 = (bf16[1,1,32,128,256]{4,3,2,1,0:T(8,128)(2,1)S(1)}, bf16[256,256]{1,0:T(8,128)(2,1)S(1)}) custom-call(bf16[1,1,32,128,256]{4,3,2,1,0:T(8,128)(2,1)} %lam_ref.1), custom_call_target="tpu_custom_call" | custom-call | bytes 4194304 | tf_op jit(solution)/shard_map/pallas_call | solution.py:154
  7.5 0.0 collective-permute-done.1.refs_2_
  7.5 2.6 %collective-permute-done.refs_1_ = bf16[1,128,128]{2,1,0:T(8,128)(2,1)S(1)} collective-permute-done((bf16[1,128,128]{2,1,0:T(8,128)(2,1)}, bf16[1,128,128]{2,1,0:T(8,128)(2,1)S(1)}, u32[]{:S(2)}, u32[]{:S(2)}) %collective-permute-start) | collective-permute-done | bytes 32800 | tf_op jit(solution)/shard_map/ppermute | solution.py:412
  10.1 0.0 collective-permute-done.2.refs_3_
  10.2 0.0 copy-done
  10.2 0.0 copy-done.1
  10.2 0.0 copy-done.2
  10.2 2.1 %shard_map.92 = (bf16[1,16,32,256]{3,2,1,0:T(8,128)(2,1)S(1)}, bf16[1,16,32,256]{3,2,1,0:T(8,128)(2,1)S(1)}, bf16[1,16,32,256]{3,2,1,0:T(8,128)(2,1)S(1)}, bf16[...) custom-call(s32[2]{0:T(128)S(1)} %pad_add_fusion.place_ref, ...), custom_call_target="tpu_custom_call" | custom-call | flops 268435456 | bytes 3145728 | tf_op jit(solution)/shard_map/pallas_call | solution.py:272
  12.3 1.5 %collective-permute-start.5 = (bf16[1,16,32,256]{3,2,1,0:T(8,128)(2,1)S(1)}, bf16[1,16,32,256]{3,2,1,0:T(8,128)(2,1)S(1)}, u32[]{:S(2)}, u32[]{:S(2)}) collective-permute-start(bf16[1,16,32,256]{3,2,1,0:T(8,128)(2,1)S(1)} %get-tuple-element.25), channel_id=1, source_target_pairs={{0,12},{4,8},{8,4},{12,0},{1,13},{5,9},{9,5},{13,1},{2,14},{6,10},... | collective-permute-start | bytes 786440 | tf_op jit(solution)/shard_map/ppermute | solution.py:412
  13.8 1.1 %collective-permute-start.3 = (bf16[2,16,32,256]{3,2,1,0:T(8,128)(2,1)S(1)}, bf16[2,16,32,256]{3,2,1,0:T(8,128)(2,1)S(1)}, u32[]{:S(2)}, u32[]{:S(2)}) collective-permute-start(bf16[2,16,32,256]{3,2,1,0:T(8,128)(2,1)S(1)} %get-tuple-element.30), channel_id=1, source_target_pairs={{0,4},{4,0},{8,12},{12,8},{1,5},{5,1},{9,13},{13,9},{2,6},{6,2},{1... | collective-permute-start | bytes 1572872 | tf_op jit(solution)/shard_map/ppermute | solution.py:412
  14.9 1.8 %collective-permute-start.4 = (bf16[1,16,32,256]{3,2,1,0:T(8,128)(2,1)S(1)}, bf16[1,16,32,256]{3,2,1,0:T(8,128)(2,1)S(1)}, u32[]{:S(2)}, u32[]{:S(2)}) collective-permute-start(bf16[1,16,32,256]{3,2,1,0:T(8,128)(2,1)S(1)} %get-tuple-element.31), channel_id=1, source_target_pairs={{0,8},{4,12},{8,0},{12,4},{1,9},{5,13},{9,1},{13,5},{2,10},{6,14},... | collective-permute-start | bytes 786440 | tf_op jit(solution)/shard_map/ppermute | solution.py:412
  16.7 0.0 copy-done.3
  16.7 0.0 copy-done.4
  16.7 0.0 copy-done.5
  16.7 0.0 copy-done.6
  16.8 0.0 copy-done.7
  16.8 3.5 %shard_map.93 = (bf16[128,256]{1,0:T(8,128)(2,1)S(1)}, f32[32,128,256]{2,1,0:T(8,128)S(1)}) custom-call(s32[2,256]{1,0:T(2,128)S(1)} %bitcast.6, f32[400,400]{1,0:T(8,128)S(1)} %copy-done.3, f32[4,1,32]{2,1,0:T(1,128)S(1)} %copy-done.5, s32[2]{0:T(128)S(1)} %pad_add_fusion.place_ref, f32[32]{0:T(128)S(1)} %copy-done.7, f32[1,256]{1,0:T(1,128)S(1)} %bitcast.7), custom_call_target="tpu_custom_call" | custom-call | flops 491520000 | bytes 640000 | tf_op jit(solution)/shard_map/pallas_call | solution.py:207
  20.3 3.1 %collective-permute-done.5.refs_3_ = bf16[1,16,32,256]{3,2,1,0:T(8,128)(2,1)S(1)} collective-permute-done((bf16[1,16,32,256]{3,2,1,0:T(8,128)(2,1)S(1)}, bf16[1,16,32,256]{3,2,1,0:T(8,128)(2,1)S(1)}, u32[]{:S(2)}, u32[]{:S(2)}) %collective-permute-start.5) | collective-permute-done | bytes 262176 | tf_op jit(solution)/shard_map/ppermute | solution.py:412
  23.4 0.0 collective-permute-start.7
  23.4 1.5 %collective-permute-start.11 = (bf16[1,16,32,256]{3,2,1,0:T(8,128)(2,1)S(1)}, bf16[1,16,32,256]{3,2,1,0:T(8,128)(2,1)S(1)}, u32[]{:S(2)}, u32[]{:S(2)}) collective-permute-start(bf16[1,16,32,256]{3,2,1,0:T(8,128)(2,1)S(1)} %get-tuple-element.38), channel_id=1, source_target_pairs={{0,12},{4,8},{8,4},{12,0},{1,13},{5,9},{9,5},{13,1},{2,14},{6,10},... | collective-permute-start | bytes 786440 | tf_op jit(solution)/shard_map/ppermute | solution.py:412
  24.9 12.6 %collective-permute-done.4.refs_2_ = bf16[1,16,32,256]{3,2,1,0:T(8,128)(2,1)S(1)} collective-permute-done((bf16[1,16,32,256]{3,2,1,0:T(8,128)(2,1)S(1)}, bf16[1,16,32,256]{3,2,1,0:T(8,128)(2,1)S(1)}, u32[]{:S(2)}, u32[]{:S(2)}) %collective-permute-start.4) | collective-permute-done | bytes 262176 | tf_op jit(solution)/shard_map/ppermute | solution.py:412
  37.5 0.0 collective-permute-start.9
  37.5 0.0 collective-permute-done.7.refs_7_
  37.5 3.4 %collective-permute-start.10 = (bf16[1,16,32,256]{3,2,1,0:T(8,128)(2,1)S(1)}, bf16[1,16,32,256]{3,2,1,0:T(8,128)(2,1)S(1)}, u32[]{:S(2)}, u32[]{:S(2)}) collective-permute-start(bf16[1,16,32,256]{3,2,1,0:T(8,128)(2,1)S(1)} %get-tuple-element.36), channel_id=1, source_target_pairs={{0,8},{4,12},{8,0},{12,4},{1,9},{5,13},{9,1},{13,5},{2,10},{6,14},... | collective-permute-start | bytes 786440 | tf_op jit(solution)/shard_map/ppermute | solution.py:412
  40.9 0.0 collective-permute-done.3.refs_1_.refs_2_
  40.9 0.2 collective-permute-start.6
  41.2 0.3 collective-permute-start.8
  41.4 0.0 collective-permute-done.9.refs_6_
  41.5 1.9 %collective-permute-done.11.refs_4_ = bf16[1,16,32,256]{3,2,1,0:T(8,128)(2,1)S(1)} collective-permute-done((bf16[1,16,32,256]{3,2,1,0:T(8,128)(2,1)S(1)}, bf16[1,16,32,256]{3,2,1,0:T(8,128)(2,1)S(1)}, u32[]{:S(2)}, u32[]{:S(2)}) %collective-permute-start.11) | collective-permute-done | bytes 262176 | tf_op jit(solution)/shard_map/ppermute | solution.py:412
  43.4 0.0 collective-permute-start.13
  43.4 15.2 %collective-permute-done.10.refs_3_ = bf16[1,16,32,256]{3,2,1,0:T(8,128)(2,1)S(1)} collective-permute-done((bf16[1,16,32,256]{3,2,1,0:T(8,128)(2,1)S(1)}, bf16[1,16,32,256]{3,2,1,0:T(8,128)(2,1)S(1)}, u32[]{:S(2)}, u32[]{:S(2)}) %collective-permute-start.10) | collective-permute-done | bytes 262176 | tf_op jit(solution)/shard_map/ppermute | solution.py:412
  58.6 0.0 collective-permute-start.12
  58.6 0.0 collective-permute-done.6.refs_4_.refs_5_
  58.6 0.0 collective-permute-done.8.refs_5_.refs_6_
  58.6 0.9 %shard_map.94.refs_0_ = bf16[8,16,16,256]{3,2,1,0:T(8,128)(2,1)S(1)} custom-call(bf16[256,256]{1,0:T(8,128)(2,1)S(1)} %get-tuple-element.23.refs_5_.swap_ref, bf16[128,256]{1,0:T(8,128)(2,1)S(1)} %get-tuple-element.27.w_ref, f32[32,128,256]{2,1,0:T(8,128)S(1)} %get-tuple-element.28.inverse_ref, ...), custom_call_target="tpu_custom_call" | custom-call | tf_op jit(solution)/shard_map/pallas_call | solution.py:381
  59.5 0.0 collective-permute-done.13.refs_8_
  59.5 0.6 collective-permute-done.12.refs_7_
  60.1 2.4 %shard_map.95 = bf16[4,1,32,32,256]{4,3,2,1,0:T(8,128)(2,1)} custom-call(bf16[256,256]{1,0:T(8,128)(2,1)S(1)} %get-tuple-element.23.refs_5_.swap_ref, bf16[128,256]{1,0:T(8,128)(2,1)S(1)} %get-tuple-element.27.w_ref, f32[32,128,256]{2,1,0:T(8,128)S(1)} %get-tuple-element.28.inverse_ref, s32[2]{0:T(128)S(1)} %pad_add_fusion.place_ref, ...), custom_call_target="tpu_custom_call" | custom-call | tf_op jit(solution)/shard_map/pallas_call | solution.py:381
  (2 shorter events, 0.0 us)
Async XLA Ops:
  0.0 10.2 %copy-start = (bf16[1,128,128]{2,1,0:T(8,128)(2,1)S(1)}, bf16[1,128,128]{2,1,0:T(8,128)(2,1)}, u32[]{:S(2)}) copy-start(bf16[1,128,128]{2,1,0:T(8,128)(2,1)} %refs_0_.1) | copy-start | bytes 98308
  0.0 10.2 %copy-start.1 = (s32[1,1,32,2]{2,3,1,0:T(2,128)S(1)}, s32[1,1,32,2]{2,3,1,0:T(2,128)}, u32[]{:S(2)}) copy-start(s32[1,1,32,2]{2,3,1,0:T(2,128)} %param.12) | copy-start | bytes 772
  0.0 10.2 %copy-start.2 = (s32[1,1,32]{2,1,0:T(1,128)S(1)}, s32[1,1,32]{2,1,0:T(1,128)}, u32[]{:S(2)}) copy-start(s32[1,1,32]{2,1,0:T(1,128)} %tile_of_ref.1) | copy-start | bytes 388
  0.0 7.5 %collective-permute-start.1 = (bf16[1,128,128]{2,1,0:T(8,128)(2,1)}, bf16[1,128,128]{2,1,0:T(8,128)(2,1)S(1)}, u32[]{:S(2)}, u32[]{:S(2)}) collective-permute-start(bf16[1,128,128]{2,1,0:T(8,128)(2,1)} %refs_0_.1), channel_id=1, source_target_pairs={{0,12},{4,8},{8,4},{12,0},{1,13},{5,9},{9,5},{13,1},{2,14},{6,10},... | collective-permute-start | bytes 98312 | tf_op jit(solution)/shard_map/ppermute | solution.py:412
  5.1 5.0 %collective-permute-start = (bf16[1,128,128]{2,1,0:T(8,128)(2,1)}, bf16[1,128,128]{2,1,0:T(8,128)(2,1)S(1)}, u32[]{:S(2)}, u32[]{:S(2)}) collective-permute-start(bf16[1,128,128]{2,1,0:T(8,128)(2,1)} %refs_0_.1), channel_id=1, source_target_pairs={{0,8},{4,12},{8,0},{12,4},{1,9},{5,13},{9,1},{13,5},{2,10},{6,14},... | collective-permute-start | bytes 98312 | tf_op jit(solution)/shard_map/ppermute | solution.py:412
  5.1 5.0 %collective-permute-start.2 = (bf16[1,128,128]{2,1,0:T(8,128)(2,1)}, bf16[1,128,128]{2,1,0:T(8,128)(2,1)S(1)}, u32[]{:S(2)}, u32[]{:S(2)}) collective-permute-start(bf16[1,128,128]{2,1,0:T(8,128)(2,1)} %refs_0_.1), channel_id=1, source_target_pairs={{0,4},{4,0},{8,12},{12,8},{1,5},{5,1},{9,13},{13,9},{2,6},{6,2},{1... | collective-permute-start | bytes 98312 | tf_op jit(solution)/shard_map/ppermute | solution.py:412
  5.8 10.9 %copy-start.3 = (f32[400,400]{1,0:T(8,128)S(1)}, f32[400,400]{1,0:T(8,128)}, u32[]{:S(2)}) copy-start(f32[400,400]{1,0:T(8,128)} %coupling_ref.1) | copy-start | bytes 1920004
  5.8 10.9 %copy-start.4 = (s32[256,2]{0,1:T(2,128)S(1)}, s32[256,2]{0,1:T(2,128)}, u32[]{:S(2)}) copy-start(s32[256,2]{0,1:T(2,128)} %param.13) | copy-start | bytes 6148
  5.8 10.9 %copy-start.5 = (f32[4,1,32]{2,1,0:T(1,128)S(1)}, f32[4,1,32]{2,1,0:T(1,128)}, u32[]{:S(2)}) copy-start(f32[4,1,32]{2,1,0:T(1,128)} %gap_ref.1) | copy-start | bytes 1540
  5.8 10.9 %copy-start.6 = (f32[256]{0:T(256)S(1)}, f32[256]{0:T(256)}, u32[]{:S(2)}) copy-start(f32[256]{0:T(256)} %param.17) | copy-start | bytes 3076
  5.9 10.9 %copy-start.7 = (f32[32]{0:T(128)S(1)}, f32[32]{0:T(128)}, u32[]{:S(2)}) copy-start(f32[32]{0:T(128)} %row_ref.1) | copy-start | bytes 388
  12.3 11.1 %collective-permute-start.5 = (bf16[1,16,32,256]{3,2,1,0:T(8,128)(2,1)S(1)}, bf16[1,16,32,256]{3,2,1,0:T(8,128)(2,1)S(1)}, u32[]{:S(2)}, u32[]{:S(2)}) collective-permute-start(bf16[1,16,32,256]{3,2,1,0:T(8,128)(2,1)S(1)} %get-tuple-element.25), channel_id=1, source_target_pairs={{0,12},{4,8},{8,4},{12,0},{1,13},{5,9},{9,5},{13,1},{2,14},{6,10},... | collective-permute-start | bytes 786440 | tf_op jit(solution)/shard_map/ppermute | solution.py:412
  13.8 27.1 %collective-permute-start.3 = (bf16[2,16,32,256]{3,2,1,0:T(8,128)(2,1)S(1)}, bf16[2,16,32,256]{3,2,1,0:T(8,128)(2,1)S(1)}, u32[]{:S(2)}, u32[]{:S(2)}) collective-permute-start(bf16[2,16,32,256]{3,2,1,0:T(8,128)(2,1)S(1)} %get-tuple-element.30), channel_id=1, source_target_pairs={{0,4},{4,0},{8,12},{12,8},{1,5},{5,1},{9,13},{13,9},{2,6},{6,2},{1... | collective-permute-start | bytes 1572872 | tf_op jit(solution)/shard_map/ppermute | solution.py:412
  14.9 22.6 %collective-permute-start.4 = (bf16[1,16,32,256]{3,2,1,0:T(8,128)(2,1)S(1)}, bf16[1,16,32,256]{3,2,1,0:T(8,128)(2,1)S(1)}, u32[]{:S(2)}, u32[]{:S(2)}) collective-permute-start(bf16[1,16,32,256]{3,2,1,0:T(8,128)(2,1)S(1)} %get-tuple-element.31), channel_id=1, source_target_pairs={{0,8},{4,12},{8,0},{12,4},{1,9},{5,13},{9,1},{13,5},{2,10},{6,14},... | collective-permute-start | bytes 786440 | tf_op jit(solution)/shard_map/ppermute | solution.py:412
  23.4 14.1 %collective-permute-start.7 = (bf16[1,16,32,256]{3,2,1,0:T(8,128)(2,1)S(1)}, bf16[1,16,32,256]{3,2,1,0:T(8,128)(2,1)S(1)}, u32[]{:S(2)}, u32[]{:S(2)}) collective-permute-start(bf16[1,16,32,256]{3,2,1,0:T(8,128)(2,1)S(1)} %collective-permute-done.5.refs_3_), channel_id=1, source_target_pairs={{0,1},{1,0},{2,3},{3,2},{4,5},{5,4},{6,7},{7,6},{8,9},{9,8},{10,11... | collective-permute-start | bytes 786440 | tf_op jit(solution)/shard_map/ppermute | solution.py:415
  23.4 20.0 %collective-permute-start.11 = (bf16[1,16,32,256]{3,2,1,0:T(8,128)(2,1)S(1)}, bf16[1,16,32,256]{3,2,1,0:T(8,128)(2,1)S(1)}, u32[]{:S(2)}, u32[]{:S(2)}) collective-permute-start(bf16[1,16,32,256]{3,2,1,0:T(8,128)(2,1)S(1)} %get-tuple-element.38), channel_id=1, source_target_pairs={{0,12},{4,8},{8,4},{12,0},{1,13},{5,9},{9,5},{13,1},{2,14},{6,10},... | collective-permute-start | bytes 786440 | tf_op jit(solution)/shard_map/ppermute | solution.py:412
  37.5 4.0 %collective-permute-start.9 = (bf16[1,16,32,256]{3,2,1,0:T(8,128)(2,1)S(1)}, bf16[1,16,32,256]{3,2,1,0:T(8,128)(2,1)S(1)}, u32[]{:S(2)}, u32[]{:S(2)}) collective-permute-start(bf16[1,16,32,256]{3,2,1,0:T(8,128)(2,1)S(1)} %collective-permute-done.4.refs_2_), channel_id=1, source_target_pairs={{0,1},{1,0},{2,3},{3,2},{4,5},{5,4},{6,7},{7,6},{8,9},{9,8},{10,11... | collective-permute-start | bytes 786440 | tf_op jit(solution)/shard_map/ppermute | solution.py:415
  37.5 21.1 %collective-permute-start.10 = (bf16[1,16,32,256]{3,2,1,0:T(8,128)(2,1)S(1)}, bf16[1,16,32,256]{3,2,1,0:T(8,128)(2,1)S(1)}, u32[]{:S(2)}, u32[]{:S(2)}) collective-permute-start(bf16[1,16,32,256]{3,2,1,0:T(8,128)(2,1)S(1)} %get-tuple-element.36), channel_id=1, source_target_pairs={{0,8},{4,12},{8,0},{12,4},{1,9},{5,13},{9,1},{13,5},{2,10},{6,14},... | collective-permute-start | bytes 786440 | tf_op jit(solution)/shard_map/ppermute | solution.py:412
  40.9 17.6 %collective-permute-start.6 = (bf16[2,16,32,256]{3,2,1,0:T(8,128)(2,1)S(1)}, bf16[2,16,32,256]{3,2,1,0:T(8,128)(2,1)S(1)}, u32[]{:S(2)}, u32[]{:S(2)}) collective-permute-start(bf16[2,16,32,256]{3,2,1,0:T(8,128)(2,1)S(1)} %get-tuple-element.32.refs_0_.refs_1_), channel_id=1, source_target_pairs={{0,1},{1,0},{2,3},{3,2},{4,5},{5,4},{6,7},{7,6},{8,9},{9,8},{10,11... | collective-permute-start | bytes 1572872 | tf_op jit(solution)/shard_map/ppermute | solution.py:415
  41.2 17.4 %collective-permute-start.8 = (bf16[2,16,32,256]{3,2,1,0:T(8,128)(2,1)S(1)}, bf16[2,16,32,256]{3,2,1,0:T(8,128)(2,1)S(1)}, u32[]{:S(2)}, u32[]{:S(2)}) collective-permute-start(bf16[2,16,32,256]{3,2,1,0:T(8,128)(2,1)S(1)} %collective-permute-done.3.refs_1_.refs_2_), channel_id=1, source_target_pairs={{0,1},{1,0},{2,3},{3,2},{4,5},{5,4},{6,7},{7,6},{8,9},{9,8},{10,11... | collective-permute-start | bytes 1572872 | tf_op jit(solution)/shard_map/ppermute | solution.py:415
  43.4 16.1 %collective-permute-start.13 = (bf16[1,16,32,256]{3,2,1,0:T(8,128)(2,1)S(1)}, bf16[1,16,32,256]{3,2,1,0:T(8,128)(2,1)S(1)}, u32[]{:S(2)}, u32[]{:S(2)}) collective-permute-start(bf16[1,16,32,256]{3,2,1,0:T(8,128)(2,1)S(1)} %collective-permute-done.11.refs_4_), channel_id=1, source_target_pairs={{0,1},{1,0},{2,3},{3,2},{4,5},{5,4},{6,7},{7,6},{8,9},{9,8},{10,11... | collective-permute-start | bytes 786440 | tf_op jit(solution)/shard_map/ppermute | solution.py:415
  58.6 1.5 %collective-permute-start.12 = (bf16[1,16,32,256]{3,2,1,0:T(8,128)(2,1)S(1)}, bf16[1,16,32,256]{3,2,1,0:T(8,128)(2,1)S(1)}, u32[]{:S(2)}, u32[]{:S(2)}) collective-permute-start(bf16[1,16,32,256]{3,2,1,0:T(8,128)(2,1)S(1)} %collective-permute-done.10.refs_3_), channel_id=1, source_target_pairs={{0,1},{1,0},{2,3},{3,2},{4,5},{5,4},{6,7},{7,6},{8,9},{9,8},{10,11... | collective-permute-start | bytes 786440 | tf_op jit(solution)/shard_map/ppermute | solution.py:415

commit v16 on v13

--- a/solution.py
+++ b/solution.py
@@ -299,28 +299,32 @@
     )
 
 
-def finish_blocks(indices, chunk, swap_ref, w_ref, inverse_ref, piece_refs, done, ys, then):
+def finish_blocks(indices, chunk, swap_ref, w_ref, inverse_ref, piece_refs, done, ys, then, turns):
     groups, _, rows, _ = done.shape
-    mine = groups * ROWS
-    weights = w_ref[...]
-    for a in range(rows):
-        amps = jnp.concatenate([ref[index, a] for ref, index in zip(piece_refs, indices)], axis=0)
-        cycle = jnp.dot(weights, amps, preferred_element_type=jnp.float32)
-        total = amps[:mine].astype(jnp.float32) + cycle
-        value = (total * inverse_ref[chunk * rows + a]).astype(jnp.bfloat16)
-        for g in range(groups):
-            ys[g, pl.ds(a * ROWS, ROWS), :] = value[g * ROWS : (g + 1) * ROWS]
     swap = swap_ref[...]
-    for g in range(groups):
-        turned = jnp.dot(swap, ys[g], preferred_element_type=jnp.float32)
-        done[g] = turned.astype(jnp.bfloat16).reshape(done.shape[1:])
-        then(g)
+    share = groups // turns
+    for turn in range(turns):
+        mine = slice(turn * share * ROWS, (turn + 1) * share * ROWS)
+        weights = w_ref[mine, :]
+        for a in range(rows):
+            amps = jnp.concatenate(
+                [ref[index, a] for ref, index in zip(piece_refs, indices)], axis=0
+            )
+            cycle = jnp.dot(weights, amps, preferred_element_type=jnp.float32)
+            total = amps[mine].astype(jnp.float32) + cycle
+            value = (total * inverse_ref[chunk * rows + a, mine, :]).astype(jnp.bfloat16)
+            for g in range(share):
+                ys[turn * share + g, pl.ds(a * ROWS, ROWS), :] = value[g * ROWS : (g + 1) * ROWS]
+        for g in range(turn * share, (turn + 1) * share):
+            turned = jnp.dot(swap, ys[g], preferred_element_type=jnp.float32)
+            done[g] = turned.astype(jnp.bfloat16).reshape(done.shape[1:])
+            then(g)
 
 
 def early_kernel(indices, chunk, swap_ref, w_ref, inverse_ref, *refs):
     piece_refs, (done, ys) = refs[:-2], refs[-2:]
     finish_blocks(
-        indices, chunk, swap_ref, w_ref, inverse_ref, piece_refs, done, ys, lambda g: None
+        indices, chunk, swap_ref, w_ref, inverse_ref, piece_refs, done, ys, lambda g: None, 1
     )
 
 
@@ -354,6 +358,7 @@
         done,
         ys,
         lambda g: write(done, chunk, g),
+        2,
     )
     for copy in leaving:
         copy.wait()

time: 60.8 us -> 61.1 us (level)
  the two profiles are of different devices: /device:TPU:23 before, /device:TPU:17 now
where the time goes in v16:
time: 61.1 us; the launch traced here: 61 us
  waiting for transfers between devices  30.5 us (50%)
  starting transfers between devices  19.3 us (32%)
  Pallas kernels  10.9 us (18%)
    ppermute x8, waiting for transfers between devices, to_owner(): return lax.ppermute(value, 'pair', [(o, o ^ k) for o in range(owners)])  30.2 us
    ppermute x6, starting transfers between devices, to_sibling(): return lax.ppermute(value, 'sub', [(0, 1), (1, 0)])  12.4 us
    ppermute x8, starting transfers between devices, to_owner(): return lax.ppermute(value, 'pair', [(o, o ^ k) for o in range(owners)])  6.94 us
    pallas_call x2, Pallas kernels, finish(): pl.pallas_call(kernel, in_specs=in_specs + [vmem] * len(pieces), out_spec...  3.68 us
    pallas_call x1, Pallas kernels, make_weights(): pl.pallas_call(weights_kernel, in_specs=[vmem, vmem, vmem, smem, smem, vm...  3.52 us
    pallas_call x1, Pallas kernels, dress(): pl.pallas_call(functools.partial(dress_kernel, owners, rows, groups), in_...  2.1 us
    pallas_call x1, Pallas kernels, hold(): pl.pallas_call(hold_kernel, in_specs=[anywhere], out_specs=[anywhere, pl....  1.64 us
  transfers between devices with their start and end apart: 14, of which 7 were waited for; matrix products, arithmetic and copies ran while one was open for 0% of the time, Pallas kernels for 10%

profile of v16, /device:TPU:17, one launch (start us, length us, event | category | flops | bytes accessed | tf_op | source)
XLA Modules:
  0.0 61.0 jit_solution(17896132961981357442)
XLA Ops:
  0.0 0.0 copy-start
  0.0 0.0 copy-start.1
  0.0 0.0 copy-start.2
  0.0 0.2 collective-permute-start.1
  0.2 3.2 %collective-permute-start = (bf16[1,128,128]{2,1,0:T(8,128)(2,1)}, bf16[1,128,128]{2,1,0:T(8,128)(2,1)S(1)}, u32[]{:S(2)}, u32[]{:S(2)}) collective-permute-start(bf16[1,128,128]{2,1,0:T(8,128)(2,1)} %refs_0_.1), channel_id=1, source_target_pairs={{0,8},{4,12},{8,0},{12,4},{1,9},{5,13},{9,1},{13,5},{2,10},{6,14},... | collective-permute-start | bytes 98312 | tf_op jit(solution)/shard_map/ppermute | solution.py:417
  3.5 0.0 collective-permute-start.2
  3.5 0.1 pad_add_fusion.place_ref
  3.5 0.0 copy-start.3
  3.5 0.0 copy-start.4
  3.5 0.0 copy-start.7
  3.6 1.6 %shard_map.91 = (bf16[1,1,32,128,256]{4,3,2,1,0:T(8,128)(2,1)S(1)}, bf16[256,256]{1,0:T(8,128)(2,1)S(1)}) custom-call(bf16[1,1,32,128,256]{4,3,2,1,0:T(8,128)(2,1)} %lam_ref.1), custom_call_target="tpu_custom_call" | custom-call | bytes 4194304 | tf_op jit(solution)/shard_map/pallas_call | solution.py:154
  5.2 0.0 collective-permute-done.1.refs_2_
  5.2 0.1 collective-permute-done.refs_1_
  5.4 1.4 %collective-permute-done.2.refs_3_ = bf16[1,128,128]{2,1,0:T(8,128)(2,1)S(1)} collective-permute-done((bf16[1,128,128]{2,1,0:T(8,128)(2,1)}, bf16[1,128,128]{2,1,0:T(8,128)(2,1)S(1)}, u32[]{:S(2)}, u32[]{:S(2)}) %collective-permute-start.2) | collective-permute-done | bytes 32800 | tf_op jit(solution)/shard_map/ppermute | solution.py:417
  6.7 0.0 copy-done
  6.7 0.0 copy-done.1
  6.7 0.0 copy-done.2
  6.7 2.1 %shard_map.92 = (bf16[1,16,32,256]{3,2,1,0:T(8,128)(2,1)S(1)}, bf16[1,16,32,256]{3,2,1,0:T(8,128)(2,1)S(1)}, bf16[1,16,32,256]{3,2,1,0:T(8,128)(2,1)S(1)}, bf16[...) custom-call(s32[2]{0:T(128)S(1)} %pad_add_fusion.place_ref, ...), custom_call_target="tpu_custom_call" | custom-call | flops 268435456 | bytes 3145728 | tf_op jit(solution)/shard_map/pallas_call | solution.py:272
  8.8 0.1 collective-permute-start.5
  8.9 1.8 %collective-permute-start.3 = (bf16[2,16,32,256]{3,2,1,0:T(8,128)(2,1)S(1)}, bf16[2,16,32,256]{3,2,1,0:T(8,128)(2,1)S(1)}, u32[]{:S(2)}, u32[]{:S(2)}) collective-permute-start(bf16[2,16,32,256]{3,2,1,0:T(8,128)(2,1)S(1)} %get-tuple-element.29), channel_id=1, source_target_pairs={{0,4},{4,0},{8,12},{12,8},{1,5},{5,1},{9,13},{13,9},{2,6},{6,2},{1... | collective-permute-start | bytes 1572872 | tf_op jit(solution)/shard_map/ppermute | solution.py:417
  10.7 0.8 %collective-permute-start.4 = (bf16[1,16,32,256]{3,2,1,0:T(8,128)(2,1)S(1)}, bf16[1,16,32,256]{3,2,1,0:T(8,128)(2,1)S(1)}, u32[]{:S(2)}, u32[]{:S(2)}) collective-permute-start(bf16[1,16,32,256]{3,2,1,0:T(8,128)(2,1)S(1)} %get-tuple-element.30), channel_id=1, source_target_pairs={{0,8},{4,12},{8,0},{12,4},{1,9},{5,13},{9,1},{13,5},{2,10},{6,14},... | collective-permute-start | bytes 786440 | tf_op jit(solution)/shard_map/ppermute | solution.py:417
  11.6 0.0 copy-done.3
  11.6 0.0 copy-done.4
  11.6 0.0 copy-done.5
  11.6 0.0 copy-done.6
  11.6 0.0 copy-done.7
  11.6 3.5 %shard_map.93 = (bf16[128,256]{1,0:T(8,128)(2,1)S(1)}, f32[32,128,256]{2,1,0:T(8,128)S(1)}) custom-call(s32[2,256]{1,0:T(2,128)S(1)} %bitcast.6, f32[400,400]{1,0:T(8,128)S(1)} %copy-done.3, f32[4,1,32]{2,1,0:T(1,128)S(1)} %copy-done.5, s32[2]{0:T(128)S(1)} %pad_add_fusion.place_ref, f32[32]{0:T(128)S(1)} %copy-done.7, f32[1,256]{1,0:T(1,128)S(1)} %bitcast.7), custom_call_target="tpu_custom_call" | custom-call | flops 491520000 | bytes 640000 | tf_op jit(solution)/shard_map/pallas_call | solution.py:207
  15.1 6.8 %collective-permute-done.5.refs_3_ = bf16[1,16,32,256]{3,2,1,0:T(8,128)(2,1)S(1)} collective-permute-done((bf16[1,16,32,256]{3,2,1,0:T(8,128)(2,1)S(1)}, bf16[1,16,32,256]{3,2,1,0:T(8,128)(2,1)S(1)}, u32[]{:S(2)}, u32[]{:S(2)}) %collective-permute-start.5) | collective-permute-done | bytes 262176 | tf_op jit(solution)/shard_map/ppermute | solution.py:417
  21.9 2.2 %collective-permute-start.7 = (bf16[1,16,32,256]{3,2,1,0:T(8,128)(2,1)S(1)}, bf16[1,16,32,256]{3,2,1,0:T(8,128)(2,1)S(1)}, u32[]{:S(2)}, u32[]{:S(2)}) collective-permute-start(bf16[1,16,32,256]{3,2,1,0:T(8,128)(2,1)S(1)} %collective-permute-done.5.refs_3_), channel_id=1, source_target_pairs={{0,1},{1,0},{2,3},{3,2},{4,5},{5,4},{6,7},{7,6},{8,9},{9,8},{10,11... | collective-permute-start | bytes 786440 | tf_op jit(solution)/shard_map/ppermute | solution.py:420
  24.1 0.0 collective-permute-start.10
  24.1 0.8 %collective-permute-start.11 = (bf16[1,16,32,256]{3,2,1,0:T(8,128)(2,1)S(1)}, bf16[1,16,32,256]{3,2,1,0:T(8,128)(2,1)S(1)}, u32[]{:S(2)}, u32[]{:S(2)}) collective-permute-start(bf16[1,16,32,256]{3,2,1,0:T(8,128)(2,1)S(1)} %get-tuple-element.36), channel_id=1, source_target_pairs={{0,12},{4,8},{8,4},{12,0},{1,13},{5,9},{9,5},{13,1},{2,14},{6,10},... | collective-permute-start | bytes 786440 | tf_op jit(solution)/shard_map/ppermute | solution.py:417
  24.9 7.8 %collective-permute-done.4.refs_2_ = bf16[1,16,32,256]{3,2,1,0:T(8,128)(2,1)S(1)} collective-permute-done((bf16[1,16,32,256]{3,2,1,0:T(8,128)(2,1)S(1)}, bf16[1,16,32,256]{3,2,1,0:T(8,128)(2,1)S(1)}, u32[]{:S(2)}, u32[]{:S(2)}) %collective-permute-start.4) | collective-permute-done | bytes 262176 | tf_op jit(solution)/shard_map/ppermute | solution.py:417
  32.7 4.9 %collective-permute-start.9 = (bf16[1,16,32,256]{3,2,1,0:T(8,128)(2,1)S(1)}, bf16[1,16,32,256]{3,2,1,0:T(8,128)(2,1)S(1)}, u32[]{:S(2)}, u32[]{:S(2)}) collective-permute-start(bf16[1,16,32,256]{3,2,1,0:T(8,128)(2,1)S(1)} %collective-permute-done.4.refs_2_), channel_id=1, source_target_pairs={{0,1},{1,0},{2,3},{3,2},{4,5},{5,4},{6,7},{7,6},{8,9},{9,8},{10,11... | collective-permute-start | bytes 786440 | tf_op jit(solution)/shard_map/ppermute | solution.py:420
  37.6 0.0 collective-permute-done.3.refs_1_.refs_2_
  37.6 0.0 collective-permute-start.6
  37.6 0.0 collective-permute-done.7.refs_7_
  37.6 0.5 collective-permute-start.8
  38.1 9.1 %collective-permute-done.10.refs_3_ = bf16[1,16,32,256]{3,2,1,0:T(8,128)(2,1)S(1)} collective-permute-done((bf16[1,16,32,256]{3,2,1,0:T(8,128)(2,1)S(1)}, bf16[1,16,32,256]{3,2,1,0:T(8,128)(2,1)S(1)}, u32[]{:S(2)}, u32[]{:S(2)}) %collective-permute-start.10) | collective-permute-done | bytes 262176 | tf_op jit(solution)/shard_map/ppermute | solution.py:417
  47.2 0.0 collective-permute-done.9.refs_6_
  47.2 3.5 %collective-permute-start.12 = (bf16[1,16,32,256]{3,2,1,0:T(8,128)(2,1)S(1)}, bf16[1,16,32,256]{3,2,1,0:T(8,128)(2,1)S(1)}, u32[]{:S(2)}, u32[]{:S(2)}) collective-permute-start(bf16[1,16,32,256]{3,2,1,0:T(8,128)(2,1)S(1)} %collective-permute-done.10.refs_3_), channel_id=1, source_target_pairs={{0,1},{1,0},{2,3},{3,2},{4,5},{5,4},{6,7},{7,6},{8,9},{9,8},{10,11... | collective-permute-start | bytes 786440 | tf_op jit(solution)/shard_map/ppermute | solution.py:420
  50.7 5.0 %collective-permute-done.11.refs_4_ = bf16[1,16,32,256]{3,2,1,0:T(8,128)(2,1)S(1)} collective-permute-done((bf16[1,16,32,256]{3,2,1,0:T(8,128)(2,1)S(1)}, bf16[1,16,32,256]{3,2,1,0:T(8,128)(2,1)S(1)}, u32[]{:S(2)}, u32[]{:S(2)}) %collective-permute-start.11) | collective-permute-done | bytes 262176 | tf_op jit(solution)/shard_map/ppermute | solution.py:417
  55.7 1.3 %collective-permute-start.13 = (bf16[1,16,32,256]{3,2,1,0:T(8,128)(2,1)S(1)}, bf16[1,16,32,256]{3,2,1,0:T(8,128)(2,1)S(1)}, u32[]{:S(2)}, u32[]{:S(2)}) collective-permute-start(bf16[1,16,32,256]{3,2,1,0:T(8,128)(2,1)S(1)} %collective-permute-done.11.refs_4_), channel_id=1, source_target_pairs={{0,1},{1,0},{2,3},{3,2},{4,5},{5,4},{6,7},{7,6},{8,9},{9,8},{10,11... | collective-permute-start | bytes 786440 | tf_op jit(solution)/shard_map/ppermute | solution.py:420
  57.0 0.0 collective-permute-done.6.refs_4_.refs_5_
  57.0 0.0 collective-permute-done.8.refs_5_.refs_6_
  57.0 0.9 %shard_map.94.refs_0_ = bf16[8,16,16,256]{3,2,1,0:T(8,128)(2,1)S(1)} custom-call(bf16[256,256]{1,0:T(8,128)(2,1)S(1)} %get-tuple-element.22.refs_5_.swap_ref, bf16[128,256]{1,0:T(8,128)(2,1)S(1)} %get-tuple-element.26.w_ref, f32[32,128,256]{2,1,0:T(8,128)S(1)} %get-tuple-element.27.inverse_ref, ...), custom_call_target="tpu_custom_call" | custom-call | tf_op jit(solution)/shard_map/pallas_call | solution.py:386
  57.9 0.0 collective-permute-done.12.refs_7_
  57.9 0.2 collective-permute-done.13.refs_8_
  58.2 2.8 %shard_map.95 = bf16[4,1,32,32,256]{4,3,2,1,0:T(8,128)(2,1)} custom-call(bf16[256,256]{1,0:T(8,128)(2,1)S(1)} %get-tuple-element.22.refs_5_.swap_ref, bf16[128,256]{1,0:T(8,128)(2,1)S(1)} %get-tuple-element.26.w_ref, f32[32,128,256]{2,1,0:T(8,128)S(1)} %get-tuple-element.27.inverse_ref, s32[2]{0:T(128)S(1)} %pad_add_fusion.place_ref, ...), custom_call_target="tpu_custom_call" | custom-call | tf_op jit(solution)/shard_map/pallas_call | solution.py:386
  (2 shorter events, 0.0 us)
Async XLA Ops:
  0.0 6.7 %copy-start = (bf16[1,128,128]{2,1,0:T(8,128)(2,1)S(1)}, bf16[1,128,128]{2,1,0:T(8,128)(2,1)}, u32[]{:S(2)}) copy-start(bf16[1,128,128]{2,1,0:T(8,128)(2,1)} %refs_0_.1) | copy-start | bytes 98308
  0.0 6.7 %copy-start.1 = (s32[1,1,32,2]{2,3,1,0:T(2,128)S(1)}, s32[1,1,32,2]{2,3,1,0:T(2,128)}, u32[]{:S(2)}) copy-start(s32[1,1,32,2]{2,3,1,0:T(2,128)} %param.12) | copy-start | bytes 772
  0.0 6.7 %copy-start.2 = (s32[1,1,32]{2,1,0:T(1,128)S(1)}, s32[1,1,32]{2,1,0:T(1,128)}, u32[]{:S(2)}) copy-start(s32[1,1,32]{2,1,0:T(1,128)} %tile_of_ref.1) | copy-start | bytes 388
  0.0 5.2 %collective-permute-start.1 = (bf16[1,128,128]{2,1,0:T(8,128)(2,1)}, bf16[1,128,128]{2,1,0:T(8,128)(2,1)S(1)}, u32[]{:S(2)}, u32[]{:S(2)}) collective-permute-start(bf16[1,128,128]{2,1,0:T(8,128)(2,1)} %refs_0_.1), channel_id=1, source_target_pairs={{0,12},{4,8},{8,4},{12,0},{1,13},{5,9},{9,5},{13,1},{2,14},{6,10},... | collective-permute-start | bytes 98312 | tf_op jit(solution)/shard_map/ppermute | solution.py:417
  0.2 5.1 %collective-permute-start = (bf16[1,128,128]{2,1,0:T(8,128)(2,1)}, bf16[1,128,128]{2,1,0:T(8,128)(2,1)S(1)}, u32[]{:S(2)}, u32[]{:S(2)}) collective-permute-start(bf16[1,128,128]{2,1,0:T(8,128)(2,1)} %refs_0_.1), channel_id=1, source_target_pairs={{0,8},{4,12},{8,0},{12,4},{1,9},{5,13},{9,1},{13,5},{2,10},{6,14},... | collective-permute-start | bytes 98312 | tf_op jit(solution)/shard_map/ppermute | solution.py:417
  3.5 3.3 %collective-permute-start.2 = (bf16[1,128,128]{2,1,0:T(8,128)(2,1)}, bf16[1,128,128]{2,1,0:T(8,128)(2,1)S(1)}, u32[]{:S(2)}, u32[]{:S(2)}) collective-permute-start(bf16[1,128,128]{2,1,0:T(8,128)(2,1)} %refs_0_.1), channel_id=1, source_target_pairs={{0,4},{4,0},{8,12},{12,8},{1,5},{5,1},{9,13},{13,9},{2,6},{6,2},{1... | collective-permute-start | bytes 98312 | tf_op jit(solution)/shard_map/ppermute | solution.py:417
  3.5 8.0 %copy-start.3 = (f32[400,400]{1,0:T(8,128)S(1)}, f32[400,400]{1,0:T(8,128)}, u32[]{:S(2)}) copy-start(f32[400,400]{1,0:T(8,128)} %coupling_ref.1) | copy-start | bytes 1920004
  3.5 8.0 %copy-start.4 = (s32[256,2]{0,1:T(2,128)S(1)}, s32[256,2]{0,1:T(2,128)}, u32[]{:S(2)}) copy-start(s32[256,2]{0,1:T(2,128)} %param.13) | copy-start | bytes 6148
  3.5 8.0 %copy-start.5 = (f32[4,1,32]{2,1,0:T(1,128)S(1)}, f32[4,1,32]{2,1,0:T(1,128)}, u32[]{:S(2)}) copy-start(f32[4,1,32]{2,1,0:T(1,128)} %gap_ref.1) | copy-start | bytes 1540
  3.5 8.0 %copy-start.6 = (f32[256]{0:T(256)S(1)}, f32[256]{0:T(256)}, u32[]{:S(2)}) copy-start(f32[256]{0:T(256)} %param.17) | copy-start | bytes 3076
  3.5 8.0 %copy-start.7 = (f32[32]{0:T(128)S(1)}, f32[32]{0:T(128)}, u32[]{:S(2)}) copy-start(f32[32]{0:T(128)} %row_ref.1) | copy-start | bytes 388
  8.8 13.1 %collective-permute-start.5 = (bf16[1,16,32,256]{3,2,1,0:T(8,128)(2,1)S(1)}, bf16[1,16,32,256]{3,2,1,0:T(8,128)(2,1)S(1)}, u32[]{:S(2)}, u32[]{:S(2)}) collective-permute-start(bf16[1,16,32,256]{3,2,1,0:T(8,128)(2,1)S(1)} %get-tuple-element.24), channel_id=1, source_target_pairs={{0,12},{4,8},{8,4},{12,0},{1,13},{5,9},{9,5},{13,1},{2,14},{6,10},... | collective-permute-start | bytes 786440 | tf_op jit(solution)/shard_map/ppermute | solution.py:417
  8.9 28.7 %collective-permute-start.3 = (bf16[2,16,32,256]{3,2,1,0:T(8,128)(2,1)S(1)}, bf16[2,16,32,256]{3,2,1,0:T(8,128)(2,1)S(1)}, u32[]{:S(2)}, u32[]{:S(2)}) collective-permute-start(bf16[2,16,32,256]{3,2,1,0:T(8,128)(2,1)S(1)} %get-tuple-element.29), channel_id=1, source_target_pairs={{0,4},{4,0},{8,12},{12,8},{1,5},{5,1},{9,13},{13,9},{2,6},{6,2},{1... | collective-permute-start | bytes 1572872 | tf_op jit(solution)/shard_map/ppermute | solution.py:417
  10.7 22.0 %collective-permute-start.4 = (bf16[1,16,32,256]{3,2,1,0:T(8,128)(2,1)S(1)}, bf16[1,16,32,256]{3,2,1,0:T(8,128)(2,1)S(1)}, u32[]{:S(2)}, u32[]{:S(2)}) collective-permute-start(bf16[1,16,32,256]{3,2,1,0:T(8,128)(2,1)S(1)} %get-tuple-element.30), channel_id=1, source_target_pairs={{0,8},{4,12},{8,0},{12,4},{1,9},{5,13},{9,1},{13,5},{2,10},{6,14},... | collective-permute-start | bytes 786440 | tf_op jit(solution)/shard_map/ppermute | solution.py:417
  21.9 15.6 %collective-permute-start.7 = (bf16[1,16,32,256]{3,2,1,0:T(8,128)(2,1)S(1)}, bf16[1,16,32,256]{3,2,1,0:T(8,128)(2,1)S(1)}, u32[]{:S(2)}, u32[]{:S(2)}) collective-permute-start(bf16[1,16,32,256]{3,2,1,0:T(8,128)(2,1)S(1)} %collective-permute-done.5.refs_3_), channel_id=1, source_target_pairs={{0,1},{1,0},{2,3},{3,2},{4,5},{5,4},{6,7},{7,6},{8,9},{9,8},{10,11... | collective-permute-start | bytes 786440 | tf_op jit(solution)/shard_map/ppermute | solution.py:420
  24.1 23.0 %collective-permute-start.10 = (bf16[1,16,32,256]{3,2,1,0:T(8,128)(2,1)S(1)}, bf16[1,16,32,256]{3,2,1,0:T(8,128)(2,1)S(1)}, u32[]{:S(2)}, u32[]{:S(2)}) collective-permute-start(bf16[1,16,32,256]{3,2,1,0:T(8,128)(2,1)S(1)} %get-tuple-element.34), channel_id=1, source_target_pairs={{0,8},{4,12},{8,0},{12,4},{1,9},{5,13},{9,1},{13,5},{2,10},{6,14},... | collective-permute-start | bytes 786440 | tf_op jit(solution)/shard_map/ppermute | solution.py:417
  24.1 31.6 %collective-permute-start.11 = (bf16[1,16,32,256]{3,2,1,0:T(8,128)(2,1)S(1)}, bf16[1,16,32,256]{3,2,1,0:T(8,128)(2,1)S(1)}, u32[]{:S(2)}, u32[]{:S(2)}) collective-permute-start(bf16[1,16,32,256]{3,2,1,0:T(8,128)(2,1)S(1)} %get-tuple-element.36), channel_id=1, source_target_pairs={{0,12},{4,8},{8,4},{12,0},{1,13},{5,9},{9,5},{13,1},{2,14},{6,10},... | collective-permute-start | bytes 786440 | tf_op jit(solution)/shard_map/ppermute | solution.py:417
  32.7 14.5 %collective-permute-start.9 = (bf16[1,16,32,256]{3,2,1,0:T(8,128)(2,1)S(1)}, bf16[1,16,32,256]{3,2,1,0:T(8,128)(2,1)S(1)}, u32[]{:S(2)}, u32[]{:S(2)}) collective-permute-start(bf16[1,16,32,256]{3,2,1,0:T(8,128)(2,1)S(1)} %collective-permute-done.4.refs_2_), channel_id=1, source_target_pairs={{0,1},{1,0},{2,3},{3,2},{4,5},{5,4},{6,7},{7,6},{8,9},{9,8},{10,11... | collective-permute-start | bytes 786440 | tf_op jit(solution)/shard_map/ppermute | solution.py:420
  37.6 19.4 %collective-permute-start.6 = (bf16[2,16,32,256]{3,2,1,0:T(8,128)(2,1)S(1)}, bf16[2,16,32,256]{3,2,1,0:T(8,128)(2,1)S(1)}, u32[]{:S(2)}, u32[]{:S(2)}) collective-permute-start(bf16[2,16,32,256]{3,2,1,0:T(8,128)(2,1)S(1)} %get-tuple-element.31.refs_0_.refs_1_), channel_id=1, source_target_pairs={{0,1},{1,0},{2,3},{3,2},{4,5},{5,4},{6,7},{7,6},{8,9},{9,8},{10,11... | collective-permute-start | bytes 1572872 | tf_op jit(solution)/shard_map/ppermute | solution.py:420
  37.6 19.4 %collective-permute-start.8 = (bf16[2,16,32,256]{3,2,1,0:T(8,128)(2,1)S(1)}, bf16[2,16,32,256]{3,2,1,0:T(8,128)(2,1)S(1)}, u32[]{:S(2)}, u32[]{:S(2)}) collective-permute-start(bf16[2,16,32,256]{3,2,1,0:T(8,128)(2,1)S(1)} %collective-permute-done.3.refs_1_.refs_2_), channel_id=1, source_target_pairs={{0,1},{1,0},{2,3},{3,2},{4,5},{5,4},{6,7},{7,6},{8,9},{9,8},{10,11... | collective-permute-start | bytes 1572872 | tf_op jit(solution)/shard_map/ppermute | solution.py:420
  47.2 10.7 %collective-permute-start.12 = (bf16[1,16,32,256]{3,2,1,0:T(8,128)(2,1)S(1)}, bf16[1,16,32,256]{3,2,1,0:T(8,128)(2,1)S(1)}, u32[]{:S(2)}, u32[]{:S(2)}) collective-permute-start(bf16[1,16,32,256]{3,2,1,0:T(8,128)(2,1)S(1)} %collective-permute-done.10.refs_3_), channel_id=1, source_target_pairs={{0,1},{1,0},{2,3},{3,2},{4,5},{5,4},{6,7},{7,6},{8,9},{9,8},{10,11... | collective-permute-start | bytes 786440 | tf_op jit(solution)/shard_map/ppermute | solution.py:420
  55.7 2.5 %collective-permute-start.13 = (bf16[1,16,32,256]{3,2,1,0:T(8,128)(2,1)S(1)}, bf16[1,16,32,256]{3,2,1,0:T(8,128)(2,1)S(1)}, u32[]{:S(2)}, u32[]{:S(2)}) collective-permute-start(bf16[1,16,32,256]{3,2,1,0:T(8,128)(2,1)S(1)} %collective-permute-done.11.refs_4_), channel_id=1, source_target_pairs={{0,1},{1,0},{2,3},{3,2},{4,5},{5,4},{6,7},{7,6},{8,9},{9,8},{10,11... | collective-permute-start | bytes 786440 | tf_op jit(solution)/shard_map/ppermute | solution.py:420

commit v17 on v13

--- a/solution.py
+++ b/solution.py
@@ -442,7 +442,7 @@
 
     @functools.cache
     def passed_whole(k):
-        return to_sibling(after(near, (weights, inverse, passed(last, 0))) if k else after(own, near))
+        return to_sibling(after(near, (weights, inverse, passed(last, 0))) if k else after(own, landed(last, 0)))
 
     chunk_pieces = []
     for c in range(chunks - 1, -1, -1):

time: 60.8 us -> 60.8 us (level)
  no operation moved by 1% of the time
where the time goes in v17:
time: 60.8 us; the launch traced here: 60.6 us
  waiting for transfers between devices  30.4 us (50%)
  starting transfers between devices  19.3 us (32%)
  Pallas kernels  10.6 us (17%)
    ppermute x8, waiting for transfers between devices, to_owner(): return lax.ppermute(value, 'pair', [(o, o ^ k) for o in range(owners)])  30.2 us
    ppermute x6, starting transfers between devices, to_sibling(): return lax.ppermute(value, 'sub', [(0, 1), (1, 0)])  12.4 us
    ppermute x8, starting transfers between devices, to_owner(): return lax.ppermute(value, 'pair', [(o, o ^ k) for o in range(owners)])  6.95 us
    pallas_call x1, Pallas kernels, make_weights(): pl.pallas_call(weights_kernel, in_specs=[vmem, vmem, vmem, smem, smem, vm...  3.52 us
    pallas_call x2, Pallas kernels, finish(): pl.pallas_call(kernel, in_specs=in_specs + [vmem] * len(pieces), out_spec...  3.36 us
    pallas_call x1, Pallas kernels, dress(): pl.pallas_call(functools.partial(dress_kernel, owners, rows, groups), in_...  2.1 us
    pallas_call x1, Pallas kernels, hold(): pl.pallas_call(hold_kernel, in_specs=[anywhere], out_specs=[anywhere, pl....  1.64 us
  transfers between devices with their start and end apart: 14, of which 7 were waited for; matrix products, arithmetic and copies ran while one was open for 0% of the time, Pallas kernels for 10%

profile of v17, /device:TPU:23, one launch (start us, length us, event | category | flops | bytes accessed | tf_op | source)
XLA Modules:
  0.0 60.6 jit_solution(9501830313800103754)
XLA Ops:
  0.0 0.0 copy-start
  0.0 0.0 copy-start.1
  0.0 0.0 copy-start.2
  0.0 0.2 collective-permute-start.1
  0.2 3.2 %collective-permute-start = (bf16[1,128,128]{2,1,0:T(8,128)(2,1)}, bf16[1,128,128]{2,1,0:T(8,128)(2,1)S(1)}, u32[]{:S(2)}, u32[]{:S(2)}) collective-permute-start(bf16[1,128,128]{2,1,0:T(8,128)(2,1)} %refs_0_.1), channel_id=1, source_target_pairs={{0,8},{4,12},{8,0},{12,4},{1,9},{5,13},{9,1},{13,5},{2,10},{6,14},... | collective-permute-start | bytes 98312 | tf_op jit(solution)/shard_map/ppermute | solution.py:412
  3.5 0.0 collective-permute-start.2
  3.5 0.1 pad_add_fusion.place_ref
  3.5 0.0 copy-start.3
  3.5 0.0 copy-start.4
  3.5 0.0 copy-start.7
  3.6 1.6 %shard_map.91 = (bf16[1,1,32,128,256]{4,3,2,1,0:T(8,128)(2,1)S(1)}, bf16[256,256]{1,0:T(8,128)(2,1)S(1)}) custom-call(bf16[1,1,32,128,256]{4,3,2,1,0:T(8,128)(2,1)} %lam_ref.1), custom_call_target="tpu_custom_call" | custom-call | bytes 4194304 | tf_op jit(solution)/shard_map/pallas_call | solution.py:154
  5.2 0.0 collective-permute-done.1.refs_2_
  5.2 0.1 collective-permute-done.refs_1_
  5.3 1.4 %collective-permute-done.2.refs_3_ = bf16[1,128,128]{2,1,0:T(8,128)(2,1)S(1)} collective-permute-done((bf16[1,128,128]{2,1,0:T(8,128)(2,1)}, bf16[1,128,128]{2,1,0:T(8,128)(2,1)S(1)}, u32[]{:S(2)}, u32[]{:S(2)}) %collective-permute-start.2) | collective-permute-done | bytes 32800 | tf_op jit(solution)/shard_map/ppermute | solution.py:412
  6.7 0.0 copy-done
  6.7 0.0 copy-done.1
  6.7 0.0 copy-done.2
  6.7 2.1 %shard_map.92 = (bf16[1,16,32,256]{3,2,1,0:T(8,128)(2,1)S(1)}, bf16[1,16,32,256]{3,2,1,0:T(8,128)(2,1)S(1)}, bf16[1,16,32,256]{3,2,1,0:T(8,128)(2,1)S(1)}, bf16[...) custom-call(s32[2]{0:T(128)S(1)} %pad_add_fusion.place_ref, ...), custom_call_target="tpu_custom_call" | custom-call | flops 268435456 | bytes 3145728 | tf_op jit(solution)/shard_map/pallas_call | solution.py:272
  8.8 0.1 collective-permute-start.5
  8.9 1.8 %collective-permute-start.3 = (bf16[2,16,32,256]{3,2,1,0:T(8,128)(2,1)S(1)}, bf16[2,16,32,256]{3,2,1,0:T(8,128)(2,1)S(1)}, u32[]{:S(2)}, u32[]{:S(2)}) collective-permute-start(bf16[2,16,32,256]{3,2,1,0:T(8,128)(2,1)S(1)} %get-tuple-element.29), channel_id=1, source_target_pairs={{0,4},{4,0},{8,12},{12,8},{1,5},{5,1},{9,13},{13,9},{2,6},{6,2},{1... | collective-permute-start | bytes 1572872 | tf_op jit(solution)/shard_map/ppermute | solution.py:412
  10.7 0.9 %collective-permute-start.4 = (bf16[1,16,32,256]{3,2,1,0:T(8,128)(2,1)S(1)}, bf16[1,16,32,256]{3,2,1,0:T(8,128)(2,1)S(1)}, u32[]{:S(2)}, u32[]{:S(2)}) collective-permute-start(bf16[1,16,32,256]{3,2,1,0:T(8,128)(2,1)S(1)} %get-tuple-element.30), channel_id=1, source_target_pairs={{0,8},{4,12},{8,0},{12,4},{1,9},{5,13},{9,1},{13,5},{2,10},{6,14},... | collective-permute-start | bytes 786440 | tf_op jit(solution)/shard_map/ppermute | solution.py:412
  11.6 0.0 copy-done.3
  11.6 0.0 copy-done.4
  11.6 0.0 copy-done.5
  11.6 0.0 copy-done.6
  11.6 0.0 copy-done.7
  11.6 3.5 %shard_map.93 = (bf16[128,256]{1,0:T(8,128)(2,1)S(1)}, f32[32,128,256]{2,1,0:T(8,128)S(1)}) custom-call(s32[2,256]{1,0:T(2,128)S(1)} %bitcast.6, f32[400,400]{1,0:T(8,128)S(1)} %copy-done.3, f32[4,1,32]{2,1,0:T(1,128)S(1)} %copy-done.5, s32[2]{0:T(128)S(1)} %pad_add_fusion.place_ref, f32[32]{0:T(128)S(1)} %copy-done.7, f32[1,256]{1,0:T(1,128)S(1)} %bitcast.7), custom_call_target="tpu_custom_call" | custom-call | flops 491520000 | bytes 640000 | tf_op jit(solution)/shard_map/pallas_call | solution.py:207
  15.1 6.9 %collective-permute-done.5.refs_3_ = bf16[1,16,32,256]{3,2,1,0:T(8,128)(2,1)S(1)} collective-permute-done((bf16[1,16,32,256]{3,2,1,0:T(8,128)(2,1)S(1)}, bf16[1,16,32,256]{3,2,1,0:T(8,128)(2,1)S(1)}, u32[]{:S(2)}, u32[]{:S(2)}) %collective-permute-start.5) | collective-permute-done | bytes 262176 | tf_op jit(solution)/shard_map/ppermute | solution.py:412
  22.0 2.1 %collective-permute-start.7 = (bf16[1,16,32,256]{3,2,1,0:T(8,128)(2,1)S(1)}, bf16[1,16,32,256]{3,2,1,0:T(8,128)(2,1)S(1)}, u32[]{:S(2)}, u32[]{:S(2)}) collective-permute-start(bf16[1,16,32,256]{3,2,1,0:T(8,128)(2,1)S(1)} %collective-permute-done.5.refs_3_), channel_id=1, source_target_pairs={{0,1},{1,0},{2,3},{3,2},{4,5},{5,4},{6,7},{7,6},{8,9},{9,8},{10,11... | collective-permute-start | bytes 786440 | tf_op jit(solution)/shard_map/ppermute | solution.py:415
  24.1 0.0 collective-permute-start.10
  24.1 0.8 %collective-permute-start.11 = (bf16[1,16,32,256]{3,2,1,0:T(8,128)(2,1)S(1)}, bf16[1,16,32,256]{3,2,1,0:T(8,128)(2,1)S(1)}, u32[]{:S(2)}, u32[]{:S(2)}) collective-permute-start(bf16[1,16,32,256]{3,2,1,0:T(8,128)(2,1)S(1)} %get-tuple-element.36), channel_id=1, source_target_pairs={{0,12},{4,8},{8,4},{12,0},{1,13},{5,9},{9,5},{13,1},{2,14},{6,10},... | collective-permute-start | bytes 786440 | tf_op jit(solution)/shard_map/ppermute | solution.py:412
  24.9 7.7 %collective-permute-done.4.refs_2_ = bf16[1,16,32,256]{3,2,1,0:T(8,128)(2,1)S(1)} collective-permute-done((bf16[1,16,32,256]{3,2,1,0:T(8,128)(2,1)S(1)}, bf16[1,16,32,256]{3,2,1,0:T(8,128)(2,1)S(1)}, u32[]{:S(2)}, u32[]{:S(2)}) %collective-permute-start.4) | collective-permute-done | bytes 262176 | tf_op jit(solution)/shard_map/ppermute | solution.py:412
  32.7 4.9 %collective-permute-start.9 = (bf16[1,16,32,256]{3,2,1,0:T(8,128)(2,1)S(1)}, bf16[1,16,32,256]{3,2,1,0:T(8,128)(2,1)S(1)}, u32[]{:S(2)}, u32[]{:S(2)}) collective-permute-start(bf16[1,16,32,256]{3,2,1,0:T(8,128)(2,1)S(1)} %collective-permute-done.4.refs_2_), channel_id=1, source_target_pairs={{0,1},{1,0},{2,3},{3,2},{4,5},{5,4},{6,7},{7,6},{8,9},{9,8},{10,11... | collective-permute-start | bytes 786440 | tf_op jit(solution)/shard_map/ppermute | solution.py:415
  37.6 0.0 collective-permute-done.7.refs_7_
  37.6 0.0 collective-permute-start.6
  37.6 0.0 collective-permute-done.3.refs_1_.refs_2_
  37.6 0.5 collective-permute-start.8
  38.1 9.1 %collective-permute-done.10.refs_3_ = bf16[1,16,32,256]{3,2,1,0:T(8,128)(2,1)S(1)} collective-permute-done((bf16[1,16,32,256]{3,2,1,0:T(8,128)(2,1)S(1)}, bf16[1,16,32,256]{3,2,1,0:T(8,128)(2,1)S(1)}, u32[]{:S(2)}, u32[]{:S(2)}) %collective-permute-start.10) | collective-permute-done | bytes 262176 | tf_op jit(solution)/shard_map/ppermute | solution.py:412
  47.2 0.0 collective-permute-done.9.refs_6_
  47.2 3.5 %collective-permute-start.12 = (bf16[1,16,32,256]{3,2,1,0:T(8,128)(2,1)S(1)}, bf16[1,16,32,256]{3,2,1,0:T(8,128)(2,1)S(1)}, u32[]{:S(2)}, u32[]{:S(2)}) collective-permute-start(bf16[1,16,32,256]{3,2,1,0:T(8,128)(2,1)S(1)} %collective-permute-done.10.refs_3_), channel_id=1, source_target_pairs={{0,1},{1,0},{2,3},{3,2},{4,5},{5,4},{6,7},{7,6},{8,9},{9,8},{10,11... | collective-permute-start | bytes 786440 | tf_op jit(solution)/shard_map/ppermute | solution.py:415
  50.7 5.0 %collective-permute-done.11.refs_4_ = bf16[1,16,32,256]{3,2,1,0:T(8,128)(2,1)S(1)} collective-permute-done((bf16[1,16,32,256]{3,2,1,0:T(8,128)(2,1)S(1)}, bf16[1,16,32,256]{3,2,1,0:T(8,128)(2,1)S(1)}, u32[]{:S(2)}, u32[]{:S(2)}) %collective-permute-start.11) | collective-permute-done | bytes 262176 | tf_op jit(solution)/shard_map/ppermute | solution.py:412
  55.7 1.3 %collective-permute-start.13 = (bf16[1,16,32,256]{3,2,1,0:T(8,128)(2,1)S(1)}, bf16[1,16,32,256]{3,2,1,0:T(8,128)(2,1)S(1)}, u32[]{:S(2)}, u32[]{:S(2)}) collective-permute-start(bf16[1,16,32,256]{3,2,1,0:T(8,128)(2,1)S(1)} %collective-permute-done.11.refs_4_), channel_id=1, source_target_pairs={{0,1},{1,0},{2,3},{3,2},{4,5},{5,4},{6,7},{7,6},{8,9},{9,8},{10,11... | collective-permute-start | bytes 786440 | tf_op jit(solution)/shard_map/ppermute | solution.py:415
  57.0 0.0 collective-permute-done.6.refs_4_.refs_5_
  57.0 0.0 collective-permute-done.8.refs_5_.refs_6_
  57.0 0.9 %shard_map.94.refs_0_ = bf16[8,16,16,256]{3,2,1,0:T(8,128)(2,1)S(1)} custom-call(bf16[256,256]{1,0:T(8,128)(2,1)S(1)} %get-tuple-element.22.refs_5_.swap_ref, bf16[128,256]{1,0:T(8,128)(2,1)S(1)} %get-tuple-element.26.w_ref, f32[32,128,256]{2,1,0:T(8,128)S(1)} %get-tuple-element.27.inverse_ref, ...), custom_call_target="tpu_custom_call" | custom-call | tf_op jit(solution)/shard_map/pallas_call | solution.py:381
  57.9 0.0 collective-permute-done.12.refs_7_
  57.9 0.2 collective-permute-done.13.refs_8_
  58.2 2.5 %shard_map.95 = bf16[4,1,32,32,256]{4,3,2,1,0:T(8,128)(2,1)} custom-call(bf16[256,256]{1,0:T(8,128)(2,1)S(1)} %get-tuple-element.22.refs_5_.swap_ref, bf16[128,256]{1,0:T(8,128)(2,1)S(1)} %get-tuple-element.26.w_ref, f32[32,128,256]{2,1,0:T(8,128)S(1)} %get-tuple-element.27.inverse_ref, s32[2]{0:T(128)S(1)} %pad_add_fusion.place_ref, ...), custom_call_target="tpu_custom_call" | custom-call | tf_op jit(solution)/shard_map/pallas_call | solution.py:381
  (2 shorter events, 0.0 us)
Async XLA Ops:
  0.0 6.7 %copy-start = (bf16[1,128,128]{2,1,0:T(8,128)(2,1)S(1)}, bf16[1,128,128]{2,1,0:T(8,128)(2,1)}, u32[]{:S(2)}) copy-start(bf16[1,128,128]{2,1,0:T(8,128)(2,1)} %refs_0_.1) | copy-start | bytes 98308
  0.0 6.7 %copy-start.1 = (s32[1,1,32,2]{2,3,1,0:T(2,128)S(1)}, s32[1,1,32,2]{2,3,1,0:T(2,128)}, u32[]{:S(2)}) copy-start(s32[1,1,32,2]{2,3,1,0:T(2,128)} %param.12) | copy-start | bytes 772
  0.0 6.7 %copy-start.2 = (s32[1,1,32]{2,1,0:T(1,128)S(1)}, s32[1,1,32]{2,1,0:T(1,128)}, u32[]{:S(2)}) copy-start(s32[1,1,32]{2,1,0:T(1,128)} %tile_of_ref.1) | copy-start | bytes 388
  0.0 5.2 %collective-permute-start.1 = (bf16[1,128,128]{2,1,0:T(8,128)(2,1)}, bf16[1,128,128]{2,1,0:T(8,128)(2,1)S(1)}, u32[]{:S(2)}, u32[]{:S(2)}) collective-permute-start(bf16[1,128,128]{2,1,0:T(8,128)(2,1)} %refs_0_.1), channel_id=1, source_target_pairs={{0,12},{4,8},{8,4},{12,0},{1,13},{5,9},{9,5},{13,1},{2,14},{6,10},... | collective-permute-start | bytes 98312 | tf_op jit(solution)/shard_map/ppermute | solution.py:412
  0.2 5.1 %collective-permute-start = (bf16[1,128,128]{2,1,0:T(8,128)(2,1)}, bf16[1,128,128]{2,1,0:T(8,128)(2,1)S(1)}, u32[]{:S(2)}, u32[]{:S(2)}) collective-permute-start(bf16[1,128,128]{2,1,0:T(8,128)(2,1)} %refs_0_.1), channel_id=1, source_target_pairs={{0,8},{4,12},{8,0},{12,4},{1,9},{5,13},{9,1},{13,5},{2,10},{6,14},... | collective-permute-start | bytes 98312 | tf_op jit(solution)/shard_map/ppermute | solution.py:412
  3.5 3.3 %collective-permute-start.2 = (bf16[1,128,128]{2,1,0:T(8,128)(2,1)}, bf16[1,128,128]{2,1,0:T(8,128)(2,1)S(1)}, u32[]{:S(2)}, u32[]{:S(2)}) collective-permute-start(bf16[1,128,128]{2,1,0:T(8,128)(2,1)} %refs_0_.1), channel_id=1, source_target_pairs={{0,4},{4,0},{8,12},{12,8},{1,5},{5,1},{9,13},{13,9},{2,6},{6,2},{1... | collective-permute-start | bytes 98312 | tf_op jit(solution)/shard_map/ppermute | solution.py:412
  3.5 8.0 %copy-start.3 = (f32[400,400]{1,0:T(8,128)S(1)}, f32[400,400]{1,0:T(8,128)}, u32[]{:S(2)}) copy-start(f32[400,400]{1,0:T(8,128)} %coupling_ref.1) | copy-start | bytes 1920004
  3.5 8.0 %copy-start.4 = (s32[256,2]{0,1:T(2,128)S(1)}, s32[256,2]{0,1:T(2,128)}, u32[]{:S(2)}) copy-start(s32[256,2]{0,1:T(2,128)} %param.13) | copy-start | bytes 6148
  3.5 8.0 %copy-start.5 = (f32[4,1,32]{2,1,0:T(1,128)S(1)}, f32[4,1,32]{2,1,0:T(1,128)}, u32[]{:S(2)}) copy-start(f32[4,1,32]{2,1,0:T(1,128)} %gap_ref.1) | copy-start | bytes 1540
  3.5 8.0 %copy-start.6 = (f32[256]{0:T(256)S(1)}, f32[256]{0:T(256)}, u32[]{:S(2)}) copy-start(f32[256]{0:T(256)} %param.17) | copy-start | bytes 3076
  3.5 8.0 %copy-start.7 = (f32[32]{0:T(128)S(1)}, f32[32]{0:T(128)}, u32[]{:S(2)}) copy-start(f32[32]{0:T(128)} %row_ref.1) | copy-start | bytes 388
  8.8 13.1 %collective-permute-start.5 = (bf16[1,16,32,256]{3,2,1,0:T(8,128)(2,1)S(1)}, bf16[1,16,32,256]{3,2,1,0:T(8,128)(2,1)S(1)}, u32[]{:S(2)}, u32[]{:S(2)}) collective-permute-start(bf16[1,16,32,256]{3,2,1,0:T(8,128)(2,1)S(1)} %get-tuple-element.24), channel_id=1, source_target_pairs={{0,12},{4,8},{8,4},{12,0},{1,13},{5,9},{9,5},{13,1},{2,14},{6,10},... | collective-permute-start | bytes 786440 | tf_op jit(solution)/shard_map/ppermute | solution.py:412
  8.9 28.7 %collective-permute-start.3 = (bf16[2,16,32,256]{3,2,1,0:T(8,128)(2,1)S(1)}, bf16[2,16,32,256]{3,2,1,0:T(8,128)(2,1)S(1)}, u32[]{:S(2)}, u32[]{:S(2)}) collective-permute-start(bf16[2,16,32,256]{3,2,1,0:T(8,128)(2,1)S(1)} %get-tuple-element.29), channel_id=1, source_target_pairs={{0,4},{4,0},{8,12},{12,8},{1,5},{5,1},{9,13},{13,9},{2,6},{6,2},{1... | collective-permute-start | bytes 1572872 | tf_op jit(solution)/shard_map/ppermute | solution.py:412
  10.7 21.9 %collective-permute-start.4 = (bf16[1,16,32,256]{3,2,1,0:T(8,128)(2,1)S(1)}, bf16[1,16,32,256]{3,2,1,0:T(8,128)(2,1)S(1)}, u32[]{:S(2)}, u32[]{:S(2)}) collective-permute-start(bf16[1,16,32,256]{3,2,1,0:T(8,128)(2,1)S(1)} %get-tuple-element.30), channel_id=1, source_target_pairs={{0,8},{4,12},{8,0},{12,4},{1,9},{5,13},{9,1},{13,5},{2,10},{6,14},... | collective-permute-start | bytes 786440 | tf_op jit(solution)/shard_map/ppermute | solution.py:412
  22.0 15.6 %collective-permute-start.7 = (bf16[1,16,32,256]{3,2,1,0:T(8,128)(2,1)S(1)}, bf16[1,16,32,256]{3,2,1,0:T(8,128)(2,1)S(1)}, u32[]{:S(2)}, u32[]{:S(2)}) collective-permute-start(bf16[1,16,32,256]{3,2,1,0:T(8,128)(2,1)S(1)} %collective-permute-done.5.refs_3_), channel_id=1, source_target_pairs={{0,1},{1,0},{2,3},{3,2},{4,5},{5,4},{6,7},{7,6},{8,9},{9,8},{10,11... | collective-permute-start | bytes 786440 | tf_op jit(solution)/shard_map/ppermute | solution.py:415
  24.1 23.0 %collective-permute-start.10 = (bf16[1,16,32,256]{3,2,1,0:T(8,128)(2,1)S(1)}, bf16[1,16,32,256]{3,2,1,0:T(8,128)(2,1)S(1)}, u32[]{:S(2)}, u32[]{:S(2)}) collective-permute-start(bf16[1,16,32,256]{3,2,1,0:T(8,128)(2,1)S(1)} %get-tuple-element.34), channel_id=1, source_target_pairs={{0,8},{4,12},{8,0},{12,4},{1,9},{5,13},{9,1},{13,5},{2,10},{6,14},... | collective-permute-start | bytes 786440 | tf_op jit(solution)/shard_map/ppermute | solution.py:412
  24.1 31.6 %collective-permute-start.11 = (bf16[1,16,32,256]{3,2,1,0:T(8,128)(2,1)S(1)}, bf16[1,16,32,256]{3,2,1,0:T(8,128)(2,1)S(1)}, u32[]{:S(2)}, u32[]{:S(2)}) collective-permute-start(bf16[1,16,32,256]{3,2,1,0:T(8,128)(2,1)S(1)} %get-tuple-element.36), channel_id=1, source_target_pairs={{0,12},{4,8},{8,4},{12,0},{1,13},{5,9},{9,5},{13,1},{2,14},{6,10},... | collective-permute-start | bytes 786440 | tf_op jit(solution)/shard_map/ppermute | solution.py:412
  32.7 14.5 %collective-permute-start.9 = (bf16[1,16,32,256]{3,2,1,0:T(8,128)(2,1)S(1)}, bf16[1,16,32,256]{3,2,1,0:T(8,128)(2,1)S(1)}, u32[]{:S(2)}, u32[]{:S(2)}) collective-permute-start(bf16[1,16,32,256]{3,2,1,0:T(8,128)(2,1)S(1)} %collective-permute-done.4.refs_2_), channel_id=1, source_target_pairs={{0,1},{1,0},{2,3},{3,2},{4,5},{5,4},{6,7},{7,6},{8,9},{9,8},{10,11... | collective-permute-start | bytes 786440 | tf_op jit(solution)/shard_map/ppermute | solution.py:415
  37.6 19.4 %collective-permute-start.6 = (bf16[2,16,32,256]{3,2,1,0:T(8,128)(2,1)S(1)}, bf16[2,16,32,256]{3,2,1,0:T(8,128)(2,1)S(1)}, u32[]{:S(2)}, u32[]{:S(2)}) collective-permute-start(bf16[2,16,32,256]{3,2,1,0:T(8,128)(2,1)S(1)} %get-tuple-element.31.refs_0_.refs_1_), channel_id=1, source_target_pairs={{0,1},{1,0},{2,3},{3,2},{4,5},{5,4},{6,7},{7,6},{8,9},{9,8},{10,11... | collective-permute-start | bytes 1572872 | tf_op jit(solution)/shard_map/ppermute | solution.py:415
  37.6 19.4 %collective-permute-start.8 = (bf16[2,16,32,256]{3,2,1,0:T(8,128)(2,1)S(1)}, bf16[2,16,32,256]{3,2,1,0:T(8,128)(2,1)S(1)}, u32[]{:S(2)}, u32[]{:S(2)}) collective-permute-start(bf16[2,16,32,256]{3,2,1,0:T(8,128)(2,1)S(1)} %collective-permute-done.3.refs_1_.refs_2_), channel_id=1, source_target_pairs={{0,1},{1,0},{2,3},{3,2},{4,5},{5,4},{6,7},{7,6},{8,9},{9,8},{10,11... | collective-permute-start | bytes 1572872 | tf_op jit(solution)/shard_map/ppermute | solution.py:415
  47.2 10.7 %collective-permute-start.12 = (bf16[1,16,32,256]{3,2,1,0:T(8,128)(2,1)S(1)}, bf16[1,16,32,256]{3,2,1,0:T(8,128)(2,1)S(1)}, u32[]{:S(2)}, u32[]{:S(2)}) collective-permute-start(bf16[1,16,32,256]{3,2,1,0:T(8,128)(2,1)S(1)} %collective-permute-done.10.refs_3_), channel_id=1, source_target_pairs={{0,1},{1,0},{2,3},{3,2},{4,5},{5,4},{6,7},{7,6},{8,9},{9,8},{10,11... | collective-permute-start | bytes 786440 | tf_op jit(solution)/shard_map/ppermute | solution.py:415
  55.7 2.4 %collective-permute-start.13 = (bf16[1,16,32,256]{3,2,1,0:T(8,128)(2,1)S(1)}, bf16[1,16,32,256]{3,2,1,0:T(8,128)(2,1)S(1)}, u32[]{:S(2)}, u32[]{:S(2)}) collective-permute-start(bf16[1,16,32,256]{3,2,1,0:T(8,128)(2,1)S(1)} %collective-permute-done.11.refs_4_), channel_id=1, source_target_pairs={{0,1},{1,0},{2,3},{3,2},{4,5},{5,4},{6,7},{7,6},{8,9},{9,8},{10,11... | collective-permute-start | bytes 786440 | tf_op jit(solution)/shard_map/ppermute | solution.py:415
